TPU v7x, 32 devices: a whole 2x2x4 slice. The times are simulated.
32 devices in a mesh: src: 4 (over y, x), ch: 8 (over z, core).
Axes of the slice: x: 2, y: 2, z: 4, core: 2. Of those that a mesh axis runs over, the one named last changes fastest.
Arguments:
- dry_signal: bfloat16 [64, 40960], P(('src', 'ch')), may hold values from -6 to 6
- room_spectra: bfloat16 [64, 8, 64, 2, 1024], P('src', None, 'ch'), may hold values from -0.1875 to 0.1875
- render_slot: int32 [64], P('src'), may hold values from 0 to 63, as said below
- decoder: bfloat16 [64, 1024], replicated, may hold values from -0.75 to 0.75
Outputs:
- speakers: bfloat16 [32768, 1024], P(('src', 'ch'))
Inputs may be any that keep to these rules, and one draw needn't show every extreme that they name: render_slot is a permutation that keeps each group: sources g * 16 to (g + 1) * 16 - 1 are mapped onto the rows of that same range, each row once.
All inputs are finite; a program needn't handle non-finite values.
Results may differ from a plain program's by a relative error of at most 0.018.
Values may be sent and summed in bfloat16 or wider, within the bound.
No kernel may reach another device: no remote copies, remote signals or barrier semaphores. Data moves between devices by JAX's collectives and lax.ppermute only.
A program may use at most 128 MiB of HBM per device.

v0:
```python
import math

import jax
import jax.numpy as jnp
from jax import lax
from jax.sharding import PartitionSpec as P


def make_tables(block_len):
    size = 2 * block_len
    rows = jnp.arange(size, dtype=jnp.int32)[:, None]
    bins = jnp.arange(block_len, dtype=jnp.int32)[None, :]
    phase = (rows * bins % size).astype(jnp.float32) * (2.0 * math.pi / size)
    signs = (1 - 2 * (rows % 2)).astype(jnp.float32)
    fwd_imag = jnp.where(bins == 0, signs, -jnp.sin(phase))
    fwd_real = jnp.cos(phase)
    freq = jnp.arange(block_len, dtype=jnp.int32)[:, None]
    times = jnp.arange(block_len, dtype=jnp.int32)[None, :] + block_len
    angle = (freq * times % size).astype(jnp.float32) * (2.0 * math.pi / size)
    weight = jnp.where(freq == 0, 1.0, 2.0).astype(jnp.float32)
    inv_real = weight * jnp.cos(angle) / size
    tsign = (1 - 2 * (times % 2)).astype(jnp.float32) / size
    inv_imag = jnp.where(freq == 0, tsign, -2.0 * jnp.sin(angle) / size)
    return (fwd_real.astype(jnp.bfloat16), fwd_imag.astype(jnp.bfloat16), inv_real, inv_imag)


def per_device(dry_signal, room_spectra, render_slot, decoder):
    block_len = room_spectra.shape[-1]
    part_count = room_spectra.shape[1]
    source_rows = dry_signal.shape[0]
    block_count = dry_signal.shape[1] // block_len
    out_blocks = block_count - part_count
    channels = room_spectra.shape[2]
    fwd_real, fwd_imag, inv_real, inv_imag = make_tables(block_len)
    slot_local = render_slot % room_spectra.shape[0]
    bin_index = jnp.arange(block_len, dtype=jnp.int32)
    first_bin = bin_index == 0
    resp_real_all = jnp.take(room_spectra[:, :, :, 0, :], slot_local, axis=0)
    resp_imag_all = jnp.take(room_spectra[:, :, :, 1, :], slot_local, axis=0)

    def transform(earlier, later, upper, lower):
        left = jnp.einsum("sfn,nk->sfk", earlier, upper, preferred_element_type=jnp.float32)
        right = jnp.einsum("sfn,nk->sfk", later, lower, preferred_element_type=jnp.float32)
        return (left + right).astype(jnp.bfloat16)

    empty = jnp.zeros((channels, out_blocks, block_len), jnp.float32)
    samples_own = dry_signal.reshape(source_rows, block_count, block_len)
    earlier = samples_own[:, :-1]
    later = samples_own[:, 1:]
    spec_real = transform(earlier, later, fwd_real[:block_len], fwd_real[block_len:])
    spec_imag = transform(earlier, later, fwd_imag[:block_len], fwd_imag[block_len:])
    spectra_real = lax.all_gather(spec_real, "ch", axis=0, tiled=True)
    spectra_imag = lax.all_gather(spec_imag, "ch", axis=0, tiled=True)
    mix_real = empty
    mix_imag = empty
    for p in range(part_count):
        start = part_count - 1 - p
        accumulate_spec_real = spectra_real[:, start : start + out_blocks].astype(jnp.float32)[
            :, None
        ]
        accumulate_spec_imag = spectra_imag[:, start : start + out_blocks].astype(jnp.float32)[
            :, None
        ]
        resp_real = resp_real_all[:, p].astype(jnp.float32)[:, :, None]
        resp_imag = resp_imag_all[:, p].astype(jnp.float32)[:, :, None]
        resp_masked = jnp.where(first_bin, 0.0, resp_imag)
        resp_mixed = jnp.where(first_bin, resp_imag, resp_real)
        mix_real = mix_real + jnp.sum(
            accumulate_spec_real * resp_real - accumulate_spec_imag * resp_masked, axis=0
        )
        mix_imag = mix_imag + jnp.sum(
            accumulate_spec_real * resp_masked + accumulate_spec_imag * resp_mixed, axis=0
        )
    mix_real, mix_imag = (mix_real, mix_imag)
    first = jnp.einsum("cbk,km->cbm", mix_real, inv_real)
    second = jnp.einsum("cbk,km->cbm", mix_imag, inv_imag)
    partial_sum = first + second
    sh_sum = lax.psum_scatter(
        partial_sum.astype(jnp.bfloat16), "src", scatter_dimension=1, tiled=True
    ).astype(jnp.float32)
    sh_signal = sh_sum.reshape(channels, -1).astype(jnp.bfloat16)
    gathered = lax.all_to_all(sh_signal, "ch", split_axis=1, concat_axis=0, tiled=True)
    decoded = lax.dot_general(
        gathered, decoder, (((0,), (0,)), ((), ())), preferred_element_type=jnp.float32
    )
    return decoded.astype(jnp.bfloat16)


def solution(mesh):
    return jax.shard_map(
        per_device,
        mesh=mesh,
        in_specs=(P(("src", "ch"), None), P("src", None, "ch", None, None), P("src"), P()),
        out_specs=P(("src", "ch"), None),
        check_vma=False,
    )
```

profile of v0, /device:TPU:0, one launch (start us, length us, event | category | flops | bytes accessed | tf_op | source)
XLA Modules:
  0.0 298.0 jit_solution(15923750038611128057)
XLA Ops:
  6.6 1.0 copy.71
  7.5 32.2 %select_convert_fusion = bf16[2048,1024]{1,0:T(8,128)(2,1)S(1)} fusion(bf16[2048]{0:T(1024)(128)(2,1)S(1)} %fusion.74, pred[1024]{0:T(1024)(128)(4,1)S(1)} %iota_compare_fusion), kind=kLoop, calls=%fused_computation.24 | loop fusion | flops 33554432 | bytes 4199424 | tf_op jit(solution)/shard_map/convert_element_type | solution.py:24
  39.8 0.5 fusion.22
  40.3 1.2 fusion.44
  41.4 0.0 all-gather.5.cloned.1.call-update
  41.4 0.0 all-gather.3.cloned.1.call-start
  41.5 31.0 %cosine_convert_fusion = bf16[2048,1024]{1,0:T(8,128)(2,1)S(1)} fusion(), kind=kLoop, calls=%fused_computation.25 | loop fusion | flops 31457280 | bytes 4194304 | tf_op jit(solution)/shard_map/convert_element_type | solution.py:24
  72.5 0.5 fusion.24
  73.0 1.2 fusion.43
  74.2 0.0 all-gather.3.cloned.1.call-update
  74.2 0.3 all-reduce.3.cloned.1.call-start
  74.5 0.0 copy-start.33
  74.5 13.7 %fusion.94 = (bf16[16,8,8,1,1024]{4,3,2,1,0:T(2,128)(2,1)S(1)}, bf16[16,8,8,1,1024]{4,3,2,1,0:T(2,128)(2,1)S(1)}) fusion(bf16[16,8,8,2,1024]{4,3,2,1,0:T(2,128)(2,1)} %param.7), kind=kLoop, calls=%fused_computation.187 | loop fusion | bytes 8388608 | tf_op jit(solution)/shard_map/slice | solution.py:38
  88.2 0.0 copy-done.33
  88.2 3.7 %copy_bitcast_fusion = (bf16[16,8,8,1024]{3,2,1,0:T(8,128)(2,1)}, bf16[16,8,8,1024]{3,2,1,0:T(8,128)(2,1)}) fusion(bf16[16,8,8,1,1024]{4,3,2,1,0:T(2,128)(2,1)S(1)} %get-tuple-element.33, bf16[16,8,8,1,1024]{4,3,2,1,0:T(2,128)(2,1)S(1)} %get-tuple-element.32), kind=kLoop, calls=%fused_computation.56 | loop fusion | bytes 8388608 | tf_op jit(solution)/shard_map/squeeze | solution.py:39
  91.9 2.3 gather_fusion
  94.2 3.6 %gather_fusion.1 = bf16[16,8,8,1024]{3,2,1,0:T(8,128)(2,1)} fusion(bf16[16,8,8,1024]{3,2,1,0:T(8,128)(2,1)} %get-tuple-element.66, s32[1024]{0:T(1024)S(1)} %pad_clamp_fusion), kind=kCustom, calls=%fused_computation.1.clone | custom fusion | bytes 4194368 | tf_op jit(solution)/shard_map/jit(_take)/gather | solution.py:39
  97.8 1.9 copy_select_fusion
  99.7 1.6 convert_select_fusion.13
  101.3 0.3 broadcast_select_fusion
  101.6 2.0 fusion.65
  103.6 2.4 convert_select_fusion.12
  106.1 11.2 %slice_convert_fusion.12 = (f32[16,32,1024]{2,1,0:T(8,128)}, f32[16,32,1024]{2,1,0:T(8,128)S(1)}, f32[16,32,1024]{2,1,0:T(8,128)}, f32[16,32,1024]{2,1,0:T(8,128...) fusion(bf16[16,39,1024]{2,1,0:T(8,128)(2,1)} %all-gather.5.cloned.1, ...), kind=kLoop, calls=%fused_computation.86 | loop fusion | flops 4194304 | bytes 25165824 | tf_op jit(solution)/shard_map/convert_element_type | solution.py:61
  117.3 12.5 %slice_convert_fusion.13 = (f32[16,32,1024]{2,1,0:T(8,128)}, f32[16,32,1024]{2,1,0:T(8,128)}, f32[16,32,1024]{2,1,0:T(8,128)}, f32[16,32,1024]{2,1,0:T(8,128)}, ...) fusion(bf16[16,39,1024]{2,1,0:T(8,128)(2,1)} %all-gather.3.cloned.1.cal, ...), kind=kLoop, calls=%fused_computation.87 | loop fusion | flops 4194304 | bytes 25165824 | tf_op jit(solution)/shard_map/convert_element_type | solution.py:58
  129.8 0.0 copy-start.13
  129.8 0.0 copy-start.29
  129.8 0.0 copy-start.31
  129.8 0.0 copy-start.32
  129.9 8.5 %subtract_reduce_fusion.5 = (f32[8,32,1024]{2,1,0:T(8,128)S(1)}, f32[8,32,1024]{2,1,0:T(8,128)S(1)}) fusion(f32[16,8,1024]{2,1,0:T(8,128)} %get-tuple-element.34, f32[16,32,1024]{2,1,0:T(8,128)} %get-tuple-element.64, f32[16,8,1024]{2,1,0:T(8,128)} %get-tuple-element.46, f32[16,32,1024]{2,1,0:T(8,128)} %get-tuple-element.56, f32[16,8,1024]{2,1,0:T(8,128)} %get-tuple-element.26), kind=kLoop, calls=%fused_computation.15 | loop fusion | flops 33030144 | bytes 7864320 | tf_op jit(solution)/shard_map/reduce_sum | solution.py:68
  138.4 0.0 copy-start.9
  138.4 0.0 copy-start.12
  138.5 8.0 %subtract_reduce_fusion.4 = (f32[8,32,1024]{2,1,0:T(8,128)S(1)}, f32[8,32,1024]{2,1,0:T(8,128)S(1)}) fusion(f32[16,8,1024]{2,1,0:T(8,128)S(1)} %copy-done.32, f32[16,32,1024]{2,1,0:T(8,128)S(1)} %copy-done.11, f32[16,8,1024]{2,1,0:T(8,128)S(1)} %copy-done.29, f32[16,32,1024]{2,1,0:T(8,128)S(1)} %copy-done.13, f32[16,8,1024]{2,1,0:T(8,128)S(1)} %copy-done.31), kind=kLoop, calls=%fused_computation.14 | loop fusion | flops 33030144 | bytes 7864320 | tf_op jit(solution)/shard_map/reduce_sum | solution.py:68
  146.5 8.0 %subtract_reduce_fusion.6 = (f32[8,32,1024]{2,1,0:T(8,128)S(1)}, f32[8,32,1024]{2,1,0:T(8,128)S(1)}) fusion(f32[16,8,1024]{2,1,0:T(8,128)S(1)} %copy-done.23, f32[16,32,1024]{2,1,0:T(8,128)S(1)} %copy-done.9, f32[16,8,1024]{2,1,0:T(8,128)S(1)} %copy-done.27, f32[16,32,1024]{2,1,0:T(8,128)S(1)} %copy-done.12, f32[16,8,1024]{2,1,0:T(8,128)S(1)} %copy-done.30), kind=kLoop, calls=%fused_computation.16 | loop fusion | flops 33030144 | bytes 7864320 | tf_op jit(solution)/shard_map/reduce_sum | solution.py:68
  154.6 8.0 %subtract_reduce_fusion.7 = (f32[8,32,1024]{2,1,0:T(8,128)S(1)}, f32[8,32,1024]{2,1,0:T(8,128)S(1)}) fusion(f32[16,8,1024]{2,1,0:T(8,128)S(1)} %copy-done.20, f32[16,32,1024]{2,1,0:T(8,128)S(1)} %copy-done.7, f32[16,8,1024]{2,1,0:T(8,128)S(1)} %copy-done.25, f32[16,32,1024]{2,1,0:T(8,128)S(1)} %copy-done.10, f32[16,8,1024]{2,1,0:T(8,128)S(1)} %copy-done.28), kind=kLoop, calls=%fused_computation.17 | loop fusion | flops 33030144 | bytes 7864320 | tf_op jit(solution)/shard_map/reduce_sum | solution.py:68
  162.7 8.0 %subtract_reduce_fusion.3 = (f32[8,32,1024]{2,1,0:T(8,128)S(1)}, f32[8,32,1024]{2,1,0:T(8,128)S(1)}) fusion(f32[16,8,1024]{2,1,0:T(8,128)S(1)} %copy-done.18, f32[16,32,1024]{2,1,0:T(8,128)S(1)} %copy-done.5, f32[16,8,1024]{2,1,0:T(8,128)S(1)} %copy-done.22, f32[16,32,1024]{2,1,0:T(8,128)S(1)} %copy-done.8, f32[16,8,1024]{2,1,0:T(8,128)S(1)} %copy-done.26), kind=kLoop, calls=%fused_computation.13 | loop fusion | flops 33030144 | bytes 7864320 | tf_op jit(solution)/shard_map/reduce_sum | solution.py:68
  170.7 7.9 %subtract_reduce_fusion.2 = (f32[8,32,1024]{2,1,0:T(8,128)S(1)}, f32[8,32,1024]{2,1,0:T(8,128)S(1)}) fusion(f32[16,8,1024]{2,1,0:T(8,128)S(1)} %copy-done.15, f32[16,32,1024]{2,1,0:T(8,128)S(1)} %copy-done.3, f32[16,8,1024]{2,1,0:T(8,128)S(1)} %copy-done.19, f32[16,32,1024]{2,1,0:T(8,128)S(1)} %copy-done.6, f32[16,8,1024]{2,1,0:T(8,128)S(1)} %copy-done.24), kind=kLoop, calls=%fused_computation.12 | loop fusion | flops 33030144 | bytes 7864320 | tf_op jit(solution)/shard_map/reduce_sum | solution.py:68
  178.7 7.9 %subtract_reduce_fusion.1 = (f32[8,32,1024]{2,1,0:T(8,128)S(1)}, f32[8,32,1024]{2,1,0:T(8,128)S(1)}) fusion(f32[16,8,1024]{2,1,0:T(8,128)S(1)} %get-tuple-element.39, f32[16,32,1024]{2,1,0:T(8,128)S(1)} %copy-done.1, f32[16,8,1024]{2,1,0:T(8,128)S(1)} %copy-done.17, f32[16,32,1024]{2,1,0:T(8,128)S(1)} %copy-done.4, f32[16,8,1024]{2,1,0:T(8,128)S(1)} %copy-done.21), kind=kLoop, calls=%fused_computation.11 | loop fusion | flops 33030144 | bytes 7864320 | tf_op jit(solution)/shard_map/reduce_sum | solution.py:68
  186.7 8.1 %subtract_reduce_fusion = (f32[8,32,1024]{2,1,0:T(8,128)S(1)}, f32[8,32,1024]{2,1,0:T(8,128)S(1)}) fusion(f32[16,8,1024]{2,1,0:T(8,128)S(1)} %get-tuple-element.40, f32[16,32,1024]{2,1,0:T(8,128)S(1)} %get-tuple-element.59, f32[16,8,1024]{2,1,0:T(8,128)S(1)} %copy-done.14, f32[16,32,1024]{2,1,0:T(8,128)S(1)} %copy-done.2, f32[16,8,1024]{2,1,0:T(8,128)S(1)} %copy-done.16), kind=kLoop, calls=%fused_computation.10 | loop fusion | flops 33030144 | bytes 7864320 | tf_op jit(solution)/shard_map/reduce_sum | solution.py:68
  194.8 16.5 %fusion.9 = f32[8,32,1024]{2,1,0:T(8,128)S(1)} fusion(bf16[1024]{0:T(1024)(128)(2,1)S(1)} %fusion.82, s32[1024]{0:T(1024)S(1)} %iota_add_fusion, pred[1024]{0:T(1024)(128)(4,1)S(1)} %iota_compare_fusion, f32[8,32,1024]{2,1,0:T(8,128)S(1)} %get-tuple-element.21, f32[8,32,1024]{2,1,0:T(8,128)S(1)} %get-tuple-element.19, ...), kind=kOutput, calls=%fused_computation.35 | convolution fusion | flops 555483136 | bytes 9444352 | tf_op jit(solution)/shard_map/cbk,km->cbm/dot_general | solution.py:76
  211.4 0.0 copy-start.34
  211.4 17.2 %fusion.36 = bf16[8,32,1024]{2,1,0:T(8,128)(2,1)} fusion(f32[8,32,1024]{2,1,0:T(8,128)S(1)} %fusion.9, s32[1024]{0:T(1024)S(1)} %iota_add_fusion, f32[1024]{0:T(1024)S(1)} %broadcast_select_fusion.1, f32[8,32,1024]{2,1,0:T(8,128)S(1)} %get-tuple-element.20, f32[8,32,1024]{2,1,0:T(8,128)S(1)} %get-tuple-element.18, ...), kind=kOutput, calls=%fused_computation.67 | convolution fusion | flops 556007424 | bytes 9969664 | tf_op jit(solution)/shard_map/cbk,km->cbm/dot_general | solution.py:75
  228.5 0.0 all-reduce.3.cloned.1.call-update
  228.6 0.6 dynamic-slice
  229.8 46.9 %all-reduce.3.cloned.1.call-done = bf16[8,32,1024]{2,1,0:T(8,128)(2,1)} async-done(((bf16[8,32,1024]{2,1,0:T(8,128)(2,1)}), bf16[8,32,1024]{2,1,0:T(8,128)(2,1)}) %all-reduce.3.cloned.1.call-update) | async-done | bytes 524304
  276.8 0.9 constant_dynamic-slice_fusion
  277.7 0.1 copy.54
  277.8 11.2 %all_to_all.16 = bf16[8,8,1024]{2,0,1:T(8,128)(2,1)S(1)} all-to-all(bf16[8,8,1024]{2,0,1:T(8,128)(2,1)S(1)} %copy.54), channel_id=1, replica_groups=mesh['src'=4,'ch'=8] {'ch'}, dimensions={1} | all-to-all | bytes 262144 | tf_op jit(solution)/shard_map/all_to_all | solution.py:82
  289.0 2.1 convolution_convert_fusion
  (71 shorter events, 0.2 us)
Async XLA Ops:
  6.5 282.4 %copy-start = (bf16[64,1024]{1,0:T(8,128)(2,1)S(1)}, bf16[64,1024]{1,0:T(8,128)(2,1)}, u32[]{:S(2)}) copy-start(bf16[64,1024]{1,0:T(8,128)(2,1)} %param.9) | copy-start | bytes 393220
  6.5 99.5 %all-gather.5.cloned.1.call-start = ((), (), s32[]{:S(2)}) async-start(), calls=%async_computation.2 | async-start | bytes 1474560 | tf_op jit(solution)/shard_map/all_gather | solution.py:53
  41.4 75.8 %all-gather.3.cloned.1.call-start = ((), (), s32[]{:S(2)}) async-start(), calls=%async_computation.1 | async-start | bytes 1474560 | tf_op jit(solution)/shard_map/all_gather | solution.py:52
  74.2 202.6 %all-reduce.3.cloned.1.call-start = ((), (), s32[]{:S(2)}) async-start(), calls=%async_computation.3 | async-start | bytes 1048576
  74.5 13.7 %copy-start.33 = (s32[16]{0:T(128)S(1)}, s32[16]{0:T(128)}, u32[]{:S(2)}) copy-start(s32[16]{0:T(128)} %param.8) | copy-start | bytes 196
  129.8 8.6 %copy-start.11 = (f32[16,32,1024]{2,1,0:T(8,128)S(1)}, f32[16,32,1024]{2,1,0:T(8,128)}, u32[]{:S(2)}) copy-start(f32[16,32,1024]{2,1,0:T(8,128)} %get-tuple-element.63) | copy-start | bytes 6291460
  129.8 8.6 %copy-start.13 = (f32[16,32,1024]{2,1,0:T(8,128)S(1)}, f32[16,32,1024]{2,1,0:T(8,128)}, u32[]{:S(2)}) copy-start(f32[16,32,1024]{2,1,0:T(8,128)} %get-tuple-element.55) | copy-start | bytes 6291460
  129.8 8.6 %copy-start.29 = (f32[16,8,1024]{2,1,0:T(8,128)S(1)}, f32[16,8,1024]{2,1,0:T(8,128)}, u32[]{:S(2)}) copy-start(f32[16,8,1024]{2,1,0:T(8,128)} %get-tuple-element.45) | copy-start | bytes 1572868
  129.8 8.6 %copy-start.31 = (f32[16,8,1024]{2,1,0:T(8,128)S(1)}, f32[16,8,1024]{2,1,0:T(8,128)}, u32[]{:S(2)}) copy-start(f32[16,8,1024]{2,1,0:T(8,128)} %get-tuple-element.27) | copy-start | bytes 1572868
  129.8 8.6 %copy-start.32 = (f32[16,8,1024]{2,1,0:T(8,128)S(1)}, f32[16,8,1024]{2,1,0:T(8,128)}, u32[]{:S(2)}) copy-start(f32[16,8,1024]{2,1,0:T(8,128)} %get-tuple-element.35) | copy-start | bytes 1572868
  138.4 8.1 %copy-start.9 = (f32[16,32,1024]{2,1,0:T(8,128)S(1)}, f32[16,32,1024]{2,1,0:T(8,128)}, u32[]{:S(2)}) copy-start(f32[16,32,1024]{2,1,0:T(8,128)} %get-tuple-element.58) | copy-start | bytes 6291460
  138.4 8.1 %copy-start.12 = (f32[16,32,1024]{2,1,0:T(8,128)S(1)}, f32[16,32,1024]{2,1,0:T(8,128)}, u32[]{:S(2)}) copy-start(f32[16,32,1024]{2,1,0:T(8,128)} %get-tuple-element.50) | copy-start | bytes 6291460
  138.4 8.1 %copy-start.23 = (f32[16,8,1024]{2,1,0:T(8,128)S(1)}, f32[16,8,1024]{2,1,0:T(8,128)}, u32[]{:S(2)}) copy-start(f32[16,8,1024]{2,1,0:T(8,128)} %get-tuple-element.36) | copy-start | bytes 1572868
  138.4 8.1 %copy-start.27 = (f32[16,8,1024]{2,1,0:T(8,128)S(1)}, f32[16,8,1024]{2,1,0:T(8,128)}, u32[]{:S(2)}) copy-start(f32[16,8,1024]{2,1,0:T(8,128)} %get-tuple-element.42) | copy-start | bytes 1572868
  138.4 8.1 %copy-start.30 = (f32[16,8,1024]{2,1,0:T(8,128)S(1)}, f32[16,8,1024]{2,1,0:T(8,128)}, u32[]{:S(2)}) copy-start(f32[16,8,1024]{2,1,0:T(8,128)} %get-tuple-element.24) | copy-start | bytes 1572868
  146.4 8.1 %copy-start.7 = (f32[16,32,1024]{2,1,0:T(8,128)S(1)}, f32[16,32,1024]{2,1,0:T(8,128)}, u32[]{:S(2)}) copy-start(f32[16,32,1024]{2,1,0:T(8,128)} %get-tuple-element.65) | copy-start | bytes 6291460
  146.4 8.1 %copy-start.10 = (f32[16,32,1024]{2,1,0:T(8,128)S(1)}, f32[16,32,1024]{2,1,0:T(8,128)}, u32[]{:S(2)}) copy-start(f32[16,32,1024]{2,1,0:T(8,128)} %get-tuple-element.57) | copy-start | bytes 6291460
  146.4 8.1 %copy-start.20 = (f32[16,8,1024]{2,1,0:T(8,128)S(1)}, f32[16,8,1024]{2,1,0:T(8,128)}, u32[]{:S(2)}) copy-start(f32[16,8,1024]{2,1,0:T(8,128)} %get-tuple-element.41) | copy-start | bytes 1572868
  146.5 8.1 %copy-start.25 = (f32[16,8,1024]{2,1,0:T(8,128)S(1)}, f32[16,8,1024]{2,1,0:T(8,128)}, u32[]{:S(2)}) copy-start(f32[16,8,1024]{2,1,0:T(8,128)} %get-tuple-element.47) | copy-start | bytes 1572868
  146.5 8.1 %copy-start.28 = (f32[16,8,1024]{2,1,0:T(8,128)S(1)}, f32[16,8,1024]{2,1,0:T(8,128)}, u32[]{:S(2)}) copy-start(f32[16,8,1024]{2,1,0:T(8,128)} %get-tuple-element.25) | copy-start | bytes 1572868
  154.5 8.1 %copy-start.5 = (f32[16,32,1024]{2,1,0:T(8,128)S(1)}, f32[16,32,1024]{2,1,0:T(8,128)}, u32[]{:S(2)}) copy-start(f32[16,32,1024]{2,1,0:T(8,128)} %get-tuple-element.62) | copy-start | bytes 6291460
  154.5 8.1 %copy-start.8 = (f32[16,32,1024]{2,1,0:T(8,128)S(1)}, f32[16,32,1024]{2,1,0:T(8,128)}, u32[]{:S(2)}) copy-start(f32[16,32,1024]{2,1,0:T(8,128)} %get-tuple-element.54) | copy-start | bytes 6291460
  154.5 8.1 %copy-start.18 = (f32[16,8,1024]{2,1,0:T(8,128)S(1)}, f32[16,8,1024]{2,1,0:T(8,128)}, u32[]{:S(2)}) copy-start(f32[16,8,1024]{2,1,0:T(8,128)} %get-tuple-element.37) | copy-start | bytes 1572868
  154.5 8.1 %copy-start.22 = (f32[16,8,1024]{2,1,0:T(8,128)S(1)}, f32[16,8,1024]{2,1,0:T(8,128)}, u32[]{:S(2)}) copy-start(f32[16,8,1024]{2,1,0:T(8,128)} %get-tuple-element.44) | copy-start | bytes 1572868
  154.5 8.1 %copy-start.26 = (f32[16,8,1024]{2,1,0:T(8,128)S(1)}, f32[16,8,1024]{2,1,0:T(8,128)}, u32[]{:S(2)}) copy-start(f32[16,8,1024]{2,1,0:T(8,128)} %get-tuple-element.28) | copy-start | bytes 1572868
  162.6 8.1 %copy-start.3 = (f32[16,32,1024]{2,1,0:T(8,128)S(1)}, f32[16,32,1024]{2,1,0:T(8,128)}, u32[]{:S(2)}) copy-start(f32[16,32,1024]{2,1,0:T(8,128)} %get-tuple-element.61) | copy-start | bytes 6291460
  162.6 8.1 %copy-start.6 = (f32[16,32,1024]{2,1,0:T(8,128)S(1)}, f32[16,32,1024]{2,1,0:T(8,128)}, u32[]{:S(2)}) copy-start(f32[16,32,1024]{2,1,0:T(8,128)} %get-tuple-element.53) | copy-start | bytes 6291460
  162.6 8.1 %copy-start.15 = (f32[16,8,1024]{2,1,0:T(8,128)S(1)}, f32[16,8,1024]{2,1,0:T(8,128)}, u32[]{:S(2)}) copy-start(f32[16,8,1024]{2,1,0:T(8,128)} %get-tuple-element.38) | copy-start | bytes 1572868
  162.6 8.1 %copy-start.19 = (f32[16,8,1024]{2,1,0:T(8,128)S(1)}, f32[16,8,1024]{2,1,0:T(8,128)}, u32[]{:S(2)}) copy-start(f32[16,8,1024]{2,1,0:T(8,128)} %get-tuple-element.43) | copy-start | bytes 1572868
  162.6 8.1 %copy-start.24 = (f32[16,8,1024]{2,1,0:T(8,128)S(1)}, f32[16,8,1024]{2,1,0:T(8,128)}, u32[]{:S(2)}) copy-start(f32[16,8,1024]{2,1,0:T(8,128)} %get-tuple-element.29) | copy-start | bytes 1572868
  170.6 8.1 %copy-start.1 = (f32[16,32,1024]{2,1,0:T(8,128)S(1)}, f32[16,32,1024]{2,1,0:T(8,128)}, u32[]{:S(2)}) copy-start(f32[16,32,1024]{2,1,0:T(8,128)} %get-tuple-element.60) | copy-start | bytes 6291460
  170.7 8.1 %copy-start.4 = (f32[16,32,1024]{2,1,0:T(8,128)S(1)}, f32[16,32,1024]{2,1,0:T(8,128)}, u32[]{:S(2)}) copy-start(f32[16,32,1024]{2,1,0:T(8,128)} %get-tuple-element.52) | copy-start | bytes 6291460
  170.7 8.1 %copy-start.17 = (f32[16,8,1024]{2,1,0:T(8,128)S(1)}, f32[16,8,1024]{2,1,0:T(8,128)}, u32[]{:S(2)}) copy-start(f32[16,8,1024]{2,1,0:T(8,128)} %get-tuple-element.49) | copy-start | bytes 1572868
  170.7 8.1 %copy-start.21 = (f32[16,8,1024]{2,1,0:T(8,128)S(1)}, f32[16,8,1024]{2,1,0:T(8,128)}, u32[]{:S(2)}) copy-start(f32[16,8,1024]{2,1,0:T(8,128)} %get-tuple-element.30) | copy-start | bytes 1572868
  178.7 8.0 %copy-start.2 = (f32[16,32,1024]{2,1,0:T(8,128)S(1)}, f32[16,32,1024]{2,1,0:T(8,128)}, u32[]{:S(2)}) copy-start(f32[16,32,1024]{2,1,0:T(8,128)} %get-tuple-element.51) | copy-start | bytes 6291460
  178.7 8.0 %copy-start.14 = (f32[16,8,1024]{2,1,0:T(8,128)S(1)}, f32[16,8,1024]{2,1,0:T(8,128)}, u32[]{:S(2)}) copy-start(f32[16,8,1024]{2,1,0:T(8,128)} %get-tuple-element.48) | copy-start | bytes 1572868
  178.7 8.0 %copy-start.16 = (f32[16,8,1024]{2,1,0:T(8,128)S(1)}, f32[16,8,1024]{2,1,0:T(8,128)}, u32[]{:S(2)}) copy-start(f32[16,8,1024]{2,1,0:T(8,128)} %get-tuple-element.31) | copy-start | bytes 1572868
  211.4 17.2 %copy-start.34 = (u32[32]{0:T(128)S(1)}, u32[32]{0:T(128)}, u32[]{:S(2)}) copy-start(u32[32]{0:T(128)} %constant.100) | copy-start | bytes 388
Sparse Core Ops, SparseCore 0:
  41.6 26.1 all-gather.4
  74.3 26.1 all-gather.2
  228.7 48.0 all-reduce.2
where the time goes:
time: 303 us; the launch traced here: 298 us
  other arithmetic  159 us (52%)
  waiting for transfers between devices  47 us (16%)
  matrix products  39.1 us (13%)
  local copies, waits for them, and re-layouts  26 us (9%)
  between operations  14.9 us (5%)
  blocking collectives  11.2 us (4%)
    reduce_sum x8, other arithmetic, per_device(): jnp.sum(accumulate_spec_real * resp_real - accumulate_spec_imag * resp_ma...  64.3 us
    unnamed x4, waiting for transfers between devices  47 us
    convert_element_type x1, other arithmetic, make_tables(): fwd_imag.astype(jnp.bfloat16)  32.2 us
    convert_element_type x1, other arithmetic, make_tables(): fwd_real.astype(jnp.bfloat16)  31 us
    dot_general x1, matrix products, per_device(): first = jnp.einsum('cbk,km->cbm', mix_real, inv_real)  17.2 us
    dot_general x1, matrix products, per_device(): second = jnp.einsum('cbk,km->cbm', mix_imag, inv_imag)  16.5 us
    slice x1, local copies, waits for them, and re-layouts, per_device(): resp_real_all = jnp.take(room_spectra[:, :, :, 0, :], slot_local, axis=0)  13.7 us
    convert_element_type x1, other arithmetic, per_device(): spectra_real[:, start:start + out_blocks].astype(jnp.float32)[:, None]  12.5 us
  transfers between devices with their start and end apart: 3, of which 1 were waited for; matrix products, arithmetic and copies ran while one was open for 26% of the time, Pallas kernels for 0%

commit v1 on v0

v1 whole, which is shorter than its diff:
```python
import functools
import math

import jax
import jax.numpy as jnp
import ml_dtypes
import numpy as np
from jax import lax
from jax.experimental import pallas as pl
from jax.experimental.pallas import tpu as pltpu
from jax.sharding import PartitionSpec as P

BF16 = jnp.bfloat16
F32 = jnp.float32
LANES = 256
STEPS = 24
SEGS = 2
KEEP = 16


def bf16_table(values):
    return np.asarray(values, dtype=np.float32).astype(ml_dtypes.bfloat16)


@functools.lru_cache(maxsize=None)
def block_tables(block_len):
    size = 2 * block_len
    n = np.arange(block_len)[:, None]
    k = np.arange(block_len)[None, :]
    angle = ((n * k) % size) * (2.0 * math.pi / size)
    fwd_real = np.cos(angle)
    fwd_imag = np.where(k == 0, 1.0 - 2.0 * (n % 2), -np.sin(angle))
    kk = np.arange(block_len)[:, None]
    m = np.arange(block_len)[None, :] + block_len
    angle = ((kk * m) % size) * (2.0 * math.pi / size)
    weight = np.where(kk == 0, 1.0, 2.0)
    inv_real = weight * np.cos(angle) / size
    inv_imag = np.where(kk == 0, (1.0 - 2.0 * (m % 2)) / size, -2.0 * np.sin(angle) / size)
    return (
        bf16_table(np.stack([fwd_real, fwd_imag])),
        bf16_table(np.stack([inv_real, inv_imag])),
    )


@functools.lru_cache(maxsize=None)
def step_tables(parts, frames, rows):
    half = STEPS // 2
    theta = 2.0 * math.pi * (np.arange(STEPS) + 0.5) / STEPS
    first = (np.arange(STEPS) < half).astype(np.float64)[:, None]

    def forward(steps):
        cos = np.cos(theta[:, None] * steps[None, :])
        sin = np.sin(theta[:, None] * steps[None, :])
        plain = np.block([[cos, sin], [-sin, cos]])
        packed = np.block([[cos * first, cos * (1 - first)], [-sin * first, -sin * (1 - first)]])
        return plain, packed

    spec = np.zeros((2, 2, SEGS, STEPS, 2, frames))
    used = parts - 1 + KEEP
    for kind, table in enumerate(forward(np.arange(used))):
        table = table.reshape(2, STEPS, 2, used)
        for seg in range(SEGS):
            spec[kind, :, seg, :, :, seg * KEEP : seg * KEEP + used] = table
    spec = spec.reshape(2, 2 * SEGS * STEPS, 2 * frames)
    spec = np.concatenate([spec[0], spec[1]], axis=1)

    resp = np.zeros((rows, 2, STEPS, 2, rows, parts, 2))
    for kind, table in enumerate(forward(np.arange(parts))):
        table = table.reshape(2, STEPS, 2, parts).transpose(0, 1, 3, 2)
        for r in range(rows):
            resp[r, :, :, kind, r] = table
    resp = resp.reshape(rows * 2 * STEPS, 2 * rows * parts * 2)

    back = np.zeros((2, 2, SEGS, KEEP, 2, SEGS, STEPS))
    steps = np.arange(KEEP) + parts - 1
    cos = np.cos(theta[None, :] * steps[:, None]) / STEPS
    sin = np.sin(theta[None, :] * steps[:, None]) / STEPS
    firsts = first[:, 0][None, :]
    for seg in range(SEGS):
        back[0, 0, seg, :, 0, seg] = cos
        back[0, 0, seg, :, 1, seg] = -sin
        back[0, 1, seg, :, 0, seg] = sin
        back[0, 1, seg, :, 1, seg] = cos
        back[1, 0, seg, :, 0, seg] = 2 * cos * firsts
        back[1, 0, seg, :, 1, seg] = -2 * sin * firsts
        back[1, 1, seg, :, 0, seg] = 2 * cos * (1 - firsts)
        back[1, 1, seg, :, 1, seg] = -2 * sin * (1 - firsts)
    back = back.reshape(2, 2 * SEGS * KEEP, 2 * SEGS * STEPS)
    back = np.concatenate([back[0], back[1]], axis=1)
    return bf16_table(spec), bf16_table(resp), bf16_table(back)


def dot(left, right):
    return jnp.dot(left, right, preferred_element_type=F32)


def mix_kernel(pieces, rows, channels, blocks, shares, has_total, last, scal, *refs):
    refs = list(refs)
    x_refs = [refs.pop(0) for _ in range(pieces)]
    h_refs = [refs.pop(0) for _ in range(rows)]
    table_ref, spec_ref, resp_ref = [refs.pop(0) for _ in range(3)]
    total_ref = refs.pop(0) if has_total else None
    if last:
        back_ref, inv_ref = refs.pop(0), refs.pop(0)
        out_refs = [refs.pop(0) for _ in range(shares)]
    else:
        out_ref = refs.pop(0)
    s_ref, hat_ref = refs.pop(0), refs.pop(0)
    if last:
        y_ref, left_re, left_im, time_ref = refs

    step = pl.program_id(0)
    lane = lax.broadcasted_iota(jnp.int32, (1, LANES), 1) + step * LANES
    packed = (lane == 0).astype(F32)
    plain = 1.0 - packed
    packed16, plain16 = packed.astype(BF16), plain.astype(BF16)
    sign = (1 - 2 * (lane % 2)).astype(F32)

    x = jnp.concatenate([ref[...] for ref in x_refs], axis=0)
    count = x.shape[0] // rows
    spectra = []
    for j in range(2):
        one = dot(x, table_ref[j])
        spectra.append(one + sign * pltpu.roll(one, one.shape[0] - 1, axis=0))
    for r in range(rows):
        both = jnp.concatenate([s[r * count : (r + 1) * count] for s in spectra], axis=0)
        both = jnp.concatenate([both * plain, both * packed], axis=0).astype(BF16)
        s_ref[r] = dot(spec_ref[...], both)

    wide = SEGS * STEPS
    for c in range(channels):
        h = jnp.concatenate([ref[0, c] for ref in h_refs], axis=0)
        h = jnp.concatenate([h * plain16, h * packed16], axis=0)
        hat = hat_ref.at[c % 2]
        hat[...] = dot(resp_ref[...], h)
        for cut in range(LANES // 128):
            at = slice(cut * 128, (cut + 1) * 128)
            for seg in range(SEGS):
                re_rows = slice(seg * STEPS, (seg + 1) * STEPS)
                im_rows = slice(wide + seg * STEPS, wide + (seg + 1) * STEPS)
                if has_total:
                    re, im = total_ref[c, re_rows, at], total_ref[c, im_rows, at]
                else:
                    re, im = None, None
                for r in range(rows):
                    base = r * 2 * STEPS
                    h_re = hat[base : base + STEPS, at]
                    h_im = hat[base + STEPS : base + 2 * STEPS, at]
                    s_re, s_im = s_ref[r, re_rows, at], s_ref[r, im_rows, at]
                    add_re = s_re * h_re - s_im * h_im
                    add_im = s_re * h_im + s_im * h_re
                    re = add_re if re is None else re + add_re
                    im = add_im if im is None else im + add_im
                if last:
                    y_ref[re_rows, at] = re
                    y_ref[im_rows, at] = im
                else:
                    out_ref[c, re_rows, at] = re
                    out_ref[c, im_rows, at] = im
        if last:
            y = y_ref[...]
            y = jnp.concatenate([y * plain, y * packed], axis=0).astype(BF16)
            mix = dot(back_ref[...], y).astype(BF16)
            left_re[c * blocks : (c + 1) * blocks] = mix[:blocks]
            left_im[c * blocks : (c + 1) * blocks] = mix[blocks:]

    if last:
        part = dot(left_re[...], inv_ref[0]) + dot(left_im[...], inv_ref[1])
        each = blocks // shares
        spans = [
            (t, c, part[c * blocks + t * each : c * blocks + (t + 1) * each])
            for t in range(shares)
            for c in range(channels)
        ]

        @pl.when(step == 0)
        def _():
            for t, c, span in spans:
                time_ref[t, c] = span

        @pl.when(step > 0)
        def _():
            for t, c, span in spans:
                time_ref[t, c] += span

        @pl.when(step == pl.num_programs(0) - 1)
        def _():
            me = scal[rows]
            for d in range(shares):
                out_refs[d][...] = time_ref[me ^ d].astype(BF16)


def add_sources(x_list, slots, responses, total, last, shares, me):
    rows_total, channels, _, block_len = responses.shape
    parts = responses.shape[2] // 2
    rows = slots.shape[0]
    frames = x_list[0].shape[0] * len(x_list) // rows
    blocks = frames - parts
    wide = 2 * SEGS * STEPS
    table, inverse = block_tables(block_len)
    spec, resp, back = step_tables(parts, frames, rows)
    scal = jnp.concatenate([slots, me[None]]).astype(jnp.int32)
    grid = (block_len // LANES,)

    def whole(shape):
        return pl.BlockSpec(shape, lambda k, s: (0,) * len(shape))

    def row_of(i):
        return pl.BlockSpec((1, channels, 2 * parts, LANES), lambda k, s: (s[i], 0, 0, k))

    operands = list(x_list) + [responses] * rows + [jnp.asarray(table), jnp.asarray(spec), jnp.asarray(resp)]
    specs = [whole(x.shape) for x in x_list] + [row_of(i) for i in range(rows)]
    specs += [
        pl.BlockSpec((2, block_len, LANES), lambda k, s: (0, 0, k)),
        whole(spec.shape),
        whole(resp.shape),
    ]
    total_spec = pl.BlockSpec((channels, wide, LANES), lambda k, s: (0, 0, k))
    if total is not None:
        operands.append(total)
        specs.append(total_spec)
    scratch = [
        pltpu.VMEM((rows, wide, LANES), F32),
        pltpu.VMEM((2, rows * 2 * STEPS, LANES), F32),
    ]
    if last:
        operands += [jnp.asarray(back), jnp.asarray(inverse)]
        specs += [
            whole(back.shape),
            pl.BlockSpec((2, LANES, block_len), lambda k, s: (0, k, 0)),
        ]
        each = blocks // shares
        out_shape = [jax.ShapeDtypeStruct((channels, each, block_len), BF16)] * shares
        out_specs = [whole((channels, each, block_len))] * shares
        scratch += [
            pltpu.VMEM((wide, LANES), F32),
            pltpu.VMEM((channels * blocks, LANES), BF16),
            pltpu.VMEM((channels * blocks, LANES), BF16),
            pltpu.VMEM((shares, channels, each, block_len), F32),
        ]
    else:
        out_shape = jax.ShapeDtypeStruct((channels, wide, block_len), F32)
        out_specs = total_spec
    flops = 2 * block_len * (
        rows * frames * 2 * block_len + channels * rows * wide * 8 + (channels * blocks * 2 * block_len if last else 0)
    )
    body = functools.partial(
        mix_kernel, len(x_list), rows, channels, blocks, shares, total is not None, last
    )
    return pl.pallas_call(
        body,
        grid_spec=pltpu.PrefetchScalarGridSpec(
            num_scalar_prefetch=1,
            grid=grid,
            in_specs=specs,
            out_specs=out_specs,
            scratch_shapes=scratch,
        ),
        out_shape=out_shape,
        compiler_params=pltpu.CompilerParams(
            dimension_semantics=("arbitrary",), vmem_limit_bytes=40 * 2**20
        ),
        cost_estimate=pl.CostEstimate(flops=flops, bytes_accessed=12 * 2**20, transcendentals=0),
    )(scal, *operands)


def per_device(src_count, ch_count, dry_signal, room_spectra, render_slot, decoder):
    rows_total, parts, channels, _, block_len = room_spectra.shape
    own = dry_signal.shape[0]
    frames = dry_signal.shape[1] // block_len
    blocks = frames - parts
    src_me = lax.axis_index("src").astype(jnp.int32)
    ch_me = lax.axis_index("ch").astype(jnp.int32)

    x_own = dry_signal.reshape(own * frames, block_len)

    def swap(value, axis, count, flip):
        return lax.ppermute(value, axis, [(i, i ^ flip) for i in range(count)])

    lanes = [x_own] + [swap(x_own, "ch", ch_count, 2 * d) for d in range(1, ch_count // 2)]
    mates = [swap(x, "ch", ch_count, 1) for x in lanes]

    responses = room_spectra.transpose(0, 2, 1, 3, 4).reshape(
        rows_total, channels, 2 * parts, block_len
    )
    slot_local = render_slot % rows_total

    def slots_of(flip):
        start = (ch_me ^ flip) * own
        return lax.dynamic_slice(slot_local, (start,), (own,))

    total = None
    chips = ch_count // 2
    per_call = max(1, chips // 4)
    calls = chips // per_call
    for call in range(calls):
        x_list, slots = [], []
        for d in range(call * per_call, (call + 1) * per_call):
            x_list += [lanes[d], mates[d]]
            slots += [slots_of(2 * d), slots_of(2 * d + 1)]
        total = add_sources(
            x_list, jnp.concatenate(slots), responses, total, call == calls - 1, src_count, src_me
        )

    signal = total[0].astype(F32)
    for d in range(1, src_count):
        signal = signal + swap(total[d], "src", src_count, d).astype(F32)
    signal = signal.astype(BF16).reshape(channels, -1)
    gathered = lax.all_to_all(signal, "ch", split_axis=1, concat_axis=0, tiled=True)
    decoded = lax.dot_general(
        gathered, decoder, (((0,), (0,)), ((), ())), preferred_element_type=F32
    )
    return decoded.astype(BF16)


def solution(mesh):
    body = functools.partial(per_device, mesh.shape["src"], mesh.shape["ch"])
    return jax.shard_map(
        body,
        mesh=mesh,
        in_specs=(P(("src", "ch"), None), P("src", None, "ch", None, None), P("src"), P()),
        out_specs=P(("src", "ch"), None),
        check_vma=False,
    )
```

time: 303 us -> 96.5 us (0.32); the launches traced: 298 us -> 96 us
  other arithmetic: 159 us -> 1.04 us
  matrix products: 39.1 us -> 2.05 us
  Pallas kernels: 0 us -> 33.4 us
  waiting for transfers between devices: 47 us -> 17.4 us
  between operations: 14.9 us -> 0.14 us
  starting transfers between devices: 0.3 us -> 9.82 us
  local copies, waits for them, and re-layouts: 26 us -> 21.8 us
    convert_element_type x6 -> x1, other arithmetic: 89 us -> 0.07 us  [per_device(): signal = signal.astype(BF16).reshape(channels, -1)]
    reduce_sum x8 -> x0, other arithmetic: 64.3 us -> none  [per_device(): jnp.sum(accumulate_spec_real * resp_real - accumulate_spec_imag * resp_ma...]
    unnamed x4 -> x0, waiting for transfers between devices: 47 us -> none
    dot_general x6 -> x0, matrix products: 37 us -> none  [the longest x1 17.2 us: per_device(): first = jnp.einsum('cbk,km->cbm', mix_real, inv_real)]
    pallas_call x0 -> x4, Pallas kernels: none -> 33.4 us  [add_sources(): pl.pallas_call(body, grid_spec=pltpu.PrefetchScalarGridSpec(num_scalar_pr...]
    ppermute x0 -> x10, waiting for transfers between devices: none -> 17.4 us  [swap(): return lax.ppermute(value, axis, [(i, i ^ flip) for i in range(count)])]
    slice x1 -> x0, local copies, waits for them, and re-layouts: 13.7 us -> none  [per_device(): resp_real_all = jnp.take(room_spectra[:, :, :, 0, :], slot_local, axis=0)]
    ppermute x0 -> x10, starting transfers between devices: none -> 9.82 us  [swap(): return lax.ppermute(value, axis, [(i, i ^ flip) for i in range(count)])]
  transfers between devices with their start and end apart: 3 -> 10, of which waited for: 1 -> 4; matrix products, arithmetic and copies ran while one was open for 26% -> 18% of each run, Pallas kernels for 0% -> 21%
where the time goes in v1:
time: 96.5 us; the launch traced here: 96 us
  Pallas kernels  33.4 us (35%)
  local copies, waits for them, and re-layouts  21.8 us (23%)
  waiting for transfers between devices  17.4 us (18%)
  blocking collectives  10.3 us (11%)
  starting transfers between devices  9.82 us (10%)
  matrix products  2.05 us (2%)
  other arithmetic  1.04 us (1%)
    pallas_call x4, Pallas kernels, add_sources(): pl.pallas_call(body, grid_spec=pltpu.PrefetchScalarGridSpec(num_scalar_pr...  33.4 us
    ppermute x10, waiting for transfers between devices, swap(): return lax.ppermute(value, axis, [(i, i ^ flip) for i in range(count)])  17.4 us
    all_to_all x1, blocking collectives, per_device(): lax.all_to_all(signal, 'ch', split_axis=1, concat_axis=0, tiled=True)  10.3 us
    ppermute x10, starting transfers between devices, swap(): return lax.ppermute(value, axis, [(i, i ^ flip) for i in range(count)])  9.82 us
    transpose x1, local copies, waits for them, and re-layouts, per_device(): room_spectra.transpose(0, 2, 1, 3, 4)  8.89 us
    reshape x1, local copies, waits for them, and re-layouts, per_device(): room_spectra.transpose(0, 2, 1, 3, 4)  7.27 us
    unnamed x16, local copies, waits for them, and re-layouts  4.4 us
    dot_general x1, matrix products, per_device(): lax.dot_general(gathered, decoder, (((0,), (0,)), ((), ())), preferred_el...  2.05 us
  transfers between devices with their start and end apart: 10, of which 4 were waited for; matrix products, arithmetic and copies ran while one was open for 18% of the time, Pallas kernels for 21%

profile of v1, /device:TPU:0, one launch (start us, length us, event | category | flops | bytes accessed | tf_op | source)
XLA Modules:
  0.0 96.0 jit_solution(13603501559428307376)
XLA Ops:
  0.0 0.0 copy-start
  0.0 1.1 %reshape.11.refs_0_ = bf16[80,1024]{1,0:T(8,128)(2,1)S(1)} reshape(bf16[2,40960]{1,0:T(2,128)(2,1)} %param.9) | data formatting | bytes 327680 | tf_op jit(solution)/shard_map/reshape | solution.py:275
  1.1 0.5 collective-permute-start.6
  1.6 2.6 %collective-permute-start.4 = (bf16[80,1024]{1,0:T(8,128)(2,1)S(1)}, bf16[80,1024]{1,0:T(8,128)(2,1)S(1)}, u32[]{:S(2)}, u32[]{:S(2)}) collective-permute-start(bf16[80,1024]{1,0:T(8,128)(2,1)S(1)} %reshape.11.refs_0_), channel_id=1, source_target_pairs={{0,2},{1,3},{2,0},{3,1},{4,6},{5,7},{6,4},{7,5},{8,10},{9,11},{10,... | collective-permute-start | bytes 491528 | tf_op jit(solution)/shard_map/ppermute | solution.py:278
  4.2 2.6 %collective-permute-start.2 = (bf16[80,1024]{1,0:T(8,128)(2,1)S(1)}, bf16[80,1024]{1,0:T(8,128)(2,1)S(1)}, u32[]{:S(2)}, u32[]{:S(2)}) collective-permute-start(bf16[80,1024]{1,0:T(8,128)(2,1)S(1)} %reshape.11.refs_0_), channel_id=1, source_target_pairs={{0,4},{1,5},{2,6},{3,7},{4,0},{5,1},{6,2},{7,3},{8,12},{9,13},{10,... | collective-permute-start | bytes 491528 | tf_op jit(solution)/shard_map/ppermute | solution.py:278
  6.8 0.0 collective-permute-start
  6.8 0.7 and_select_fusion
  7.5 0.1 fusion.2
  7.6 0.1 add_add_fusion.3.scal
  7.7 0.1 add_add_fusion.2.scal
  7.7 0.1 add_add_fusion.1.scal
  7.8 4.3 %collective-permute-done.4.refs_0_ = bf16[80,1024]{1,0:T(8,128)(2,1)S(1)} collective-permute-done((bf16[80,1024]{1,0:T(8,128)(2,1)S(1)}, bf16[80,1024]{1,0:T(8,128)(2,1)S(1)}, u32[]{:S(2)}, u32[]{:S(2)}) %collective-permute-start.4) | collective-permute-done | bytes 163872 | tf_op jit(solution)/shard_map/ppermute | solution.py:278
  12.1 0.0 collective-permute-start.5
  12.1 7.1 %collective-permute-done.2.refs_0_ = bf16[80,1024]{1,0:T(8,128)(2,1)S(1)} collective-permute-done((bf16[80,1024]{1,0:T(8,128)(2,1)S(1)}, bf16[80,1024]{1,0:T(8,128)(2,1)S(1)}, u32[]{:S(2)}, u32[]{:S(2)}) %collective-permute-start.2) | collective-permute-done | bytes 163872 | tf_op jit(solution)/shard_map/ppermute | solution.py:278
  19.3 0.0 collective-permute-start.3
  19.3 0.1 add_add_fusion.scal
  19.3 8.9 %copy.13 = bf16[16,8,8,2,1024]{4,3,2,1,0:T(2,128)(2,1)} copy(bf16[16,8,8,2,1024]{4,3,1,2,0:T(2,128)(2,1)} %bitcast.8) | data formatting | bytes 8388608 | tf_op jit(solution)/shard_map/transpose | solution.py:283
  28.2 7.3 %reshape.12.refs_2_.refs_3_.refs_4_.refs_5_ = bf16[16,8,16,1024]{3,2,1,0:T(8,128)(2,1)} reshape(bf16[16,8,8,2,1024]{4,3,2,1,0:T(2,128)(2,1)} %copy.13) | data formatting | bytes 8388608 | tf_op jit(solution)/shard_map/reshape | solution.py:283
  35.5 0.0 collective-permute-done.refs_0_
  35.5 0.5 collective-permute-start.1
  36.0 0.0 collective-permute-done.6.refs_1_
  36.0 0.0 copy-done.5
  36.0 0.0 copy-done.6
  36.0 0.0 copy-start.1
  36.0 2.2 %copy-done.1 = bf16[16,8,16,1024]{3,2,1,0:T(8,128)(2,1)S(1)} copy-done((bf16[16,8,16,1024]{3,2,1,0:T(8,128)(2,1)S(1)}, bf16[16,8,16,1024]{3,2,1,0:T(8,128)(2,1)}, u32[]{:S(2)}) %copy-start.1) | copy-done | bytes 4194328
  38.2 2.2 %copy-done.3 = bf16[2,1024,1024]{2,1,0:T(8,128)(2,1)S(1)} copy-done((bf16[2,1024,1024]{2,1,0:T(8,128)(2,1)S(1)}, bf16[2,1024,1024]{2,1,0:T(8,128)(2,1)}, u32[]{:S(2)}) %copy-start.3) | copy-done | bytes 4194328
  40.4 5.9 %shard_map.91.refs_9_ = f32[8,96,1024]{2,1,0:T(8,128)S(1)} custom-call(s32[5]{0:T(128)S(1)} %add_add_fusion.3.scal, bf16[80,1024]{1,0:T(8,128)(2,1)S(1)} %reshape.11.refs_0_, bf16[80,1024]{1,0:T(8,128)(2,1)S(1)} %collective-permute-done.6.refs_1_, bf16[16,8,16,1024]{3,2,1,0:T(8,128)(2,1)S(1)} %copy-done.1, bf16[16,8,16,1024]{3,2,1,0:T(8,128)(2,1)S(1)} %copy-done.1, ...), custom_call_target="tpu_custom_call" | custom-call | flops 721420288 | bytes 12582912 | tf_op jit(solution)/shard_map/pallas_call | solution.py:250
  46.4 0.0 collective-permute-done.5.refs_1_
  46.4 0.0 copy-done.2
  46.4 6.8 %shard_map.92.refs_9_ = f32[8,96,1024]{2,1,0:T(8,128)S(1)} custom-call(s32[5]{0:T(128)S(1)} %add_add_fusion.2.scal, bf16[80,1024]{1,0:T(8,128)(2,1)S(1)} %collective-permute-done.4.refs_0_, bf16[80,1024]{1,0:T(8,128)(2,1)S(1)} %collective-permute-done.5.refs_1_, bf16[16,8,16,1024]{3,2,1,0:T(8,128)(2,1)S(1)} %copy-done.2, ...), custom_call_target="tpu_custom_call" | custom-call | flops 721420288 | bytes 12582912 | tf_op jit(solution)/shard_map/pallas_call | solution.py:250
  53.2 0.0 copy-start.4
  53.2 0.0 copy-start.7
  53.2 0.0 collective-permute-done.3.refs_1_
  53.2 7.1 %shard_map.93.refs_9_ = f32[8,96,1024]{2,1,0:T(8,128)S(1)} custom-call(s32[5]{0:T(128)S(1)} %add_add_fusion.1.scal, bf16[80,1024]{1,0:T(8,128)(2,1)S(1)} %collective-permute-done.2.refs_0_, bf16[80,1024]{1,0:T(8,128)(2,1)S(1)} %collective-permute-done.3.refs_1_, bf16[16,8,16,1024]{3,2,1,0:T(8,128)(2,1)S(1)} %copy-done.2, ...), custom_call_target="tpu_custom_call" | custom-call | flops 721420288 | bytes 12582912 | tf_op jit(solution)/shard_map/pallas_call | solution.py:250
  60.3 0.0 collective-permute-done.1.refs_1_
  60.3 0.0 copy-done.4
  60.3 0.0 copy-done.7
  60.3 13.6 %shard_map.94 = (bf16[8,8,1024]{2,1,0:T(8,128)(2,1)S(1)}, bf16[8,8,1024]{2,1,0:T(8,128)(2,1)S(1)}, bf16[8,8,1024]{2,1,0:T(8,128)(2,1)S(1)}, bf16[8,8,1024]{2,1,0:T(8,128)(2,1)S(1)}) custom-call(s32[5]{0:T(128)S(1)} %add_add_fusion.scal, bf16[80,1024]{1,0:T(8,128)(2,1)S(1)} %collective-permute-done.refs_0_, ...), custom_call_target="tpu_custom_call" | custom-call | flops 1795162112 | bytes 12582912 | tf_op jit(solution)/shard_map/pallas_call | solution.py:250
  73.9 1.6 %collective-permute-start.7 = (bf16[8,8,1024]{2,1,0:T(8,128)(2,1)S(1)}, bf16[8,8,1024]{2,1,0:T(8,128)(2,1)S(1)}, u32[]{:S(2)}, u32[]{:S(2)}) collective-permute-start(bf16[8,8,1024]{2,1,0:T(8,128)(2,1)S(1)} %get-tuple-element.10), channel_id=1, source_target_pairs={{0,8},{8,0},{16,24},{24,16},{1,9},{9,1},{17,25},{25,17},{2,10},{10... | collective-permute-start | bytes 393224 | tf_op jit(solution)/shard_map/ppermute | solution.py:278
  75.5 1.5 %collective-permute-start.8 = (bf16[8,8,1024]{2,1,0:T(8,128)(2,1)S(1)}, bf16[8,8,1024]{2,1,0:T(8,128)(2,1)S(1)}, u32[]{:S(2)}, u32[]{:S(2)}) collective-permute-start(bf16[8,8,1024]{2,1,0:T(8,128)(2,1)S(1)} %get-tuple-element.11), channel_id=1, source_target_pairs={{0,16},{8,24},{16,0},{24,8},{1,17},{9,25},{17,1},{25,9},{2,18},{10... | collective-permute-start | bytes 393224 | tf_op jit(solution)/shard_map/ppermute | solution.py:278
  77.0 0.5 collective-permute-start.9
  77.5 2.3 %collective-permute-done.7 = bf16[8,8,1024]{2,1,0:T(8,128)(2,1)S(1)} collective-permute-done((bf16[8,8,1024]{2,1,0:T(8,128)(2,1)S(1)}, bf16[8,8,1024]{2,1,0:T(8,128)(2,1)S(1)}, u32[]{:S(2)}, u32[]{:S(2)}) %collective-permute-start.7) | collective-permute-done | bytes 131104 | tf_op jit(solution)/shard_map/ppermute | solution.py:278
  79.7 3.7 %collective-permute-done.8 = bf16[8,8,1024]{2,1,0:T(8,128)(2,1)S(1)} collective-permute-done((bf16[8,8,1024]{2,1,0:T(8,128)(2,1)S(1)}, bf16[8,8,1024]{2,1,0:T(8,128)(2,1)S(1)}, u32[]{:S(2)}, u32[]{:S(2)}) %collective-permute-start.8) | collective-permute-done | bytes 131104 | tf_op jit(solution)/shard_map/ppermute | solution.py:278
  83.4 0.0 collective-permute-done.9
  83.4 0.1 add_convert_fusion
  83.5 0.1 copy.14
  83.6 10.3 %all_to_all.16 = bf16[8,8,1024]{2,0,1:T(8,128)(2,1)S(1)} all-to-all(bf16[8,8,1024]{2,0,1:T(8,128)(2,1)S(1)} %copy.14), channel_id=1, replica_groups=mesh['src'=4,'ch'=8] {'ch'}, dimensions={1} | all-to-all | bytes 262144 | tf_op jit(solution)/shard_map/all_to_all | solution.py:309
  93.9 2.1 %convolution_convert_fusion = bf16[1024,1024]{1,0:T(8,128)(2,1)} fusion(bf16[64,1024]{1,0:T(8,128)(2,1)S(1)} %copy-done, bf16[8,8,1024]{2,0,1:T(8,128)(2,1)S(1)} %all_to_all.16), kind=kOutput, calls=%fused_computation | convolution fusion | flops 135266304 | bytes 2359296 | tf_op jit(solution)/shard_map/dot_general | solution.py:310
  (5 shorter events, 0.0 us)
Async XLA Ops:
  0.0 93.9 %copy-start = (bf16[64,1024]{1,0:T(8,128)(2,1)S(1)}, bf16[64,1024]{1,0:T(8,128)(2,1)}, u32[]{:S(2)}) copy-start(bf16[64,1024]{1,0:T(8,128)(2,1)} %param.12) | copy-start | bytes 393220
  1.1 34.9 %collective-permute-start.6 = (bf16[80,1024]{1,0:T(8,128)(2,1)S(1)}, bf16[80,1024]{1,0:T(8,128)(2,1)S(1)}, u32[]{:S(2)}, u32[]{:S(2)}) collective-permute-start(bf16[80,1024]{1,0:T(8,128)(2,1)S(1)} %reshape.11.refs_0_), channel_id=1, source_target_pairs={{0,1},{1,0},{2,3},{3,2},{4,5},{5,4},{6,7},{7,6},{8,9},{9,8},{10,11... | collective-permute-start | bytes 491528 | tf_op jit(solution)/shard_map/ppermute | solution.py:278
  1.6 10.5 %collective-permute-start.4 = (bf16[80,1024]{1,0:T(8,128)(2,1)S(1)}, bf16[80,1024]{1,0:T(8,128)(2,1)S(1)}, u32[]{:S(2)}, u32[]{:S(2)}) collective-permute-start(bf16[80,1024]{1,0:T(8,128)(2,1)S(1)} %reshape.11.refs_0_), channel_id=1, source_target_pairs={{0,2},{1,3},{2,0},{3,1},{4,6},{5,7},{6,4},{7,5},{8,10},{9,11},{10,... | collective-permute-start | bytes 491528 | tf_op jit(solution)/shard_map/ppermute | solution.py:278
  4.2 15.0 %collective-permute-start.2 = (bf16[80,1024]{1,0:T(8,128)(2,1)S(1)}, bf16[80,1024]{1,0:T(8,128)(2,1)S(1)}, u32[]{:S(2)}, u32[]{:S(2)}) collective-permute-start(bf16[80,1024]{1,0:T(8,128)(2,1)S(1)} %reshape.11.refs_0_), channel_id=1, source_target_pairs={{0,4},{1,5},{2,6},{3,7},{4,0},{5,1},{6,2},{7,3},{8,12},{9,13},{10,... | collective-permute-start | bytes 491528 | tf_op jit(solution)/shard_map/ppermute | solution.py:278
  6.8 28.7 %collective-permute-start = (bf16[80,1024]{1,0:T(8,128)(2,1)S(1)}, bf16[80,1024]{1,0:T(8,128)(2,1)S(1)}, u32[]{:S(2)}, u32[]{:S(2)}) collective-permute-start(bf16[80,1024]{1,0:T(8,128)(2,1)S(1)} %reshape.11.refs_0_), channel_id=1, source_target_pairs={{0,6},{1,7},{2,4},{3,5},{4,2},{5,3},{6,0},{7,1},{8,14},{9,15},{10,... | collective-permute-start | bytes 491528 | tf_op jit(solution)/shard_map/ppermute | solution.py:278
  12.1 34.3 %collective-permute-start.5 = (bf16[80,1024]{1,0:T(8,128)(2,1)S(1)}, bf16[80,1024]{1,0:T(8,128)(2,1)S(1)}, u32[]{:S(2)}, u32[]{:S(2)}) collective-permute-start(bf16[80,1024]{1,0:T(8,128)(2,1)S(1)} %collective-permute-done.4.refs_0_), channel_id=1, source_target_pairs={{0,1},{1,0},{2,3},{3,2},{4,5},{5,4},{6,7},{7,6},{8,9},{9,8},{10,11... | collective-permute-start | bytes 491528 | tf_op jit(solution)/shard_map/ppermute | solution.py:278
  19.3 33.9 %collective-permute-start.3 = (bf16[80,1024]{1,0:T(8,128)(2,1)S(1)}, bf16[80,1024]{1,0:T(8,128)(2,1)S(1)}, u32[]{:S(2)}, u32[]{:S(2)}) collective-permute-start(bf16[80,1024]{1,0:T(8,128)(2,1)S(1)} %collective-permute-done.2.refs_0_), channel_id=1, source_target_pairs={{0,1},{1,0},{2,3},{3,2},{4,5},{5,4},{6,7},{7,6},{8,9},{9,8},{10,11... | collective-permute-start | bytes 491528 | tf_op jit(solution)/shard_map/ppermute | solution.py:278
  28.2 7.8 %copy-start.5 = (bf16[96,160]{1,0:T(8,128)(2,1)S(1)}, bf16[96,160]{1,0:T(8,128)(2,1)}, u32[]{:S(2)}) copy-start(bf16[96,160]{1,0:T(8,128)(2,1)} %constant.49.clone.refs_7_) | copy-start | bytes 92164
  28.2 7.8 %copy-start.6 = (bf16[192,128]{1,0:T(8,128)(2,1)S(1)}, bf16[192,128]{1,0:T(8,128)(2,1)}, u32[]{:S(2)}) copy-start(bf16[192,128]{1,0:T(8,128)(2,1)} %constant.50.clone.refs_8_) | copy-start | bytes 147460
  35.5 24.8 %collective-permute-start.1 = (bf16[80,1024]{1,0:T(8,128)(2,1)S(1)}, bf16[80,1024]{1,0:T(8,128)(2,1)S(1)}, u32[]{:S(2)}, u32[]{:S(2)}) collective-permute-start(bf16[80,1024]{1,0:T(8,128)(2,1)S(1)} %collective-permute-done.refs_0_), channel_id=1, source_target_pairs={{0,1},{1,0},{2,3},{3,2},{4,5},{5,4},{6,7},{7,6},{8,9},{9,8},{10,11... | collective-permute-start | bytes 491528 | tf_op jit(solution)/shard_map/ppermute | solution.py:278
  36.0 2.2 %copy-start.1 = (bf16[16,8,16,1024]{3,2,1,0:T(8,128)(2,1)S(1)}, bf16[16,8,16,1024]{3,2,1,0:T(8,128)(2,1)}, u32[]{:S(2)}) copy-start(bf16[16,8,16,1024]{3,2,1,0:T(8,128)(2,1)} %reshape.12.refs_2_.refs_3_.refs_4_.refs_5_) | copy-start | bytes 12582916
  38.2 2.2 %copy-start.3 = (bf16[2,1024,1024]{2,1,0:T(8,128)(2,1)S(1)}, bf16[2,1024,1024]{2,1,0:T(8,128)(2,1)}, u32[]{:S(2)}) copy-start(bf16[2,1024,1024]{2,1,0:T(8,128)(2,1)} %constant.48.clone.refs_6_) | copy-start | bytes 12582916
  40.4 6.0 %copy-start.2 = (bf16[16,8,16,1024]{3,2,1,0:T(8,128)(2,1)S(1)}, bf16[16,8,16,1024]{3,2,1,0:T(8,128)(2,1)}, u32[]{:S(2)}) copy-start(bf16[16,8,16,1024]{3,2,1,0:T(8,128)(2,1)} %reshape.12.refs_2_.refs_3_.refs_4_.refs_5_) | copy-start | bytes 12582916
  53.2 7.1 %copy-start.4 = (bf16[2,1024,1024]{2,1,0:T(8,128)(2,1)S(1)}, bf16[2,1024,1024]{2,1,0:T(8,128)(2,1)}, u32[]{:S(2)}) copy-start(bf16[2,1024,1024]{2,1,0:T(8,128)(2,1)} %constant.48.clone.refs_6_) | copy-start | bytes 12582916
  53.2 7.1 %copy-start.7 = (bf16[64,192]{1,0:T(8,128)(2,1)S(1)}, bf16[64,192]{1,0:T(8,128)(2,1)}, u32[]{:S(2)}) copy-start(bf16[64,192]{1,0:T(8,128)(2,1)} %constant.51.clone.refs_10_) | copy-start | bytes 73732
  73.9 5.8 %collective-permute-start.7 = (bf16[8,8,1024]{2,1,0:T(8,128)(2,1)S(1)}, bf16[8,8,1024]{2,1,0:T(8,128)(2,1)S(1)}, u32[]{:S(2)}, u32[]{:S(2)}) collective-permute-start(bf16[8,8,1024]{2,1,0:T(8,128)(2,1)S(1)} %get-tuple-element.10), channel_id=1, source_target_pairs={{0,8},{8,0},{16,24},{24,16},{1,9},{9,1},{17,25},{25,17},{2,10},{10... | collective-permute-start | bytes 393224 | tf_op jit(solution)/shard_map/ppermute | solution.py:278
  75.5 8.0 %collective-permute-start.8 = (bf16[8,8,1024]{2,1,0:T(8,128)(2,1)S(1)}, bf16[8,8,1024]{2,1,0:T(8,128)(2,1)S(1)}, u32[]{:S(2)}, u32[]{:S(2)}) collective-permute-start(bf16[8,8,1024]{2,1,0:T(8,128)(2,1)S(1)} %get-tuple-element.11), channel_id=1, source_target_pairs={{0,16},{8,24},{16,0},{24,8},{1,17},{9,25},{17,1},{25,9},{2,18},{10... | collective-permute-start | bytes 393224 | tf_op jit(solution)/shard_map/ppermute | solution.py:278
  77.0 6.4 %collective-permute-start.9 = (bf16[8,8,1024]{2,1,0:T(8,128)(2,1)S(1)}, bf16[8,8,1024]{2,1,0:T(8,128)(2,1)S(1)}, u32[]{:S(2)}, u32[]{:S(2)}) collective-permute-start(bf16[8,8,1024]{2,1,0:T(8,128)(2,1)S(1)} %get-tuple-element.12), channel_id=1, source_target_pairs={{0,24},{8,16},{16,8},{24,0},{1,25},{9,17},{17,9},{25,1},{2,26},{10... | collective-permute-start | bytes 393224 | tf_op jit(solution)/shard_map/ppermute | solution.py:278

commit v2 on v1

v2 whole, which is shorter than its diff:
```python
import functools
import math

import jax
import jax.numpy as jnp
import ml_dtypes
import numpy as np
from jax import lax
from jax.experimental import pallas as pl
from jax.experimental.pallas import tpu as pltpu
from jax.sharding import PartitionSpec as P

BF16 = jnp.bfloat16
F32 = jnp.float32
LANES = 256
STEPS = 24
SEGS = 2
KEEP = 16


def bf16_table(values):
    return np.asarray(values, dtype=np.float32).astype(ml_dtypes.bfloat16)


@functools.lru_cache(maxsize=None)
def block_tables(block_len):
    size = 2 * block_len
    n = np.arange(block_len)[:, None]
    k = np.arange(block_len)[None, :]
    angle = ((n * k) % size) * (2.0 * math.pi / size)
    fwd_real = np.cos(angle)
    fwd_imag = np.where(k == 0, 1.0 - 2.0 * (n % 2), -np.sin(angle))
    kk = np.arange(block_len)[:, None]
    m = np.arange(block_len)[None, :] + block_len
    angle = ((kk * m) % size) * (2.0 * math.pi / size)
    weight = np.where(kk == 0, 1.0, 2.0)
    inv_real = weight * np.cos(angle) / size
    inv_imag = np.where(kk == 0, (1.0 - 2.0 * (m % 2)) / size, -2.0 * np.sin(angle) / size)
    return (
        bf16_table(np.stack([fwd_real, fwd_imag])),
        bf16_table(np.stack([inv_real, inv_imag])),
    )


@functools.lru_cache(maxsize=None)
def step_tables(parts, frames, channels):
    half = STEPS // 2
    theta = 2.0 * math.pi * (np.arange(STEPS) + 0.5) / STEPS
    first = (np.arange(STEPS) < half).astype(np.float64)[:, None]

    def forward(steps):
        cos = np.cos(theta[:, None] * steps[None, :])
        sin = np.sin(theta[:, None] * steps[None, :])
        plain = np.block([[cos, sin], [-sin, cos]])
        packed = np.block([[cos * first, cos * (1 - first)], [-sin * first, -sin * (1 - first)]])
        return plain, packed

    spec = np.zeros((2, 2, SEGS, STEPS, 2, frames))
    used = parts - 1 + KEEP
    for kind, table in enumerate(forward(np.arange(used))):
        table = table.reshape(2, STEPS, 2, used)
        for seg in range(SEGS):
            spec[kind, :, seg, :, :, seg * KEEP : seg * KEEP + used] = table
    spec = spec.reshape(2, 2 * SEGS * STEPS, 2 * frames)
    spec = np.concatenate([spec[0], spec[1]], axis=1)

    resp = np.zeros((channels, 2, STEPS, 2, parts, channels, 2))
    for kind, table in enumerate(forward(np.arange(parts))):
        table = table.reshape(2, STEPS, 2, parts).transpose(0, 1, 3, 2)
        for c in range(channels):
            resp[c, :, :, kind, :, c] = table
    resp = resp.reshape(channels * 2 * STEPS, 2 * parts * channels * 2)

    back = np.zeros((2, 2, SEGS, KEEP, 2, SEGS, STEPS))
    steps = np.arange(KEEP) + parts - 1
    cos = np.cos(theta[None, :] * steps[:, None]) / STEPS
    sin = np.sin(theta[None, :] * steps[:, None]) / STEPS
    firsts = first[:, 0][None, :]
    for seg in range(SEGS):
        back[0, 0, seg, :, 0, seg] = cos
        back[0, 0, seg, :, 1, seg] = -sin
        back[0, 1, seg, :, 0, seg] = sin
        back[0, 1, seg, :, 1, seg] = cos
        back[1, 0, seg, :, 0, seg] = 2 * cos * firsts
        back[1, 0, seg, :, 1, seg] = -2 * sin * firsts
        back[1, 1, seg, :, 0, seg] = 2 * cos * (1 - firsts)
        back[1, 1, seg, :, 1, seg] = -2 * sin * (1 - firsts)
    back = back.reshape(2, 2 * SEGS * KEEP, 2 * SEGS * STEPS)
    back = np.concatenate([back[0], back[1]], axis=1)
    return bf16_table(spec), bf16_table(resp), bf16_table(back)


def dot(left, right):
    return jnp.dot(left, right, preferred_element_type=F32)


def lane_masks(start, width):
    lane = lax.broadcasted_iota(jnp.int32, (1, width), 1) + start
    packed = (lane == 0).astype(F32)
    sign = (1 - 2 * (lane % 2)).astype(F32)
    return 1.0 - packed, packed, sign


def response_kernel(rows, bins, room_ref, table_ref, hat_ref):
    depth = room_ref.shape[1] * room_ref.shape[2] * 2
    flat = room_ref.reshape(rows, depth, bins)
    plain, packed, _ = lane_masks(0, LANES)
    plain, packed = plain.astype(BF16), packed.astype(BF16)

    def one(r, carry):
        for step in range(bins // LANES):
            at = slice(step * LANES, (step + 1) * LANES)
            h = flat[r, :, at]
            if step == 0:
                h = jnp.concatenate([h * plain, h * packed], axis=0)
                hat = dot(table_ref[...], h)
            else:
                hat = dot(table_ref[:, :depth], h)
            hat_ref[r, :, at] = hat.astype(BF16)
        return carry

    lax.fori_loop(0, rows, one, 0)


def transform_responses(room):
    rows, parts, channels, _, bins = room.shape
    _, resp, _ = step_tables(parts, parts + SEGS * KEEP, channels)
    vmem = pl.BlockSpec(memory_space=pltpu.VMEM)
    flops = 2 * rows * channels * 2 * STEPS * parts * channels * 2 * bins
    return pl.pallas_call(
        functools.partial(response_kernel, rows, bins),
        in_specs=[vmem, vmem],
        out_specs=vmem,
        out_shape=jax.ShapeDtypeStruct((rows, channels * 2 * STEPS, bins), BF16),
        compiler_params=pltpu.CompilerParams(vmem_limit_bytes=24 * 2**20),
        cost_estimate=pl.CostEstimate(flops=flops, bytes_accessed=16 * 2**20, transcendentals=0),
    )(room, jnp.asarray(resp))


def mix_kernel(pieces, rows, channels, blocks, shares, has_total, last, scal, *refs):
    refs = list(refs)
    x_refs = [refs.pop(0) for _ in range(pieces)]
    hat_ref, table_ref, spec_ref = [refs.pop(0) for _ in range(3)]
    total_ref = refs.pop(0) if has_total else None
    if last:
        back_ref, inv_ref = refs.pop(0), refs.pop(0)
        out_refs = [refs.pop(0) for _ in range(shares)]
    else:
        out_ref = refs.pop(0)
    s_ref = refs.pop(0)
    if last:
        y_ref, left_re, left_im, time_ref = refs

    bins = table_ref.shape[2]
    wide = SEGS * STEPS
    x = jnp.concatenate([ref[...] for ref in x_refs], axis=0)
    count = x.shape[0] // rows

    def bin_step(step, carry):
        start = pl.multiple_of(step * LANES, LANES)
        here = pl.ds(start, LANES)
        plain, packed, sign = lane_masks(start, LANES)
        spectra = []
        for j in range(2):
            one = dot(x, table_ref[j, :, here])
            spectra.append(one + sign * pltpu.roll(one, one.shape[0] - 1, axis=0))
        for r in range(rows):
            both = jnp.concatenate([s[r * count : (r + 1) * count] for s in spectra], axis=0)
            both = jnp.concatenate([both * plain, both * packed], axis=0).astype(BF16)
            s_ref[r] = dot(spec_ref[...], both)

        for c in range(channels):
            for cut in range(LANES // 128):
                at = slice(cut * 128, (cut + 1) * 128)
                far = pl.ds(pl.multiple_of(start + cut * 128, 128), 128)
                for seg in range(SEGS):
                    re_rows = slice(seg * STEPS, (seg + 1) * STEPS)
                    im_rows = slice(wide + seg * STEPS, wide + (seg + 1) * STEPS)
                    if has_total:
                        re, im = total_ref[c, re_rows, far], total_ref[c, im_rows, far]
                    else:
                        re, im = None, None
                    for r in range(rows):
                        hat = hat_ref[scal[r], c * 2 * STEPS : (c + 1) * 2 * STEPS, far].astype(F32)
                        h_re, h_im = hat[:STEPS], hat[STEPS:]
                        s_re, s_im = s_ref[r, re_rows, at], s_ref[r, im_rows, at]
                        add_re = s_re * h_re - s_im * h_im
                        add_im = s_re * h_im + s_im * h_re
                        re = add_re if re is None else re + add_re
                        im = add_im if im is None else im + add_im
                    if last:
                        y_ref[re_rows, at] = re
                        y_ref[im_rows, at] = im
                    else:
                        out_ref[c, re_rows, far] = re
                        out_ref[c, im_rows, far] = im
            if last:
                y = y_ref[...]
                y = jnp.concatenate([y * plain, y * packed], axis=0).astype(BF16)
                mix = dot(back_ref[...], y).astype(BF16)
                left_re[c * blocks : (c + 1) * blocks, here] = mix[:blocks]
                left_im[c * blocks : (c + 1) * blocks, here] = mix[blocks:]
        return carry

    lax.fori_loop(0, bins // LANES, bin_step, 0)
    if last:
        each = blocks // shares

        def time_step(step, carry):
            here = pl.ds(pl.multiple_of(step * LANES, LANES), LANES)
            part = dot(left_re[...], inv_ref[0, :, here]) + dot(left_im[...], inv_ref[1, :, here])
            for t in range(shares):
                for c in range(channels):
                    row = c * blocks + t * each
                    time_ref[t, c, :, here] = part[row : row + each]
            return carry

        lax.fori_loop(0, bins // LANES, time_step, 0)
        me = scal[rows]
        for d in range(shares):
            out_refs[d][...] = time_ref[me ^ d].astype(BF16)


def add_sources(x_list, slots, hat, total, last, shares, me, channels, parts):
    bins = hat.shape[2]
    rows = slots.shape[0]
    frames = x_list[0].shape[0] * len(x_list) // rows
    blocks = frames - parts
    wide = 2 * SEGS * STEPS
    table, inverse = block_tables(bins)
    spec, _, back = step_tables(parts, frames, channels)
    scal = jnp.concatenate([slots, me[None]]).astype(jnp.int32)
    vmem = pl.BlockSpec(memory_space=pltpu.VMEM)

    operands = [scal] + list(x_list) + [hat, jnp.asarray(table), jnp.asarray(spec)]
    aliases = {}
    if total is not None:
        if not last:
            aliases = {len(operands): 0}
        operands.append(total)
    scratch = [pltpu.VMEM((rows, wide, LANES), F32)]
    if last:
        operands += [jnp.asarray(back), jnp.asarray(inverse)]
        each = blocks // shares
        out_shape = [jax.ShapeDtypeStruct((channels, each, bins), BF16)] * shares
        scratch += [
            pltpu.VMEM((wide, LANES), F32),
            pltpu.VMEM((channels * blocks, bins), BF16),
            pltpu.VMEM((channels * blocks, bins), BF16),
            pltpu.VMEM((shares, channels, each, bins), F32),
        ]
    else:
        out_shape = jax.ShapeDtypeStruct((channels, wide, bins), F32)
    flops = 2 * bins * (
        rows * frames * 2 * bins + channels * rows * wide * 16 + (channels * blocks * 2 * bins if last else 0)
    )
    body = functools.partial(
        mix_kernel, len(x_list), rows, channels, blocks, shares, total is not None, last
    )
    return pl.pallas_call(
        body,
        in_specs=[pl.BlockSpec(memory_space=pltpu.SMEM)] + [vmem] * (len(operands) - 1),
        out_specs=[vmem] * shares if last else vmem,
        out_shape=out_shape,
        scratch_shapes=scratch,
        input_output_aliases=aliases,
        compiler_params=pltpu.CompilerParams(vmem_limit_bytes=16 * 2**20),
        cost_estimate=pl.CostEstimate(flops=flops, bytes_accessed=8 * 2**20, transcendentals=0),
    )(*operands)


def per_device(src_count, ch_count, dry_signal, room_spectra, render_slot, decoder):
    rows_total, parts, channels, _, block_len = room_spectra.shape
    own = dry_signal.shape[0]
    frames = dry_signal.shape[1] // block_len
    blocks = frames - parts
    src_me = lax.axis_index("src").astype(jnp.int32)
    ch_me = lax.axis_index("ch").astype(jnp.int32)

    x_own = dry_signal.reshape(own * frames, block_len)

    def swap(value, axis, count, flip):
        return lax.ppermute(value, axis, [(i, i ^ flip) for i in range(count)])

    lanes = [x_own] + [swap(x_own, "ch", ch_count, 2 * d) for d in range(1, ch_count // 2)]
    mates = [swap(x, "ch", ch_count, 1) for x in lanes]

    hat = transform_responses(room_spectra)
    slot_local = render_slot % rows_total

    def slots_of(flip):
        start = (ch_me ^ flip) * own
        return lax.dynamic_slice(slot_local, (start,), (own,))

    total = None
    chips = ch_count // 2
    per_call = max(1, chips // 4)
    calls = chips // per_call
    for call in range(calls):
        x_list, slots = [], []
        for d in range(call * per_call, (call + 1) * per_call):
            x_list += [lanes[d], mates[d]]
            slots += [slots_of(2 * d), slots_of(2 * d + 1)]
        total = add_sources(
            x_list,
            jnp.concatenate(slots),
            hat,
            total,
            call == calls - 1,
            src_count,
            src_me,
            channels,
            parts,
        )

    signal = total[0].astype(F32)
    for d in range(1, src_count):
        signal = signal + swap(total[d], "src", src_count, d).astype(F32)
    signal = signal.astype(BF16).reshape(channels, -1)
    gathered = lax.all_to_all(signal, "ch", split_axis=1, concat_axis=0, tiled=True)
    decoded = lax.dot_general(
        gathered, decoder, (((0,), (0,)), ((), ())), preferred_element_type=F32
    )
    return decoded.astype(BF16)


def solution(mesh):
    body = functools.partial(per_device, mesh.shape["src"], mesh.shape["ch"])
    return jax.shard_map(
        body,
        mesh=mesh,
        in_specs=(P(("src", "ch"), None), P("src", None, "ch", None, None), P("src"), P()),
        out_specs=P(("src", "ch"), None),
        check_vma=False,
    )
```

time: 96.5 us -> 72.4 us (0.75)
  local copies, waits for them, and re-layouts: 21.8 us -> 4.38 us
  waiting for transfers between devices: 17.4 us -> 7.8 us
  blocking collectives: 10.3 us -> 12 us
  Pallas kernels: 33.4 us -> 34.9 us
    ppermute x10, waiting for transfers between devices: 17.4 us -> 7.8 us  [swap(): return lax.ppermute(value, axis, [(i, i ^ flip) for i in range(count)])]
    transpose x1 -> x0, local copies, waits for them, and re-layouts: 8.89 us -> none  [per_device(): room_spectra.transpose(0, 2, 1, 3, 4)]
    reshape x1 -> x0, local copies, waits for them, and re-layouts: 7.27 us -> none  [per_device(): room_spectra.transpose(0, 2, 1, 3, 4)]
    all_to_all x1, blocking collectives: 10.3 us -> 12 us  [per_device(): lax.all_to_all(signal, 'ch', split_axis=1, concat_axis=0, tiled=True)]
    pallas_call x4 -> x5, Pallas kernels: 33.4 us -> 34.9 us  [the longest x4 28.4 us: add_sources(): pl.pallas_call(body, in_specs=[pl.BlockSpec(memory_space=pltpu.SMEM)] + [...]
    unnamed x16 -> x14, local copies, waits for them, and re-layouts: 4.4 us -> 3.14 us
  transfers between devices with their start and end apart: 10 -> 10, of which waited for: 4 -> 3; matrix products, arithmetic and copies ran while one was open for 18% -> 1% of each run, Pallas kernels for 21% -> 36%
where the time goes in v2:
time: 72.4 us; the launch traced here: 72.2 us
  Pallas kernels  34.9 us (48%)
  blocking collectives  12 us (17%)
  starting transfers between devices  9.85 us (14%)
  waiting for transfers between devices  7.8 us (11%)
  local copies, waits for them, and re-layouts  4.38 us (6%)
  matrix products  2.05 us (3%)
  other arithmetic  1.04 us (1%)
    pallas_call x4, Pallas kernels, add_sources(): pl.pallas_call(body, in_specs=[pl.BlockSpec(memory_space=pltpu.SMEM)] + [...  28.4 us
    all_to_all x1, blocking collectives, per_device(): lax.all_to_all(signal, 'ch', split_axis=1, concat_axis=0, tiled=True)  12 us
    ppermute x10, starting transfers between devices, swap(): return lax.ppermute(value, axis, [(i, i ^ flip) for i in range(count)])  9.85 us
    ppermute x10, waiting for transfers between devices, swap(): return lax.ppermute(value, axis, [(i, i ^ flip) for i in range(count)])  7.8 us
    pallas_call x1, Pallas kernels, transform_responses(): pl.pallas_call(functools.partial(response_kernel, rows, bins), in_specs=[...  6.45 us
    unnamed x14, local copies, waits for them, and re-layouts  3.14 us
    dot_general x1, matrix products, per_device(): lax.dot_general(gathered, decoder, (((0,), (0,)), ((), ())), preferred_el...  2.05 us
  transfers between devices with their start and end apart: 10, of which 3 were waited for; matrix products, arithmetic and copies ran while one was open for 1% of the time, Pallas kernels for 36%

profile of v2, /device:TPU:0, one launch (start us, length us, event | category | flops | bytes accessed | tf_op | source)
XLA Modules:
  0.0 72.2 jit_solution(13381444142087634858)
XLA Ops:
  0.0 0.0 copy-start
  0.0 1.1 %reshape.8.refs_0_ = bf16[80,1024]{1,0:T(8,128)(2,1)S(1)} reshape(bf16[2,40960]{1,0:T(2,128)(2,1)} %param.9) | data formatting | bytes 327680 | tf_op jit(solution)/shard_map/reshape | solution.py:280
  1.1 0.5 collective-permute-start.6
  1.6 2.6 %collective-permute-start.4 = (bf16[80,1024]{1,0:T(8,128)(2,1)S(1)}, bf16[80,1024]{1,0:T(8,128)(2,1)S(1)}, u32[]{:S(2)}, u32[]{:S(2)}) collective-permute-start(bf16[80,1024]{1,0:T(8,128)(2,1)S(1)} %reshape.8.refs_0_), channel_id=1, source_target_pairs={{0,2},{1,3},{2,0},{3,1},{4,6},{5,7},{6,4},{7,5},{8,10},{9,11},{10,... | collective-permute-start | bytes 491528 | tf_op jit(solution)/shard_map/ppermute | solution.py:283
  4.2 2.6 %collective-permute-start.2 = (bf16[80,1024]{1,0:T(8,128)(2,1)S(1)}, bf16[80,1024]{1,0:T(8,128)(2,1)S(1)}, u32[]{:S(2)}, u32[]{:S(2)}) collective-permute-start(bf16[80,1024]{1,0:T(8,128)(2,1)S(1)} %reshape.8.refs_0_), channel_id=1, source_target_pairs={{0,4},{1,5},{2,6},{3,7},{4,0},{5,1},{6,2},{7,3},{8,12},{9,13},{10,... | collective-permute-start | bytes 491528 | tf_op jit(solution)/shard_map/ppermute | solution.py:283
  6.8 0.0 collective-permute-start
  6.8 0.7 and_select_fusion
  7.5 0.0 copy-start.2
  7.5 2.2 %copy-done.2 = bf16[16,8,8,2,1024]{4,3,2,1,0:T(2,128)(2,1)S(1)} copy-done((bf16[16,8,8,2,1024]{4,3,2,1,0:T(2,128)(2,1)S(1)}, bf16[16,8,8,2,1024]{4,3,2,1,0:T(2,128)(2,1)}, u32[]{:S(2)}) %copy-start.2) | copy-done | bytes 4194328
  9.7 0.0 copy-start.5
  9.7 0.9 %copy-done.5 = bf16[384,256]{1,0:T(8,128)(2,1)S(1)} copy-done((bf16[384,256]{1,0:T(8,128)(2,1)S(1)}, bf16[384,256]{1,0:T(8,128)(2,1)}, u32[]{:S(2)}) %copy-start.5) | copy-done | bytes 196632
  10.6 6.5 %shard_map.91.refs_2_ = bf16[16,384,1024]{2,1,0:T(8,128)(2,1)S(1)} custom-call(bf16[16,8,8,2,1024]{4,3,2,1,0:T(2,128)(2,1)S(1)} %copy-done.2, bf16[384,256]{1,0:T(8,128)(2,1)S(1)} %copy-done.5), custom_call_target="tpu_custom_call" | custom-call | flops 1610612736 | bytes 16777216 | tf_op jit(solution)/shard_map/pallas_call | solution.py:130
  17.1 0.1 fusion.2
  17.2 0.1 add_add_fusion.3.scal
  17.3 0.1 add_add_fusion.2.scal
  17.3 0.1 add_add_fusion.1.scal
  17.4 0.0 collective-permute-done.4.refs_0_
  17.4 0.0 collective-permute-start.5
  17.4 1.8 %collective-permute-done.2.refs_0_ = bf16[80,1024]{1,0:T(8,128)(2,1)S(1)} collective-permute-done((bf16[80,1024]{1,0:T(8,128)(2,1)S(1)}, bf16[80,1024]{1,0:T(8,128)(2,1)S(1)}, u32[]{:S(2)}, u32[]{:S(2)}) %collective-permute-start.2) | collective-permute-done | bytes 163872 | tf_op jit(solution)/shard_map/ppermute | solution.py:283
  19.3 0.0 collective-permute-start.3
  19.3 0.1 add_add_fusion.scal
  19.3 0.0 collective-permute-done.refs_0_
  19.3 0.5 collective-permute-start.1
  19.8 0.0 collective-permute-done.6.refs_1_
  19.9 0.0 copy-done.1
  19.9 0.0 copy-done.4
  19.9 6.2 %shard_map.92.refs_5_ = f32[8,96,1024]{2,1,0:T(8,128)S(1)} custom-call(s32[5]{0:T(128)S(1)} %add_add_fusion.3.scal, bf16[80,1024]{1,0:T(8,128)(2,1)S(1)} %reshape.8.refs_0_, bf16[80,1024]{1,0:T(8,128)(2,1)S(1)} %collective-permute-done.6.refs_1_, bf16[16,384,1024]{2,1,0:T(8,128)(2,1)S(1)} %shard_map.91.refs_2_, bf16[2,1024,1024]{2,1,0:T(8,128)(2,1)S(1)} %copy-done.1, ...), custom_call_target="tpu_custom_call" | custom-call | flops 771751936 | bytes 8388608 | tf_op jit(solution)/shard_map/pallas_call | solution.py:260
  26.1 0.0 collective-permute-done.5.refs_1_
  26.1 6.8 %shard_map.93.refs_5_ = f32[8,96,1024]{2,1,0:T(8,128)S(1)} custom-call(s32[5]{0:T(128)S(1)} %add_add_fusion.2.scal, bf16[80,1024]{1,0:T(8,128)(2,1)S(1)} %collective-permute-done.4.refs_0_, bf16[80,1024]{1,0:T(8,128)(2,1)S(1)} %collective-permute-done.5.refs_1_, bf16[16,384,1024]{2,1,0:T(8,128)(2,1)S(1)} %shard_map.91.refs_2_, ...), custom_call_target="tpu_custom_call", output_to_operand_aliasing={{}: (6, {})} | custom-call | flops 771751936 | bytes 8388608 | tf_op jit(solution)/shard_map/pallas_call | solution.py:260
  32.9 0.0 copy-start.3
  32.9 0.0 copy-start.6
  32.9 0.0 collective-permute-done.3.refs_1_
  32.9 6.8 %shard_map.94.refs_5_ = f32[8,96,1024]{2,1,0:T(8,128)S(1)} custom-call(s32[5]{0:T(128)S(1)} %add_add_fusion.1.scal, bf16[80,1024]{1,0:T(8,128)(2,1)S(1)} %collective-permute-done.2.refs_0_, bf16[80,1024]{1,0:T(8,128)(2,1)S(1)} %collective-permute-done.3.refs_1_, bf16[16,384,1024]{2,1,0:T(8,128)(2,1)S(1)} %shard_map.91.refs_2_, ...), custom_call_target="tpu_custom_call", output_to_operand_aliasing={{}: (6, {})} | custom-call | flops 771751936 | bytes 8388608 | tf_op jit(solution)/shard_map/pallas_call | solution.py:260
  39.7 0.0 collective-permute-done.1.refs_1_
  39.7 0.0 copy-done.3
  39.8 0.0 copy-done.6
  39.8 8.6 %shard_map.95 = (bf16[8,8,1024]{2,1,0:T(8,128)(2,1)S(1)}, bf16[8,8,1024]{2,1,0:T(8,128)(2,1)S(1)}, bf16[8,8,1024]{2,1,0:T(8,128)(2,1)S(1)}, bf16[8,8,1024]{2,1,0:T(8,128)(2,1)S(1)}) custom-call(s32[5]{0:T(128)S(1)} %add_add_fusion.scal, bf16[80,1024]{1,0:T(8,128)(2,1)S(1)} %collective-permute-done.refs_0_, ...), custom_call_target="tpu_custom_call" | custom-call | flops 1845493760 | bytes 8388608 | tf_op jit(solution)/shard_map/pallas_call | solution.py:260
  48.4 1.6 %collective-permute-start.7 = (bf16[8,8,1024]{2,1,0:T(8,128)(2,1)S(1)}, bf16[8,8,1024]{2,1,0:T(8,128)(2,1)S(1)}, u32[]{:S(2)}, u32[]{:S(2)}) collective-permute-start(bf16[8,8,1024]{2,1,0:T(8,128)(2,1)S(1)} %get-tuple-element.10), channel_id=1, source_target_pairs={{0,8},{8,0},{16,24},{24,16},{1,9},{9,1},{17,25},{25,17},{2,10},{10... | collective-permute-start | bytes 393224 | tf_op jit(solution)/shard_map/ppermute | solution.py:283
  50.0 1.5 %collective-permute-start.8 = (bf16[8,8,1024]{2,1,0:T(8,128)(2,1)S(1)}, bf16[8,8,1024]{2,1,0:T(8,128)(2,1)S(1)}, u32[]{:S(2)}, u32[]{:S(2)}) collective-permute-start(bf16[8,8,1024]{2,1,0:T(8,128)(2,1)S(1)} %get-tuple-element.11), channel_id=1, source_target_pairs={{0,16},{8,24},{16,0},{24,8},{1,17},{9,25},{17,1},{25,9},{2,18},{10... | collective-permute-start | bytes 393224 | tf_op jit(solution)/shard_map/ppermute | solution.py:283
  51.5 0.5 collective-permute-start.9
  52.0 2.3 %collective-permute-done.7 = bf16[8,8,1024]{2,1,0:T(8,128)(2,1)S(1)} collective-permute-done((bf16[8,8,1024]{2,1,0:T(8,128)(2,1)S(1)}, bf16[8,8,1024]{2,1,0:T(8,128)(2,1)S(1)}, u32[]{:S(2)}, u32[]{:S(2)}) %collective-permute-start.7) | collective-permute-done | bytes 131104 | tf_op jit(solution)/shard_map/ppermute | solution.py:283
  54.3 3.7 %collective-permute-done.8 = bf16[8,8,1024]{2,1,0:T(8,128)(2,1)S(1)} collective-permute-done((bf16[8,8,1024]{2,1,0:T(8,128)(2,1)S(1)}, bf16[8,8,1024]{2,1,0:T(8,128)(2,1)S(1)}, u32[]{:S(2)}, u32[]{:S(2)}) %collective-permute-start.8) | collective-permute-done | bytes 131104 | tf_op jit(solution)/shard_map/ppermute | solution.py:283
  57.9 0.0 collective-permute-done.9
  57.9 0.1 add_convert_fusion
  58.0 0.1 copy.13
  58.1 12.0 %all_to_all.16 = bf16[8,8,1024]{2,0,1:T(8,128)(2,1)S(1)} all-to-all(bf16[8,8,1024]{2,0,1:T(8,128)(2,1)S(1)} %copy.13), channel_id=1, replica_groups=mesh['src'=4,'ch'=8] {'ch'}, dimensions={1} | all-to-all | bytes 262144 | tf_op jit(solution)/shard_map/all_to_all | solution.py:320
  70.1 0.0 copy-done
  70.1 2.1 %convolution_convert_fusion = bf16[1024,1024]{1,0:T(8,128)(2,1)} fusion(bf16[64,1024]{1,0:T(8,128)(2,1)S(1)} %copy-done, bf16[8,8,1024]{2,0,1:T(8,128)(2,1)S(1)} %all_to_all.16), kind=kOutput, calls=%fused_computation | convolution fusion | flops 135266304 | bytes 2359296 | tf_op jit(solution)/shard_map/dot_general | solution.py:321
  (2 shorter events, 0.0 us)
Async XLA Ops:
  0.0 70.1 %copy-start = (bf16[64,1024]{1,0:T(8,128)(2,1)S(1)}, bf16[64,1024]{1,0:T(8,128)(2,1)}, u32[]{:S(2)}) copy-start(bf16[64,1024]{1,0:T(8,128)(2,1)} %param.12) | copy-start | bytes 393220
  1.1 18.8 %collective-permute-start.6 = (bf16[80,1024]{1,0:T(8,128)(2,1)S(1)}, bf16[80,1024]{1,0:T(8,128)(2,1)S(1)}, u32[]{:S(2)}, u32[]{:S(2)}) collective-permute-start(bf16[80,1024]{1,0:T(8,128)(2,1)S(1)} %reshape.8.refs_0_), channel_id=1, source_target_pairs={{0,1},{1,0},{2,3},{3,2},{4,5},{5,4},{6,7},{7,6},{8,9},{9,8},{10,11... | collective-permute-start | bytes 491528 | tf_op jit(solution)/shard_map/ppermute | solution.py:283
  1.6 15.8 %collective-permute-start.4 = (bf16[80,1024]{1,0:T(8,128)(2,1)S(1)}, bf16[80,1024]{1,0:T(8,128)(2,1)S(1)}, u32[]{:S(2)}, u32[]{:S(2)}) collective-permute-start(bf16[80,1024]{1,0:T(8,128)(2,1)S(1)} %reshape.8.refs_0_), channel_id=1, source_target_pairs={{0,2},{1,3},{2,0},{3,1},{4,6},{5,7},{6,4},{7,5},{8,10},{9,11},{10,... | collective-permute-start | bytes 491528 | tf_op jit(solution)/shard_map/ppermute | solution.py:283
  4.2 15.0 %collective-permute-start.2 = (bf16[80,1024]{1,0:T(8,128)(2,1)S(1)}, bf16[80,1024]{1,0:T(8,128)(2,1)S(1)}, u32[]{:S(2)}, u32[]{:S(2)}) collective-permute-start(bf16[80,1024]{1,0:T(8,128)(2,1)S(1)} %reshape.8.refs_0_), channel_id=1, source_target_pairs={{0,4},{1,5},{2,6},{3,7},{4,0},{5,1},{6,2},{7,3},{8,12},{9,13},{10,... | collective-permute-start | bytes 491528 | tf_op jit(solution)/shard_map/ppermute | solution.py:283
  6.8 12.5 %collective-permute-start = (bf16[80,1024]{1,0:T(8,128)(2,1)S(1)}, bf16[80,1024]{1,0:T(8,128)(2,1)S(1)}, u32[]{:S(2)}, u32[]{:S(2)}) collective-permute-start(bf16[80,1024]{1,0:T(8,128)(2,1)S(1)} %reshape.8.refs_0_), channel_id=1, source_target_pairs={{0,6},{1,7},{2,4},{3,5},{4,2},{5,3},{6,0},{7,1},{8,14},{9,15},{10,... | collective-permute-start | bytes 491528 | tf_op jit(solution)/shard_map/ppermute | solution.py:283
  7.5 2.2 %copy-start.2 = (bf16[16,8,8,2,1024]{4,3,2,1,0:T(2,128)(2,1)S(1)}, bf16[16,8,8,2,1024]{4,3,2,1,0:T(2,128)(2,1)}, u32[]{:S(2)}) copy-start(bf16[16,8,8,2,1024]{4,3,2,1,0:T(2,128)(2,1)} %room_ref.1) | copy-start | bytes 12582916
  9.7 0.9 %copy-start.5 = (bf16[384,256]{1,0:T(8,128)(2,1)S(1)}, bf16[384,256]{1,0:T(8,128)(2,1)}, u32[]{:S(2)}) copy-start(bf16[384,256]{1,0:T(8,128)(2,1)} %constant.48.clone.table_ref) | copy-start | bytes 589828
  10.6 9.2 %copy-start.1 = (bf16[2,1024,1024]{2,1,0:T(8,128)(2,1)S(1)}, bf16[2,1024,1024]{2,1,0:T(8,128)(2,1)}, u32[]{:S(2)}) copy-start(bf16[2,1024,1024]{2,1,0:T(8,128)(2,1)} %constant.49.clone.refs_3_) | copy-start | bytes 12582916
  10.6 9.2 %copy-start.4 = (bf16[96,160]{1,0:T(8,128)(2,1)S(1)}, bf16[96,160]{1,0:T(8,128)(2,1)}, u32[]{:S(2)}) copy-start(bf16[96,160]{1,0:T(8,128)(2,1)} %constant.50.clone.refs_4_) | copy-start | bytes 92164
  17.4 8.7 %collective-permute-start.5 = (bf16[80,1024]{1,0:T(8,128)(2,1)S(1)}, bf16[80,1024]{1,0:T(8,128)(2,1)S(1)}, u32[]{:S(2)}, u32[]{:S(2)}) collective-permute-start(bf16[80,1024]{1,0:T(8,128)(2,1)S(1)} %collective-permute-done.4.refs_0_), channel_id=1, source_target_pairs={{0,1},{1,0},{2,3},{3,2},{4,5},{5,4},{6,7},{7,6},{8,9},{9,8},{10,11... | collective-permute-start | bytes 491528 | tf_op jit(solution)/shard_map/ppermute | solution.py:283
  19.3 13.7 %collective-permute-start.3 = (bf16[80,1024]{1,0:T(8,128)(2,1)S(1)}, bf16[80,1024]{1,0:T(8,128)(2,1)S(1)}, u32[]{:S(2)}, u32[]{:S(2)}) collective-permute-start(bf16[80,1024]{1,0:T(8,128)(2,1)S(1)} %collective-permute-done.2.refs_0_), channel_id=1, source_target_pairs={{0,1},{1,0},{2,3},{3,2},{4,5},{5,4},{6,7},{7,6},{8,9},{9,8},{10,11... | collective-permute-start | bytes 491528 | tf_op jit(solution)/shard_map/ppermute | solution.py:283
  19.3 20.4 %collective-permute-start.1 = (bf16[80,1024]{1,0:T(8,128)(2,1)S(1)}, bf16[80,1024]{1,0:T(8,128)(2,1)S(1)}, u32[]{:S(2)}, u32[]{:S(2)}) collective-permute-start(bf16[80,1024]{1,0:T(8,128)(2,1)S(1)} %collective-permute-done.refs_0_), channel_id=1, source_target_pairs={{0,1},{1,0},{2,3},{3,2},{4,5},{5,4},{6,7},{7,6},{8,9},{9,8},{10,11... | collective-permute-start | bytes 491528 | tf_op jit(solution)/shard_map/ppermute | solution.py:283
  32.9 6.8 %copy-start.3 = (bf16[2,1024,1024]{2,1,0:T(8,128)(2,1)S(1)}, bf16[2,1024,1024]{2,1,0:T(8,128)(2,1)}, u32[]{:S(2)}) copy-start(bf16[2,1024,1024]{2,1,0:T(8,128)(2,1)} %constant.52.clone.refs_7_) | copy-start | bytes 12582916
  32.9 6.8 %copy-start.6 = (bf16[64,192]{1,0:T(8,128)(2,1)S(1)}, bf16[64,192]{1,0:T(8,128)(2,1)}, u32[]{:S(2)}) copy-start(bf16[64,192]{1,0:T(8,128)(2,1)} %constant.51.clone.refs_6_) | copy-start | bytes 73732
  48.4 5.8 %collective-permute-start.7 = (bf16[8,8,1024]{2,1,0:T(8,128)(2,1)S(1)}, bf16[8,8,1024]{2,1,0:T(8,128)(2,1)S(1)}, u32[]{:S(2)}, u32[]{:S(2)}) collective-permute-start(bf16[8,8,1024]{2,1,0:T(8,128)(2,1)S(1)} %get-tuple-element.10), channel_id=1, source_target_pairs={{0,8},{8,0},{16,24},{24,16},{1,9},{9,1},{17,25},{25,17},{2,10},{10... | collective-permute-start | bytes 393224 | tf_op jit(solution)/shard_map/ppermute | solution.py:283
  50.0 8.0 %collective-permute-start.8 = (bf16[8,8,1024]{2,1,0:T(8,128)(2,1)S(1)}, bf16[8,8,1024]{2,1,0:T(8,128)(2,1)S(1)}, u32[]{:S(2)}, u32[]{:S(2)}) collective-permute-start(bf16[8,8,1024]{2,1,0:T(8,128)(2,1)S(1)} %get-tuple-element.11), channel_id=1, source_target_pairs={{0,16},{8,24},{16,0},{24,8},{1,17},{9,25},{17,1},{25,9},{2,18},{10... | collective-permute-start | bytes 393224 | tf_op jit(solution)/shard_map/ppermute | solution.py:283
  51.5 6.4 %collective-permute-start.9 = (bf16[8,8,1024]{2,1,0:T(8,128)(2,1)S(1)}, bf16[8,8,1024]{2,1,0:T(8,128)(2,1)S(1)}, u32[]{:S(2)}, u32[]{:S(2)}) collective-permute-start(bf16[8,8,1024]{2,1,0:T(8,128)(2,1)S(1)} %get-tuple-element.12), channel_id=1, source_target_pairs={{0,24},{8,16},{16,8},{24,0},{1,25},{9,17},{17,9},{25,1},{2,26},{10... | collective-permute-start | bytes 393224 | tf_op jit(solution)/shard_map/ppermute | solution.py:283

commit v3 on v2

--- a/solution.py
+++ b/solution.py
@@ -55,38 +55,38 @@
         packed = np.block([[cos * first, cos * (1 - first)], [-sin * first, -sin * (1 - first)]])
         return plain, packed
 
-    spec = np.zeros((2, 2, SEGS, STEPS, 2, frames))
+    spec = np.zeros((2, SEGS, 2, 2, STEPS, 2, frames))
     used = parts - 1 + KEEP
     for kind, table in enumerate(forward(np.arange(used))):
-        table = table.reshape(2, STEPS, 2, used)
+        table = table.reshape(2, 1, STEPS, 2, used)
         for seg in range(SEGS):
-            spec[kind, :, seg, :, :, seg * KEEP : seg * KEEP + used] = table
-    spec = spec.reshape(2, 2 * SEGS * STEPS, 2 * frames)
+            spec[kind, seg, :, :, :, :, seg * KEEP : seg * KEEP + used] = table
+    spec = spec.reshape(2, SEGS * 4 * STEPS, 2 * frames)
     spec = np.concatenate([spec[0], spec[1]], axis=1)
 
-    resp = np.zeros((channels, 2, STEPS, 2, parts, channels, 2))
+    resp = np.zeros((channels // 2, 2, 2, STEPS, 2, parts, channels, 2))
     for kind, table in enumerate(forward(np.arange(parts))):
         table = table.reshape(2, STEPS, 2, parts).transpose(0, 1, 3, 2)
         for c in range(channels):
-            resp[c, :, :, kind, :, c] = table
+            resp[c // 2, :, c % 2, :, kind, :, c] = table
     resp = resp.reshape(channels * 2 * STEPS, 2 * parts * channels * 2)
 
-    back = np.zeros((2, 2, SEGS, KEEP, 2, SEGS, STEPS))
+    back = np.zeros((2, 2, 2, SEGS, KEEP, SEGS, 2, 2, STEPS))
     steps = np.arange(KEEP) + parts - 1
     cos = np.cos(theta[None, :] * steps[:, None]) / STEPS
     sin = np.sin(theta[None, :] * steps[:, None]) / STEPS
     firsts = first[:, 0][None, :]
     for seg in range(SEGS):
-        back[0, 0, seg, :, 0, seg] = cos
-        back[0, 0, seg, :, 1, seg] = -sin
-        back[0, 1, seg, :, 0, seg] = sin
-        back[0, 1, seg, :, 1, seg] = cos
-        back[1, 0, seg, :, 0, seg] = 2 * cos * firsts
-        back[1, 0, seg, :, 1, seg] = -2 * sin * firsts
-        back[1, 1, seg, :, 0, seg] = 2 * cos * (1 - firsts)
-        back[1, 1, seg, :, 1, seg] = -2 * sin * (1 - firsts)
-    back = back.reshape(2, 2 * SEGS * KEEP, 2 * SEGS * STEPS)
-    back = np.concatenate([back[0], back[1]], axis=1)
+        for c in range(2):
+            back[0, c, 0, seg, :, seg, 0, c] = cos
+            back[0, c, 0, seg, :, seg, 1, c] = -sin
+            back[0, c, 1, seg, :, seg, 0, c] = sin
+            back[0, c, 1, seg, :, seg, 1, c] = cos
+            back[1, c, 0, seg, :, seg, 0, c] = 2 * cos * firsts
+            back[1, c, 0, seg, :, seg, 1, c] = -2 * sin * firsts
+            back[1, c, 1, seg, :, seg, 0, c] = 2 * cos * (1 - firsts)
+            back[1, c, 1, seg, :, seg, 1, c] = -2 * sin * (1 - firsts)
+    back = back.reshape(2, 4 * SEGS * KEEP, 4 * SEGS * STEPS)
     return bf16_table(spec), bf16_table(resp), bf16_table(back)
 
 
@@ -101,13 +101,20 @@
     return 1.0 - packed, packed, sign
 
 
-def response_kernel(rows, bins, room_ref, table_ref, hat_ref):
+def response_kernel(rows, bins, room_hbm, table_ref, hat_ref, room_ref, sems):
     depth = room_ref.shape[1] * room_ref.shape[2] * 2
     flat = room_ref.reshape(rows, depth, bins)
     plain, packed, _ = lane_masks(0, LANES)
     plain, packed = plain.astype(BF16), packed.astype(BF16)
 
+    def copy(r):
+        return pltpu.make_async_copy(room_hbm.at[r], room_ref.at[r], sems.at[r])
+
+    for r in range(rows):
+        copy(r).start()
+
     def one(r, carry):
+        copy(r).wait()
         for step in range(bins // LANES):
             at = slice(step * LANES, (step + 1) * LANES)
             h = flat[r, :, at]
@@ -129,9 +136,10 @@
     flops = 2 * rows * channels * 2 * STEPS * parts * channels * 2 * bins
     return pl.pallas_call(
         functools.partial(response_kernel, rows, bins),
-        in_specs=[vmem, vmem],
+        in_specs=[pl.BlockSpec(memory_space=pl.ANY), vmem],
         out_specs=vmem,
         out_shape=jax.ShapeDtypeStruct((rows, channels * 2 * STEPS, bins), BF16),
+        scratch_shapes=[pltpu.VMEM(room.shape, BF16), pltpu.SemaphoreType.DMA((rows,))],
         compiler_params=pltpu.CompilerParams(vmem_limit_bytes=24 * 2**20),
         cost_estimate=pl.CostEstimate(flops=flops, bytes_accessed=16 * 2**20, transcendentals=0),
     )(room, jnp.asarray(resp))
@@ -152,70 +160,86 @@
         y_ref, left_re, left_im, time_ref = refs
 
     bins = table_ref.shape[2]
-    wide = SEGS * STEPS
+    half = 2 * STEPS
     x = jnp.concatenate([ref[...] for ref in x_refs], axis=0)
     count = x.shape[0] // rows
-
-    def bin_step(step, carry):
-        start = pl.multiple_of(step * LANES, LANES)
-        here = pl.ds(start, LANES)
-        plain, packed, sign = lane_masks(start, LANES)
+    cols = 2 * count
+
+    def spectra_step(step):
+        here = slice(step * LANES, (step + 1) * LANES)
+        plain, packed, sign = lane_masks(step * LANES, LANES)
         spectra = []
         for j in range(2):
             one = dot(x, table_ref[j, :, here])
             spectra.append(one + sign * pltpu.roll(one, one.shape[0] - 1, axis=0))
         for r in range(rows):
             both = jnp.concatenate([s[r * count : (r + 1) * count] for s in spectra], axis=0)
-            both = jnp.concatenate([both * plain, both * packed], axis=0).astype(BF16)
-            s_ref[r] = dot(spec_ref[...], both)
-
-        for c in range(channels):
+            if step == 0:
+                both = jnp.concatenate([both * plain, both * packed], axis=0).astype(BF16)
+                s_ref[step, r] = dot(spec_ref[...], both).astype(BF16)
+            else:
+                s_ref[step, r] = dot(spec_ref[:, :cols], both.astype(BF16)).astype(BF16)
+
+    def product_step(step):
+        for pair in range(channels // 2):
             for cut in range(LANES // 128):
                 at = slice(cut * 128, (cut + 1) * 128)
-                far = pl.ds(pl.multiple_of(start + cut * 128, 128), 128)
+                far = slice(step * LANES + cut * 128, step * LANES + (cut + 1) * 128)
+                base = pair * 2 * half
+                hats = [
+                    (hat_ref[scal[r], base : base + half, far], hat_ref[scal[r], base + half : base + 2 * half, far])
+                    for r in range(rows)
+                ]
                 for seg in range(SEGS):
-                    re_rows = slice(seg * STEPS, (seg + 1) * STEPS)
-                    im_rows = slice(wide + seg * STEPS, wide + (seg + 1) * STEPS)
-                    if has_total:
-                        re, im = total_ref[c, re_rows, far], total_ref[c, im_rows, far]
-                    else:
-                        re, im = None, None
+                    re_rows = slice(2 * seg * half, (2 * seg + 1) * half)
+                    im_rows = slice((2 * seg + 1) * half, (2 * seg + 2) * half)
+                    re, im = None, None
                     for r in range(rows):
-                        hat = hat_ref[scal[r], c * 2 * STEPS : (c + 1) * 2 * STEPS, far].astype(F32)
-                        h_re, h_im = hat[:STEPS], hat[STEPS:]
-                        s_re, s_im = s_ref[r, re_rows, at], s_ref[r, im_rows, at]
+                        h_re, h_im = hats[r]
+                        s_re, s_im = s_ref[step, r, re_rows, at], s_ref[step, r, im_rows, at]
                         add_re = s_re * h_re - s_im * h_im
                         add_im = s_re * h_im + s_im * h_re
                         re = add_re if re is None else re + add_re
                         im = add_im if im is None else im + add_im
+                    re, im = re.astype(F32), im.astype(F32)
+                    if has_total:
+                        re, im = re + total_ref[pair, re_rows, far], im + total_ref[pair, im_rows, far]
                     if last:
-                        y_ref[re_rows, at] = re
-                        y_ref[im_rows, at] = im
+                        y_ref[step, pair, re_rows, at] = re.astype(BF16)
+                        y_ref[step, pair, im_rows, at] = im.astype(BF16)
                     else:
-                        out_ref[c, re_rows, far] = re
-                        out_ref[c, im_rows, far] = im
+                        out_ref[pair, re_rows, far] = re
+                        out_ref[pair, im_rows, far] = im
             if last:
-                y = y_ref[...]
-                y = jnp.concatenate([y * plain, y * packed], axis=0).astype(BF16)
-                mix = dot(back_ref[...], y).astype(BF16)
-                left_re[c * blocks : (c + 1) * blocks, here] = mix[:blocks]
-                left_im[c * blocks : (c + 1) * blocks, here] = mix[blocks:]
-        return carry
-
-    lax.fori_loop(0, bins // LANES, bin_step, 0)
+                here = slice(step * LANES, (step + 1) * LANES)
+                y = y_ref[step, pair]
+                if step == 0:
+                    plain, packed, _ = lane_masks(0, LANES)
+                    mix = dot(back_ref[0], y * plain.astype(BF16)) + dot(back_ref[1], y * packed.astype(BF16))
+                else:
+                    mix = dot(back_ref[0], y)
+                mix = mix.astype(BF16)
+                for c in range(2):
+                    rows_to = slice((2 * pair + c) * blocks, (2 * pair + c + 1) * blocks)
+                    left_re[rows_to, here] = mix[2 * c * blocks : (2 * c + 1) * blocks]
+                    left_im[rows_to, here] = mix[(2 * c + 1) * blocks : (2 * c + 2) * blocks]
+
+    steps = bins // LANES
+    spectra_step(0)
+    for step in range(steps):
+        if step + 1 < steps:
+            spectra_step(step + 1)
+        product_step(step)
+
     if last:
         each = blocks // shares
-
-        def time_step(step, carry):
-            here = pl.ds(pl.multiple_of(step * LANES, LANES), LANES)
+        for step in range(steps):
+            here = slice(step * LANES, (step + 1) * LANES)
             part = dot(left_re[...], inv_ref[0, :, here]) + dot(left_im[...], inv_ref[1, :, here])
             for t in range(shares):
                 for c in range(channels):
                     row = c * blocks + t * each
                     time_ref[t, c, :, here] = part[row : row + each]
-            return carry
-
-        lax.fori_loop(0, bins // LANES, time_step, 0)
         me = scal[rows]
         for d in range(shares):
             out_refs[d][...] = time_ref[me ^ d].astype(BF16)
@@ -238,19 +262,19 @@
         if not last:
             aliases = {len(operands): 0}
         operands.append(total)
-    scratch = [pltpu.VMEM((rows, wide, LANES), F32)]
+    scratch = [pltpu.VMEM((bins // LANES, rows, 2 * wide, LANES), BF16)]
     if last:
         operands += [jnp.asarray(back), jnp.asarray(inverse)]
         each = blocks // shares
         out_shape = [jax.ShapeDtypeStruct((channels, each, bins), BF16)] * shares
         scratch += [
-            pltpu.VMEM((wide, LANES), F32),
+            pltpu.VMEM((bins // LANES, channels // 2, 2 * wide, LANES), BF16),
             pltpu.VMEM((channels * blocks, bins), BF16),
             pltpu.VMEM((channels * blocks, bins), BF16),
             pltpu.VMEM((shares, channels, each, bins), F32),
         ]
     else:
-        out_shape = jax.ShapeDtypeStruct((channels, wide, bins), F32)
+        out_shape = jax.ShapeDtypeStruct((channels // 2, 2 * wide, bins), F32)
     flops = 2 * bins * (
         rows * frames * 2 * bins + channels * rows * wide * 16 + (channels * blocks * 2 * bins if last else 0)
     )
@@ -264,9 +288,32 @@
         out_shape=out_shape,
         scratch_shapes=scratch,
         input_output_aliases=aliases,
-        compiler_params=pltpu.CompilerParams(vmem_limit_bytes=16 * 2**20),
+        compiler_params=pltpu.CompilerParams(vmem_limit_bytes=20 * 2**20),
         cost_estimate=pl.CostEstimate(flops=flops, bytes_accessed=8 * 2**20, transcendentals=0),
     )(*operands)
+
+
+def sum_kernel(count, each, me_ref, *refs):
+    parts, outs, sum_ref = refs[:count], refs[count:-1], refs[-1]
+    total = parts[0][...].astype(F32)
+    for part in parts[1:]:
+        total = total + part[...].astype(F32)
+    sum_ref[...] = total
+    for d in range(each):
+        outs[d][...] = sum_ref[:, pl.ds(me_ref[0] ^ d, 1), :].reshape(outs[d].shape).astype(BF16)
+
+
+def sum_groups(parts, me):
+    channels, each, bins = parts[0].shape
+    vmem = pl.BlockSpec(memory_space=pltpu.VMEM)
+    return pl.pallas_call(
+        functools.partial(sum_kernel, len(parts), each),
+        in_specs=[pl.BlockSpec(memory_space=pltpu.SMEM)] + [vmem] * len(parts),
+        out_specs=[vmem] * each,
+        out_shape=[jax.ShapeDtypeStruct((channels, bins), BF16)] * each,
+        scratch_shapes=[pltpu.VMEM(parts[0].shape, F32)],
+        compiler_params=pltpu.CompilerParams(vmem_limit_bytes=8 * 2**20),
+    )(me[None], *parts)
 
 
 def per_device(src_count, ch_count, dry_signal, room_spectra, render_slot, decoder):
@@ -287,6 +334,11 @@
 
     hat = transform_responses(room_spectra)
     slot_local = render_slot % rows_total
+
+    row = jnp.arange(ch_count * channels, dtype=jnp.int32)
+    takes = ((row // channels) ^ ch_me) * channels + row % channels
+    order = (takes[:, None] == row[None, :]).astype(BF16)
+    own_order = dot(order, decoder).astype(BF16)
 
     def slots_of(flip):
         start = (ch_me ^ flip) * own
@@ -313,13 +365,22 @@
             parts,
         )
 
-    signal = total[0].astype(F32)
-    for d in range(1, src_count):
-        signal = signal + swap(total[d], "src", src_count, d).astype(F32)
-    signal = signal.astype(BF16).reshape(channels, -1)
-    gathered = lax.all_to_all(signal, "ch", split_axis=1, concat_axis=0, tiled=True)
+    parts_in = [total[0]] + [swap(total[d], "src", src_count, d) for d in range(1, src_count)]
+    each = blocks // src_count
+    if each == ch_count:
+        pieces = sum_groups(parts_in, ch_me)
+        pieces = [pieces[0]] + [swap(pieces[d], "ch", ch_count, d) for d in range(1, ch_count)]
+        gathered = jnp.concatenate(pieces, axis=0)
+        matrix = own_order
+    else:
+        signal = parts_in[0].astype(F32)
+        for part in parts_in[1:]:
+            signal = signal + part.astype(F32)
+        signal = signal.astype(BF16).reshape(channels, -1)
+        gathered = lax.all_to_all(signal, "ch", split_axis=1, concat_axis=0, tiled=True)
+        matrix = decoder
     decoded = lax.dot_general(
-        gathered, decoder, (((0,), (0,)), ((), ())), preferred_element_type=F32
+        gathered, matrix, (((0,), (0,)), ((), ())), preferred_element_type=F32
     )
     return decoded.astype(BF16)
 

time: 72.4 us -> 68.4 us (0.945)
  blocking collectives: 12 us -> 0 us
  starting transfers between devices: 9.85 us -> 19.4 us
  Pallas kernels: 34.9 us -> 30.2 us
  waiting for transfers between devices: 7.8 us -> 10.9 us
    all_to_all x1 -> x0, blocking collectives: 12 us -> none  [per_device(): lax.all_to_all(signal, 'ch', split_axis=1, concat_axis=0, tiled=True)]
    ppermute x10 -> x17, starting transfers between devices: 9.85 us -> 19.4 us  [swap(): return lax.ppermute(value, axis, [(i, i ^ flip) for i in range(count)])]
    pallas_call x4, Pallas kernels: 28.4 us -> 22.8 us  [add_sources(): pl.pallas_call(body, in_specs=[pl.BlockSpec(memory_space=pltpu.SMEM)] + [...]
    ppermute x10 -> x17, waiting for transfers between devices: 7.8 us -> 10.9 us  [swap(): return lax.ppermute(value, axis, [(i, i ^ flip) for i in range(count)])]
    unnamed x14 -> x21, local copies, waits for them, and re-layouts: 3.14 us -> 3.16 us
  transfers between devices with their start and end apart: 10 -> 17, of which waited for: 3 -> 6; matrix products, arithmetic and copies ran while one was open for 1% -> 2% of each run, Pallas kernels for 36% -> 33%
where the time goes in v3:
time: 68.4 us; the launch traced here: 68.3 us
  Pallas kernels  30.2 us (44%)
  starting transfers between devices  19.4 us (28%)
  waiting for transfers between devices  10.9 us (16%)
  local copies, waits for them, and re-layouts  4.32 us (6%)
  matrix products  2.2 us (3%)
  other arithmetic  0.97 us (1%)
    pallas_call x4, Pallas kernels, add_sources(): pl.pallas_call(body, in_specs=[pl.BlockSpec(memory_space=pltpu.SMEM)] + [...  22.8 us
    ppermute x17, starting transfers between devices, swap(): return lax.ppermute(value, axis, [(i, i ^ flip) for i in range(count)])  19.4 us
    ppermute x17, waiting for transfers between devices, swap(): return lax.ppermute(value, axis, [(i, i ^ flip) for i in range(count)])  10.9 us
    pallas_call x1, Pallas kernels, transform_responses(): pl.pallas_call(functools.partial(response_kernel, rows, bins), in_specs=[...  6.93 us
    unnamed x21, local copies, waits for them, and re-layouts  3.16 us
    dot_general x1, matrix products, per_device(): lax.dot_general(gathered, matrix, (((0,), (0,)), ((), ())), preferred_ele...  2.2 us
  transfers between devices with their start and end apart: 17, of which 6 were waited for; matrix products, arithmetic and copies ran while one was open for 2% of the time, Pallas kernels for 33%

profile of v3, /device:TPU:0, one launch (start us, length us, event | category | flops | bytes accessed | tf_op | source)
XLA Modules:
  0.0 68.3 jit_solution(2318599593705324257)
XLA Ops:
  0.0 1.1 %reshape.26.refs_0_ = bf16[80,1024]{1,0:T(8,128)(2,1)S(1)} reshape(bf16[2,40960]{1,0:T(2,128)(2,1)} %param.9) | data formatting | bytes 327680 | tf_op jit(solution)/shard_map/reshape | solution.py:327
  1.1 0.5 collective-permute-start.6
  1.6 2.6 %collective-permute-start.4 = (bf16[80,1024]{1,0:T(8,128)(2,1)S(1)}, bf16[80,1024]{1,0:T(8,128)(2,1)S(1)}, u32[]{:S(2)}, u32[]{:S(2)}) collective-permute-start(bf16[80,1024]{1,0:T(8,128)(2,1)S(1)} %reshape.26.refs_0_), channel_id=1, source_target_pairs={{0,2},{1,3},{2,0},{3,1},{4,6},{5,7},{6,4},{7,5},{8,10},{9,11},{10,... | collective-permute-start | bytes 491528 | tf_op jit(solution)/shard_map/ppermute | solution.py:330
  4.2 2.6 %collective-permute-start.2 = (bf16[80,1024]{1,0:T(8,128)(2,1)S(1)}, bf16[80,1024]{1,0:T(8,128)(2,1)S(1)}, u32[]{:S(2)}, u32[]{:S(2)}) collective-permute-start(bf16[80,1024]{1,0:T(8,128)(2,1)S(1)} %reshape.26.refs_0_), channel_id=1, source_target_pairs={{0,4},{1,5},{2,6},{3,7},{4,0},{5,1},{6,2},{7,3},{8,12},{9,13},{10,... | collective-permute-start | bytes 491528 | tf_op jit(solution)/shard_map/ppermute | solution.py:330
  6.8 0.0 collective-permute-start
  6.8 0.7 and_select_fusion.2
  7.5 2.2 %copy-done.2 = bf16[16,8,8,2,1024]{4,3,2,1,0:T(2,128)(2,1)S(1)} copy-done((bf16[16,8,8,2,1024]{4,3,2,1,0:T(2,128)(2,1)S(1)}, bf16[16,8,8,2,1024]{4,3,2,1,0:T(2,128)(2,1)}, u32[]{:S(2)}) %copy-start.2) | copy-done | bytes 4194328
  9.7 0.9 %copy-done.5 = bf16[384,256]{1,0:T(8,128)(2,1)S(1)} copy-done((bf16[384,256]{1,0:T(8,128)(2,1)S(1)}, bf16[384,256]{1,0:T(8,128)(2,1)}, u32[]{:S(2)}) %copy-start.5) | copy-done | bytes 196632
  10.6 6.9 %shard_map.91.refs_2_ = bf16[16,384,1024]{2,1,0:T(8,128)(2,1)S(1)} custom-call(bf16[16,8,8,2,1024]{4,3,2,1,0:T(2,128)(2,1)S(1)} %copy-done.2, bf16[384,256]{1,0:T(8,128)(2,1)S(1)} %copy-done.5), custom_call_target="tpu_custom_call" | custom-call | flops 1610612736 | bytes 16777216 | tf_op jit(solution)/shard_map/pallas_call | solution.py:137
  17.5 0.1 fusion.6
  17.6 0.1 add_add_fusion.3.scal
  17.7 0.1 add_add_fusion.2.scal
  17.8 0.1 add_add_fusion.1.scal
  17.9 0.0 collective-permute-done.4.refs_0_
  17.9 0.0 collective-permute-start.5
  17.9 1.3 %collective-permute-done.2.refs_0_ = bf16[80,1024]{1,0:T(8,128)(2,1)S(1)} collective-permute-done((bf16[80,1024]{1,0:T(8,128)(2,1)S(1)}, bf16[80,1024]{1,0:T(8,128)(2,1)S(1)}, u32[]{:S(2)}, u32[]{:S(2)}) %collective-permute-start.2) | collective-permute-done | bytes 163872 | tf_op jit(solution)/shard_map/ppermute | solution.py:330
  19.3 0.1 add_add_fusion.scal
  19.3 0.0 collective-permute-done.refs_0_
  19.3 0.5 collective-permute-start.1
  19.8 0.0 collective-permute-done.6.refs_1_
  19.9 5.1 %shard_map.92.refs_5_ = f32[4,192,1024]{2,1,0:T(8,128)S(1)} custom-call(s32[5]{0:T(128)S(1)} %add_add_fusion.3.scal, bf16[80,1024]{1,0:T(8,128)(2,1)S(1)} %reshape.26.refs_0_, bf16[80,1024]{1,0:T(8,128)(2,1)S(1)} %collective-permute-done.6.refs_1_, bf16[16,384,1024]{2,1,0:T(8,128)(2,1)S(1)} %shard_map.91.refs_2_, bf16[2,1024,1024]{2,1,0:T(8,128)(2,1)S(1)} %copy-done.1, ...), custom_call_target="tpu_custom_call" | custom-call | flops 771751936 | bytes 8388608 | tf_op jit(solution)/shard_map/pallas_call | solution.py:284
  25.0 0.0 collective-permute-done.5.refs_1_
  25.0 5.3 %shard_map.93.refs_5_ = f32[4,192,1024]{2,1,0:T(8,128)S(1)} custom-call(s32[5]{0:T(128)S(1)} %add_add_fusion.2.scal, bf16[80,1024]{1,0:T(8,128)(2,1)S(1)} %collective-permute-done.4.refs_0_, bf16[80,1024]{1,0:T(8,128)(2,1)S(1)} %collective-permute-done.5.refs_1_, bf16[16,384,1024]{2,1,0:T(8,128)(2,1)S(1)} %shard_map.91.refs_2_, ...), custom_call_target="tpu_custom_call", output_to_operand_aliasing={{}: (6, {})} | custom-call | flops 771751936 | bytes 8388608 | tf_op jit(solution)/shard_map/pallas_call | solution.py:284
  30.3 0.0 copy-start.3
  30.3 0.0 copy-start.6
  30.3 5.5 %shard_map.94.refs_5_ = f32[4,192,1024]{2,1,0:T(8,128)S(1)} custom-call(s32[5]{0:T(128)S(1)} %add_add_fusion.1.scal, bf16[80,1024]{1,0:T(8,128)(2,1)S(1)} %collective-permute-done.2.refs_0_, bf16[80,1024]{1,0:T(8,128)(2,1)S(1)} %collective-permute-done.3.refs_1_, bf16[16,384,1024]{2,1,0:T(8,128)(2,1)S(1)} %shard_map.91.refs_2_, ...), custom_call_target="tpu_custom_call", output_to_operand_aliasing={{}: (6, {})} | custom-call | flops 771751936 | bytes 8388608 | tf_op jit(solution)/shard_map/pallas_call | solution.py:284
  35.9 7.0 %shard_map.95 = (bf16[8,8,1024]{2,1,0:T(8,128)(2,1)S(1)}, bf16[8,8,1024]{2,1,0:T(8,128)(2,1)S(1)}, bf16[8,8,1024]{2,1,0:T(8,128)(2,1)S(1)}, bf16[8,8,1024]{2,1,0:T(8,128)(2,1)S(1)}) custom-call(s32[5]{0:T(128)S(1)} %add_add_fusion.scal, bf16[80,1024]{1,0:T(8,128)(2,1)S(1)} %collective-permute-done.refs_0_, ...), custom_call_target="tpu_custom_call" | custom-call | flops 1845493760 | bytes 8388608 | tf_op jit(solution)/shard_map/pallas_call | solution.py:284
  42.8 1.6 %collective-permute-start.7 = (bf16[8,8,1024]{2,1,0:T(8,128)(2,1)S(1)}, bf16[8,8,1024]{2,1,0:T(8,128)(2,1)S(1)}, u32[]{:S(2)}, u32[]{:S(2)}) collective-permute-start(bf16[8,8,1024]{2,1,0:T(8,128)(2,1)S(1)} %get-tuple-element.18), channel_id=1, source_target_pairs={{0,8},{8,0},{16,24},{24,16},{1,9},{9,1},{17,25},{25,17},{2,10},{10... | collective-permute-start | bytes 393224 | tf_op jit(solution)/shard_map/ppermute | solution.py:330
  44.4 1.5 %collective-permute-start.8 = (bf16[8,8,1024]{2,1,0:T(8,128)(2,1)S(1)}, bf16[8,8,1024]{2,1,0:T(8,128)(2,1)S(1)}, u32[]{:S(2)}, u32[]{:S(2)}) collective-permute-start(bf16[8,8,1024]{2,1,0:T(8,128)(2,1)S(1)} %get-tuple-element.19), channel_id=1, source_target_pairs={{0,16},{8,24},{16,0},{24,8},{1,17},{9,25},{17,1},{25,9},{2,18},{10... | collective-permute-start | bytes 393224 | tf_op jit(solution)/shard_map/ppermute | solution.py:330
  45.9 0.5 collective-permute-start.9
  46.4 2.3 %collective-permute-done.7.refs_1_ = bf16[8,8,1024]{2,1,0:T(8,128)(2,1)S(1)} collective-permute-done((bf16[8,8,1024]{2,1,0:T(8,128)(2,1)S(1)}, bf16[8,8,1024]{2,1,0:T(8,128)(2,1)S(1)}, u32[]{:S(2)}, u32[]{:S(2)}) %collective-permute-start.7) | collective-permute-done | bytes 131104 | tf_op jit(solution)/shard_map/ppermute | solution.py:330
  48.6 3.7 %collective-permute-done.8.refs_2_ = bf16[8,8,1024]{2,1,0:T(8,128)(2,1)S(1)} collective-permute-done((bf16[8,8,1024]{2,1,0:T(8,128)(2,1)S(1)}, bf16[8,8,1024]{2,1,0:T(8,128)(2,1)S(1)}, u32[]{:S(2)}, u32[]{:S(2)}) %collective-permute-start.8) | collective-permute-done | bytes 131104 | tf_op jit(solution)/shard_map/ppermute | solution.py:330
  52.3 0.0 collective-permute-done.9.refs_3_
  52.3 0.5 shard_map.96
  52.8 0.1 collective-permute-start.10
  52.9 3.2 %collective-permute-start.11 = (bf16[8,1024]{1,0:T(8,128)(2,1)S(1)}, bf16[8,1024]{1,0:T(8,128)(2,1)S(1)}, u32[]{:S(2)}, u32[]{:S(2)}) collective-permute-start(bf16[8,1024]{1,0:T(8,128)(2,1)S(1)} %get-tuple-element.23), channel_id=1, source_target_pairs={{0,2},{1,3},{2,0},{3,1},{4,6},{5,7},{6,4},{7,5},{8,10},{9,11},{10,... | collective-permute-start | bytes 49160 | tf_op jit(solution)/shard_map/ppermute | solution.py:330
  56.1 0.1 collective-permute-start.12
  56.2 2.7 %collective-permute-start.13 = (bf16[8,1024]{1,0:T(8,128)(2,1)S(1)}, bf16[8,1024]{1,0:T(8,128)(2,1)S(1)}, u32[]{:S(2)}, u32[]{:S(2)}) collective-permute-start(bf16[8,1024]{1,0:T(8,128)(2,1)S(1)} %get-tuple-element.25), channel_id=1, source_target_pairs={{0,4},{1,5},{2,6},{3,7},{4,0},{5,1},{6,2},{7,3},{8,12},{9,13},{10,... | collective-permute-start | bytes 49160 | tf_op jit(solution)/shard_map/ppermute | solution.py:330
  58.9 0.0 collective-permute-start.14
  58.9 0.0 collective-permute-done.10
  58.9 2.1 %collective-permute-start.15 = (bf16[8,1024]{1,0:T(8,128)(2,1)S(1)}, bf16[8,1024]{1,0:T(8,128)(2,1)S(1)}, u32[]{:S(2)}, u32[]{:S(2)}) collective-permute-start(bf16[8,1024]{1,0:T(8,128)(2,1)S(1)} %get-tuple-element.27), channel_id=1, source_target_pairs={{0,6},{1,7},{2,4},{3,5},{4,2},{5,3},{6,0},{7,1},{8,14},{9,15},{10,... | collective-permute-start | bytes 49160 | tf_op jit(solution)/shard_map/ppermute | solution.py:330
  61.1 0.0 collective-permute-done.11
  61.1 1.3 %collective-permute-start.16 = (bf16[8,1024]{1,0:T(8,128)(2,1)S(1)}, bf16[8,1024]{1,0:T(8,128)(2,1)S(1)}, u32[]{:S(2)}, u32[]{:S(2)}) collective-permute-start(bf16[8,1024]{1,0:T(8,128)(2,1)S(1)} %get-tuple-element.28), channel_id=1, source_target_pairs={{0,7},{1,6},{2,5},{3,4},{4,3},{5,2},{6,1},{7,0},{8,15},{9,14},{10,... | collective-permute-start | bytes 49160 | tf_op jit(solution)/shard_map/ppermute | solution.py:330
  62.4 0.0 collective-permute-done.12
  62.4 0.7 collective-permute-done.14
  63.1 1.4 %collective-permute-done.15 = bf16[8,1024]{1,0:T(8,128)(2,1)S(1)} collective-permute-done((bf16[8,1024]{1,0:T(8,128)(2,1)S(1)}, bf16[8,1024]{1,0:T(8,128)(2,1)S(1)}, u32[]{:S(2)}, u32[]{:S(2)}) %collective-permute-start.15) | collective-permute-done | bytes 16416 | tf_op jit(solution)/shard_map/ppermute | solution.py:330
  64.5 1.6 %collective-permute-done.16 = bf16[8,1024]{1,0:T(8,128)(2,1)S(1)} collective-permute-done((bf16[8,1024]{1,0:T(8,128)(2,1)S(1)}, bf16[8,1024]{1,0:T(8,128)(2,1)S(1)}, u32[]{:S(2)}, u32[]{:S(2)}) %collective-permute-start.16) | collective-permute-done | bytes 16416 | tf_op jit(solution)/shard_map/ppermute | solution.py:330
  66.0 2.2 %convolution_convert_fusion = bf16[1024,1024]{1,0:T(8,128)(2,1)} fusion(bf16[64,1024]{1,0:T(8,128)(2,1)S(1)} %constant_dynamic-update-slice_fusion, bf16[64,1024]{1,0:T(8,128)(2,1)S(1)} %copy-done, s32[64]{0:T(128)S(1)} %fusion.2), kind=kOutput, calls=%fused_computation | convolution fusion | flops 143724544 | bytes 2359552 | tf_op jit(solution)/shard_map/dot_general | solution.py:382
  (23 shorter events, 0.1 us)
Async XLA Ops:
  0.0 66.0 %copy-start = (bf16[64,1024]{1,0:T(8,128)(2,1)S(1)}, bf16[64,1024]{1,0:T(8,128)(2,1)}, u32[]{:S(2)}) copy-start(bf16[64,1024]{1,0:T(8,128)(2,1)} %param.12) | copy-start | bytes 393220
  1.1 18.8 %collective-permute-start.6 = (bf16[80,1024]{1,0:T(8,128)(2,1)S(1)}, bf16[80,1024]{1,0:T(8,128)(2,1)S(1)}, u32[]{:S(2)}, u32[]{:S(2)}) collective-permute-start(bf16[80,1024]{1,0:T(8,128)(2,1)S(1)} %reshape.26.refs_0_), channel_id=1, source_target_pairs={{0,1},{1,0},{2,3},{3,2},{4,5},{5,4},{6,7},{7,6},{8,9},{9,8},{10,11... | collective-permute-start | bytes 491528 | tf_op jit(solution)/shard_map/ppermute | solution.py:330
  1.6 16.3 %collective-permute-start.4 = (bf16[80,1024]{1,0:T(8,128)(2,1)S(1)}, bf16[80,1024]{1,0:T(8,128)(2,1)S(1)}, u32[]{:S(2)}, u32[]{:S(2)}) collective-permute-start(bf16[80,1024]{1,0:T(8,128)(2,1)S(1)} %reshape.26.refs_0_), channel_id=1, source_target_pairs={{0,2},{1,3},{2,0},{3,1},{4,6},{5,7},{6,4},{7,5},{8,10},{9,11},{10,... | collective-permute-start | bytes 491528 | tf_op jit(solution)/shard_map/ppermute | solution.py:330
  4.2 15.0 %collective-permute-start.2 = (bf16[80,1024]{1,0:T(8,128)(2,1)S(1)}, bf16[80,1024]{1,0:T(8,128)(2,1)S(1)}, u32[]{:S(2)}, u32[]{:S(2)}) collective-permute-start(bf16[80,1024]{1,0:T(8,128)(2,1)S(1)} %reshape.26.refs_0_), channel_id=1, source_target_pairs={{0,4},{1,5},{2,6},{3,7},{4,0},{5,1},{6,2},{7,3},{8,12},{9,13},{10,... | collective-permute-start | bytes 491528 | tf_op jit(solution)/shard_map/ppermute | solution.py:330
  6.8 12.5 %collective-permute-start = (bf16[80,1024]{1,0:T(8,128)(2,1)S(1)}, bf16[80,1024]{1,0:T(8,128)(2,1)S(1)}, u32[]{:S(2)}, u32[]{:S(2)}) collective-permute-start(bf16[80,1024]{1,0:T(8,128)(2,1)S(1)} %reshape.26.refs_0_), channel_id=1, source_target_pairs={{0,6},{1,7},{2,4},{3,5},{4,2},{5,3},{6,0},{7,1},{8,14},{9,15},{10,... | collective-permute-start | bytes 491528 | tf_op jit(solution)/shard_map/ppermute | solution.py:330
  7.5 2.2 %copy-start.2 = (bf16[16,8,8,2,1024]{4,3,2,1,0:T(2,128)(2,1)S(1)}, bf16[16,8,8,2,1024]{4,3,2,1,0:T(2,128)(2,1)}, u32[]{:S(2)}) copy-start(bf16[16,8,8,2,1024]{4,3,2,1,0:T(2,128)(2,1)} %room_hbm.1) | copy-start | bytes 12582916
  9.7 0.9 %copy-start.5 = (bf16[384,256]{1,0:T(8,128)(2,1)S(1)}, bf16[384,256]{1,0:T(8,128)(2,1)}, u32[]{:S(2)}) copy-start(bf16[384,256]{1,0:T(8,128)(2,1)} %constant.76.clone.table_ref) | copy-start | bytes 589828
  10.6 9.2 %copy-start.1 = (bf16[2,1024,1024]{2,1,0:T(8,128)(2,1)S(1)}, bf16[2,1024,1024]{2,1,0:T(8,128)(2,1)}, u32[]{:S(2)}) copy-start(bf16[2,1024,1024]{2,1,0:T(8,128)(2,1)} %constant.77.clone.refs_3_) | copy-start | bytes 12582916
  10.6 9.2 %copy-start.4 = (bf16[192,160]{1,0:T(8,128)(2,1)S(1)}, bf16[192,160]{1,0:T(8,128)(2,1)}, u32[]{:S(2)}) copy-start(bf16[192,160]{1,0:T(8,128)(2,1)} %constant.78.clone.refs_4_) | copy-start | bytes 184324
  17.9 7.1 %collective-permute-start.5 = (bf16[80,1024]{1,0:T(8,128)(2,1)S(1)}, bf16[80,1024]{1,0:T(8,128)(2,1)S(1)}, u32[]{:S(2)}, u32[]{:S(2)}) collective-permute-start(bf16[80,1024]{1,0:T(8,128)(2,1)S(1)} %collective-permute-done.4.refs_0_), channel_id=1, source_target_pairs={{0,1},{1,0},{2,3},{3,2},{4,5},{5,4},{6,7},{7,6},{8,9},{9,8},{10,11... | collective-permute-start | bytes 491528 | tf_op jit(solution)/shard_map/ppermute | solution.py:330
  19.3 11.1 %collective-permute-start.3 = (bf16[80,1024]{1,0:T(8,128)(2,1)S(1)}, bf16[80,1024]{1,0:T(8,128)(2,1)S(1)}, u32[]{:S(2)}, u32[]{:S(2)}) collective-permute-start(bf16[80,1024]{1,0:T(8,128)(2,1)S(1)} %collective-permute-done.2.refs_0_), channel_id=1, source_target_pairs={{0,1},{1,0},{2,3},{3,2},{4,5},{5,4},{6,7},{7,6},{8,9},{9,8},{10,11... | collective-permute-start | bytes 491528 | tf_op jit(solution)/shard_map/ppermute | solution.py:330
  19.3 16.5 %collective-permute-start.1 = (bf16[80,1024]{1,0:T(8,128)(2,1)S(1)}, bf16[80,1024]{1,0:T(8,128)(2,1)S(1)}, u32[]{:S(2)}, u32[]{:S(2)}) collective-permute-start(bf16[80,1024]{1,0:T(8,128)(2,1)S(1)} %collective-permute-done.refs_0_), channel_id=1, source_target_pairs={{0,1},{1,0},{2,3},{3,2},{4,5},{5,4},{6,7},{7,6},{8,9},{9,8},{10,11... | collective-permute-start | bytes 491528 | tf_op jit(solution)/shard_map/ppermute | solution.py:330
  30.3 5.5 %copy-start.3 = (bf16[2,1024,1024]{2,1,0:T(8,128)(2,1)S(1)}, bf16[2,1024,1024]{2,1,0:T(8,128)(2,1)}, u32[]{:S(2)}) copy-start(bf16[2,1024,1024]{2,1,0:T(8,128)(2,1)} %constant.80.clone.refs_7_) | copy-start | bytes 12582916
  30.3 5.5 %copy-start.6 = (bf16[2,128,192]{2,1,0:T(8,128)(2,1)S(1)}, bf16[2,128,192]{2,1,0:T(8,128)(2,1)}, u32[]{:S(2)}) copy-start(bf16[2,128,192]{2,1,0:T(8,128)(2,1)} %constant.79.clone.refs_6_) | copy-start | bytes 294916
  42.8 5.8 %collective-permute-start.7 = (bf16[8,8,1024]{2,1,0:T(8,128)(2,1)S(1)}, bf16[8,8,1024]{2,1,0:T(8,128)(2,1)S(1)}, u32[]{:S(2)}, u32[]{:S(2)}) collective-permute-start(bf16[8,8,1024]{2,1,0:T(8,128)(2,1)S(1)} %get-tuple-element.18), channel_id=1, source_target_pairs={{0,8},{8,0},{16,24},{24,16},{1,9},{9,1},{17,25},{25,17},{2,10},{10... | collective-permute-start | bytes 393224 | tf_op jit(solution)/shard_map/ppermute | solution.py:330
  44.4 8.0 %collective-permute-start.8 = (bf16[8,8,1024]{2,1,0:T(8,128)(2,1)S(1)}, bf16[8,8,1024]{2,1,0:T(8,128)(2,1)S(1)}, u32[]{:S(2)}, u32[]{:S(2)}) collective-permute-start(bf16[8,8,1024]{2,1,0:T(8,128)(2,1)S(1)} %get-tuple-element.19), channel_id=1, source_target_pairs={{0,16},{8,24},{16,0},{24,8},{1,17},{9,25},{17,1},{25,9},{2,18},{10... | collective-permute-start | bytes 393224 | tf_op jit(solution)/shard_map/ppermute | solution.py:330
  45.9 6.4 %collective-permute-start.9 = (bf16[8,8,1024]{2,1,0:T(8,128)(2,1)S(1)}, bf16[8,8,1024]{2,1,0:T(8,128)(2,1)S(1)}, u32[]{:S(2)}, u32[]{:S(2)}) collective-permute-start(bf16[8,8,1024]{2,1,0:T(8,128)(2,1)S(1)} %get-tuple-element.20), channel_id=1, source_target_pairs={{0,24},{8,16},{16,8},{24,0},{1,25},{9,17},{17,9},{25,1},{2,26},{10... | collective-permute-start | bytes 393224 | tf_op jit(solution)/shard_map/ppermute | solution.py:330
  52.8 6.1 %collective-permute-start.10 = (bf16[8,1024]{1,0:T(8,128)(2,1)S(1)}, bf16[8,1024]{1,0:T(8,128)(2,1)S(1)}, u32[]{:S(2)}, u32[]{:S(2)}) collective-permute-start(bf16[8,1024]{1,0:T(8,128)(2,1)S(1)} %get-tuple-element.22), channel_id=1, source_target_pairs={{0,1},{1,0},{2,3},{3,2},{4,5},{5,4},{6,7},{7,6},{8,9},{9,8},{10,11... | collective-permute-start | bytes 49160 | tf_op jit(solution)/shard_map/ppermute | solution.py:330
  52.9 8.2 %collective-permute-start.11 = (bf16[8,1024]{1,0:T(8,128)(2,1)S(1)}, bf16[8,1024]{1,0:T(8,128)(2,1)S(1)}, u32[]{:S(2)}, u32[]{:S(2)}) collective-permute-start(bf16[8,1024]{1,0:T(8,128)(2,1)S(1)} %get-tuple-element.23), channel_id=1, source_target_pairs={{0,2},{1,3},{2,0},{3,1},{4,6},{5,7},{6,4},{7,5},{8,10},{9,11},{10,... | collective-permute-start | bytes 49160 | tf_op jit(solution)/shard_map/ppermute | solution.py:330
  56.1 6.3 %collective-permute-start.12 = (bf16[8,1024]{1,0:T(8,128)(2,1)S(1)}, bf16[8,1024]{1,0:T(8,128)(2,1)S(1)}, u32[]{:S(2)}, u32[]{:S(2)}) collective-permute-start(bf16[8,1024]{1,0:T(8,128)(2,1)S(1)} %get-tuple-element.24), channel_id=1, source_target_pairs={{0,3},{1,2},{2,1},{3,0},{4,7},{5,6},{6,5},{7,4},{8,11},{9,10},{10,... | collective-permute-start | bytes 49160 | tf_op jit(solution)/shard_map/ppermute | solution.py:330
  56.2 6.2 %collective-permute-start.13 = (bf16[8,1024]{1,0:T(8,128)(2,1)S(1)}, bf16[8,1024]{1,0:T(8,128)(2,1)S(1)}, u32[]{:S(2)}, u32[]{:S(2)}) collective-permute-start(bf16[8,1024]{1,0:T(8,128)(2,1)S(1)} %get-tuple-element.25), channel_id=1, source_target_pairs={{0,4},{1,5},{2,6},{3,7},{4,0},{5,1},{6,2},{7,3},{8,12},{9,13},{10,... | collective-permute-start | bytes 49160 | tf_op jit(solution)/shard_map/ppermute | solution.py:330
  58.9 4.1 %collective-permute-start.14 = (bf16[8,1024]{1,0:T(8,128)(2,1)S(1)}, bf16[8,1024]{1,0:T(8,128)(2,1)S(1)}, u32[]{:S(2)}, u32[]{:S(2)}) collective-permute-start(bf16[8,1024]{1,0:T(8,128)(2,1)S(1)} %get-tuple-element.26), channel_id=1, source_target_pairs={{0,5},{1,4},{2,7},{3,6},{4,1},{5,0},{6,3},{7,2},{8,13},{9,12},{10,... | collective-permute-start | bytes 49160 | tf_op jit(solution)/shard_map/ppermute | solution.py:330
  58.9 5.5 %collective-permute-start.15 = (bf16[8,1024]{1,0:T(8,128)(2,1)S(1)}, bf16[8,1024]{1,0:T(8,128)(2,1)S(1)}, u32[]{:S(2)}, u32[]{:S(2)}) collective-permute-start(bf16[8,1024]{1,0:T(8,128)(2,1)S(1)} %get-tuple-element.27), channel_id=1, source_target_pairs={{0,6},{1,7},{2,4},{3,5},{4,2},{5,3},{6,0},{7,1},{8,14},{9,15},{10,... | collective-permute-start | bytes 49160 | tf_op jit(solution)/shard_map/ppermute | solution.py:330
  61.1 5.0 %collective-permute-start.16 = (bf16[8,1024]{1,0:T(8,128)(2,1)S(1)}, bf16[8,1024]{1,0:T(8,128)(2,1)S(1)}, u32[]{:S(2)}, u32[]{:S(2)}) collective-permute-start(bf16[8,1024]{1,0:T(8,128)(2,1)S(1)} %get-tuple-element.28), channel_id=1, source_target_pairs={{0,7},{1,6},{2,5},{3,4},{4,3},{5,2},{6,1},{7,0},{8,15},{9,14},{10,... | collective-permute-start | bytes 49160 | tf_op jit(solution)/shard_map/ppermute | solution.py:330

commit v4 on v3

--- a/solution.py
+++ b/solution.py
@@ -13,6 +13,8 @@
 BF16 = jnp.bfloat16
 F32 = jnp.float32
 LANES = 256
+SLAB = 128
+GROUP = 4
 STEPS = 24
 SEGS = 2
 KEEP = 16
@@ -36,10 +38,10 @@
     weight = np.where(kk == 0, 1.0, 2.0)
     inv_real = weight * np.cos(angle) / size
     inv_imag = np.where(kk == 0, (1.0 - 2.0 * (m % 2)) / size, -2.0 * np.sin(angle) / size)
-    return (
-        bf16_table(np.stack([fwd_real, fwd_imag])),
-        bf16_table(np.stack([inv_real, inv_imag])),
-    )
+    def slabs(pair):
+        return bf16_table(np.stack(pair).reshape(2, block_len, -1, SLAB).transpose(0, 2, 1, 3))
+
+    return slabs([fwd_real, fwd_imag]), slabs([inv_real, inv_imag])
 
 
 @functools.lru_cache(maxsize=None)
@@ -101,29 +103,43 @@
     return 1.0 - packed, packed, sign
 
 
+def two_slabs(ref, step, *index):
+    first = step * (LANES // SLAB)
+    return jnp.concatenate([ref[(*index, first + i)] for i in range(LANES // SLAB)], axis=-1)
+
+
 def response_kernel(rows, bins, room_hbm, table_ref, hat_ref, room_ref, sems):
-    depth = room_ref.shape[1] * room_ref.shape[2] * 2
-    flat = room_ref.reshape(rows, depth, bins)
+    slabs = bins // SLAB
+    depth = room_ref.shape[2] * room_ref.shape[3] * 2
+    flat = room_ref.reshape(rows, slabs, depth, SLAB)
     plain, packed, _ = lane_masks(0, LANES)
     plain, packed = plain.astype(BF16), packed.astype(BF16)
 
-    def copy(r):
-        return pltpu.make_async_copy(room_hbm.at[r], room_ref.at[r], sems.at[r])
+    def copies(r):
+        return [
+            pltpu.make_async_copy(
+                room_hbm.at[r, :, :, :, pl.ds(i * SLAB, SLAB)], room_ref.at[r, i], sems.at[r, i]
+            )
+            for i in range(slabs)
+        ]
 
     for r in range(rows):
-        copy(r).start()
+        for copy in copies(r):
+            copy.start()
 
     def one(r, carry):
-        copy(r).wait()
+        for copy in copies(r):
+            copy.wait()
         for step in range(bins // LANES):
-            at = slice(step * LANES, (step + 1) * LANES)
-            h = flat[r, :, at]
+            h = two_slabs(flat, step, r)
             if step == 0:
                 h = jnp.concatenate([h * plain, h * packed], axis=0)
                 hat = dot(table_ref[...], h)
             else:
                 hat = dot(table_ref[:, :depth], h)
-            hat_ref[r, :, at] = hat.astype(BF16)
+            hat = hat.astype(BF16)
+            for i in range(LANES // SLAB):
+                hat_ref[r, step * (LANES // SLAB) + i] = hat[:, i * SLAB : (i + 1) * SLAB]
         return carry
 
     lax.fori_loop(0, rows, one, 0)
@@ -131,23 +147,27 @@
 
 def transform_responses(room):
     rows, parts, channels, _, bins = room.shape
+    slabs = bins // SLAB
     _, resp, _ = step_tables(parts, parts + SEGS * KEEP, channels)
     vmem = pl.BlockSpec(memory_space=pltpu.VMEM)
     flops = 2 * rows * channels * 2 * STEPS * parts * channels * 2 * bins
     return pl.pallas_call(
         functools.partial(response_kernel, rows, bins),
-        in_specs=[pl.BlockSpec(memory_space=pl.ANY), vmem],
+        in_specs=[pl.BlockSpec(memory_space=pltpu.HBM), vmem],
         out_specs=vmem,
-        out_shape=jax.ShapeDtypeStruct((rows, channels * 2 * STEPS, bins), BF16),
-        scratch_shapes=[pltpu.VMEM(room.shape, BF16), pltpu.SemaphoreType.DMA((rows,))],
+        out_shape=jax.ShapeDtypeStruct((rows, slabs, channels * 2 * STEPS, SLAB), BF16),
+        scratch_shapes=[
+            pltpu.VMEM((rows, slabs, parts, channels, 2, SLAB), BF16),
+            pltpu.SemaphoreType.DMA((rows, slabs)),
+        ],
         compiler_params=pltpu.CompilerParams(vmem_limit_bytes=24 * 2**20),
         cost_estimate=pl.CostEstimate(flops=flops, bytes_accessed=16 * 2**20, transcendentals=0),
     )(room, jnp.asarray(resp))
 
 
-def mix_kernel(pieces, rows, channels, blocks, shares, has_total, last, scal, *refs):
+def mix_kernel(flips, own, channels, blocks, shares, has_total, last, me_ref, slot_ref, *refs):
     refs = list(refs)
-    x_refs = [refs.pop(0) for _ in range(pieces)]
+    x_refs = [refs.pop(0) for _ in flips]
     hat_ref, table_ref, spec_ref = [refs.pop(0) for _ in range(3)]
     total_ref = refs.pop(0) if has_total else None
     if last:
@@ -159,72 +179,83 @@
     if last:
         y_ref, left_re, left_im, time_ref = refs
 
-    bins = table_ref.shape[2]
+    slabs = hat_ref.shape[1]
+    bins = slabs * SLAB
+    steps = bins // LANES
+    rows = own * len(flips)
     half = 2 * STEPS
     x = jnp.concatenate([ref[...] for ref in x_refs], axis=0)
     count = x.shape[0] // rows
     cols = 2 * count
+    slots = [
+        lax.rem(slot_ref[(me_ref[1] ^ flip) * own + i], hat_ref.shape[0])
+        for flip in flips
+        for i in range(own)
+    ]
 
     def spectra_step(step):
-        here = slice(step * LANES, (step + 1) * LANES)
         plain, packed, sign = lane_masks(step * LANES, LANES)
         spectra = []
         for j in range(2):
-            one = dot(x, table_ref[j, :, here])
+            one = dot(x, two_slabs(table_ref, step, j))
             spectra.append(one + sign * pltpu.roll(one, one.shape[0] - 1, axis=0))
         for r in range(rows):
             both = jnp.concatenate([s[r * count : (r + 1) * count] for s in spectra], axis=0)
             if step == 0:
                 both = jnp.concatenate([both * plain, both * packed], axis=0).astype(BF16)
-                s_ref[step, r] = dot(spec_ref[...], both).astype(BF16)
+                hat = dot(spec_ref[...], both).astype(BF16)
             else:
-                s_ref[step, r] = dot(spec_ref[:, :cols], both.astype(BF16)).astype(BF16)
+                hat = dot(spec_ref[:, :cols], both.astype(BF16)).astype(BF16)
+            for i in range(LANES // SLAB):
+                s_ref[step * (LANES // SLAB) + i, r] = hat[:, i * SLAB : (i + 1) * SLAB]
+
+    def product_slab(slab, pair):
+        far = slice(slab * SLAB, (slab + 1) * SLAB)
+        base = pair * 2 * half
+        for seg in range(SEGS):
+            re_rows = slice(2 * seg * half, (2 * seg + 1) * half)
+            im_rows = slice((2 * seg + 1) * half, (2 * seg + 2) * half)
+            re_sum = total_ref[pair, re_rows, far] if has_total else None
+            im_sum = total_ref[pair, im_rows, far] if has_total else None
+            for start in range(0, rows, GROUP):
+                re, im = None, None
+                for r in range(start, min(start + GROUP, rows)):
+                    h_re = hat_ref[slots[r], slab, base : base + half]
+                    h_im = hat_ref[slots[r], slab, base + half : base + 2 * half]
+                    s_re, s_im = s_ref[slab, r, re_rows], s_ref[slab, r, im_rows]
+                    add_re = s_re * h_re - s_im * h_im
+                    add_im = s_re * h_im + s_im * h_re
+                    re = add_re if re is None else re + add_re
+                    im = add_im if im is None else im + add_im
+                re, im = re.astype(F32), im.astype(F32)
+                re_sum = re if re_sum is None else re_sum + re
+                im_sum = im if im_sum is None else im_sum + im
+            if last:
+                y_ref[slab, pair, re_rows] = re_sum.astype(BF16)
+                y_ref[slab, pair, im_rows] = im_sum.astype(BF16)
+            else:
+                out_ref[pair, re_rows, far] = re_sum
+                out_ref[pair, im_rows, far] = im_sum
 
     def product_step(step):
         for pair in range(channels // 2):
-            for cut in range(LANES // 128):
-                at = slice(cut * 128, (cut + 1) * 128)
-                far = slice(step * LANES + cut * 128, step * LANES + (cut + 1) * 128)
-                base = pair * 2 * half
-                hats = [
-                    (hat_ref[scal[r], base : base + half, far], hat_ref[scal[r], base + half : base + 2 * half, far])
-                    for r in range(rows)
-                ]
-                for seg in range(SEGS):
-                    re_rows = slice(2 * seg * half, (2 * seg + 1) * half)
-                    im_rows = slice((2 * seg + 1) * half, (2 * seg + 2) * half)
-                    re, im = None, None
-                    for r in range(rows):
-                        h_re, h_im = hats[r]
-                        s_re, s_im = s_ref[step, r, re_rows, at], s_ref[step, r, im_rows, at]
-                        add_re = s_re * h_re - s_im * h_im
-                        add_im = s_re * h_im + s_im * h_re
-                        re = add_re if re is None else re + add_re
-                        im = add_im if im is None else im + add_im
-                    re, im = re.astype(F32), im.astype(F32)
-                    if has_total:
-                        re, im = re + total_ref[pair, re_rows, far], im + total_ref[pair, im_rows, far]
-                    if last:
-                        y_ref[step, pair, re_rows, at] = re.astype(BF16)
-                        y_ref[step, pair, im_rows, at] = im.astype(BF16)
-                    else:
-                        out_ref[pair, re_rows, far] = re
-                        out_ref[pair, im_rows, far] = im
+            first = step * (LANES // SLAB)
+            for i in range(LANES // SLAB):
+                product_slab(first + i, pair)
             if last:
-                here = slice(step * LANES, (step + 1) * LANES)
-                y = y_ref[step, pair]
+                y = jnp.concatenate([y_ref[first + i, pair] for i in range(LANES // SLAB)], axis=-1)
                 if step == 0:
                     plain, packed, _ = lane_masks(0, LANES)
                     mix = dot(back_ref[0], y * plain.astype(BF16)) + dot(back_ref[1], y * packed.astype(BF16))
                 else:
                     mix = dot(back_ref[0], y)
                 mix = mix.astype(BF16)
+                here = slice(step * LANES, (step + 1) * LANES)
                 for c in range(2):
                     rows_to = slice((2 * pair + c) * blocks, (2 * pair + c + 1) * blocks)
                     left_re[rows_to, here] = mix[2 * c * blocks : (2 * c + 1) * blocks]
                     left_im[rows_to, here] = mix[(2 * c + 1) * blocks : (2 * c + 2) * blocks]
 
-    steps = bins // LANES
     spectra_step(0)
     for step in range(steps):
         if step + 1 < steps:
@@ -235,40 +266,41 @@
         each = blocks // shares
         for step in range(steps):
             here = slice(step * LANES, (step + 1) * LANES)
-            part = dot(left_re[...], inv_ref[0, :, here]) + dot(left_im[...], inv_ref[1, :, here])
+            part = dot(left_re[...], two_slabs(inv_ref, step, 0)) + dot(left_im[...], two_slabs(inv_ref, step, 1))
             for t in range(shares):
                 for c in range(channels):
                     row = c * blocks + t * each
                     time_ref[t, c, :, here] = part[row : row + each]
-        me = scal[rows]
         for d in range(shares):
-            out_refs[d][...] = time_ref[me ^ d].astype(BF16)
-
-
-def add_sources(x_list, slots, hat, total, last, shares, me, channels, parts):
-    bins = hat.shape[2]
-    rows = slots.shape[0]
-    frames = x_list[0].shape[0] * len(x_list) // rows
+            out_refs[d][...] = time_ref[me_ref[0] ^ d].astype(BF16)
+
+
+def add_sources(x_list, flips, me, slots, hat, total, last, shares, channels, parts):
+    slabs = hat.shape[1]
+    bins = slabs * SLAB
+    frames = parts + SEGS * KEEP
+    own = x_list[0].shape[0] // frames
+    rows = own * len(x_list)
     blocks = frames - parts
     wide = 2 * SEGS * STEPS
     table, inverse = block_tables(bins)
     spec, _, back = step_tables(parts, frames, channels)
-    scal = jnp.concatenate([slots, me[None]]).astype(jnp.int32)
     vmem = pl.BlockSpec(memory_space=pltpu.VMEM)
-
-    operands = [scal] + list(x_list) + [hat, jnp.asarray(table), jnp.asarray(spec)]
+    smem = pl.BlockSpec(memory_space=pltpu.SMEM)
+
+    operands = [me, slots] + list(x_list) + [hat, jnp.asarray(table), jnp.asarray(spec)]
     aliases = {}
     if total is not None:
         if not last:
             aliases = {len(operands): 0}
         operands.append(total)
-    scratch = [pltpu.VMEM((bins // LANES, rows, 2 * wide, LANES), BF16)]
+    scratch = [pltpu.VMEM((slabs, rows, 2 * wide, SLAB), BF16)]
     if last:
         operands += [jnp.asarray(back), jnp.asarray(inverse)]
         each = blocks // shares
         out_shape = [jax.ShapeDtypeStruct((channels, each, bins), BF16)] * shares
         scratch += [
-            pltpu.VMEM((bins // LANES, channels // 2, 2 * wide, LANES), BF16),
+            pltpu.VMEM((slabs, channels // 2, 2 * wide, SLAB), BF16),
             pltpu.VMEM((channels * blocks, bins), BF16),
             pltpu.VMEM((channels * blocks, bins), BF16),
             pltpu.VMEM((shares, channels, each, bins), F32),
@@ -279,16 +311,16 @@
         rows * frames * 2 * bins + channels * rows * wide * 16 + (channels * blocks * 2 * bins if last else 0)
     )
     body = functools.partial(
-        mix_kernel, len(x_list), rows, channels, blocks, shares, total is not None, last
+        mix_kernel, tuple(flips), own, channels, blocks, shares, total is not None, last
     )
     return pl.pallas_call(
         body,
-        in_specs=[pl.BlockSpec(memory_space=pltpu.SMEM)] + [vmem] * (len(operands) - 1),
+        in_specs=[smem, smem] + [vmem] * (len(operands) - 2),
         out_specs=[vmem] * shares if last else vmem,
         out_shape=out_shape,
         scratch_shapes=scratch,
         input_output_aliases=aliases,
-        compiler_params=pltpu.CompilerParams(vmem_limit_bytes=20 * 2**20),
+        compiler_params=pltpu.CompilerParams(vmem_limit_bytes=24 * 2**20),
         cost_estimate=pl.CostEstimate(flops=flops, bytes_accessed=8 * 2**20, transcendentals=0),
     )(*operands)
 
@@ -329,48 +361,45 @@
     def swap(value, axis, count, flip):
         return lax.ppermute(value, axis, [(i, i ^ flip) for i in range(count)])
 
-    lanes = [x_own] + [swap(x_own, "ch", ch_count, 2 * d) for d in range(1, ch_count // 2)]
-    mates = [swap(x, "ch", ch_count, 1) for x in lanes]
-
-    hat = transform_responses(room_spectra)
-    slot_local = render_slot % rows_total
+    chips = ch_count // 2
+    lanes = [x_own] + [swap(x_own, "ch", ch_count, 2 * d) for d in range(1, chips)]
+    mates = [swap(x_own, "ch", ch_count, 1)]
 
     row = jnp.arange(ch_count * channels, dtype=jnp.int32)
     takes = ((row // channels) ^ ch_me) * channels + row % channels
     order = (takes[:, None] == row[None, :]).astype(BF16)
     own_order = dot(order, decoder).astype(BF16)
 
-    def slots_of(flip):
-        start = (ch_me ^ flip) * own
-        return lax.dynamic_slice(slot_local, (start,), (own,))
-
-    total = None
-    chips = ch_count // 2
-    per_call = max(1, chips // 4)
-    calls = chips // per_call
-    for call in range(calls):
-        x_list, slots = [], []
-        for d in range(call * per_call, (call + 1) * per_call):
-            x_list += [lanes[d], mates[d]]
-            slots += [slots_of(2 * d), slots_of(2 * d + 1)]
-        total = add_sources(
-            x_list,
-            jnp.concatenate(slots),
-            hat,
-            total,
-            call == calls - 1,
-            src_count,
-            src_me,
-            channels,
-            parts,
+    hat = transform_responses(room_spectra)
+    me = jnp.stack([src_me, ch_me])
+
+    def add(x_list, flips, total, last):
+        return add_sources(
+            x_list, flips, me, render_slot, hat, total, last, src_count, channels, parts
         )
+
+    total = add([lanes[0], mates[0]], [0, 1], None, False)
+    mates.append(swap(lanes[1], "ch", ch_count, 1))
+    *late, total = lax.optimization_barrier((*lanes[2:], total))
+    lanes[2:] = late
+    mates += [swap(x, "ch", ch_count, 1) for x in late]
+    x_list, flips = [], []
+    for d in range(1, chips):
+        x_list += [lanes[d], mates[d]]
+        flips += [2 * d, 2 * d + 1]
+    total = add(x_list, flips, total, True)
 
     parts_in = [total[0]] + [swap(total[d], "src", src_count, d) for d in range(1, src_count)]
     each = blocks // src_count
     if each == ch_count:
         pieces = sum_groups(parts_in, ch_me)
-        pieces = [pieces[0]] + [swap(pieces[d], "ch", ch_count, d) for d in range(1, ch_count)]
-        gathered = jnp.concatenate(pieces, axis=0)
+        given = swap(jnp.concatenate(pieces[1::2], axis=0), "ch", ch_count, 1)
+        both = [
+            jnp.concatenate([pieces[2 * d], given[d * channels : (d + 1) * channels]], axis=0)
+            for d in range(chips)
+        ]
+        both[1:] = [swap(both[d], "ch", ch_count, 2 * d) for d in range(1, chips)]
+        gathered = jnp.concatenate(both, axis=0)
         matrix = own_order
     else:
         signal = parts_in[0].astype(F32)

time: 68.4 us -> 74 us (1.082)
  local copies, waits for them, and re-layouts: 4.32 us -> 15.5 us
  starting transfers between devices: 19.4 us -> 14.5 us
  waiting for transfers between devices: 10.9 us -> 12.5 us
  Pallas kernels: 30.2 us -> 28.9 us
  other arithmetic: 0.97 us -> 0.1 us
    unnamed x21 -> x25, local copies, waits for them, and re-layouts: 3.16 us -> 14.4 us
    pallas_call x4 -> x2, Pallas kernels: 22.8 us -> 17.5 us  [add_sources(): pl.pallas_call(body, in_specs=[smem, smem] + [vmem] * (len(operands) - 2)...]
    ppermute x17 -> x14, starting transfers between devices: 19.4 us -> 14.5 us  [swap(): return lax.ppermute(value, axis, [(i, i ^ flip) for i in range(count)])]
    pallas_call x1, Pallas kernels: 6.93 us -> 11 us  [transform_responses(): pl.pallas_call(functools.partial(response_kernel, rows, bins), in_specs=[...]
    ppermute x17 -> x14, waiting for transfers between devices: 10.9 us -> 12.5 us  [swap(): return lax.ppermute(value, axis, [(i, i ^ flip) for i in range(count)])]
  transfers between devices with their start and end apart: 17 -> 14, of which waited for: 6 -> 8; matrix products, arithmetic and copies ran while one was open for 2% -> 0% of each run, Pallas kernels for 33% -> 21%
where the time goes in v4:
time: 74 us; the launch traced here: 73.8 us
  Pallas kernels  28.9 us (39%)
  local copies, waits for them, and re-layouts  15.5 us (21%)
  starting transfers between devices  14.5 us (20%)
  waiting for transfers between devices  12.5 us (17%)
  matrix products  2.2 us (3%)
    pallas_call x2, Pallas kernels, add_sources(): pl.pallas_call(body, in_specs=[smem, smem] + [vmem] * (len(operands) - 2)...  17.5 us
    ppermute x14, starting transfers between devices, swap(): return lax.ppermute(value, axis, [(i, i ^ flip) for i in range(count)])  14.5 us
    unnamed x25, local copies, waits for them, and re-layouts  14.4 us
    ppermute x14, waiting for transfers between devices, swap(): return lax.ppermute(value, axis, [(i, i ^ flip) for i in range(count)])  12.5 us
    pallas_call x1, Pallas kernels, transform_responses(): pl.pallas_call(functools.partial(response_kernel, rows, bins), in_specs=[...  11 us
    dot_general x1, matrix products, per_device(): lax.dot_general(gathered, matrix, (((0,), (0,)), ((), ())), preferred_ele...  2.2 us
  transfers between devices with their start and end apart: 14, of which 8 were waited for; matrix products, arithmetic and copies ran while one was open for 0% of the time, Pallas kernels for 21%

profile of v4, /device:TPU:0, one launch (start us, length us, event | category | flops | bytes accessed | tf_op | source)
XLA Modules:
  0.0 73.8 jit_solution(13902221408266659590)
XLA Ops:
  0.0 0.0 copy-start
  0.0 1.1 %reshape.26.refs_0_ = bf16[80,1024]{1,0:T(8,128)(2,1)S(1)} reshape(bf16[2,40960]{1,0:T(2,128)(2,1)} %param.9) | data formatting | bytes 327680 | tf_op jit(solution)/shard_map/reshape | solution.py:359
  1.1 0.5 collective-permute-start.4
  1.6 3.7 %collective-permute-start.2 = (bf16[80,1024]{1,0:T(8,128)(2,1)S(1)}, bf16[80,1024]{1,0:T(8,128)(2,1)S(1)}, u32[]{:S(2)}, u32[]{:S(2)}) collective-permute-start(bf16[80,1024]{1,0:T(8,128)(2,1)S(1)} %reshape.26.refs_0_), channel_id=1, source_target_pairs={{0,4},{1,5},{2,6},{3,7},{4,0},{5,1},{6,2},{7,3},{8,12},{9,13},{10,... | collective-permute-start | bytes 491528 | tf_op jit(solution)/shard_map/ppermute | solution.py:362
  5.3 1.3 %collective-permute-start.3 = (bf16[80,1024]{1,0:T(8,128)(2,1)S(1)}, bf16[80,1024]{1,0:T(8,128)(2,1)S(1)}, u32[]{:S(2)}, u32[]{:S(2)}) collective-permute-start(bf16[80,1024]{1,0:T(8,128)(2,1)S(1)} %reshape.26.refs_0_), channel_id=1, source_target_pairs={{0,6},{1,7},{2,4},{3,5},{4,2},{5,3},{6,0},{7,1},{8,14},{9,15},{10,... | collective-permute-start | bytes 491528 | tf_op jit(solution)/shard_map/ppermute | solution.py:362
  6.6 0.2 collective-permute-start
  6.8 2.2 %copy-done.6 = bf16[16,8,8,2,1024]{4,3,2,1,0:T(2,128)(2,1)S(1)} copy-done((bf16[16,8,8,2,1024]{4,3,2,1,0:T(2,128)(2,1)S(1)}, bf16[16,8,8,2,1024]{4,3,2,1,0:T(2,128)(2,1)}, u32[]{:S(2)}) %copy-start.6) | copy-done | bytes 4194328
  9.0 0.9 %copy-done.8 = bf16[384,256]{1,0:T(8,128)(2,1)S(1)} copy-done((bf16[384,256]{1,0:T(8,128)(2,1)S(1)}, bf16[384,256]{1,0:T(8,128)(2,1)}, u32[]{:S(2)}) %copy-start.8) | copy-done | bytes 196632
  10.0 11.0 %shard_map.91.refs_2_.refs_6_ = bf16[16,8,384,128]{3,2,1,0:T(8,128)(2,1)S(1)} custom-call(bf16[16,8,8,2,1024]{4,3,2,1,0:T(2,128)(2,1)S(1)} %copy-done.6, bf16[384,256]{1,0:T(8,128)(2,1)S(1)} %copy-done.8), custom_call_target="tpu_custom_call" | custom-call | flops 1610612736 | bytes 16777216 | tf_op jit(solution)/shard_map/pallas_call | solution.py:154
  20.9 0.0 copy-start.1
  20.9 4.5 %copy-done.1 = bf16[16,8,384,128]{3,2,1,0:T(8,128)(2,1)} copy-done((bf16[16,8,384,128]{3,2,1,0:T(8,128)(2,1)}, bf16[16,8,384,128]{3,2,1,0:T(8,128)(2,1)S(1)}, u32[]{:S(2)}) %copy-start.1) | copy-done | bytes 12582936
  25.4 0.1 pad_add_fusion.me_ref
  25.5 0.0 collective-permute-done.4.refs_1_
  25.5 0.0 copy-done.7
  25.5 0.0 copy-done.10
  25.5 0.0 copy-start.2
  25.5 4.6 %copy-done.2 = bf16[16,8,384,128]{3,2,1,0:T(8,128)(2,1)S(1)} copy-done((bf16[16,8,384,128]{3,2,1,0:T(8,128)(2,1)S(1)}, bf16[16,8,384,128]{3,2,1,0:T(8,128)(2,1)}, u32[]{:S(2)}) %copy-start.2) | copy-done | bytes 12582936
  30.1 2.2 %copy-done.3 = bf16[2,8,1024,128]{3,2,1,0:T(8,128)(2,1)S(1)} copy-done((bf16[2,8,1024,128]{3,2,1,0:T(8,128)(2,1)S(1)}, bf16[2,8,1024,128]{3,2,1,0:T(8,128)(2,1)}, u32[]{:S(2)}) %copy-start.3) | copy-done | bytes 4194328
  32.3 4.7 %shard_map.92.refs_9_ = f32[4,192,1024]{2,1,0:T(8,128)S(1)} custom-call(s32[2]{0:T(128)S(1)} %pad_add_fusion.me_ref, s32[16]{0:T(128)S(1)} %copy-done.10, bf16[80,1024]{1,0:T(8,128)(2,1)S(1)} %reshape.26.refs_0_, bf16[80,1024]{1,0:T(8,128)(2,1)S(1)} %collective-permute-done.4.refs_1_, bf16[16,8,384,128]{3,2,1,0:T(8,128)(2,1)S(1)} %copy-done.2, ...), custom_call_target="tpu_custom_call" | custom-call | flops 771751936 | bytes 8388608 | tf_op jit(solution)/shard_map/pallas_call | solution.py:316
  37.0 0.0 collective-permute-done.2.refs_2_
  37.0 0.0 collective-permute-done.3.refs_4_
  37.0 0.1 collective-permute-start.5
  37.1 0.5 collective-permute-start.6
  37.6 0.0 collective-permute-done.refs_0_
  37.6 0.1 collective-permute-start.1
  37.7 0.8 %collective-permute-done.5.refs_3_ = bf16[80,1024]{1,0:T(8,128)(2,1)S(1)} collective-permute-done((bf16[80,1024]{1,0:T(8,128)(2,1)S(1)}, bf16[80,1024]{1,0:T(8,128)(2,1)S(1)}, u32[]{:S(2)}, u32[]{:S(2)}) %collective-permute-start.5) | collective-permute-done | bytes 163872 | tf_op jit(solution)/shard_map/ppermute | solution.py:362
  38.5 0.2 collective-permute-done.6.refs_5_
  38.7 0.3 collective-permute-done.1.refs_1_
  39.0 0.0 copy-done.4
  39.0 0.0 copy-done.5
  39.0 12.8 %shard_map.93 = (bf16[8,8,1024]{2,1,0:T(8,128)(2,1)S(1)}, bf16[8,8,1024]{2,1,0:T(8,128)(2,1)S(1)}, bf16[8,8,1024]{2,1,0:T(8,128)(2,1)S(1)}, bf16[8,8,1024]{2,1,0:T(8,128)(2,1)S(1)}) custom-call(s32[2]{0:T(128)S(1)} %pad_add_fusion.me_ref, s32[16]{0:T(128)S(1)} %copy-done.10, bf16[80,1024]{1,0:T(8,128)(2,1)S(1)} %collective-permute-done.refs_0_, ...), custom_call_target="tpu_custom_call" | custom-call | flops 3388997632 | bytes 8388608 | tf_op jit(solution)/shard_map/pallas_call | solution.py:316
  51.8 1.5 %collective-permute-start.7 = (bf16[8,8,1024]{2,1,0:T(8,128)(2,1)S(1)}, bf16[8,8,1024]{2,1,0:T(8,128)(2,1)S(1)}, u32[]{:S(2)}, u32[]{:S(2)}) collective-permute-start(bf16[8,8,1024]{2,1,0:T(8,128)(2,1)S(1)} %get-tuple-element.24), channel_id=1, source_target_pairs={{0,8},{8,0},{16,24},{24,16},{1,9},{9,1},{17,25},{25,17},{2,10},{10... | collective-permute-start | bytes 393224 | tf_op jit(solution)/shard_map/ppermute | solution.py:362
  53.3 1.5 %collective-permute-start.8 = (bf16[8,8,1024]{2,1,0:T(8,128)(2,1)S(1)}, bf16[8,8,1024]{2,1,0:T(8,128)(2,1)S(1)}, u32[]{:S(2)}, u32[]{:S(2)}) collective-permute-start(bf16[8,8,1024]{2,1,0:T(8,128)(2,1)S(1)} %get-tuple-element.25), channel_id=1, source_target_pairs={{0,16},{8,24},{16,0},{24,8},{1,17},{9,25},{17,1},{25,9},{2,18},{10... | collective-permute-start | bytes 393224 | tf_op jit(solution)/shard_map/ppermute | solution.py:362
  54.9 0.5 collective-permute-start.9
  55.4 2.5 %collective-permute-done.7.refs_1_ = bf16[8,8,1024]{2,1,0:T(8,128)(2,1)S(1)} collective-permute-done((bf16[8,8,1024]{2,1,0:T(8,128)(2,1)S(1)}, bf16[8,8,1024]{2,1,0:T(8,128)(2,1)S(1)}, u32[]{:S(2)}, u32[]{:S(2)}) %collective-permute-start.7) | collective-permute-done | bytes 131104 | tf_op jit(solution)/shard_map/ppermute | solution.py:362
  57.8 3.7 %collective-permute-done.8.refs_2_ = bf16[8,8,1024]{2,1,0:T(8,128)(2,1)S(1)} collective-permute-done((bf16[8,8,1024]{2,1,0:T(8,128)(2,1)S(1)}, bf16[8,8,1024]{2,1,0:T(8,128)(2,1)S(1)}, u32[]{:S(2)}, u32[]{:S(2)}) %collective-permute-start.8) | collective-permute-done | bytes 131104 | tf_op jit(solution)/shard_map/ppermute | solution.py:362
  61.5 0.0 collective-permute-done.9.refs_3_
  61.5 0.5 shard_map.94
  62.0 0.1 collective-permute-start.10
  62.1 1.2 %collective-permute-done.10 = bf16[32,1024]{1,0:T(8,128)(2,1)S(1)} collective-permute-done((bf16[32,1024]{1,0:T(8,128)(2,1)S(1)}, bf16[32,1024]{1,0:T(8,128)(2,1)S(1)}, u32[]{:S(2)}, u32[]{:S(2)}) %collective-permute-start.10) | collective-permute-done | bytes 65568 | tf_op jit(solution)/shard_map/ppermute | solution.py:362
  63.3 3.0 %collective-permute-start.13 = (bf16[16,1024]{1,0:T(8,128)(2,1)S(1)}, bf16[16,1024]{1,0:T(8,128)(2,1)S(1)}, u32[]{:S(2)}, u32[]{:S(2)}) collective-permute-start(bf16[16,1024]{1,0:T(8,128)(2,1)S(1)} %pad_maximum_fusion.3), channel_id=1, source_target_pairs={{0,6},{1,7},{2,4},{3,5},{4,2},{5,3},{6,0},{7,1},{8,14},{9,15},{10,... | collective-permute-start | bytes 98312 | tf_op jit(solution)/shard_map/ppermute | solution.py:362
  66.3 0.4 collective-permute-start.11
  66.7 1.0 %collective-permute-start.12 = (bf16[16,1024]{1,0:T(8,128)(2,1)S(1)}, bf16[16,1024]{1,0:T(8,128)(2,1)S(1)}, u32[]{:S(2)}, u32[]{:S(2)}) collective-permute-start(bf16[16,1024]{1,0:T(8,128)(2,1)S(1)} %pad_maximum_fusion.2), channel_id=1, source_target_pairs={{0,4},{1,5},{2,6},{3,7},{4,0},{5,1},{6,2},{7,3},{8,12},{9,13},{10,... | collective-permute-start | bytes 98312 | tf_op jit(solution)/shard_map/ppermute | solution.py:362
  67.8 2.8 %collective-permute-done.11 = bf16[16,1024]{1,0:T(8,128)(2,1)S(1)} collective-permute-done((bf16[16,1024]{1,0:T(8,128)(2,1)S(1)}, bf16[16,1024]{1,0:T(8,128)(2,1)S(1)}, u32[]{:S(2)}, u32[]{:S(2)}) %collective-permute-start.11) | collective-permute-done | bytes 32800 | tf_op jit(solution)/shard_map/ppermute | solution.py:362
  70.5 1.0 %collective-permute-done.12 = bf16[16,1024]{1,0:T(8,128)(2,1)S(1)} collective-permute-done((bf16[16,1024]{1,0:T(8,128)(2,1)S(1)}, bf16[16,1024]{1,0:T(8,128)(2,1)S(1)}, u32[]{:S(2)}, u32[]{:S(2)}) %collective-permute-start.12) | collective-permute-done | bytes 32800 | tf_op jit(solution)/shard_map/ppermute | solution.py:362
  71.6 0.0 collective-permute-done.13
  71.6 0.0 copy-done
  71.6 2.2 %convolution_convert_fusion = bf16[1024,1024]{1,0:T(8,128)(2,1)} fusion(bf16[64,1024]{1,0:T(8,128)(2,1)S(1)} %constant_dynamic-update-slice_fusion, bf16[64,1024]{1,0:T(8,128)(2,1)S(1)} %copy-done, s32[64]{0:T(128)S(1)} %fusion.2), kind=kOutput, calls=%fused_computation | convolution fusion | flops 143724544 | bytes 2359552 | tf_op jit(solution)/shard_map/dot_general | solution.py:411
  (19 shorter events, 0.1 us)
Async XLA Ops:
  0.0 71.6 %copy-start = (bf16[64,1024]{1,0:T(8,128)(2,1)S(1)}, bf16[64,1024]{1,0:T(8,128)(2,1)}, u32[]{:S(2)}) copy-start(bf16[64,1024]{1,0:T(8,128)(2,1)} %param.12) | copy-start | bytes 393220
  0.0 25.5 %copy-start.7 = (bf16[192,160]{1,0:T(8,128)(2,1)S(1)}, bf16[192,160]{1,0:T(8,128)(2,1)}, u32[]{:S(2)}) copy-start(bf16[192,160]{1,0:T(8,128)(2,1)} %constant.52.clone.refs_4_.refs_8_) | copy-start | bytes 184324
  0.0 25.5 %copy-start.10 = (s32[16]{0:T(128)S(1)}, s32[16]{0:T(128)}, u32[]{:S(2)}) copy-start(s32[16]{0:T(128)} %slot_ref.3) | copy-start | bytes 196
  1.1 24.4 %collective-permute-start.4 = (bf16[80,1024]{1,0:T(8,128)(2,1)S(1)}, bf16[80,1024]{1,0:T(8,128)(2,1)S(1)}, u32[]{:S(2)}, u32[]{:S(2)}) collective-permute-start(bf16[80,1024]{1,0:T(8,128)(2,1)S(1)} %reshape.26.refs_0_), channel_id=1, source_target_pairs={{0,1},{1,0},{2,3},{3,2},{4,5},{5,4},{6,7},{7,6},{8,9},{9,8},{10,11... | collective-permute-start | bytes 491528 | tf_op jit(solution)/shard_map/ppermute | solution.py:362
  1.6 35.4 %collective-permute-start.2 = (bf16[80,1024]{1,0:T(8,128)(2,1)S(1)}, bf16[80,1024]{1,0:T(8,128)(2,1)S(1)}, u32[]{:S(2)}, u32[]{:S(2)}) collective-permute-start(bf16[80,1024]{1,0:T(8,128)(2,1)S(1)} %reshape.26.refs_0_), channel_id=1, source_target_pairs={{0,4},{1,5},{2,6},{3,7},{4,0},{5,1},{6,2},{7,3},{8,12},{9,13},{10,... | collective-permute-start | bytes 491528 | tf_op jit(solution)/shard_map/ppermute | solution.py:362
  5.3 31.8 %collective-permute-start.3 = (bf16[80,1024]{1,0:T(8,128)(2,1)S(1)}, bf16[80,1024]{1,0:T(8,128)(2,1)S(1)}, u32[]{:S(2)}, u32[]{:S(2)}) collective-permute-start(bf16[80,1024]{1,0:T(8,128)(2,1)S(1)} %reshape.26.refs_0_), channel_id=1, source_target_pairs={{0,6},{1,7},{2,4},{3,5},{4,2},{5,3},{6,0},{7,1},{8,14},{9,15},{10,... | collective-permute-start | bytes 491528 | tf_op jit(solution)/shard_map/ppermute | solution.py:362
  6.6 31.0 %collective-permute-start = (bf16[80,1024]{1,0:T(8,128)(2,1)S(1)}, bf16[80,1024]{1,0:T(8,128)(2,1)S(1)}, u32[]{:S(2)}, u32[]{:S(2)}) collective-permute-start(bf16[80,1024]{1,0:T(8,128)(2,1)S(1)} %reshape.26.refs_0_), channel_id=1, source_target_pairs={{0,2},{1,3},{2,0},{3,1},{4,6},{5,7},{6,4},{7,5},{8,10},{9,11},{10,... | collective-permute-start | bytes 491528 | tf_op jit(solution)/shard_map/ppermute | solution.py:362
  6.8 2.2 %copy-start.6 = (bf16[16,8,8,2,1024]{4,3,2,1,0:T(2,128)(2,1)S(1)}, bf16[16,8,8,2,1024]{4,3,2,1,0:T(2,128)(2,1)}, u32[]{:S(2)}) copy-start(bf16[16,8,8,2,1024]{4,3,2,1,0:T(2,128)(2,1)} %room_hbm.1) | copy-start | bytes 12582916
  9.0 0.9 %copy-start.8 = (bf16[384,256]{1,0:T(8,128)(2,1)S(1)}, bf16[384,256]{1,0:T(8,128)(2,1)}, u32[]{:S(2)}) copy-start(bf16[384,256]{1,0:T(8,128)(2,1)} %constant.50.clone.table_ref) | copy-start | bytes 589828
  20.9 4.5 %copy-start.1 = (bf16[16,8,384,128]{3,2,1,0:T(8,128)(2,1)}, bf16[16,8,384,128]{3,2,1,0:T(8,128)(2,1)S(1)}, u32[]{:S(2)}) copy-start(bf16[16,8,384,128]{3,2,1,0:T(8,128)(2,1)S(1)} %shard_map.91.refs_2_.refs_6_) | copy-start | bytes 37748740
  25.5 4.6 %copy-start.2 = (bf16[16,8,384,128]{3,2,1,0:T(8,128)(2,1)S(1)}, bf16[16,8,384,128]{3,2,1,0:T(8,128)(2,1)}, u32[]{:S(2)}) copy-start(bf16[16,8,384,128]{3,2,1,0:T(8,128)(2,1)} %copy-done.1) | copy-start | bytes 37748740
  30.1 2.2 %copy-start.3 = (bf16[2,8,1024,128]{3,2,1,0:T(8,128)(2,1)S(1)}, bf16[2,8,1024,128]{3,2,1,0:T(8,128)(2,1)}, u32[]{:S(2)}) copy-start(bf16[2,8,1024,128]{3,2,1,0:T(8,128)(2,1)} %constant.51.clone.refs_3_.refs_7_) | copy-start | bytes 12582916
  32.3 6.7 %copy-start.4 = (bf16[2,8,1024,128]{3,2,1,0:T(8,128)(2,1)S(1)}, bf16[2,8,1024,128]{3,2,1,0:T(8,128)(2,1)}, u32[]{:S(2)}) copy-start(bf16[2,8,1024,128]{3,2,1,0:T(8,128)(2,1)} %constant.51.clone.refs_3_.refs_7_) | copy-start | bytes 12582916
  32.3 6.7 %copy-start.5 = (bf16[2,8,1024,128]{3,2,1,0:T(8,128)(2,1)S(1)}, bf16[2,8,1024,128]{3,2,1,0:T(8,128)(2,1)}, u32[]{:S(2)}) copy-start(bf16[2,8,1024,128]{3,2,1,0:T(8,128)(2,1)} %constant.54.clone.refs_11_) | copy-start | bytes 12582916
  32.3 6.7 %copy-start.9 = (bf16[2,128,192]{2,1,0:T(8,128)(2,1)S(1)}, bf16[2,128,192]{2,1,0:T(8,128)(2,1)}, u32[]{:S(2)}) copy-start(bf16[2,128,192]{2,1,0:T(8,128)(2,1)} %constant.53.clone.refs_10_) | copy-start | bytes 294916
  37.0 1.5 %collective-permute-start.5 = (bf16[80,1024]{1,0:T(8,128)(2,1)S(1)}, bf16[80,1024]{1,0:T(8,128)(2,1)S(1)}, u32[]{:S(2)}, u32[]{:S(2)}) collective-permute-start(bf16[80,1024]{1,0:T(8,128)(2,1)S(1)} %collective-permute-done.2.refs_2_), channel_id=1, source_target_pairs={{0,1},{1,0},{2,3},{3,2},{4,5},{5,4},{6,7},{7,6},{8,9},{9,8},{10,11... | collective-permute-start | bytes 491528 | tf_op jit(solution)/shard_map/ppermute | solution.py:362
  37.1 1.6 %collective-permute-start.6 = (bf16[80,1024]{1,0:T(8,128)(2,1)S(1)}, bf16[80,1024]{1,0:T(8,128)(2,1)S(1)}, u32[]{:S(2)}, u32[]{:S(2)}) collective-permute-start(bf16[80,1024]{1,0:T(8,128)(2,1)S(1)} %collective-permute-done.3.refs_4_), channel_id=1, source_target_pairs={{0,1},{1,0},{2,3},{3,2},{4,5},{5,4},{6,7},{7,6},{8,9},{9,8},{10,11... | collective-permute-start | bytes 491528 | tf_op jit(solution)/shard_map/ppermute | solution.py:362
  37.6 1.4 %collective-permute-start.1 = (bf16[80,1024]{1,0:T(8,128)(2,1)S(1)}, bf16[80,1024]{1,0:T(8,128)(2,1)S(1)}, u32[]{:S(2)}, u32[]{:S(2)}) collective-permute-start(bf16[80,1024]{1,0:T(8,128)(2,1)S(1)} %collective-permute-done.refs_0_), channel_id=1, source_target_pairs={{0,1},{1,0},{2,3},{3,2},{4,5},{5,4},{6,7},{7,6},{8,9},{9,8},{10,11... | collective-permute-start | bytes 491528 | tf_op jit(solution)/shard_map/ppermute | solution.py:362
  51.8 6.1 %collective-permute-start.7 = (bf16[8,8,1024]{2,1,0:T(8,128)(2,1)S(1)}, bf16[8,8,1024]{2,1,0:T(8,128)(2,1)S(1)}, u32[]{:S(2)}, u32[]{:S(2)}) collective-permute-start(bf16[8,8,1024]{2,1,0:T(8,128)(2,1)S(1)} %get-tuple-element.24), channel_id=1, source_target_pairs={{0,8},{8,0},{16,24},{24,16},{1,9},{9,1},{17,25},{25,17},{2,10},{10... | collective-permute-start | bytes 393224 | tf_op jit(solution)/shard_map/ppermute | solution.py:362
  53.3 8.2 %collective-permute-start.8 = (bf16[8,8,1024]{2,1,0:T(8,128)(2,1)S(1)}, bf16[8,8,1024]{2,1,0:T(8,128)(2,1)S(1)}, u32[]{:S(2)}, u32[]{:S(2)}) collective-permute-start(bf16[8,8,1024]{2,1,0:T(8,128)(2,1)S(1)} %get-tuple-element.25), channel_id=1, source_target_pairs={{0,16},{8,24},{16,0},{24,8},{1,17},{9,25},{17,1},{25,9},{2,18},{10... | collective-permute-start | bytes 393224 | tf_op jit(solution)/shard_map/ppermute | solution.py:362
  54.9 6.6 %collective-permute-start.9 = (bf16[8,8,1024]{2,1,0:T(8,128)(2,1)S(1)}, bf16[8,8,1024]{2,1,0:T(8,128)(2,1)S(1)}, u32[]{:S(2)}, u32[]{:S(2)}) collective-permute-start(bf16[8,8,1024]{2,1,0:T(8,128)(2,1)S(1)} %get-tuple-element.26), channel_id=1, source_target_pairs={{0,24},{8,16},{16,8},{24,0},{1,25},{9,17},{17,9},{25,1},{2,26},{10... | collective-permute-start | bytes 393224 | tf_op jit(solution)/shard_map/ppermute | solution.py:362
  62.0 1.3 %collective-permute-start.10 = (bf16[32,1024]{1,0:T(8,128)(2,1)S(1)}, bf16[32,1024]{1,0:T(8,128)(2,1)S(1)}, u32[]{:S(2)}, u32[]{:S(2)}) collective-permute-start(bf16[32,1024]{1,0:T(8,128)(2,1)S(1)} %pad_maximum_fusion), channel_id=1, source_target_pairs={{0,1},{1,0},{2,3},{3,2},{4,5},{5,4},{6,7},{7,6},{8,9},{9,8},{10,11... | collective-permute-start | bytes 196616 | tf_op jit(solution)/shard_map/ppermute | solution.py:362
  63.3 8.3 %collective-permute-start.13 = (bf16[16,1024]{1,0:T(8,128)(2,1)S(1)}, bf16[16,1024]{1,0:T(8,128)(2,1)S(1)}, u32[]{:S(2)}, u32[]{:S(2)}) collective-permute-start(bf16[16,1024]{1,0:T(8,128)(2,1)S(1)} %pad_maximum_fusion.3), channel_id=1, source_target_pairs={{0,6},{1,7},{2,4},{3,5},{4,2},{5,3},{6,0},{7,1},{8,14},{9,15},{10,... | collective-permute-start | bytes 98312 | tf_op jit(solution)/shard_map/ppermute | solution.py:362
  66.3 4.2 %collective-permute-start.11 = (bf16[16,1024]{1,0:T(8,128)(2,1)S(1)}, bf16[16,1024]{1,0:T(8,128)(2,1)S(1)}, u32[]{:S(2)}, u32[]{:S(2)}) collective-permute-start(bf16[16,1024]{1,0:T(8,128)(2,1)S(1)} %pad_maximum_fusion.1), channel_id=1, source_target_pairs={{0,2},{1,3},{2,0},{3,1},{4,6},{5,7},{6,4},{7,5},{8,10},{9,11},{10,... | collective-permute-start | bytes 98312 | tf_op jit(solution)/shard_map/ppermute | solution.py:362
  66.7 4.8 %collective-permute-start.12 = (bf16[16,1024]{1,0:T(8,128)(2,1)S(1)}, bf16[16,1024]{1,0:T(8,128)(2,1)S(1)}, u32[]{:S(2)}, u32[]{:S(2)}) collective-permute-start(bf16[16,1024]{1,0:T(8,128)(2,1)S(1)} %pad_maximum_fusion.2), channel_id=1, source_target_pairs={{0,4},{1,5},{2,6},{3,7},{4,0},{5,1},{6,2},{7,3},{8,12},{9,13},{10,... | collective-permute-start | bytes 98312 | tf_op jit(solution)/shard_map/ppermute | solution.py:362

commit v5 on v4

--- a/solution.py
+++ b/solution.py
@@ -15,6 +15,7 @@
 LANES = 256
 SLAB = 128
 GROUP = 4
+ROWS = 4
 STEPS = 24
 SEGS = 2
 KEEP = 16
@@ -57,13 +58,13 @@
         packed = np.block([[cos * first, cos * (1 - first)], [-sin * first, -sin * (1 - first)]])
         return plain, packed
 
-    spec = np.zeros((2, SEGS, 2, 2, STEPS, 2, frames))
+    spec = np.zeros((2, SEGS, 2, STEPS, 2, frames))
     used = parts - 1 + KEEP
     for kind, table in enumerate(forward(np.arange(used))):
-        table = table.reshape(2, 1, STEPS, 2, used)
+        table = table.reshape(2, STEPS, 2, used)
         for seg in range(SEGS):
-            spec[kind, seg, :, :, :, :, seg * KEEP : seg * KEEP + used] = table
-    spec = spec.reshape(2, SEGS * 4 * STEPS, 2 * frames)
+            spec[kind, seg, :, :, :, seg * KEEP : seg * KEEP + used] = table
+    spec = spec.reshape(2, SEGS * 2 * STEPS, 2 * frames)
     spec = np.concatenate([spec[0], spec[1]], axis=1)
 
     resp = np.zeros((channels // 2, 2, 2, STEPS, 2, parts, channels, 2))
@@ -108,41 +109,28 @@
     return jnp.concatenate([ref[(*index, first + i)] for i in range(LANES // SLAB)], axis=-1)
 
 
-def response_kernel(rows, bins, room_hbm, table_ref, hat_ref, room_ref, sems):
-    slabs = bins // SLAB
-    depth = room_ref.shape[2] * room_ref.shape[3] * 2
-    flat = room_ref.reshape(rows, slabs, depth, SLAB)
+def response_kernel(rows, bins, room_ref, table_ref, hat_ref):
+    depth = room_ref.shape[1] * room_ref.shape[2] * 2
+    flat = room_ref.reshape(rows, depth, bins)
     plain, packed, _ = lane_masks(0, LANES)
     plain, packed = plain.astype(BF16), packed.astype(BF16)
 
-    def copies(r):
-        return [
-            pltpu.make_async_copy(
-                room_hbm.at[r, :, :, :, pl.ds(i * SLAB, SLAB)], room_ref.at[r, i], sems.at[r, i]
-            )
-            for i in range(slabs)
-        ]
-
-    for r in range(rows):
-        for copy in copies(r):
-            copy.start()
-
-    def one(r, carry):
-        for copy in copies(r):
-            copy.wait()
-        for step in range(bins // LANES):
-            h = two_slabs(flat, step, r)
-            if step == 0:
-                h = jnp.concatenate([h * plain, h * packed], axis=0)
-                hat = dot(table_ref[...], h)
-            else:
-                hat = dot(table_ref[:, :depth], h)
-            hat = hat.astype(BF16)
-            for i in range(LANES // SLAB):
-                hat_ref[r, step * (LANES // SLAB) + i] = hat[:, i * SLAB : (i + 1) * SLAB]
+    def some(outer, carry):
+        for inner in range(ROWS):
+            r = outer * ROWS + inner
+            for step in range(bins // LANES):
+                h = flat[r, :, step * LANES : (step + 1) * LANES]
+                if step == 0:
+                    h = jnp.concatenate([h * plain, h * packed], axis=0)
+                    hat = dot(table_ref[...], h)
+                else:
+                    hat = dot(table_ref[:, :depth], h)
+                hat = hat.astype(BF16)
+                for i in range(LANES // SLAB):
+                    hat_ref[r, step * (LANES // SLAB) + i] = hat[:, i * SLAB : (i + 1) * SLAB]
         return carry
 
-    lax.fori_loop(0, rows, one, 0)
+    lax.fori_loop(0, rows // ROWS, some, 0)
 
 
 def transform_responses(room):
@@ -153,16 +141,28 @@
     flops = 2 * rows * channels * 2 * STEPS * parts * channels * 2 * bins
     return pl.pallas_call(
         functools.partial(response_kernel, rows, bins),
-        in_specs=[pl.BlockSpec(memory_space=pltpu.HBM), vmem],
+        in_specs=[vmem, vmem],
         out_specs=vmem,
         out_shape=jax.ShapeDtypeStruct((rows, slabs, channels * 2 * STEPS, SLAB), BF16),
-        scratch_shapes=[
-            pltpu.VMEM((rows, slabs, parts, channels, 2, SLAB), BF16),
-            pltpu.SemaphoreType.DMA((rows, slabs)),
-        ],
-        compiler_params=pltpu.CompilerParams(vmem_limit_bytes=24 * 2**20),
+        compiler_params=pltpu.CompilerParams(vmem_limit_bytes=8 * 2**20),
         cost_estimate=pl.CostEstimate(flops=flops, bytes_accessed=16 * 2**20, transcendentals=0),
     )(room, jnp.asarray(resp))
+
+
+def copy_kernel(x_ref, out_ref):
+    out_ref[...] = x_ref[...]
+
+
+def copy_early(x):
+    vmem = pl.BlockSpec(memory_space=pltpu.VMEM)
+    return pl.pallas_call(
+        copy_kernel,
+        in_specs=[vmem],
+        out_specs=vmem,
+        out_shape=jax.ShapeDtypeStruct(x.shape, x.dtype),
+        compiler_params=pltpu.CompilerParams(vmem_limit_bytes=2 * 2**20),
+        cost_estimate=pl.CostEstimate(flops=0, bytes_accessed=24 * 2**20, transcendentals=0),
+    )(x)
 
 
 def mix_kernel(flips, own, channels, blocks, shares, has_total, last, me_ref, slot_ref, *refs):
@@ -193,21 +193,28 @@
         for i in range(own)
     ]
 
-    def spectra_step(step):
-        plain, packed, sign = lane_masks(step * LANES, LANES)
+    def frame_spectra(step):
+        _, _, sign = lane_masks(step * LANES, LANES)
         spectra = []
         for j in range(2):
             one = dot(x, two_slabs(table_ref, step, j))
             spectra.append(one + sign * pltpu.roll(one, one.shape[0] - 1, axis=0))
-        for r in range(rows):
-            both = jnp.concatenate([s[r * count : (r + 1) * count] for s in spectra], axis=0)
-            if step == 0:
-                both = jnp.concatenate([both * plain, both * packed], axis=0).astype(BF16)
-                hat = dot(spec_ref[...], both).astype(BF16)
-            else:
-                hat = dot(spec_ref[:, :cols], both.astype(BF16)).astype(BF16)
-            for i in range(LANES // SLAB):
-                s_ref[step * (LANES // SLAB) + i, r] = hat[:, i * SLAB : (i + 1) * SLAB]
+        return spectra
+
+    def step_spectra(step, r, spectra):
+        both = jnp.concatenate([s[r * count : (r + 1) * count] for s in spectra], axis=0)
+        if step == 0:
+            plain, packed, _ = lane_masks(0, LANES)
+            both = jnp.concatenate([both * plain, both * packed], axis=0).astype(BF16)
+            hat = dot(spec_ref[...], both)
+        else:
+            hat = dot(spec_ref[:, :cols], both.astype(BF16))
+        for i in range(LANES // SLAB):
+            part = hat[:, i * SLAB : (i + 1) * SLAB]
+            for k in range(2 * SEGS):
+                one = part[k * STEPS : (k + 1) * STEPS]
+                both = jnp.concatenate([one, one], axis=0).astype(BF16)
+                s_ref[step * (LANES // SLAB) + i, r, k * half : (k + 1) * half] = both
 
     def product_slab(slab, pair):
         far = slice(slab * SLAB, (slab + 1) * SLAB)
@@ -237,30 +244,36 @@
                 out_ref[pair, re_rows, far] = re_sum
                 out_ref[pair, im_rows, far] = im_sum
 
-    def product_step(step):
-        for pair in range(channels // 2):
-            first = step * (LANES // SLAB)
-            for i in range(LANES // SLAB):
-                product_slab(first + i, pair)
-            if last:
-                y = jnp.concatenate([y_ref[first + i, pair] for i in range(LANES // SLAB)], axis=-1)
-                if step == 0:
-                    plain, packed, _ = lane_masks(0, LANES)
-                    mix = dot(back_ref[0], y * plain.astype(BF16)) + dot(back_ref[1], y * packed.astype(BF16))
-                else:
-                    mix = dot(back_ref[0], y)
-                mix = mix.astype(BF16)
-                here = slice(step * LANES, (step + 1) * LANES)
-                for c in range(2):
-                    rows_to = slice((2 * pair + c) * blocks, (2 * pair + c + 1) * blocks)
-                    left_re[rows_to, here] = mix[2 * c * blocks : (2 * c + 1) * blocks]
-                    left_im[rows_to, here] = mix[(2 * c + 1) * blocks : (2 * c + 2) * blocks]
-
-    spectra_step(0)
-    for step in range(steps):
-        if step + 1 < steps:
-            spectra_step(step + 1)
-        product_step(step)
+    def product_pair(step, pair):
+        first = step * (LANES // SLAB)
+        for i in range(LANES // SLAB):
+            product_slab(first + i, pair)
+        if last:
+            y = jnp.concatenate([y_ref[first + i, pair] for i in range(LANES // SLAB)], axis=-1)
+            if step == 0:
+                plain, packed, _ = lane_masks(0, LANES)
+                mix = dot(back_ref[0], y * plain.astype(BF16)) + dot(back_ref[1], y * packed.astype(BF16))
+            else:
+                mix = dot(back_ref[0], y)
+            mix = mix.astype(BF16)
+            here = slice(step * LANES, (step + 1) * LANES)
+            for c in range(2):
+                rows_to = slice((2 * pair + c) * blocks, (2 * pair + c + 1) * blocks)
+                left_re[rows_to, here] = mix[2 * c * blocks : (2 * c + 1) * blocks]
+                left_im[rows_to, here] = mix[(2 * c + 1) * blocks : (2 * c + 2) * blocks]
+
+    pairs = channels // 2
+    for step in range(steps + 1):
+        spectra = frame_spectra(step) if step < steps else None
+        done = 0
+        for pair in range(pairs):
+            if spectra is not None:
+                upto = rows * (pair + 1) // pairs
+                for r in range(done, upto):
+                    step_spectra(step, r, spectra)
+                done = upto
+            if step > 0:
+                product_pair(step - 1, pair)
 
     if last:
         each = blocks // shares
@@ -320,7 +333,7 @@
         out_shape=out_shape,
         scratch_shapes=scratch,
         input_output_aliases=aliases,
-        compiler_params=pltpu.CompilerParams(vmem_limit_bytes=24 * 2**20),
+        compiler_params=pltpu.CompilerParams(vmem_limit_bytes=16 * 2**20),
         cost_estimate=pl.CostEstimate(flops=flops, bytes_accessed=8 * 2**20, transcendentals=0),
     )(*operands)
 
@@ -356,7 +369,7 @@
     src_me = lax.axis_index("src").astype(jnp.int32)
     ch_me = lax.axis_index("ch").astype(jnp.int32)
 
-    x_own = dry_signal.reshape(own * frames, block_len)
+    x_own = copy_early(dry_signal.reshape(own * frames, block_len))
 
     def swap(value, axis, count, flip):
         return lax.ppermute(value, axis, [(i, i ^ flip) for i in range(count)])

time: 74 us -> 70.1 us (0.947)
  Pallas kernels: 28.9 us -> 22.7 us
  local copies, waits for them, and re-layouts: 15.5 us -> 17.7 us
    pallas_call x1, Pallas kernels: 11 us -> 4.1 us  [transform_responses(): pl.pallas_call(functools.partial(response_kernel, rows, bins), in_specs=[...]
    unnamed x25 -> x27, local copies, waits for them, and re-layouts: 14.4 us -> 16.6 us
  transfers between devices with their start and end apart: 14 -> 14, of which waited for: 8 -> 8; matrix products, arithmetic and copies ran while one was open for 0% -> 0% of each run, Pallas kernels for 21% -> 13%
where the time goes in v5:
time: 70.1 us; the launch traced here: 69.8 us
  Pallas kernels  22.7 us (32%)
  local copies, waits for them, and re-layouts  17.7 us (25%)
  starting transfers between devices  14.5 us (21%)
  waiting for transfers between devices  12.5 us (18%)
  matrix products  2.21 us (3%)
    pallas_call x2, Pallas kernels, add_sources(): pl.pallas_call(body, in_specs=[smem, smem] + [vmem] * (len(operands) - 2)...  18.1 us
    unnamed x27, local copies, waits for them, and re-layouts  16.6 us
    ppermute x14, starting transfers between devices, swap(): return lax.ppermute(value, axis, [(i, i ^ flip) for i in range(count)])  14.5 us
    ppermute x14, waiting for transfers between devices, swap(): return lax.ppermute(value, axis, [(i, i ^ flip) for i in range(count)])  12.5 us
    pallas_call x1, Pallas kernels, transform_responses(): pl.pallas_call(functools.partial(response_kernel, rows, bins), in_specs=[...  4.1 us
    dot_general x1, matrix products, per_device(): lax.dot_general(gathered, matrix, (((0,), (0,)), ((), ())), preferred_ele...  2.21 us
  transfers between devices with their start and end apart: 14, of which 8 were waited for; matrix products, arithmetic and copies ran while one was open for 0% of the time, Pallas kernels for 13%

profile of v5, /device:TPU:0, one launch (start us, length us, event | category | flops | bytes accessed | tf_op | source)
XLA Modules:
  0.0 69.8 jit_solution(2017948067134491944)
XLA Ops:
  0.0 0.0 copy-start
  0.0 1.1 %reshape.26.x_ref = bf16[80,1024]{1,0:T(8,128)(2,1)S(1)} reshape(bf16[2,40960]{1,0:T(2,128)(2,1)} %param.9) | data formatting | bytes 327680 | tf_op jit(solution)/shard_map/reshape | solution.py:372
  1.1 0.0 copy-start.9
  1.1 0.0 copy-start.11
  1.1 0.5 collective-permute-start.4
  1.6 3.7 %collective-permute-start.2 = (bf16[80,1024]{1,0:T(8,128)(2,1)S(1)}, bf16[80,1024]{1,0:T(8,128)(2,1)S(1)}, u32[]{:S(2)}, u32[]{:S(2)}) collective-permute-start(bf16[80,1024]{1,0:T(8,128)(2,1)S(1)} %shard_map.91.refs_0_), channel_id=1, source_target_pairs={{0,4},{1,5},{2,6},{3,7},{4,0},{5,1},{6,2},{7,3},{8,12},{9,13},{10,... | collective-permute-start | bytes 491528 | tf_op jit(solution)/shard_map/ppermute | solution.py:375
  5.3 1.3 %collective-permute-start.3 = (bf16[80,1024]{1,0:T(8,128)(2,1)S(1)}, bf16[80,1024]{1,0:T(8,128)(2,1)S(1)}, u32[]{:S(2)}, u32[]{:S(2)}) collective-permute-start(bf16[80,1024]{1,0:T(8,128)(2,1)S(1)} %shard_map.91.refs_0_), channel_id=1, source_target_pairs={{0,6},{1,7},{2,4},{3,5},{4,2},{5,3},{6,0},{7,1},{8,14},{9,15},{10,... | collective-permute-start | bytes 491528 | tf_op jit(solution)/shard_map/ppermute | solution.py:375
  6.6 0.2 collective-permute-start
  6.9 2.2 %copy-done.6 = bf16[16,8,8,2,1024]{4,3,2,1,0:T(2,128)(2,1)S(1)} copy-done((bf16[16,8,8,2,1024]{4,3,2,1,0:T(2,128)(2,1)S(1)}, bf16[16,8,8,2,1024]{4,3,2,1,0:T(2,128)(2,1)}, u32[]{:S(2)}) %copy-start.6) | copy-done | bytes 4194328
  9.1 0.9 %copy-done.8 = bf16[384,256]{1,0:T(8,128)(2,1)S(1)} copy-done((bf16[384,256]{1,0:T(8,128)(2,1)S(1)}, bf16[384,256]{1,0:T(8,128)(2,1)}, u32[]{:S(2)}) %copy-start.8) | copy-done | bytes 196632
  10.0 4.1 %shard_map.92.refs_2_.refs_6_ = bf16[16,8,384,128]{3,2,1,0:T(8,128)(2,1)S(1)} custom-call(bf16[16,8,8,2,1024]{4,3,2,1,0:T(2,128)(2,1)S(1)} %copy-done.6, bf16[384,256]{1,0:T(8,128)(2,1)S(1)} %copy-done.8), custom_call_target="tpu_custom_call" | custom-call | flops 1610612736 | bytes 16777216 | tf_op jit(solution)/shard_map/pallas_call | solution.py:142
  14.1 0.0 copy-start.1
  14.1 4.5 %copy-done.1 = bf16[16,8,384,128]{3,2,1,0:T(8,128)(2,1)} copy-done((bf16[16,8,384,128]{3,2,1,0:T(8,128)(2,1)}, bf16[16,8,384,128]{3,2,1,0:T(8,128)(2,1)S(1)}, u32[]{:S(2)}) %copy-start.1) | copy-done | bytes 12582936
  18.6 0.1 pad_add_fusion.me_ref
  18.7 0.0 collective-permute-done.4.refs_1_
  18.7 0.0 copy-done.11
  18.7 4.6 %copy-done.2 = bf16[16,8,384,128]{3,2,1,0:T(8,128)(2,1)S(1)} copy-done((bf16[16,8,384,128]{3,2,1,0:T(8,128)(2,1)S(1)}, bf16[16,8,384,128]{3,2,1,0:T(8,128)(2,1)}, u32[]{:S(2)}) %copy-start.2) | copy-done | bytes 12582936
  23.3 2.2 %copy-done.4 = bf16[2,8,1024,128]{3,2,1,0:T(8,128)(2,1)S(1)} copy-done((bf16[2,8,1024,128]{3,2,1,0:T(8,128)(2,1)S(1)}, bf16[2,8,1024,128]{3,2,1,0:T(8,128)(2,1)}, u32[]{:S(2)}) %copy-start.4) | copy-done | bytes 4194328
  25.5 4.7 %shard_map.93.refs_9_ = f32[4,192,1024]{2,1,0:T(8,128)S(1)} custom-call(s32[2]{0:T(128)S(1)} %pad_add_fusion.me_ref, s32[16]{0:T(128)S(1)} %copy-done.11, bf16[80,1024]{1,0:T(8,128)(2,1)S(1)} %shard_map.91.refs_0_, bf16[80,1024]{1,0:T(8,128)(2,1)S(1)} %collective-permute-done.4.refs_1_, bf16[16,8,384,128]{3,2,1,0:T(8,128)(2,1)S(1)} %copy-done.2, ...), custom_call_target="tpu_custom_call" | custom-call | flops 771751936 | bytes 8388608 | tf_op jit(solution)/shard_map/pallas_call | solution.py:329
  30.2 0.0 collective-permute-done.2.refs_2_
  30.2 0.0 collective-permute-done.3.refs_4_
  30.2 0.1 collective-permute-start.5
  30.3 0.5 collective-permute-start.6
  30.8 0.0 collective-permute-done.refs_0_
  30.8 0.1 collective-permute-start.1
  30.9 0.8 %collective-permute-done.5.refs_3_ = bf16[80,1024]{1,0:T(8,128)(2,1)S(1)} collective-permute-done((bf16[80,1024]{1,0:T(8,128)(2,1)S(1)}, bf16[80,1024]{1,0:T(8,128)(2,1)S(1)}, u32[]{:S(2)}, u32[]{:S(2)}) %collective-permute-start.5) | collective-permute-done | bytes 163872 | tf_op jit(solution)/shard_map/ppermute | solution.py:375
  31.7 0.2 collective-permute-done.6.refs_5_
  31.9 0.3 collective-permute-done.1.refs_1_
  32.2 0.0 copy-done.5
  32.2 0.0 copy-start.7
  32.2 2.2 %copy-done.7 = bf16[2,8,1024,128]{3,2,1,0:T(8,128)(2,1)S(1)} copy-done((bf16[2,8,1024,128]{3,2,1,0:T(8,128)(2,1)S(1)}, bf16[2,8,1024,128]{3,2,1,0:T(8,128)(2,1)}, u32[]{:S(2)}) %copy-start.7) | copy-done | bytes 4194328
  34.4 13.4 %shard_map.94 = (bf16[8,8,1024]{2,1,0:T(8,128)(2,1)S(1)}, bf16[8,8,1024]{2,1,0:T(8,128)(2,1)S(1)}, bf16[8,8,1024]{2,1,0:T(8,128)(2,1)S(1)}, bf16[8,8,1024]{2,1,0:T(8,128)(2,1)S(1)}) custom-call(s32[2]{0:T(128)S(1)} %pad_add_fusion.me_ref, s32[16]{0:T(128)S(1)} %copy-done.11, bf16[80,1024]{1,0:T(8,128)(2,1)S(1)} %collective-permute-done.refs_0_, ...), custom_call_target="tpu_custom_call" | custom-call | flops 3388997632 | bytes 8388608 | tf_op jit(solution)/shard_map/pallas_call | solution.py:329
  47.8 1.6 %collective-permute-start.7 = (bf16[8,8,1024]{2,1,0:T(8,128)(2,1)S(1)}, bf16[8,8,1024]{2,1,0:T(8,128)(2,1)S(1)}, u32[]{:S(2)}, u32[]{:S(2)}) collective-permute-start(bf16[8,8,1024]{2,1,0:T(8,128)(2,1)S(1)} %get-tuple-element.24), channel_id=1, source_target_pairs={{0,8},{8,0},{16,24},{24,16},{1,9},{9,1},{17,25},{25,17},{2,10},{10... | collective-permute-start | bytes 393224 | tf_op jit(solution)/shard_map/ppermute | solution.py:375
  49.4 1.5 %collective-permute-start.8 = (bf16[8,8,1024]{2,1,0:T(8,128)(2,1)S(1)}, bf16[8,8,1024]{2,1,0:T(8,128)(2,1)S(1)}, u32[]{:S(2)}, u32[]{:S(2)}) collective-permute-start(bf16[8,8,1024]{2,1,0:T(8,128)(2,1)S(1)} %get-tuple-element.25), channel_id=1, source_target_pairs={{0,16},{8,24},{16,0},{24,8},{1,17},{9,25},{17,1},{25,9},{2,18},{10... | collective-permute-start | bytes 393224 | tf_op jit(solution)/shard_map/ppermute | solution.py:375
  50.9 0.5 collective-permute-start.9
  51.4 2.5 %collective-permute-done.7.refs_1_ = bf16[8,8,1024]{2,1,0:T(8,128)(2,1)S(1)} collective-permute-done((bf16[8,8,1024]{2,1,0:T(8,128)(2,1)S(1)}, bf16[8,8,1024]{2,1,0:T(8,128)(2,1)S(1)}, u32[]{:S(2)}, u32[]{:S(2)}) %collective-permute-start.7) | collective-permute-done | bytes 131104 | tf_op jit(solution)/shard_map/ppermute | solution.py:375
  53.9 3.7 %collective-permute-done.8.refs_2_ = bf16[8,8,1024]{2,1,0:T(8,128)(2,1)S(1)} collective-permute-done((bf16[8,8,1024]{2,1,0:T(8,128)(2,1)S(1)}, bf16[8,8,1024]{2,1,0:T(8,128)(2,1)S(1)}, u32[]{:S(2)}, u32[]{:S(2)}) %collective-permute-start.8) | collective-permute-done | bytes 131104 | tf_op jit(solution)/shard_map/ppermute | solution.py:375
  57.5 0.0 collective-permute-done.9.refs_3_
  57.5 0.5 shard_map.95
  58.0 0.1 collective-permute-start.10
  58.1 1.2 %collective-permute-done.10 = bf16[32,1024]{1,0:T(8,128)(2,1)S(1)} collective-permute-done((bf16[32,1024]{1,0:T(8,128)(2,1)S(1)}, bf16[32,1024]{1,0:T(8,128)(2,1)S(1)}, u32[]{:S(2)}, u32[]{:S(2)}) %collective-permute-start.10) | collective-permute-done | bytes 65568 | tf_op jit(solution)/shard_map/ppermute | solution.py:375
  59.3 3.0 %collective-permute-start.13 = (bf16[16,1024]{1,0:T(8,128)(2,1)S(1)}, bf16[16,1024]{1,0:T(8,128)(2,1)S(1)}, u32[]{:S(2)}, u32[]{:S(2)}) collective-permute-start(bf16[16,1024]{1,0:T(8,128)(2,1)S(1)} %pad_maximum_fusion.3), channel_id=1, source_target_pairs={{0,6},{1,7},{2,4},{3,5},{4,2},{5,3},{6,0},{7,1},{8,14},{9,15},{10,... | collective-permute-start | bytes 98312 | tf_op jit(solution)/shard_map/ppermute | solution.py:375
  62.3 0.5 collective-permute-start.11
  62.8 1.0 %collective-permute-start.12 = (bf16[16,1024]{1,0:T(8,128)(2,1)S(1)}, bf16[16,1024]{1,0:T(8,128)(2,1)S(1)}, u32[]{:S(2)}, u32[]{:S(2)}) collective-permute-start(bf16[16,1024]{1,0:T(8,128)(2,1)S(1)} %pad_maximum_fusion.2), channel_id=1, source_target_pairs={{0,4},{1,5},{2,6},{3,7},{4,0},{5,1},{6,2},{7,3},{8,12},{9,13},{10,... | collective-permute-start | bytes 98312 | tf_op jit(solution)/shard_map/ppermute | solution.py:375
  63.8 2.8 %collective-permute-done.11 = bf16[16,1024]{1,0:T(8,128)(2,1)S(1)} collective-permute-done((bf16[16,1024]{1,0:T(8,128)(2,1)S(1)}, bf16[16,1024]{1,0:T(8,128)(2,1)S(1)}, u32[]{:S(2)}, u32[]{:S(2)}) %collective-permute-start.11) | collective-permute-done | bytes 32800 | tf_op jit(solution)/shard_map/ppermute | solution.py:375
  66.6 1.0 %collective-permute-done.12 = bf16[16,1024]{1,0:T(8,128)(2,1)S(1)} collective-permute-done((bf16[16,1024]{1,0:T(8,128)(2,1)S(1)}, bf16[16,1024]{1,0:T(8,128)(2,1)S(1)}, u32[]{:S(2)}, u32[]{:S(2)}) %collective-permute-start.12) | collective-permute-done | bytes 32800 | tf_op jit(solution)/shard_map/ppermute | solution.py:375
  67.6 0.0 collective-permute-done.13
  67.6 2.2 %convolution_convert_fusion = bf16[1024,1024]{1,0:T(8,128)(2,1)} fusion(bf16[64,1024]{1,0:T(8,128)(2,1)S(1)} %constant_dynamic-update-slice_fusion, bf16[64,1024]{1,0:T(8,128)(2,1)S(1)} %copy-done, s32[64]{0:T(128)S(1)} %fusion.2), kind=kOutput, calls=%fused_computation | convolution fusion | flops 143724544 | bytes 2359552 | tf_op jit(solution)/shard_map/dot_general | solution.py:424
  (22 shorter events, 0.1 us)
Async XLA Ops:
  0.0 67.6 %copy-start = (bf16[64,1024]{1,0:T(8,128)(2,1)S(1)}, bf16[64,1024]{1,0:T(8,128)(2,1)}, u32[]{:S(2)}) copy-start(bf16[64,1024]{1,0:T(8,128)(2,1)} %param.12) | copy-start | bytes 393220
  1.1 17.6 %copy-start.9 = (bf16[96,160]{1,0:T(8,128)(2,1)S(1)}, bf16[96,160]{1,0:T(8,128)(2,1)}, u32[]{:S(2)}) copy-start(bf16[96,160]{1,0:T(8,128)(2,1)} %constant.52.clone.refs_4_.refs_8_) | copy-start | bytes 92164
  1.1 17.6 %copy-start.11 = (s32[16]{0:T(128)S(1)}, s32[16]{0:T(128)}, u32[]{:S(2)}) copy-start(s32[16]{0:T(128)} %slot_ref.3) | copy-start | bytes 196
  1.1 17.6 %collective-permute-start.4 = (bf16[80,1024]{1,0:T(8,128)(2,1)S(1)}, bf16[80,1024]{1,0:T(8,128)(2,1)S(1)}, u32[]{:S(2)}, u32[]{:S(2)}) collective-permute-start(bf16[80,1024]{1,0:T(8,128)(2,1)S(1)} %shard_map.91.refs_0_), channel_id=1, source_target_pairs={{0,1},{1,0},{2,3},{3,2},{4,5},{5,4},{6,7},{7,6},{8,9},{9,8},{10,11... | collective-permute-start | bytes 491528 | tf_op jit(solution)/shard_map/ppermute | solution.py:375
  1.6 28.6 %collective-permute-start.2 = (bf16[80,1024]{1,0:T(8,128)(2,1)S(1)}, bf16[80,1024]{1,0:T(8,128)(2,1)S(1)}, u32[]{:S(2)}, u32[]{:S(2)}) collective-permute-start(bf16[80,1024]{1,0:T(8,128)(2,1)S(1)} %shard_map.91.refs_0_), channel_id=1, source_target_pairs={{0,4},{1,5},{2,6},{3,7},{4,0},{5,1},{6,2},{7,3},{8,12},{9,13},{10,... | collective-permute-start | bytes 491528 | tf_op jit(solution)/shard_map/ppermute | solution.py:375
  5.3 24.9 %collective-permute-start.3 = (bf16[80,1024]{1,0:T(8,128)(2,1)S(1)}, bf16[80,1024]{1,0:T(8,128)(2,1)S(1)}, u32[]{:S(2)}, u32[]{:S(2)}) collective-permute-start(bf16[80,1024]{1,0:T(8,128)(2,1)S(1)} %shard_map.91.refs_0_), channel_id=1, source_target_pairs={{0,6},{1,7},{2,4},{3,5},{4,2},{5,3},{6,0},{7,1},{8,14},{9,15},{10,... | collective-permute-start | bytes 491528 | tf_op jit(solution)/shard_map/ppermute | solution.py:375
  6.6 24.2 %collective-permute-start = (bf16[80,1024]{1,0:T(8,128)(2,1)S(1)}, bf16[80,1024]{1,0:T(8,128)(2,1)S(1)}, u32[]{:S(2)}, u32[]{:S(2)}) collective-permute-start(bf16[80,1024]{1,0:T(8,128)(2,1)S(1)} %shard_map.91.refs_0_), channel_id=1, source_target_pairs={{0,2},{1,3},{2,0},{3,1},{4,6},{5,7},{6,4},{7,5},{8,10},{9,11},{10,... | collective-permute-start | bytes 491528 | tf_op jit(solution)/shard_map/ppermute | solution.py:375
  6.9 2.2 %copy-start.6 = (bf16[16,8,8,2,1024]{4,3,2,1,0:T(2,128)(2,1)S(1)}, bf16[16,8,8,2,1024]{4,3,2,1,0:T(2,128)(2,1)}, u32[]{:S(2)}) copy-start(bf16[16,8,8,2,1024]{4,3,2,1,0:T(2,128)(2,1)} %room_ref.1) | copy-start | bytes 12582916
  9.1 0.9 %copy-start.8 = (bf16[384,256]{1,0:T(8,128)(2,1)S(1)}, bf16[384,256]{1,0:T(8,128)(2,1)}, u32[]{:S(2)}) copy-start(bf16[384,256]{1,0:T(8,128)(2,1)} %constant.50.clone.table_ref) | copy-start | bytes 589828
  14.1 4.5 %copy-start.1 = (bf16[16,8,384,128]{3,2,1,0:T(8,128)(2,1)}, bf16[16,8,384,128]{3,2,1,0:T(8,128)(2,1)S(1)}, u32[]{:S(2)}) copy-start(bf16[16,8,384,128]{3,2,1,0:T(8,128)(2,1)S(1)} %shard_map.92.refs_2_.refs_6_) | copy-start | bytes 37748740
  18.7 4.6 %copy-start.2 = (bf16[16,8,384,128]{3,2,1,0:T(8,128)(2,1)S(1)}, bf16[16,8,384,128]{3,2,1,0:T(8,128)(2,1)}, u32[]{:S(2)}) copy-start(bf16[16,8,384,128]{3,2,1,0:T(8,128)(2,1)} %copy-done.1) | copy-start | bytes 37748740
  23.3 2.2 %copy-start.4 = (bf16[2,8,1024,128]{3,2,1,0:T(8,128)(2,1)S(1)}, bf16[2,8,1024,128]{3,2,1,0:T(8,128)(2,1)}, u32[]{:S(2)}) copy-start(bf16[2,8,1024,128]{3,2,1,0:T(8,128)(2,1)} %constant.51.clone.refs_3_.refs_7_) | copy-start | bytes 12582916
  25.5 6.7 %copy-start.3 = (bf16[16,8,384,128]{3,2,1,0:T(8,128)(2,1)S(1)}, bf16[16,8,384,128]{3,2,1,0:T(8,128)(2,1)}, u32[]{:S(2)}) copy-start(bf16[16,8,384,128]{3,2,1,0:T(8,128)(2,1)} %copy-done.1) | copy-start | bytes 37748740
  25.5 6.7 %copy-start.5 = (bf16[2,8,1024,128]{3,2,1,0:T(8,128)(2,1)S(1)}, bf16[2,8,1024,128]{3,2,1,0:T(8,128)(2,1)}, u32[]{:S(2)}) copy-start(bf16[2,8,1024,128]{3,2,1,0:T(8,128)(2,1)} %constant.51.clone.refs_3_.refs_7_) | copy-start | bytes 12582916
  25.5 6.7 %copy-start.10 = (bf16[2,128,192]{2,1,0:T(8,128)(2,1)S(1)}, bf16[2,128,192]{2,1,0:T(8,128)(2,1)}, u32[]{:S(2)}) copy-start(bf16[2,128,192]{2,1,0:T(8,128)(2,1)} %constant.53.clone.refs_10_) | copy-start | bytes 294916
  30.2 1.5 %collective-permute-start.5 = (bf16[80,1024]{1,0:T(8,128)(2,1)S(1)}, bf16[80,1024]{1,0:T(8,128)(2,1)S(1)}, u32[]{:S(2)}, u32[]{:S(2)}) collective-permute-start(bf16[80,1024]{1,0:T(8,128)(2,1)S(1)} %collective-permute-done.2.refs_2_), channel_id=1, source_target_pairs={{0,1},{1,0},{2,3},{3,2},{4,5},{5,4},{6,7},{7,6},{8,9},{9,8},{10,11... | collective-permute-start | bytes 491528 | tf_op jit(solution)/shard_map/ppermute | solution.py:375
  30.3 1.6 %collective-permute-start.6 = (bf16[80,1024]{1,0:T(8,128)(2,1)S(1)}, bf16[80,1024]{1,0:T(8,128)(2,1)S(1)}, u32[]{:S(2)}, u32[]{:S(2)}) collective-permute-start(bf16[80,1024]{1,0:T(8,128)(2,1)S(1)} %collective-permute-done.3.refs_4_), channel_id=1, source_target_pairs={{0,1},{1,0},{2,3},{3,2},{4,5},{5,4},{6,7},{7,6},{8,9},{9,8},{10,11... | collective-permute-start | bytes 491528 | tf_op jit(solution)/shard_map/ppermute | solution.py:375
  30.8 1.4 %collective-permute-start.1 = (bf16[80,1024]{1,0:T(8,128)(2,1)S(1)}, bf16[80,1024]{1,0:T(8,128)(2,1)S(1)}, u32[]{:S(2)}, u32[]{:S(2)}) collective-permute-start(bf16[80,1024]{1,0:T(8,128)(2,1)S(1)} %collective-permute-done.refs_0_), channel_id=1, source_target_pairs={{0,1},{1,0},{2,3},{3,2},{4,5},{5,4},{6,7},{7,6},{8,9},{9,8},{10,11... | collective-permute-start | bytes 491528 | tf_op jit(solution)/shard_map/ppermute | solution.py:375
  32.2 2.2 %copy-start.7 = (bf16[2,8,1024,128]{3,2,1,0:T(8,128)(2,1)S(1)}, bf16[2,8,1024,128]{3,2,1,0:T(8,128)(2,1)}, u32[]{:S(2)}) copy-start(bf16[2,8,1024,128]{3,2,1,0:T(8,128)(2,1)} %constant.54.clone.refs_11_) | copy-start | bytes 12582916
  47.8 6.0 %collective-permute-start.7 = (bf16[8,8,1024]{2,1,0:T(8,128)(2,1)S(1)}, bf16[8,8,1024]{2,1,0:T(8,128)(2,1)S(1)}, u32[]{:S(2)}, u32[]{:S(2)}) collective-permute-start(bf16[8,8,1024]{2,1,0:T(8,128)(2,1)S(1)} %get-tuple-element.24), channel_id=1, source_target_pairs={{0,8},{8,0},{16,24},{24,16},{1,9},{9,1},{17,25},{25,17},{2,10},{10... | collective-permute-start | bytes 393224 | tf_op jit(solution)/shard_map/ppermute | solution.py:375
  49.4 8.2 %collective-permute-start.8 = (bf16[8,8,1024]{2,1,0:T(8,128)(2,1)S(1)}, bf16[8,8,1024]{2,1,0:T(8,128)(2,1)S(1)}, u32[]{:S(2)}, u32[]{:S(2)}) collective-permute-start(bf16[8,8,1024]{2,1,0:T(8,128)(2,1)S(1)} %get-tuple-element.25), channel_id=1, source_target_pairs={{0,16},{8,24},{16,0},{24,8},{1,17},{9,25},{17,1},{25,9},{2,18},{10... | collective-permute-start | bytes 393224 | tf_op jit(solution)/shard_map/ppermute | solution.py:375
  50.9 6.6 %collective-permute-start.9 = (bf16[8,8,1024]{2,1,0:T(8,128)(2,1)S(1)}, bf16[8,8,1024]{2,1,0:T(8,128)(2,1)S(1)}, u32[]{:S(2)}, u32[]{:S(2)}) collective-permute-start(bf16[8,8,1024]{2,1,0:T(8,128)(2,1)S(1)} %get-tuple-element.26), channel_id=1, source_target_pairs={{0,24},{8,16},{16,8},{24,0},{1,25},{9,17},{17,9},{25,1},{2,26},{10... | collective-permute-start | bytes 393224 | tf_op jit(solution)/shard_map/ppermute | solution.py:375
  58.0 1.3 %collective-permute-start.10 = (bf16[32,1024]{1,0:T(8,128)(2,1)S(1)}, bf16[32,1024]{1,0:T(8,128)(2,1)S(1)}, u32[]{:S(2)}, u32[]{:S(2)}) collective-permute-start(bf16[32,1024]{1,0:T(8,128)(2,1)S(1)} %pad_maximum_fusion), channel_id=1, source_target_pairs={{0,1},{1,0},{2,3},{3,2},{4,5},{5,4},{6,7},{7,6},{8,9},{9,8},{10,11... | collective-permute-start | bytes 196616 | tf_op jit(solution)/shard_map/ppermute | solution.py:375
  59.3 8.3 %collective-permute-start.13 = (bf16[16,1024]{1,0:T(8,128)(2,1)S(1)}, bf16[16,1024]{1,0:T(8,128)(2,1)S(1)}, u32[]{:S(2)}, u32[]{:S(2)}) collective-permute-start(bf16[16,1024]{1,0:T(8,128)(2,1)S(1)} %pad_maximum_fusion.3), channel_id=1, source_target_pairs={{0,6},{1,7},{2,4},{3,5},{4,2},{5,3},{6,0},{7,1},{8,14},{9,15},{10,... | collective-permute-start | bytes 98312 | tf_op jit(solution)/shard_map/ppermute | solution.py:375
  62.3 4.3 %collective-permute-start.11 = (bf16[16,1024]{1,0:T(8,128)(2,1)S(1)}, bf16[16,1024]{1,0:T(8,128)(2,1)S(1)}, u32[]{:S(2)}, u32[]{:S(2)}) collective-permute-start(bf16[16,1024]{1,0:T(8,128)(2,1)S(1)} %pad_maximum_fusion.1), channel_id=1, source_target_pairs={{0,2},{1,3},{2,0},{3,1},{4,6},{5,7},{6,4},{7,5},{8,10},{9,11},{10,... | collective-permute-start | bytes 98312 | tf_op jit(solution)/shard_map/ppermute | solution.py:375
  62.8 4.8 %collective-permute-start.12 = (bf16[16,1024]{1,0:T(8,128)(2,1)S(1)}, bf16[16,1024]{1,0:T(8,128)(2,1)S(1)}, u32[]{:S(2)}, u32[]{:S(2)}) collective-permute-start(bf16[16,1024]{1,0:T(8,128)(2,1)S(1)} %pad_maximum_fusion.2), channel_id=1, source_target_pairs={{0,4},{1,5},{2,6},{3,7},{4,0},{5,1},{6,2},{7,3},{8,12},{9,13},{10,... | collective-permute-start | bytes 98312 | tf_op jit(solution)/shard_map/ppermute | solution.py:375

commit v6 on v5

--- a/solution.py
+++ b/solution.py
@@ -65,7 +65,7 @@
         for seg in range(SEGS):
             spec[kind, seg, :, :, :, seg * KEEP : seg * KEEP + used] = table
     spec = spec.reshape(2, SEGS * 2 * STEPS, 2 * frames)
-    spec = np.concatenate([spec[0], spec[1]], axis=1)
+    spec = np.stack([np.kron(np.eye(2), one) for one in spec])
 
     resp = np.zeros((channels // 2, 2, 2, STEPS, 2, parts, channels, 2))
     for kind, table in enumerate(forward(np.arange(parts))):
@@ -109,13 +109,24 @@
     return jnp.concatenate([ref[(*index, first + i)] for i in range(LANES // SLAB)], axis=-1)
 
 
-def response_kernel(rows, bins, room_ref, table_ref, hat_ref):
+def response_kernel(rows, bins, room_hbm, table_hbm, hat_ref, done_ref, room_ref, table_ref, sems):
     depth = room_ref.shape[1] * room_ref.shape[2] * 2
     flat = room_ref.reshape(rows, depth, bins)
     plain, packed, _ = lane_masks(0, LANES)
     plain, packed = plain.astype(BF16), packed.astype(BF16)
 
+    def copy(r):
+        return pltpu.make_async_copy(room_hbm.at[r], room_ref.at[r], sems.at[r])
+
+    table_copy = pltpu.make_async_copy(table_hbm, table_ref, sems.at[rows])
+    table_copy.start()
+    for r in range(rows):
+        copy(r).start()
+    table_copy.wait()
+
     def some(outer, carry):
+        for inner in range(ROWS):
+            copy(outer * ROWS + inner).wait()
         for inner in range(ROWS):
             r = outer * ROWS + inner
             for step in range(bins // LANES):
@@ -131,105 +142,132 @@
         return carry
 
     lax.fori_loop(0, rows // ROWS, some, 0)
+    done_ref[...] = jnp.zeros_like(done_ref)
 
 
 def transform_responses(room):
     rows, parts, channels, _, bins = room.shape
     slabs = bins // SLAB
     _, resp, _ = step_tables(parts, parts + SEGS * KEEP, channels)
-    vmem = pl.BlockSpec(memory_space=pltpu.VMEM)
     flops = 2 * rows * channels * 2 * STEPS * parts * channels * 2 * bins
+    hbm = pl.BlockSpec(memory_space=pltpu.HBM)
     return pl.pallas_call(
         functools.partial(response_kernel, rows, bins),
-        in_specs=[vmem, vmem],
-        out_specs=vmem,
-        out_shape=jax.ShapeDtypeStruct((rows, slabs, channels * 2 * STEPS, SLAB), BF16),
+        in_specs=[hbm, hbm],
+        out_specs=[pl.BlockSpec(memory_space=pltpu.VMEM)] * 2,
+        out_shape=[
+            pltpu.VMEM((rows, slabs, channels * 2 * STEPS, SLAB), BF16),
+            jax.ShapeDtypeStruct((8, 128), F32),
+        ],
+        scratch_shapes=[
+            pltpu.VMEM(room.shape, BF16),
+            pltpu.VMEM(resp.shape, BF16),
+            pltpu.SemaphoreType.DMA((rows + 1,)),
+        ],
         compiler_params=pltpu.CompilerParams(vmem_limit_bytes=8 * 2**20),
         cost_estimate=pl.CostEstimate(flops=flops, bytes_accessed=16 * 2**20, transcendentals=0),
-    )(room, jnp.asarray(resp))
-
-
-def copy_kernel(x_ref, out_ref):
-    out_ref[...] = x_ref[...]
-
-
-def copy_early(x):
+    )(
+        pltpu.with_memory_space_constraint(room, pltpu.HBM),
+        pltpu.with_memory_space_constraint(jnp.asarray(resp), pltpu.HBM),
+    )
+
+
+def spectra_kernel(pieces, rows, *refs):
+    x_refs, (table_ref, spec_ref) = refs[:pieces], refs[pieces : pieces + 2]
+    out_ref = refs[-1]
+    slabs = table_ref.shape[1]
+    wide = 2 * SEGS * STEPS
+    x = jnp.concatenate([ref[...] for ref in x_refs], axis=0)
+    count = x.shape[0] // rows
+    cols = 2 * count
+    for step in range(slabs * SLAB // LANES):
+        plain, packed, sign = lane_masks(step * LANES, LANES)
+        spectra = []
+        for j in range(2):
+            one = dot(x, two_slabs(table_ref, step, j))
+            spectra.append(one + sign * pltpu.roll(one, one.shape[0] - 1, axis=0))
+        for start in range(0, rows, 2):
+            some = range(start, min(start + 2, rows))
+            n = len(some)
+            both = [s[r * count : (r + 1) * count] for r in some for s in spectra]
+            both = jnp.concatenate(both, axis=0)
+            spec = [spec_ref[kind, : n * wide, : n * cols] for kind in range(2)]
+            if step == 0:
+                hat = dot(spec[0], (both * plain).astype(BF16)) + dot(spec[1], (both * packed).astype(BF16))
+            else:
+                hat = dot(spec[0], both.astype(BF16))
+            hat = hat.astype(BF16)
+            for k, r in enumerate(some):
+                for i in range(LANES // SLAB):
+                    at = slice(i * SLAB, (i + 1) * SLAB)
+                    out_ref[step * (LANES // SLAB) + i, r] = hat[k * wide : (k + 1) * wide, at]
+
+
+def transform_signals(x_list, own, bins, parts, after=None):
+    frames = parts + SEGS * KEEP
+    rows = own * len(x_list)
+    slabs = bins // SLAB
+    table, _ = block_tables(bins)
+    spec, _, _ = step_tables(parts, frames, 2)
     vmem = pl.BlockSpec(memory_space=pltpu.VMEM)
+    flops = 2 * bins * rows * (frames * 2 * bins + 4 * SEGS * STEPS * frames)
+    operands = [*x_list, jnp.asarray(table), jnp.asarray(spec)]
+    if after is not None:
+        operands.append(after)
     return pl.pallas_call(
-        copy_kernel,
-        in_specs=[vmem],
+        functools.partial(spectra_kernel, len(x_list), rows),
+        in_specs=[vmem] * len(operands),
         out_specs=vmem,
-        out_shape=jax.ShapeDtypeStruct(x.shape, x.dtype),
-        compiler_params=pltpu.CompilerParams(vmem_limit_bytes=2 * 2**20),
-        cost_estimate=pl.CostEstimate(flops=0, bytes_accessed=24 * 2**20, transcendentals=0),
-    )(x)
+        out_shape=jax.ShapeDtypeStruct((slabs, rows, 2 * SEGS * STEPS, SLAB), BF16),
+        compiler_params=pltpu.CompilerParams(vmem_limit_bytes=8 * 2**20),
+        cost_estimate=pl.CostEstimate(flops=flops, bytes_accessed=4 * 2**20, transcendentals=0),
+    )(*operands)
 
 
 def mix_kernel(flips, own, channels, blocks, shares, has_total, last, me_ref, slot_ref, *refs):
     refs = list(refs)
-    x_refs = [refs.pop(0) for _ in flips]
-    hat_ref, table_ref, spec_ref = [refs.pop(0) for _ in range(3)]
+    s_refs = [refs.pop(0) for _ in flips]
+    hat_ref = refs.pop(0)
     total_ref = refs.pop(0) if has_total else None
     if last:
         back_ref, inv_ref = refs.pop(0), refs.pop(0)
         out_refs = [refs.pop(0) for _ in range(shares)]
+        y_ref, left_re, left_im, time_ref = refs
     else:
-        out_ref = refs.pop(0)
-    s_ref = refs.pop(0)
-    if last:
-        y_ref, left_re, left_im, time_ref = refs
+        (out_ref,) = refs
 
     slabs = hat_ref.shape[1]
-    bins = slabs * SLAB
-    steps = bins // LANES
-    rows = own * len(flips)
+    steps = slabs * SLAB // LANES
     half = 2 * STEPS
-    x = jnp.concatenate([ref[...] for ref in x_refs], axis=0)
-    count = x.shape[0] // rows
-    cols = 2 * count
-    slots = [
-        lax.rem(slot_ref[(me_ref[1] ^ flip) * own + i], hat_ref.shape[0])
-        for flip in flips
-        for i in range(own)
-    ]
-
-    def frame_spectra(step):
-        _, _, sign = lane_masks(step * LANES, LANES)
-        spectra = []
-        for j in range(2):
-            one = dot(x, two_slabs(table_ref, step, j))
-            spectra.append(one + sign * pltpu.roll(one, one.shape[0] - 1, axis=0))
-        return spectra
-
-    def step_spectra(step, r, spectra):
-        both = jnp.concatenate([s[r * count : (r + 1) * count] for s in spectra], axis=0)
-        if step == 0:
-            plain, packed, _ = lane_masks(0, LANES)
-            both = jnp.concatenate([both * plain, both * packed], axis=0).astype(BF16)
-            hat = dot(spec_ref[...], both)
-        else:
-            hat = dot(spec_ref[:, :cols], both.astype(BF16))
-        for i in range(LANES // SLAB):
-            part = hat[:, i * SLAB : (i + 1) * SLAB]
-            for k in range(2 * SEGS):
-                one = part[k * STEPS : (k + 1) * STEPS]
-                both = jnp.concatenate([one, one], axis=0).astype(BF16)
-                s_ref[step * (LANES // SLAB) + i, r, k * half : (k + 1) * half] = both
-
-    def product_slab(slab, pair):
-        far = slice(slab * SLAB, (slab + 1) * SLAB)
-        base = pair * 2 * half
-        for seg in range(SEGS):
-            re_rows = slice(2 * seg * half, (2 * seg + 1) * half)
-            im_rows = slice((2 * seg + 1) * half, (2 * seg + 2) * half)
-            re_sum = total_ref[pair, re_rows, far] if has_total else None
-            im_sum = total_ref[pair, im_rows, far] if has_total else None
-            for start in range(0, rows, GROUP):
+    pairs = channels // 2
+    sources = []
+    for ref, some in zip(s_refs, flips):
+        for k, flip in enumerate(some):
+            for i in range(own):
+                slot = lax.rem(slot_ref[(me_ref[1] ^ flip) * own + i], hat_ref.shape[0])
+                sources.append((ref, k * own + i, slot))
+    groups = -(-len(sources) // GROUP)
+    size = -(-len(sources) // groups)
+
+    def twice(rows):
+        rows = rows.astype(F32)
+        return jnp.concatenate([rows, rows], axis=0).astype(BF16)
+
+    def products(slab, seg):
+        re_in = slice(2 * seg * STEPS, (2 * seg + 1) * STEPS)
+        im_in = slice((2 * seg + 1) * STEPS, (2 * seg + 2) * STEPS)
+        re_rows = slice(2 * seg * half, (2 * seg + 1) * half)
+        im_rows = slice((2 * seg + 1) * half, (2 * seg + 2) * half)
+        spectra = [(twice(ref[slab, r, re_in]), twice(ref[slab, r, im_in])) for ref, r, _ in sources]
+        for pair in range(pairs):
+            base = pair * 2 * half
+            re_sum = total_ref[slab, pair, re_rows] if has_total else None
+            im_sum = total_ref[slab, pair, im_rows] if has_total else None
+            for start in range(0, len(sources), size):
                 re, im = None, None
-                for r in range(start, min(start + GROUP, rows)):
-                    h_re = hat_ref[slots[r], slab, base : base + half]
-                    h_im = hat_ref[slots[r], slab, base + half : base + 2 * half]
-                    s_re, s_im = s_ref[slab, r, re_rows], s_ref[slab, r, im_rows]
+                for (s_re, s_im), (_, _, slot) in list(zip(spectra, sources))[start : start + size]:
+                    h_re = hat_ref[slot, slab, base : base + half]
+                    h_im = hat_ref[slot, slab, base + half : base + 2 * half]
                     add_re = s_re * h_re - s_im * h_im
                     add_im = s_re * h_im + s_im * h_re
                     re = add_re if re is None else re + add_re
@@ -241,14 +279,17 @@
                 y_ref[slab, pair, re_rows] = re_sum.astype(BF16)
                 y_ref[slab, pair, im_rows] = im_sum.astype(BF16)
             else:
-                out_ref[pair, re_rows, far] = re_sum
-                out_ref[pair, im_rows, far] = im_sum
-
-    def product_pair(step, pair):
+                out_ref[slab, pair, re_rows] = re_sum
+                out_ref[slab, pair, im_rows] = im_sum
+
+    for step in range(steps):
         first = step * (LANES // SLAB)
         for i in range(LANES // SLAB):
-            product_slab(first + i, pair)
-        if last:
+            for seg in range(SEGS):
+                products(first + i, seg)
+        if not last:
+            continue
+        for pair in range(pairs):
             y = jnp.concatenate([y_ref[first + i, pair] for i in range(LANES // SLAB)], axis=-1)
             if step == 0:
                 plain, packed, _ = lane_masks(0, LANES)
@@ -262,19 +303,6 @@
                 left_re[rows_to, here] = mix[2 * c * blocks : (2 * c + 1) * blocks]
                 left_im[rows_to, here] = mix[(2 * c + 1) * blocks : (2 * c + 2) * blocks]
 
-    pairs = channels // 2
-    for step in range(steps + 1):
-        spectra = frame_spectra(step) if step < steps else None
-        done = 0
-        for pair in range(pairs):
-            if spectra is not None:
-                upto = rows * (pair + 1) // pairs
-                for r in range(done, upto):
-                    step_spectra(step, r, spectra)
-                done = upto
-            if step > 0:
-                product_pair(step - 1, pair)
-
     if last:
         each = blocks // shares
         for step in range(steps):
@@ -288,41 +316,38 @@
             out_refs[d][...] = time_ref[me_ref[0] ^ d].astype(BF16)
 
 
-def add_sources(x_list, flips, me, slots, hat, total, last, shares, channels, parts):
+def add_sources(s_list, flips, own, me, slots, hat, total, last, shares, channels, parts):
     slabs = hat.shape[1]
     bins = slabs * SLAB
     frames = parts + SEGS * KEEP
-    own = x_list[0].shape[0] // frames
-    rows = own * len(x_list)
     blocks = frames - parts
     wide = 2 * SEGS * STEPS
-    table, inverse = block_tables(bins)
-    spec, _, back = step_tables(parts, frames, channels)
+    _, inverse = block_tables(bins)
+    _, _, back = step_tables(parts, frames, channels)
     vmem = pl.BlockSpec(memory_space=pltpu.VMEM)
     smem = pl.BlockSpec(memory_space=pltpu.SMEM)
 
-    operands = [me, slots] + list(x_list) + [hat, jnp.asarray(table), jnp.asarray(spec)]
+    operands = [me, slots] + list(s_list) + [pltpu.with_memory_space_constraint(hat, pltpu.VMEM)]
     aliases = {}
     if total is not None:
         if not last:
             aliases = {len(operands): 0}
         operands.append(total)
-    scratch = [pltpu.VMEM((slabs, rows, 2 * wide, SLAB), BF16)]
+    scratch = []
     if last:
         operands += [jnp.asarray(back), jnp.asarray(inverse)]
         each = blocks // shares
         out_shape = [jax.ShapeDtypeStruct((channels, each, bins), BF16)] * shares
-        scratch += [
+        scratch = [
             pltpu.VMEM((slabs, channels // 2, 2 * wide, SLAB), BF16),
             pltpu.VMEM((channels * blocks, bins), BF16),
             pltpu.VMEM((channels * blocks, bins), BF16),
             pltpu.VMEM((shares, channels, each, bins), F32),
         ]
     else:
-        out_shape = jax.ShapeDtypeStruct((channels // 2, 2 * wide, bins), F32)
-    flops = 2 * bins * (
-        rows * frames * 2 * bins + channels * rows * wide * 16 + (channels * blocks * 2 * bins if last else 0)
-    )
+        out_shape = jax.ShapeDtypeStruct((slabs, channels // 2, 2 * wide, SLAB), F32)
+    count = own * sum(len(some) for some in flips)
+    flops = 2 * bins * channels * (count * wide * 8 + (blocks * 2 * bins if last else 0))
     body = functools.partial(
         mix_kernel, tuple(flips), own, channels, blocks, shares, total is not None, last
     )
@@ -333,7 +358,7 @@
         out_shape=out_shape,
         scratch_shapes=scratch,
         input_output_aliases=aliases,
-        compiler_params=pltpu.CompilerParams(vmem_limit_bytes=16 * 2**20),
+        compiler_params=pltpu.CompilerParams(vmem_limit_bytes=12 * 2**20),
         cost_estimate=pl.CostEstimate(flops=flops, bytes_accessed=8 * 2**20, transcendentals=0),
     )(*operands)
 
@@ -369,38 +394,35 @@
     src_me = lax.axis_index("src").astype(jnp.int32)
     ch_me = lax.axis_index("ch").astype(jnp.int32)
 
-    x_own = copy_early(dry_signal.reshape(own * frames, block_len))
+    x_own = dry_signal.reshape(own * frames, block_len)
 
     def swap(value, axis, count, flip):
         return lax.ppermute(value, axis, [(i, i ^ flip) for i in range(count)])
 
     chips = ch_count // 2
-    lanes = [x_own] + [swap(x_own, "ch", ch_count, 2 * d) for d in range(1, chips)]
-    mates = [swap(x_own, "ch", ch_count, 1)]
+    lanes = [swap(x_own, "ch", ch_count, 2 * d) for d in range(1, chips)]
 
     row = jnp.arange(ch_count * channels, dtype=jnp.int32)
     takes = ((row // channels) ^ ch_me) * channels + row % channels
     order = (takes[:, None] == row[None, :]).astype(BF16)
     own_order = dot(order, decoder).astype(BF16)
 
-    hat = transform_responses(room_spectra)
+    hat, done = transform_responses(room_spectra)
     me = jnp.stack([src_me, ch_me])
 
-    def add(x_list, flips, total, last):
+    def add(s_list, flips, total, last):
         return add_sources(
-            x_list, flips, me, render_slot, hat, total, last, src_count, channels, parts
+            s_list, flips, own, me, render_slot, hat, total, last, src_count, channels, parts
         )
 
-    total = add([lanes[0], mates[0]], [0, 1], None, False)
-    mates.append(swap(lanes[1], "ch", ch_count, 1))
-    *late, total = lax.optimization_barrier((*lanes[2:], total))
-    lanes[2:] = late
-    mates += [swap(x, "ch", ch_count, 1) for x in late]
-    x_list, flips = [], []
-    for d in range(1, chips):
-        x_list += [lanes[d], mates[d]]
-        flips += [2 * d, 2 * d + 1]
-    total = add(x_list, flips, total, True)
+    early = transform_signals([x_own], own, block_len, parts, done)
+    early_mate = swap(early, "ch", ch_count, 1)
+    total = add([early, early_mate], [[0], [1]], None, False)
+    *lanes, total = lax.optimization_barrier((*lanes, total))
+    late = transform_signals(lanes, own, block_len, parts)
+    late_mate = swap(late, "ch", ch_count, 1)
+    total = add([late], [[2 * d for d in range(1, chips)]], total, False)
+    total = add([late_mate], [[2 * d + 1 for d in range(1, chips)]], total, True)
 
     parts_in = [total[0]] + [swap(total[d], "src", src_count, d) for d in range(1, src_count)]
     each = blocks // src_count

time: 70.1 us -> 66.5 us (0.949)
  waiting for transfers between devices: 12.5 us -> 18.7 us
  local copies, waits for them, and re-layouts: 17.7 us -> 12.4 us
  Pallas kernels: 22.7 us -> 18.3 us
    pallas_call x2 -> x3, Pallas kernels: 18.1 us -> 8.55 us  [add_sources(): pl.pallas_call(body, in_specs=[smem, smem] + [vmem] * (len(operands) - 2)...]
    ppermute x14 -> x12, waiting for transfers between devices: 12.5 us -> 18.7 us  [swap(): return lax.ppermute(value, axis, [(i, i ^ flip) for i in range(count)])]
    unnamed x27 -> x23, local copies, waits for them, and re-layouts: 16.6 us -> 11.3 us
    pallas_call x1 -> x2, Pallas kernels: 0.01 us -> 3.57 us  [transform_signals(): pl.pallas_call(functools.partial(spectra_kernel, len(x_list), rows), in_s...]
    pallas_call x1, Pallas kernels: 4.1 us -> 5.72 us  [transform_responses(): pl.pallas_call(functools.partial(response_kernel, rows, bins), in_specs=[...]
    ppermute x14 -> x12, starting transfers between devices: 14.5 us -> 14.4 us  [swap(): return lax.ppermute(value, axis, [(i, i ^ flip) for i in range(count)])]
  transfers between devices with their start and end apart: 14 -> 12, of which waited for: 8 -> 7; matrix products, arithmetic and copies ran while one was open for 0% -> 0% of each run, Pallas kernels for 13% -> 6%
where the time goes in v6:
time: 66.5 us; the launch traced here: 66.3 us
  waiting for transfers between devices  18.7 us (28%)
  Pallas kernels  18.3 us (28%)
  starting transfers between devices  14.4 us (22%)
  local copies, waits for them, and re-layouts  12.4 us (19%)
  matrix products  2.2 us (3%)
    ppermute x12, waiting for transfers between devices, swap(): return lax.ppermute(value, axis, [(i, i ^ flip) for i in range(count)])  18.7 us
    ppermute x12, starting transfers between devices, swap(): return lax.ppermute(value, axis, [(i, i ^ flip) for i in range(count)])  14.4 us
    unnamed x23, local copies, waits for them, and re-layouts  11.3 us
    pallas_call x3, Pallas kernels, add_sources(): pl.pallas_call(body, in_specs=[smem, smem] + [vmem] * (len(operands) - 2)...  8.55 us
    pallas_call x1, Pallas kernels, transform_responses(): pl.pallas_call(functools.partial(response_kernel, rows, bins), in_specs=[...  5.72 us
    pallas_call x2, Pallas kernels, transform_signals(): pl.pallas_call(functools.partial(spectra_kernel, len(x_list), rows), in_s...  3.57 us
    dot_general x1, matrix products, per_device(): lax.dot_general(gathered, matrix, (((0,), (0,)), ((), ())), preferred_ele...  2.2 us
  transfers between devices with their start and end apart: 12, of which 7 were waited for; matrix products, arithmetic and copies ran while one was open for 0% of the time, Pallas kernels for 6%

profile of v6, /device:TPU:0, one launch (start us, length us, event | category | flops | bytes accessed | tf_op | source)
XLA Modules:
  0.0 66.3 jit_solution(16468057337646403360)
XLA Ops:
  0.0 0.0 copy-start
  0.0 1.1 %reshape.26.refs_0_ = bf16[80,1024]{1,0:T(8,128)(2,1)S(1)} reshape(bf16[2,40960]{1,0:T(2,128)(2,1)} %param.9) | data formatting | bytes 327680 | tf_op jit(solution)/shard_map/reshape | solution.py:397
  1.1 0.0 copy-start.4
  1.1 5.7 %shard_map.91 = (bf16[16,8,384,128]{3,2,1,0:T(8,128)(2,1)S(1)}, f32[8,128]{1,0:T(8,128)S(1)}) custom-call(bf16[16,8,8,2,1024]{4,3,2,1,0:T(2,128)(2,1)} %room_hbm.1, bf16[384,256]{1,0:T(8,128)(2,1)} %constant.50.clone.table_hbm), custom_call_target="tpu_custom_call" | custom-call | flops 1610612736 | bytes 16777216 | tf_op jit(solution)/shard_map/pallas_call | solution.py:154
  6.8 0.0 copy-start.1
  6.8 4.5 %copy-done.1 = bf16[16,8,384,128]{3,2,1,0:T(8,128)(2,1)} copy-done((bf16[16,8,384,128]{3,2,1,0:T(8,128)(2,1)}, bf16[16,8,384,128]{3,2,1,0:T(8,128)(2,1)S(1)}, u32[]{:S(2)}) %copy-start.1) | copy-done | bytes 12582936
  11.3 0.0 copy-done.7
  11.3 0.0 copy-done.4
  11.3 1.5 %shard_map.92.refs_0_ = bf16[8,2,96,128]{3,2,1,0:T(8,128)(2,1)S(1)} custom-call(bf16[80,1024]{1,0:T(8,128)(2,1)S(1)} %reshape.26.refs_0_, bf16[2,8,1024,128]{3,2,1,0:T(8,128)(2,1)S(1)} %copy-done.4, bf16[2,192,160]{2,1,0:T(8,128)(2,1)S(1)} %copy-done.7, f32[8,128]{1,0:T(8,128)S(1)} %get-tuple-element.23.refs_3_), custom_call_target="tpu_custom_call" | custom-call | flops 367001600 | bytes 4194304 | tf_op jit(solution)/shard_map/pallas_call | solution.py:217
  12.9 0.5 collective-permute-start.3
  13.4 2.7 %collective-permute-start = (bf16[80,1024]{1,0:T(8,128)(2,1)S(1)}, bf16[80,1024]{1,0:T(8,128)(2,1)S(1)}, u32[]{:S(2)}, u32[]{:S(2)}) collective-permute-start(bf16[80,1024]{1,0:T(8,128)(2,1)S(1)} %reshape.26.refs_0_), channel_id=1, source_target_pairs={{0,2},{1,3},{2,0},{3,1},{4,6},{5,7},{6,4},{7,5},{8,10},{9,11},{10,... | collective-permute-start | bytes 491528 | tf_op jit(solution)/shard_map/ppermute | solution.py:400
  16.0 2.6 %collective-permute-start.1 = (bf16[80,1024]{1,0:T(8,128)(2,1)S(1)}, bf16[80,1024]{1,0:T(8,128)(2,1)S(1)}, u32[]{:S(2)}, u32[]{:S(2)}) collective-permute-start(bf16[80,1024]{1,0:T(8,128)(2,1)S(1)} %reshape.26.refs_0_), channel_id=1, source_target_pairs={{0,4},{1,5},{2,6},{3,7},{4,0},{5,1},{6,2},{7,3},{8,12},{9,13},{10,... | collective-permute-start | bytes 491528 | tf_op jit(solution)/shard_map/ppermute | solution.py:400
  18.6 0.0 collective-permute-start.2
  18.6 0.1 pad_add_fusion.me_ref
  18.7 0.0 collective-permute-done.3.refs_1_
  18.7 0.0 copy-done.9
  18.7 4.6 %copy-done.2 = bf16[16,8,384,128]{3,2,1,0:T(8,128)(2,1)S(1)} copy-done((bf16[16,8,384,128]{3,2,1,0:T(8,128)(2,1)S(1)}, bf16[16,8,384,128]{3,2,1,0:T(8,128)(2,1)}, u32[]{:S(2)}) %copy-start.2) | copy-done | bytes 12582936
  23.3 1.5 %shard_map.93.refs_2_ = f32[8,4,192,128]{3,2,1,0:T(8,128)S(1)} custom-call(s32[2]{0:T(128)S(1)} %pad_add_fusion.me_ref, s32[16]{0:T(128)S(1)} %copy-done.9, bf16[8,2,96,128]{3,2,1,0:T(8,128)(2,1)S(1)} %shard_map.92.refs_0_, bf16[8,2,96,128]{3,2,1,0:T(8,128)(2,1)S(1)} %collective-permute-done.3.refs_1_, bf16[16,8,384,128]{3,2,1,0:T(8,128)(2,1)S(1)} %copy-done.2), custom_call_target="tpu_custom_call" | custom-call | flops 50331648 | bytes 8388608 | tf_op jit(solution)/shard_map/pallas_call | solution.py:354
  24.8 0.0 collective-permute-done.refs_0_
  24.8 6.2 %collective-permute-done.1.refs_1_ = bf16[80,1024]{1,0:T(8,128)(2,1)S(1)} collective-permute-done((bf16[80,1024]{1,0:T(8,128)(2,1)S(1)}, bf16[80,1024]{1,0:T(8,128)(2,1)S(1)}, u32[]{:S(2)}, u32[]{:S(2)}) %collective-permute-start.1) | collective-permute-done | bytes 163872 | tf_op jit(solution)/shard_map/ppermute | solution.py:400
  31.0 0.0 collective-permute-done.2.refs_2_
  31.0 2.2 %copy-done.5 = bf16[2,8,1024,128]{3,2,1,0:T(8,128)(2,1)S(1)} copy-done((bf16[2,8,1024,128]{3,2,1,0:T(8,128)(2,1)S(1)}, bf16[2,8,1024,128]{3,2,1,0:T(8,128)(2,1)}, u32[]{:S(2)}) %copy-start.5) | copy-done | bytes 4194328
  33.2 2.1 %shard_map.94.refs_0_ = bf16[8,6,96,128]{3,2,1,0:T(8,128)(2,1)S(1)} custom-call(bf16[80,1024]{1,0:T(8,128)(2,1)S(1)} %collective-permute-done.refs_0_, bf16[80,1024]{1,0:T(8,128)(2,1)S(1)} %collective-permute-done.1.refs_1_, bf16[80,1024]{1,0:T(8,128)(2,1)S(1)} %collective-permute-done.2.refs_2_, bf16[2,8,1024,128]{3,2,1,0:T(8,128)(2,1)S(1)} %copy-done.5, ...), custom_call_target="tpu_custom_call" | custom-call | flops 1101004800 | bytes 4194304 | tf_op jit(solution)/shard_map/pallas_call | solution.py:217
  35.3 0.0 copy-start.6
  35.3 0.0 copy-start.8
  35.3 0.1 collective-permute-start.4
  35.4 0.0 copy-done.3
  35.4 2.5 %shard_map.95.refs_2_ = f32[8,4,192,128]{3,2,1,0:T(8,128)S(1)} custom-call(s32[2]{0:T(128)S(1)} %pad_add_fusion.me_ref, s32[16]{0:T(128)S(1)} %copy-done.9, bf16[8,6,96,128]{3,2,1,0:T(8,128)(2,1)S(1)} %shard_map.94.refs_0_, bf16[16,8,384,128]{3,2,1,0:T(8,128)(2,1)S(1)} %copy-done.3, ...), custom_call_target="tpu_custom_call", output_to_operand_aliasing={{}: (4, {})} | custom-call | flops 75497472 | bytes 8388608 | tf_op jit(solution)/shard_map/pallas_call | solution.py:354
  37.9 0.3 collective-permute-done.4.refs_0_
  38.2 0.0 copy-done.6
  38.3 0.0 copy-done.8
  38.3 4.6 %shard_map.96 = (bf16[8,8,1024]{2,1,0:T(8,128)(2,1)S(1)}, bf16[8,8,1024]{2,1,0:T(8,128)(2,1)S(1)}, bf16[8,8,1024]{2,1,0:T(8,128)(2,1)S(1)}, bf16[8,8,1024]{2,1,0:T(8,128)(2,1)S(1)}) custom-call(s32[2]{0:T(128)S(1)} %pad_add_fusion.me_ref, s32[16]{0:T(128)S(1)} %copy-done.9, bf16[8,6,96,128]{3,2,1,0:T(8,128)(2,1)S(1)} %collective-permute-done.4.refs_0_, ...), custom_call_target="tpu_custom_call" | custom-call | flops 1149239296 | bytes 8388608 | tf_op jit(solution)/shard_map/pallas_call | solution.py:354
  42.8 1.6 %collective-permute-start.5 = (bf16[8,8,1024]{2,1,0:T(8,128)(2,1)S(1)}, bf16[8,8,1024]{2,1,0:T(8,128)(2,1)S(1)}, u32[]{:S(2)}, u32[]{:S(2)}) collective-permute-start(bf16[8,8,1024]{2,1,0:T(8,128)(2,1)S(1)} %get-tuple-element.30), channel_id=1, source_target_pairs={{0,8},{8,0},{16,24},{24,16},{1,9},{9,1},{17,25},{25,17},{2,10},{10... | collective-permute-start | bytes 393224 | tf_op jit(solution)/shard_map/ppermute | solution.py:400
  44.4 1.5 %collective-permute-start.6 = (bf16[8,8,1024]{2,1,0:T(8,128)(2,1)S(1)}, bf16[8,8,1024]{2,1,0:T(8,128)(2,1)S(1)}, u32[]{:S(2)}, u32[]{:S(2)}) collective-permute-start(bf16[8,8,1024]{2,1,0:T(8,128)(2,1)S(1)} %get-tuple-element.31), channel_id=1, source_target_pairs={{0,16},{8,24},{16,0},{24,8},{1,17},{9,25},{17,1},{25,9},{2,18},{10... | collective-permute-start | bytes 393224 | tf_op jit(solution)/shard_map/ppermute | solution.py:400
  45.9 0.5 collective-permute-start.7
  46.4 2.4 %collective-permute-done.5.refs_1_ = bf16[8,8,1024]{2,1,0:T(8,128)(2,1)S(1)} collective-permute-done((bf16[8,8,1024]{2,1,0:T(8,128)(2,1)S(1)}, bf16[8,8,1024]{2,1,0:T(8,128)(2,1)S(1)}, u32[]{:S(2)}, u32[]{:S(2)}) %collective-permute-start.5) | collective-permute-done | bytes 131104 | tf_op jit(solution)/shard_map/ppermute | solution.py:400
  48.8 3.7 %collective-permute-done.6.refs_2_ = bf16[8,8,1024]{2,1,0:T(8,128)(2,1)S(1)} collective-permute-done((bf16[8,8,1024]{2,1,0:T(8,128)(2,1)S(1)}, bf16[8,8,1024]{2,1,0:T(8,128)(2,1)S(1)}, u32[]{:S(2)}, u32[]{:S(2)}) %collective-permute-start.6) | collective-permute-done | bytes 131104 | tf_op jit(solution)/shard_map/ppermute | solution.py:400
  52.5 0.0 collective-permute-done.7.refs_3_
  52.5 0.5 shard_map.97
  53.0 0.1 collective-permute-start.8
  53.0 1.2 %collective-permute-done.8 = bf16[32,1024]{1,0:T(8,128)(2,1)S(1)} collective-permute-done((bf16[32,1024]{1,0:T(8,128)(2,1)S(1)}, bf16[32,1024]{1,0:T(8,128)(2,1)S(1)}, u32[]{:S(2)}, u32[]{:S(2)}) %collective-permute-start.8) | collective-permute-done | bytes 65568 | tf_op jit(solution)/shard_map/ppermute | solution.py:400
  54.3 2.5 %collective-permute-start.11 = (bf16[16,1024]{1,0:T(8,128)(2,1)S(1)}, bf16[16,1024]{1,0:T(8,128)(2,1)S(1)}, u32[]{:S(2)}, u32[]{:S(2)}) collective-permute-start(bf16[16,1024]{1,0:T(8,128)(2,1)S(1)} %pad_maximum_fusion.3), channel_id=1, source_target_pairs={{0,6},{1,7},{2,4},{3,5},{4,2},{5,3},{6,0},{7,1},{8,14},{9,15},{10,... | collective-permute-start | bytes 98312 | tf_op jit(solution)/shard_map/ppermute | solution.py:400
  56.8 2.4 %collective-permute-start.9 = (bf16[16,1024]{1,0:T(8,128)(2,1)S(1)}, bf16[16,1024]{1,0:T(8,128)(2,1)S(1)}, u32[]{:S(2)}, u32[]{:S(2)}) collective-permute-start(bf16[16,1024]{1,0:T(8,128)(2,1)S(1)} %pad_maximum_fusion.1), channel_id=1, source_target_pairs={{0,2},{1,3},{2,0},{3,1},{4,6},{5,7},{6,4},{7,5},{8,10},{9,11},{10,... | collective-permute-start | bytes 98312 | tf_op jit(solution)/shard_map/ppermute | solution.py:400
  59.2 0.0 collective-permute-start.10
  59.2 1.9 %collective-permute-done.9 = bf16[16,1024]{1,0:T(8,128)(2,1)S(1)} collective-permute-done((bf16[16,1024]{1,0:T(8,128)(2,1)S(1)}, bf16[16,1024]{1,0:T(8,128)(2,1)S(1)}, u32[]{:S(2)}, u32[]{:S(2)}) %collective-permute-start.9) | collective-permute-done | bytes 32800 | tf_op jit(solution)/shard_map/ppermute | solution.py:400
  61.1 2.9 %collective-permute-done.10 = bf16[16,1024]{1,0:T(8,128)(2,1)S(1)} collective-permute-done((bf16[16,1024]{1,0:T(8,128)(2,1)S(1)}, bf16[16,1024]{1,0:T(8,128)(2,1)S(1)}, u32[]{:S(2)}, u32[]{:S(2)}) %collective-permute-start.10) | collective-permute-done | bytes 32800 | tf_op jit(solution)/shard_map/ppermute | solution.py:400
  64.0 0.0 collective-permute-done.11
  64.1 2.2 %convolution_convert_fusion = bf16[1024,1024]{1,0:T(8,128)(2,1)} fusion(bf16[64,1024]{1,0:T(8,128)(2,1)S(1)} %constant_dynamic-update-slice_fusion, bf16[64,1024]{1,0:T(8,128)(2,1)S(1)} %copy-done, s32[64]{0:T(128)S(1)} %fusion.2), kind=kOutput, calls=%fused_computation | convolution fusion | flops 143724544 | bytes 2359552 | tf_op jit(solution)/shard_map/dot_general | solution.py:446
  (16 shorter events, 0.1 us)
Async XLA Ops:
  0.0 64.1 %copy-start = (bf16[64,1024]{1,0:T(8,128)(2,1)S(1)}, bf16[64,1024]{1,0:T(8,128)(2,1)}, u32[]{:S(2)}) copy-start(bf16[64,1024]{1,0:T(8,128)(2,1)} %param.12) | copy-start | bytes 393220
  0.0 11.3 %copy-start.7 = (bf16[2,192,160]{2,1,0:T(8,128)(2,1)S(1)}, bf16[2,192,160]{2,1,0:T(8,128)(2,1)}, u32[]{:S(2)}) copy-start(bf16[2,192,160]{2,1,0:T(8,128)(2,1)} %constant.52.clone.refs_2_.refs_4_) | copy-start | bytes 368644
  1.1 10.3 %copy-start.4 = (bf16[2,8,1024,128]{3,2,1,0:T(8,128)(2,1)S(1)}, bf16[2,8,1024,128]{3,2,1,0:T(8,128)(2,1)}, u32[]{:S(2)}) copy-start(bf16[2,8,1024,128]{3,2,1,0:T(8,128)(2,1)} %constant.51.clone.refs_1_.refs_3_) | copy-start | bytes 12582916
  6.8 4.5 %copy-start.1 = (bf16[16,8,384,128]{3,2,1,0:T(8,128)(2,1)}, bf16[16,8,384,128]{3,2,1,0:T(8,128)(2,1)S(1)}, u32[]{:S(2)}) copy-start(bf16[16,8,384,128]{3,2,1,0:T(8,128)(2,1)S(1)} %get-tuple-element.24.refs_2_.refs_1_) | copy-start | bytes 37748740
  11.3 7.4 %copy-start.9 = (s32[16]{0:T(128)S(1)}, s32[16]{0:T(128)}, u32[]{:S(2)}) copy-start(s32[16]{0:T(128)} %slot_ref.5) | copy-start | bytes 196
  12.9 5.8 %collective-permute-start.3 = (bf16[8,2,96,128]{3,2,1,0:T(8,128)(2,1)S(1)}, bf16[8,2,96,128]{3,2,1,0:T(8,128)(2,1)S(1)}, u32[]{:S(2)}, u32[]{:S(2)}) collective-permute-start(bf16[8,2,96,128]{3,2,1,0:T(8,128)(2,1)S(1)} %shard_map.92.refs_0_), channel_id=1, source_target_pairs={{0,1},{1,0},{2,3},{3,2},{4,5},{5,4},{6,7},{7,6},{8,9},{9,8},{10,11... | collective-permute-start | bytes 1179656 | tf_op jit(solution)/shard_map/ppermute | solution.py:400
  13.4 11.4 %collective-permute-start = (bf16[80,1024]{1,0:T(8,128)(2,1)S(1)}, bf16[80,1024]{1,0:T(8,128)(2,1)S(1)}, u32[]{:S(2)}, u32[]{:S(2)}) collective-permute-start(bf16[80,1024]{1,0:T(8,128)(2,1)S(1)} %reshape.26.refs_0_), channel_id=1, source_target_pairs={{0,2},{1,3},{2,0},{3,1},{4,6},{5,7},{6,4},{7,5},{8,10},{9,11},{10,... | collective-permute-start | bytes 491528 | tf_op jit(solution)/shard_map/ppermute | solution.py:400
  16.0 15.0 %collective-permute-start.1 = (bf16[80,1024]{1,0:T(8,128)(2,1)S(1)}, bf16[80,1024]{1,0:T(8,128)(2,1)S(1)}, u32[]{:S(2)}, u32[]{:S(2)}) collective-permute-start(bf16[80,1024]{1,0:T(8,128)(2,1)S(1)} %reshape.26.refs_0_), channel_id=1, source_target_pairs={{0,4},{1,5},{2,6},{3,7},{4,0},{5,1},{6,2},{7,3},{8,12},{9,13},{10,... | collective-permute-start | bytes 491528 | tf_op jit(solution)/shard_map/ppermute | solution.py:400
  18.6 12.4 %collective-permute-start.2 = (bf16[80,1024]{1,0:T(8,128)(2,1)S(1)}, bf16[80,1024]{1,0:T(8,128)(2,1)S(1)}, u32[]{:S(2)}, u32[]{:S(2)}) collective-permute-start(bf16[80,1024]{1,0:T(8,128)(2,1)S(1)} %reshape.26.refs_0_), channel_id=1, source_target_pairs={{0,6},{1,7},{2,4},{3,5},{4,2},{5,3},{6,0},{7,1},{8,14},{9,15},{10,... | collective-permute-start | bytes 491528 | tf_op jit(solution)/shard_map/ppermute | solution.py:400
  18.7 4.6 %copy-start.2 = (bf16[16,8,384,128]{3,2,1,0:T(8,128)(2,1)S(1)}, bf16[16,8,384,128]{3,2,1,0:T(8,128)(2,1)}, u32[]{:S(2)}) copy-start(bf16[16,8,384,128]{3,2,1,0:T(8,128)(2,1)} %copy-done.1) | copy-start | bytes 37748740
  23.3 12.1 %copy-start.3 = (bf16[16,8,384,128]{3,2,1,0:T(8,128)(2,1)S(1)}, bf16[16,8,384,128]{3,2,1,0:T(8,128)(2,1)}, u32[]{:S(2)}) copy-start(bf16[16,8,384,128]{3,2,1,0:T(8,128)(2,1)} %copy-done.1) | copy-start | bytes 37748740
  31.0 2.2 %copy-start.5 = (bf16[2,8,1024,128]{3,2,1,0:T(8,128)(2,1)S(1)}, bf16[2,8,1024,128]{3,2,1,0:T(8,128)(2,1)}, u32[]{:S(2)}) copy-start(bf16[2,8,1024,128]{3,2,1,0:T(8,128)(2,1)} %constant.51.clone.refs_1_.refs_3_) | copy-start | bytes 12582916
  35.3 2.9 %copy-start.6 = (bf16[2,8,1024,128]{3,2,1,0:T(8,128)(2,1)S(1)}, bf16[2,8,1024,128]{3,2,1,0:T(8,128)(2,1)}, u32[]{:S(2)}) copy-start(bf16[2,8,1024,128]{3,2,1,0:T(8,128)(2,1)} %constant.54.clone.refs_4_) | copy-start | bytes 12582916
  35.3 2.9 %copy-start.8 = (bf16[2,128,192]{2,1,0:T(8,128)(2,1)S(1)}, bf16[2,128,192]{2,1,0:T(8,128)(2,1)}, u32[]{:S(2)}) copy-start(bf16[2,128,192]{2,1,0:T(8,128)(2,1)} %constant.53.clone.refs_3_) | copy-start | bytes 294916
  35.3 2.9 %collective-permute-start.4 = (bf16[8,6,96,128]{3,2,1,0:T(8,128)(2,1)S(1)}, bf16[8,6,96,128]{3,2,1,0:T(8,128)(2,1)S(1)}, u32[]{:S(2)}, u32[]{:S(2)}) collective-permute-start(bf16[8,6,96,128]{3,2,1,0:T(8,128)(2,1)S(1)} %shard_map.94.refs_0_), channel_id=1, source_target_pairs={{0,1},{1,0},{2,3},{3,2},{4,5},{5,4},{6,7},{7,6},{8,9},{9,8},{10,11... | collective-permute-start | bytes 3538952 | tf_op jit(solution)/shard_map/ppermute | solution.py:400
  42.8 6.0 %collective-permute-start.5 = (bf16[8,8,1024]{2,1,0:T(8,128)(2,1)S(1)}, bf16[8,8,1024]{2,1,0:T(8,128)(2,1)S(1)}, u32[]{:S(2)}, u32[]{:S(2)}) collective-permute-start(bf16[8,8,1024]{2,1,0:T(8,128)(2,1)S(1)} %get-tuple-element.30), channel_id=1, source_target_pairs={{0,8},{8,0},{16,24},{24,16},{1,9},{9,1},{17,25},{25,17},{2,10},{10... | collective-permute-start | bytes 393224 | tf_op jit(solution)/shard_map/ppermute | solution.py:400
  44.4 8.1 %collective-permute-start.6 = (bf16[8,8,1024]{2,1,0:T(8,128)(2,1)S(1)}, bf16[8,8,1024]{2,1,0:T(8,128)(2,1)S(1)}, u32[]{:S(2)}, u32[]{:S(2)}) collective-permute-start(bf16[8,8,1024]{2,1,0:T(8,128)(2,1)S(1)} %get-tuple-element.31), channel_id=1, source_target_pairs={{0,16},{8,24},{16,0},{24,8},{1,17},{9,25},{17,1},{25,9},{2,18},{10... | collective-permute-start | bytes 393224 | tf_op jit(solution)/shard_map/ppermute | solution.py:400
  45.9 6.6 %collective-permute-start.7 = (bf16[8,8,1024]{2,1,0:T(8,128)(2,1)S(1)}, bf16[8,8,1024]{2,1,0:T(8,128)(2,1)S(1)}, u32[]{:S(2)}, u32[]{:S(2)}) collective-permute-start(bf16[8,8,1024]{2,1,0:T(8,128)(2,1)S(1)} %get-tuple-element.32), channel_id=1, source_target_pairs={{0,24},{8,16},{16,8},{24,0},{1,25},{9,17},{17,9},{25,1},{2,26},{10... | collective-permute-start | bytes 393224 | tf_op jit(solution)/shard_map/ppermute | solution.py:400
  53.0 1.3 %collective-permute-start.8 = (bf16[32,1024]{1,0:T(8,128)(2,1)S(1)}, bf16[32,1024]{1,0:T(8,128)(2,1)S(1)}, u32[]{:S(2)}, u32[]{:S(2)}) collective-permute-start(bf16[32,1024]{1,0:T(8,128)(2,1)S(1)} %pad_maximum_fusion), channel_id=1, source_target_pairs={{0,1},{1,0},{2,3},{3,2},{4,5},{5,4},{6,7},{7,6},{8,9},{9,8},{10,11... | collective-permute-start | bytes 196616 | tf_op jit(solution)/shard_map/ppermute | solution.py:400
  54.3 9.8 %collective-permute-start.11 = (bf16[16,1024]{1,0:T(8,128)(2,1)S(1)}, bf16[16,1024]{1,0:T(8,128)(2,1)S(1)}, u32[]{:S(2)}, u32[]{:S(2)}) collective-permute-start(bf16[16,1024]{1,0:T(8,128)(2,1)S(1)} %pad_maximum_fusion.3), channel_id=1, source_target_pairs={{0,6},{1,7},{2,4},{3,5},{4,2},{5,3},{6,0},{7,1},{8,14},{9,15},{10,... | collective-permute-start | bytes 98312 | tf_op jit(solution)/shard_map/ppermute | solution.py:400
  56.8 4.3 %collective-permute-start.9 = (bf16[16,1024]{1,0:T(8,128)(2,1)S(1)}, bf16[16,1024]{1,0:T(8,128)(2,1)S(1)}, u32[]{:S(2)}, u32[]{:S(2)}) collective-permute-start(bf16[16,1024]{1,0:T(8,128)(2,1)S(1)} %pad_maximum_fusion.1), channel_id=1, source_target_pairs={{0,2},{1,3},{2,0},{3,1},{4,6},{5,7},{6,4},{7,5},{8,10},{9,11},{10,... | collective-permute-start | bytes 98312 | tf_op jit(solution)/shard_map/ppermute | solution.py:400
  59.2 4.8 %collective-permute-start.10 = (bf16[16,1024]{1,0:T(8,128)(2,1)S(1)}, bf16[16,1024]{1,0:T(8,128)(2,1)S(1)}, u32[]{:S(2)}, u32[]{:S(2)}) collective-permute-start(bf16[16,1024]{1,0:T(8,128)(2,1)S(1)} %pad_maximum_fusion.2), channel_id=1, source_target_pairs={{0,4},{1,5},{2,6},{3,7},{4,0},{5,1},{6,2},{7,3},{8,12},{9,13},{10,... | collective-permute-start | bytes 98312 | tf_op jit(solution)/shard_map/ppermute | solution.py:400

commit v7 on v6

--- a/solution.py
+++ b/solution.py
@@ -15,6 +15,7 @@
 LANES = 256
 SLAB = 128
 GROUP = 4
+COST = pl.CostEstimate(flops=2**20, bytes_accessed=2**16, transcendentals=0)
 ROWS = 4
 STEPS = 24
 SEGS = 2
@@ -109,7 +110,7 @@
     return jnp.concatenate([ref[(*index, first + i)] for i in range(LANES // SLAB)], axis=-1)
 
 
-def response_kernel(rows, bins, room_hbm, table_hbm, hat_ref, done_ref, room_ref, table_ref, sems):
+def response_kernel(rows, bins, me_ref, room_hbm, table_hbm, hat_ref, done_ref, room_ref, table_ref, sems):
     depth = room_ref.shape[1] * room_ref.shape[2] * 2
     flat = room_ref.reshape(rows, depth, bins)
     plain, packed, _ = lane_masks(0, LANES)
@@ -145,15 +146,14 @@
     done_ref[...] = jnp.zeros_like(done_ref)
 
 
-def transform_responses(room):
+def transform_responses(room, me):
     rows, parts, channels, _, bins = room.shape
     slabs = bins // SLAB
     _, resp, _ = step_tables(parts, parts + SEGS * KEEP, channels)
-    flops = 2 * rows * channels * 2 * STEPS * parts * channels * 2 * bins
     hbm = pl.BlockSpec(memory_space=pltpu.HBM)
     return pl.pallas_call(
         functools.partial(response_kernel, rows, bins),
-        in_specs=[hbm, hbm],
+        in_specs=[pl.BlockSpec(memory_space=pltpu.SMEM), hbm, hbm],
         out_specs=[pl.BlockSpec(memory_space=pltpu.VMEM)] * 2,
         out_shape=[
             pltpu.VMEM((rows, slabs, channels * 2 * STEPS, SLAB), BF16),
@@ -165,8 +165,9 @@
             pltpu.SemaphoreType.DMA((rows + 1,)),
         ],
         compiler_params=pltpu.CompilerParams(vmem_limit_bytes=8 * 2**20),
-        cost_estimate=pl.CostEstimate(flops=flops, bytes_accessed=16 * 2**20, transcendentals=0),
+        cost_estimate=COST,
     )(
+        me,
         pltpu.with_memory_space_constraint(room, pltpu.HBM),
         pltpu.with_memory_space_constraint(jnp.asarray(resp), pltpu.HBM),
     )
@@ -210,7 +211,6 @@
     table, _ = block_tables(bins)
     spec, _, _ = step_tables(parts, frames, 2)
     vmem = pl.BlockSpec(memory_space=pltpu.VMEM)
-    flops = 2 * bins * rows * (frames * 2 * bins + 4 * SEGS * STEPS * frames)
     operands = [*x_list, jnp.asarray(table), jnp.asarray(spec)]
     if after is not None:
         operands.append(after)
@@ -220,7 +220,7 @@
         out_specs=vmem,
         out_shape=jax.ShapeDtypeStruct((slabs, rows, 2 * SEGS * STEPS, SLAB), BF16),
         compiler_params=pltpu.CompilerParams(vmem_limit_bytes=8 * 2**20),
-        cost_estimate=pl.CostEstimate(flops=flops, bytes_accessed=4 * 2**20, transcendentals=0),
+        cost_estimate=COST,
     )(*operands)
 
 
@@ -346,8 +346,6 @@
         ]
     else:
         out_shape = jax.ShapeDtypeStruct((slabs, channels // 2, 2 * wide, SLAB), F32)
-    count = own * sum(len(some) for some in flips)
-    flops = 2 * bins * channels * (count * wide * 8 + (blocks * 2 * bins if last else 0))
     body = functools.partial(
         mix_kernel, tuple(flips), own, channels, blocks, shares, total is not None, last
     )
@@ -359,7 +357,7 @@
         scratch_shapes=scratch,
         input_output_aliases=aliases,
         compiler_params=pltpu.CompilerParams(vmem_limit_bytes=12 * 2**20),
-        cost_estimate=pl.CostEstimate(flops=flops, bytes_accessed=8 * 2**20, transcendentals=0),
+        cost_estimate=COST,
     )(*operands)
 
 
@@ -407,22 +405,26 @@
     order = (takes[:, None] == row[None, :]).astype(BF16)
     own_order = dot(order, decoder).astype(BF16)
 
-    hat, done = transform_responses(room_spectra)
     me = jnp.stack([src_me, ch_me])
+    hat, done = transform_responses(room_spectra, me)
 
     def add(s_list, flips, total, last):
         return add_sources(
             s_list, flips, own, me, render_slot, hat, total, last, src_count, channels, parts
         )
 
-    early = transform_signals([x_own], own, block_len, parts, done)
-    early_mate = swap(early, "ch", ch_count, 1)
-    total = add([early, early_mate], [[0], [1]], None, False)
-    *lanes, total = lax.optimization_barrier((*lanes, total))
-    late = transform_signals(lanes, own, block_len, parts)
-    late_mate = swap(late, "ch", ch_count, 1)
-    total = add([late], [[2 * d for d in range(1, chips)]], total, False)
-    total = add([late_mate], [[2 * d + 1 for d in range(1, chips)]], total, True)
+    def transform(x_list, after=None):
+        mine = transform_signals(x_list, own, block_len, parts, after)
+        return mine, swap(mine, "ch", ch_count, 1)
+
+    near, far = range(0, 2), range(2, chips)
+    near_mine, near_given = transform([x_own, lanes[0]], done)
+    total = add([near_mine], [[2 * d for d in near]], None, False)
+    *late, total = lax.optimization_barrier((*lanes[1:], total))
+    far_mine, far_given = transform(late)
+    flips = [[2 * d + 1 for d in near], [2 * d for d in far]]
+    total = add([near_given, far_mine], flips, total, False)
+    total = add([far_given], [[2 * d + 1 for d in far]], total, True)
 
     parts_in = [total[0]] + [swap(total[d], "src", src_count, d) for d in range(1, src_count)]
     each = blocks // src_count

time: 66.5 us -> 51.1 us (0.77)
  local copies, waits for them, and re-layouts: 12.4 us -> 1.12 us
  waiting for transfers between devices: 18.7 us -> 14.9 us
    unnamed x23 -> x15, local copies, waits for them, and re-layouts: 11.3 us -> 0.04 us
    ppermute x12, waiting for transfers between devices: 18.7 us -> 14.9 us  [swap(): return lax.ppermute(value, axis, [(i, i ^ flip) for i in range(count)])]
    pallas_call x1, Pallas kernels: 5.72 us -> 6.41 us  [transform_responses(): pl.pallas_call(functools.partial(response_kernel, rows, bins), in_specs=[...]
  transfers between devices with their start and end apart: 12 -> 12, of which waited for: 7 -> 6; matrix products, arithmetic and copies ran while one was open for 0% -> 0% of each run, Pallas kernels for 6% -> 28%
where the time goes in v7:
time: 51.1 us; the launch traced here: 51 us
  Pallas kernels  18.5 us (36%)
  waiting for transfers between devices  14.9 us (29%)
  starting transfers between devices  13.9 us (27%)
  matrix products  2.2 us (4%)
  local copies, waits for them, and re-layouts  1.12 us (2%)
    ppermute x12, waiting for transfers between devices, swap(): return lax.ppermute(value, axis, [(i, i ^ flip) for i in range(count)])  14.9 us
    ppermute x12, starting transfers between devices, swap(): return lax.ppermute(value, axis, [(i, i ^ flip) for i in range(count)])  13.9 us
    pallas_call x3, Pallas kernels, add_sources(): pl.pallas_call(body, in_specs=[smem, smem] + [vmem] * (len(operands) - 2)...  8.35 us
    pallas_call x1, Pallas kernels, transform_responses(): pl.pallas_call(functools.partial(response_kernel, rows, bins), in_specs=[...  6.41 us
    pallas_call x2, Pallas kernels, transform_signals(): pl.pallas_call(functools.partial(spectra_kernel, len(x_list), rows), in_s...  3.33 us
    dot_general x1, matrix products, per_device(): lax.dot_general(gathered, matrix, (((0,), (0,)), ((), ())), preferred_ele...  2.2 us
    reshape x1, local copies, waits for them, and re-layouts, per_device(): x_own = dry_signal.reshape(own * frames, block_len)  1.08 us
  transfers between devices with their start and end apart: 12, of which 6 were waited for; matrix products, arithmetic and copies ran while one was open for 0% of the time, Pallas kernels for 28%

profile of v7, /device:TPU:0, one launch (start us, length us, event | category | flops | bytes accessed | tf_op | source)
XLA Modules:
  0.0 51.0 jit_solution(13302999160203755724)
XLA Ops:
  0.0 0.0 copy-start
  0.0 0.0 copy-start.3
  0.0 1.1 %reshape.26.refs_0_ = bf16[80,1024]{1,0:T(8,128)(2,1)S(1)} reshape(bf16[2,40960]{1,0:T(2,128)(2,1)} %param.9) | data formatting | bytes 327680 | tf_op jit(solution)/shard_map/reshape | solution.py:395
  1.1 3.1 %collective-permute-start.2 = (bf16[80,1024]{1,0:T(8,128)(2,1)S(1)}, bf16[80,1024]{1,0:T(8,128)(2,1)S(1)}, u32[]{:S(2)}, u32[]{:S(2)}) collective-permute-start(bf16[80,1024]{1,0:T(8,128)(2,1)S(1)} %reshape.26.refs_0_), channel_id=1, source_target_pairs={{0,2},{1,3},{2,0},{3,1},{4,6},{5,7},{6,4},{7,5},{8,10},{9,11},{10,... | collective-permute-start | bytes 491528 | tf_op jit(solution)/shard_map/ppermute | solution.py:398
  4.2 2.6 %collective-permute-start = (bf16[80,1024]{1,0:T(8,128)(2,1)S(1)}, bf16[80,1024]{1,0:T(8,128)(2,1)S(1)}, u32[]{:S(2)}, u32[]{:S(2)}) collective-permute-start(bf16[80,1024]{1,0:T(8,128)(2,1)S(1)} %reshape.26.refs_0_), channel_id=1, source_target_pairs={{0,4},{1,5},{2,6},{3,7},{4,0},{5,1},{6,2},{7,3},{8,12},{9,13},{10,... | collective-permute-start | bytes 491528 | tf_op jit(solution)/shard_map/ppermute | solution.py:398
  6.8 0.0 collective-permute-start.1
  6.8 0.0 copy-start.1
  6.8 0.1 pad_add_fusion.me_ref
  6.8 0.0 copy-start.5
  6.8 6.4 %shard_map.91 = (bf16[16,8,384,128]{3,2,1,0:T(8,128)(2,1)S(1)}, f32[8,128]{1,0:T(8,128)S(1)}) custom-call(s32[2]{0:T(128)S(1)} %pad_add_fusion.me_ref, bf16[16,8,8,2,1024]{4,3,2,1,0:T(2,128)(2,1)} %room_hbm.1, bf16[384,256]{1,0:T(8,128)(2,1)} %constant.50.clone.table_hbm), custom_call_target="tpu_custom_call" | custom-call | flops 1048576 | bytes 65536 | tf_op jit(solution)/shard_map/pallas_call | solution.py:154
  13.3 0.0 collective-permute-done.2.refs_1_
  13.3 0.0 copy-done.3
  13.3 0.0 copy-done.1
  13.3 1.7 %shard_map.92.refs_0_ = bf16[8,4,96,128]{3,2,1,0:T(8,128)(2,1)S(1)} custom-call(bf16[80,1024]{1,0:T(8,128)(2,1)S(1)} %reshape.26.refs_0_, bf16[80,1024]{1,0:T(8,128)(2,1)S(1)} %collective-permute-done.2.refs_1_, bf16[2,8,1024,128]{3,2,1,0:T(8,128)(2,1)S(1)} %copy-done.1, bf16[2,192,160]{2,1,0:T(8,128)(2,1)S(1)} %copy-done.3, ...), custom_call_target="tpu_custom_call" | custom-call | flops 1048576 | bytes 65536 | tf_op jit(solution)/shard_map/pallas_call | solution.py:217
  15.0 0.1 collective-permute-start.4
  15.0 0.0 copy-done.5
  15.0 1.5 %shard_map.93.refs_3_ = f32[8,4,192,128]{3,2,1,0:T(8,128)S(1)} custom-call(s32[2]{0:T(128)S(1)} %pad_add_fusion.me_ref, s32[16]{0:T(128)S(1)} %copy-done.5, bf16[8,4,96,128]{3,2,1,0:T(8,128)(2,1)S(1)} %shard_map.92.refs_0_, bf16[16,8,384,128]{3,2,1,0:T(8,128)(2,1)S(1)} %get-tuple-element.23.refs_1_.refs_2_), custom_call_target="tpu_custom_call" | custom-call | flops 1048576 | bytes 65536 | tf_op jit(solution)/shard_map/pallas_call | solution.py:352
  16.6 2.6 %collective-permute-done.refs_0_ = bf16[80,1024]{1,0:T(8,128)(2,1)S(1)} collective-permute-done((bf16[80,1024]{1,0:T(8,128)(2,1)S(1)}, bf16[80,1024]{1,0:T(8,128)(2,1)S(1)}, u32[]{:S(2)}, u32[]{:S(2)}) %collective-permute-start) | collective-permute-done | bytes 163872 | tf_op jit(solution)/shard_map/ppermute | solution.py:398
  19.2 0.0 collective-permute-done.1.refs_1_
  19.2 1.7 %shard_map.94.refs_1_ = bf16[8,4,96,128]{3,2,1,0:T(8,128)(2,1)S(1)} custom-call(bf16[80,1024]{1,0:T(8,128)(2,1)S(1)} %collective-permute-done.refs_0_, bf16[80,1024]{1,0:T(8,128)(2,1)S(1)} %collective-permute-done.1.refs_1_, bf16[2,8,1024,128]{3,2,1,0:T(8,128)(2,1)S(1)} %copy-done.1, bf16[2,192,160]{2,1,0:T(8,128)(2,1)S(1)} %copy-done.3), custom_call_target="tpu_custom_call" | custom-call | flops 1048576 | bytes 65536 | tf_op jit(solution)/shard_map/pallas_call | solution.py:217
  20.9 0.0 copy-start.2
  20.9 0.0 copy-start.4
  20.9 0.1 collective-permute-start.3
  21.0 0.0 collective-permute-done.4.refs_0_
  21.0 3.1 %shard_map.95.refs_2_ = f32[8,4,192,128]{3,2,1,0:T(8,128)S(1)} custom-call(s32[2]{0:T(128)S(1)} %pad_add_fusion.me_ref, s32[16]{0:T(128)S(1)} %copy-done.5, bf16[8,4,96,128]{3,2,1,0:T(8,128)(2,1)S(1)} %collective-permute-done.4.refs_0_, bf16[8,4,96,128]{3,2,1,0:T(8,128)(2,1)S(1)} %shard_map.94.refs_1_, ...), custom_call_target="tpu_custom_call", output_to_operand_aliasing={{}: (5, {})} | custom-call | flops 1048576 | bytes 65536 | tf_op jit(solution)/shard_map/pallas_call | solution.py:352
  24.1 0.0 collective-permute-done.3.refs_0_
  24.1 0.0 copy-done.2
  24.1 0.0 copy-done.4
  24.1 3.7 %shard_map.96 = (bf16[8,8,1024]{2,1,0:T(8,128)(2,1)S(1)}, bf16[8,8,1024]{2,1,0:T(8,128)(2,1)S(1)}, bf16[8,8,1024]{2,1,0:T(8,128)(2,1)S(1)}, bf16[8,8,1024]{2,1,0:T(8,128)(2,1)S(1)}) custom-call(s32[2]{0:T(128)S(1)} %pad_add_fusion.me_ref, s32[16]{0:T(128)S(1)} %copy-done.5, bf16[8,4,96,128]{3,2,1,0:T(8,128)(2,1)S(1)} %collective-permute-done.3.refs_0_, ...), custom_call_target="tpu_custom_call" | custom-call | flops 1048576 | bytes 65536 | tf_op jit(solution)/shard_map/pallas_call | solution.py:352
  27.9 1.6 %collective-permute-start.5 = (bf16[8,8,1024]{2,1,0:T(8,128)(2,1)S(1)}, bf16[8,8,1024]{2,1,0:T(8,128)(2,1)S(1)}, u32[]{:S(2)}, u32[]{:S(2)}) collective-permute-start(bf16[8,8,1024]{2,1,0:T(8,128)(2,1)S(1)} %get-tuple-element.28), channel_id=1, source_target_pairs={{0,8},{8,0},{16,24},{24,16},{1,9},{9,1},{17,25},{25,17},{2,10},{10... | collective-permute-start | bytes 393224 | tf_op jit(solution)/shard_map/ppermute | solution.py:398
  29.4 1.5 %collective-permute-start.6 = (bf16[8,8,1024]{2,1,0:T(8,128)(2,1)S(1)}, bf16[8,8,1024]{2,1,0:T(8,128)(2,1)S(1)}, u32[]{:S(2)}, u32[]{:S(2)}) collective-permute-start(bf16[8,8,1024]{2,1,0:T(8,128)(2,1)S(1)} %get-tuple-element.29), channel_id=1, source_target_pairs={{0,16},{8,24},{16,0},{24,8},{1,17},{9,25},{17,1},{25,9},{2,18},{10... | collective-permute-start | bytes 393224 | tf_op jit(solution)/shard_map/ppermute | solution.py:398
  30.9 0.5 collective-permute-start.7
  31.4 2.8 %collective-permute-done.5.refs_1_ = bf16[8,8,1024]{2,1,0:T(8,128)(2,1)S(1)} collective-permute-done((bf16[8,8,1024]{2,1,0:T(8,128)(2,1)S(1)}, bf16[8,8,1024]{2,1,0:T(8,128)(2,1)S(1)}, u32[]{:S(2)}, u32[]{:S(2)}) %collective-permute-start.5) | collective-permute-done | bytes 131104 | tf_op jit(solution)/shard_map/ppermute | solution.py:398
  34.2 3.6 %collective-permute-done.6.refs_2_ = bf16[8,8,1024]{2,1,0:T(8,128)(2,1)S(1)} collective-permute-done((bf16[8,8,1024]{2,1,0:T(8,128)(2,1)S(1)}, bf16[8,8,1024]{2,1,0:T(8,128)(2,1)S(1)}, u32[]{:S(2)}, u32[]{:S(2)}) %collective-permute-start.6) | collective-permute-done | bytes 131104 | tf_op jit(solution)/shard_map/ppermute | solution.py:398
  37.8 0.0 collective-permute-done.7.refs_3_
  37.8 0.5 shard_map.97
  38.3 0.1 collective-permute-start.8
  38.4 1.2 %collective-permute-done.8 = bf16[32,1024]{1,0:T(8,128)(2,1)S(1)} collective-permute-done((bf16[32,1024]{1,0:T(8,128)(2,1)S(1)}, bf16[32,1024]{1,0:T(8,128)(2,1)S(1)}, u32[]{:S(2)}, u32[]{:S(2)}) %collective-permute-start.8) | collective-permute-done | bytes 65568 | tf_op jit(solution)/shard_map/ppermute | solution.py:398
  39.6 2.4 %collective-permute-start.11 = (bf16[16,1024]{1,0:T(8,128)(2,1)S(1)}, bf16[16,1024]{1,0:T(8,128)(2,1)S(1)}, u32[]{:S(2)}, u32[]{:S(2)}) collective-permute-start(bf16[16,1024]{1,0:T(8,128)(2,1)S(1)} %pad_maximum_fusion.3), channel_id=1, source_target_pairs={{0,6},{1,7},{2,4},{3,5},{4,2},{5,3},{6,0},{7,1},{8,14},{9,15},{10,... | collective-permute-start | bytes 98312 | tf_op jit(solution)/shard_map/ppermute | solution.py:398
  42.0 1.9 %collective-permute-start.9 = (bf16[16,1024]{1,0:T(8,128)(2,1)S(1)}, bf16[16,1024]{1,0:T(8,128)(2,1)S(1)}, u32[]{:S(2)}, u32[]{:S(2)}) collective-permute-start(bf16[16,1024]{1,0:T(8,128)(2,1)S(1)} %pad_maximum_fusion.1), channel_id=1, source_target_pairs={{0,2},{1,3},{2,0},{3,1},{4,6},{5,7},{6,4},{7,5},{8,10},{9,11},{10,... | collective-permute-start | bytes 98312 | tf_op jit(solution)/shard_map/ppermute | solution.py:398
  43.9 0.2 collective-permute-start.10
  44.1 1.8 %collective-permute-done.9 = bf16[16,1024]{1,0:T(8,128)(2,1)S(1)} collective-permute-done((bf16[16,1024]{1,0:T(8,128)(2,1)S(1)}, bf16[16,1024]{1,0:T(8,128)(2,1)S(1)}, u32[]{:S(2)}, u32[]{:S(2)}) %collective-permute-start.9) | collective-permute-done | bytes 32800 | tf_op jit(solution)/shard_map/ppermute | solution.py:398
  45.9 2.8 %collective-permute-done.10 = bf16[16,1024]{1,0:T(8,128)(2,1)S(1)} collective-permute-done((bf16[16,1024]{1,0:T(8,128)(2,1)S(1)}, bf16[16,1024]{1,0:T(8,128)(2,1)S(1)}, u32[]{:S(2)}, u32[]{:S(2)}) %collective-permute-start.10) | collective-permute-done | bytes 32800 | tf_op jit(solution)/shard_map/ppermute | solution.py:398
  48.8 0.0 collective-permute-done.11
  48.8 0.0 copy-done
  48.8 2.2 %convolution_convert_fusion = bf16[1024,1024]{1,0:T(8,128)(2,1)} fusion(bf16[64,1024]{1,0:T(8,128)(2,1)S(1)} %constant_dynamic-update-slice_fusion, bf16[64,1024]{1,0:T(8,128)(2,1)S(1)} %copy-done, s32[64]{0:T(128)S(1)} %fusion.2), kind=kOutput, calls=%fused_computation | convolution fusion | flops 143724544 | bytes 2359552 | tf_op jit(solution)/shard_map/dot_general | solution.py:448
  (10 shorter events, 0.0 us)
Async XLA Ops:
  0.0 48.8 %copy-start = (bf16[64,1024]{1,0:T(8,128)(2,1)S(1)}, bf16[64,1024]{1,0:T(8,128)(2,1)}, u32[]{:S(2)}) copy-start(bf16[64,1024]{1,0:T(8,128)(2,1)} %param.12) | copy-start | bytes 393220
  0.0 13.3 %copy-start.3 = (bf16[2,192,160]{2,1,0:T(8,128)(2,1)S(1)}, bf16[2,192,160]{2,1,0:T(8,128)(2,1)}, u32[]{:S(2)}) copy-start(bf16[2,192,160]{2,1,0:T(8,128)(2,1)} %constant.52.clone.refs_3_) | copy-start | bytes 368644
  1.1 12.2 %collective-permute-start.2 = (bf16[80,1024]{1,0:T(8,128)(2,1)S(1)}, bf16[80,1024]{1,0:T(8,128)(2,1)S(1)}, u32[]{:S(2)}, u32[]{:S(2)}) collective-permute-start(bf16[80,1024]{1,0:T(8,128)(2,1)S(1)} %reshape.26.refs_0_), channel_id=1, source_target_pairs={{0,2},{1,3},{2,0},{3,1},{4,6},{5,7},{6,4},{7,5},{8,10},{9,11},{10,... | collective-permute-start | bytes 491528 | tf_op jit(solution)/shard_map/ppermute | solution.py:398
  4.2 15.0 %collective-permute-start = (bf16[80,1024]{1,0:T(8,128)(2,1)S(1)}, bf16[80,1024]{1,0:T(8,128)(2,1)S(1)}, u32[]{:S(2)}, u32[]{:S(2)}) collective-permute-start(bf16[80,1024]{1,0:T(8,128)(2,1)S(1)} %reshape.26.refs_0_), channel_id=1, source_target_pairs={{0,4},{1,5},{2,6},{3,7},{4,0},{5,1},{6,2},{7,3},{8,12},{9,13},{10,... | collective-permute-start | bytes 491528 | tf_op jit(solution)/shard_map/ppermute | solution.py:398
  6.8 12.5 %collective-permute-start.1 = (bf16[80,1024]{1,0:T(8,128)(2,1)S(1)}, bf16[80,1024]{1,0:T(8,128)(2,1)S(1)}, u32[]{:S(2)}, u32[]{:S(2)}) collective-permute-start(bf16[80,1024]{1,0:T(8,128)(2,1)S(1)} %reshape.26.refs_0_), channel_id=1, source_target_pairs={{0,6},{1,7},{2,4},{3,5},{4,2},{5,3},{6,0},{7,1},{8,14},{9,15},{10,... | collective-permute-start | bytes 491528 | tf_op jit(solution)/shard_map/ppermute | solution.py:398
  6.8 6.5 %copy-start.1 = (bf16[2,8,1024,128]{3,2,1,0:T(8,128)(2,1)S(1)}, bf16[2,8,1024,128]{3,2,1,0:T(8,128)(2,1)}, u32[]{:S(2)}) copy-start(bf16[2,8,1024,128]{3,2,1,0:T(8,128)(2,1)} %constant.51.clone.refs_2_) | copy-start | bytes 12582916
  6.8 8.2 %copy-start.5 = (s32[16]{0:T(128)S(1)}, s32[16]{0:T(128)}, u32[]{:S(2)}) copy-start(s32[16]{0:T(128)} %slot_ref.5) | copy-start | bytes 196
  15.0 6.0 %collective-permute-start.4 = (bf16[8,4,96,128]{3,2,1,0:T(8,128)(2,1)S(1)}, bf16[8,4,96,128]{3,2,1,0:T(8,128)(2,1)S(1)}, u32[]{:S(2)}, u32[]{:S(2)}) collective-permute-start(bf16[8,4,96,128]{3,2,1,0:T(8,128)(2,1)S(1)} %shard_map.92.refs_0_), channel_id=1, source_target_pairs={{0,1},{1,0},{2,3},{3,2},{4,5},{5,4},{6,7},{7,6},{8,9},{9,8},{10,11... | collective-permute-start | bytes 2359304 | tf_op jit(solution)/shard_map/ppermute | solution.py:398
  20.9 3.2 %copy-start.2 = (bf16[2,8,1024,128]{3,2,1,0:T(8,128)(2,1)S(1)}, bf16[2,8,1024,128]{3,2,1,0:T(8,128)(2,1)}, u32[]{:S(2)}) copy-start(bf16[2,8,1024,128]{3,2,1,0:T(8,128)(2,1)} %constant.54.clone.refs_4_) | copy-start | bytes 12582916
  20.9 3.2 %copy-start.4 = (bf16[2,128,192]{2,1,0:T(8,128)(2,1)S(1)}, bf16[2,128,192]{2,1,0:T(8,128)(2,1)}, u32[]{:S(2)}) copy-start(bf16[2,128,192]{2,1,0:T(8,128)(2,1)} %constant.53.clone.refs_3_) | copy-start | bytes 294916
  20.9 3.2 %collective-permute-start.3 = (bf16[8,4,96,128]{3,2,1,0:T(8,128)(2,1)S(1)}, bf16[8,4,96,128]{3,2,1,0:T(8,128)(2,1)S(1)}, u32[]{:S(2)}, u32[]{:S(2)}) collective-permute-start(bf16[8,4,96,128]{3,2,1,0:T(8,128)(2,1)S(1)} %shard_map.94.refs_1_), channel_id=1, source_target_pairs={{0,1},{1,0},{2,3},{3,2},{4,5},{5,4},{6,7},{7,6},{8,9},{9,8},{10,11... | collective-permute-start | bytes 2359304 | tf_op jit(solution)/shard_map/ppermute | solution.py:398
  27.9 6.4 %collective-permute-start.5 = (bf16[8,8,1024]{2,1,0:T(8,128)(2,1)S(1)}, bf16[8,8,1024]{2,1,0:T(8,128)(2,1)S(1)}, u32[]{:S(2)}, u32[]{:S(2)}) collective-permute-start(bf16[8,8,1024]{2,1,0:T(8,128)(2,1)S(1)} %get-tuple-element.28), channel_id=1, source_target_pairs={{0,8},{8,0},{16,24},{24,16},{1,9},{9,1},{17,25},{25,17},{2,10},{10... | collective-permute-start | bytes 393224 | tf_op jit(solution)/shard_map/ppermute | solution.py:398
  29.4 8.4 %collective-permute-start.6 = (bf16[8,8,1024]{2,1,0:T(8,128)(2,1)S(1)}, bf16[8,8,1024]{2,1,0:T(8,128)(2,1)S(1)}, u32[]{:S(2)}, u32[]{:S(2)}) collective-permute-start(bf16[8,8,1024]{2,1,0:T(8,128)(2,1)S(1)} %get-tuple-element.29), channel_id=1, source_target_pairs={{0,16},{8,24},{16,0},{24,8},{1,17},{9,25},{17,1},{25,9},{2,18},{10... | collective-permute-start | bytes 393224 | tf_op jit(solution)/shard_map/ppermute | solution.py:398
  30.9 6.9 %collective-permute-start.7 = (bf16[8,8,1024]{2,1,0:T(8,128)(2,1)S(1)}, bf16[8,8,1024]{2,1,0:T(8,128)(2,1)S(1)}, u32[]{:S(2)}, u32[]{:S(2)}) collective-permute-start(bf16[8,8,1024]{2,1,0:T(8,128)(2,1)S(1)} %get-tuple-element.30), channel_id=1, source_target_pairs={{0,24},{8,16},{16,8},{24,0},{1,25},{9,17},{17,9},{25,1},{2,26},{10... | collective-permute-start | bytes 393224 | tf_op jit(solution)/shard_map/ppermute | solution.py:398
  38.3 1.3 %collective-permute-start.8 = (bf16[32,1024]{1,0:T(8,128)(2,1)S(1)}, bf16[32,1024]{1,0:T(8,128)(2,1)S(1)}, u32[]{:S(2)}, u32[]{:S(2)}) collective-permute-start(bf16[32,1024]{1,0:T(8,128)(2,1)S(1)} %pad_maximum_fusion), channel_id=1, source_target_pairs={{0,1},{1,0},{2,3},{3,2},{4,5},{5,4},{6,7},{7,6},{8,9},{9,8},{10,11... | collective-permute-start | bytes 196616 | tf_op jit(solution)/shard_map/ppermute | solution.py:398
  39.6 9.1 %collective-permute-start.11 = (bf16[16,1024]{1,0:T(8,128)(2,1)S(1)}, bf16[16,1024]{1,0:T(8,128)(2,1)S(1)}, u32[]{:S(2)}, u32[]{:S(2)}) collective-permute-start(bf16[16,1024]{1,0:T(8,128)(2,1)S(1)} %pad_maximum_fusion.3), channel_id=1, source_target_pairs={{0,6},{1,7},{2,4},{3,5},{4,2},{5,3},{6,0},{7,1},{8,14},{9,15},{10,... | collective-permute-start | bytes 98312 | tf_op jit(solution)/shard_map/ppermute | solution.py:398
  42.0 3.9 %collective-permute-start.9 = (bf16[16,1024]{1,0:T(8,128)(2,1)S(1)}, bf16[16,1024]{1,0:T(8,128)(2,1)S(1)}, u32[]{:S(2)}, u32[]{:S(2)}) collective-permute-start(bf16[16,1024]{1,0:T(8,128)(2,1)S(1)} %pad_maximum_fusion.1), channel_id=1, source_target_pairs={{0,2},{1,3},{2,0},{3,1},{4,6},{5,7},{6,4},{7,5},{8,10},{9,11},{10,... | collective-permute-start | bytes 98312 | tf_op jit(solution)/shard_map/ppermute | solution.py:398
  43.9 4.8 %collective-permute-start.10 = (bf16[16,1024]{1,0:T(8,128)(2,1)S(1)}, bf16[16,1024]{1,0:T(8,128)(2,1)S(1)}, u32[]{:S(2)}, u32[]{:S(2)}) collective-permute-start(bf16[16,1024]{1,0:T(8,128)(2,1)S(1)} %pad_maximum_fusion.2), channel_id=1, source_target_pairs={{0,4},{1,5},{2,6},{3,7},{4,0},{5,1},{6,2},{7,3},{8,12},{9,13},{10,... | collective-permute-start | bytes 98312 | tf_op jit(solution)/shard_map/ppermute | solution.py:398

commit v8 on v7

--- a/solution.py
+++ b/solution.py
@@ -47,7 +47,7 @@
 
 
 @functools.lru_cache(maxsize=None)
-def step_tables(parts, frames, channels):
+def step_tables(parts, frames, channels, own=1):
     half = STEPS // 2
     theta = 2.0 * math.pi * (np.arange(STEPS) + 0.5) / STEPS
     first = (np.arange(STEPS) < half).astype(np.float64)[:, None]
@@ -65,8 +65,8 @@
         table = table.reshape(2, STEPS, 2, used)
         for seg in range(SEGS):
             spec[kind, seg, :, :, :, seg * KEEP : seg * KEEP + used] = table
-    spec = spec.reshape(2, SEGS * 2 * STEPS, 2 * frames)
-    spec = np.stack([np.kron(np.eye(2), one) for one in spec])
+    spec = spec.reshape(2, 1, SEGS * 2 * STEPS, 2 * frames, 1) * np.eye(own)[None, :, None, None, :]
+    spec = spec.reshape(2, own * SEGS * 2 * STEPS, 2 * frames * own)
 
     resp = np.zeros((channels // 2, 2, 2, STEPS, 2, parts, channels, 2))
     for kind, table in enumerate(forward(np.arange(parts))):
@@ -110,7 +110,7 @@
     return jnp.concatenate([ref[(*index, first + i)] for i in range(LANES // SLAB)], axis=-1)
 
 
-def response_kernel(rows, bins, me_ref, room_hbm, table_hbm, hat_ref, done_ref, room_ref, table_ref, sems):
+def response_kernel(rows, bins, me_ref, room_hbm, table_hbm, hat_ref, room_ref, table_ref, sems):
     depth = room_ref.shape[1] * room_ref.shape[2] * 2
     flat = room_ref.reshape(rows, depth, bins)
     plain, packed, _ = lane_masks(0, LANES)
@@ -143,7 +143,6 @@
         return carry
 
     lax.fori_loop(0, rows // ROWS, some, 0)
-    done_ref[...] = jnp.zeros_like(done_ref)
 
 
 def transform_responses(room, me):
@@ -154,11 +153,8 @@
     return pl.pallas_call(
         functools.partial(response_kernel, rows, bins),
         in_specs=[pl.BlockSpec(memory_space=pltpu.SMEM), hbm, hbm],
-        out_specs=[pl.BlockSpec(memory_space=pltpu.VMEM)] * 2,
-        out_shape=[
-            pltpu.VMEM((rows, slabs, channels * 2 * STEPS, SLAB), BF16),
-            jax.ShapeDtypeStruct((8, 128), F32),
-        ],
+        out_specs=pl.BlockSpec(memory_space=pltpu.VMEM),
+        out_shape=pltpu.VMEM((rows, slabs, channels * 2 * STEPS, SLAB), BF16),
         scratch_shapes=[
             pltpu.VMEM(room.shape, BF16),
             pltpu.VMEM(resp.shape, BF16),
@@ -174,46 +170,41 @@
 
 
 def spectra_kernel(pieces, rows, *refs):
-    x_refs, (table_ref, spec_ref) = refs[:pieces], refs[pieces : pieces + 2]
-    out_ref = refs[-1]
+    x_refs, (table_ref, spec_ref, out_ref) = refs[:pieces], refs[pieces:]
     slabs = table_ref.shape[1]
     wide = 2 * SEGS * STEPS
-    x = jnp.concatenate([ref[...] for ref in x_refs], axis=0)
-    count = x.shape[0] // rows
-    cols = 2 * count
+    own = rows // pieces
+    span = x_refs[0].shape[0] * own
+    flat = x_refs if own == 1 else [ref.reshape(span, slabs * SLAB) for ref in x_refs]
+    x = jnp.concatenate([ref[...] for ref in flat], axis=0)
     for step in range(slabs * SLAB // LANES):
         plain, packed, sign = lane_masks(step * LANES, LANES)
         spectra = []
         for j in range(2):
             one = dot(x, two_slabs(table_ref, step, j))
-            spectra.append(one + sign * pltpu.roll(one, one.shape[0] - 1, axis=0))
-        for start in range(0, rows, 2):
-            some = range(start, min(start + 2, rows))
-            n = len(some)
-            both = [s[r * count : (r + 1) * count] for r in some for s in spectra]
+            spectra.append(one + sign * pltpu.roll(one, one.shape[0] - own, axis=0))
+        for piece in range(pieces):
+            both = [s[piece * span : (piece + 1) * span] for s in spectra]
             both = jnp.concatenate(both, axis=0)
-            spec = [spec_ref[kind, : n * wide, : n * cols] for kind in range(2)]
             if step == 0:
-                hat = dot(spec[0], (both * plain).astype(BF16)) + dot(spec[1], (both * packed).astype(BF16))
+                hat = dot(spec_ref[0], (both * plain).astype(BF16)) + dot(spec_ref[1], (both * packed).astype(BF16))
             else:
-                hat = dot(spec[0], both.astype(BF16))
+                hat = dot(spec_ref[0], both.astype(BF16))
             hat = hat.astype(BF16)
-            for k, r in enumerate(some):
+            for k in range(own):
                 for i in range(LANES // SLAB):
                     at = slice(i * SLAB, (i + 1) * SLAB)
-                    out_ref[step * (LANES // SLAB) + i, r] = hat[k * wide : (k + 1) * wide, at]
-
-
-def transform_signals(x_list, own, bins, parts, after=None):
+                    out_ref[step * (LANES // SLAB) + i, piece * own + k] = hat[k * wide : (k + 1) * wide, at]
+
+
+def transform_signals(x_list, own, bins, parts):
     frames = parts + SEGS * KEEP
     rows = own * len(x_list)
     slabs = bins // SLAB
     table, _ = block_tables(bins)
-    spec, _, _ = step_tables(parts, frames, 2)
+    spec, _, _ = step_tables(parts, frames, 2, own)
     vmem = pl.BlockSpec(memory_space=pltpu.VMEM)
     operands = [*x_list, jnp.asarray(table), jnp.asarray(spec)]
-    if after is not None:
-        operands.append(after)
     return pl.pallas_call(
         functools.partial(spectra_kernel, len(x_list), rows),
         in_specs=[vmem] * len(operands),
@@ -392,39 +383,43 @@
     src_me = lax.axis_index("src").astype(jnp.int32)
     ch_me = lax.axis_index("ch").astype(jnp.int32)
 
-    x_own = dry_signal.reshape(own * frames, block_len)
+    if own == 1:
+        x_own = dry_signal.reshape(frames, block_len)
+    else:
+        x_own = dry_signal.reshape(own, frames, block_len).transpose(1, 0, 2)
 
     def swap(value, axis, count, flip):
         return lax.ppermute(value, axis, [(i, i ^ flip) for i in range(count)])
 
     chips = ch_count // 2
-    lanes = [swap(x_own, "ch", ch_count, 2 * d) for d in range(1, chips)]
+    first = chips // 2
+    lanes = {first: swap(x_own, "ch", ch_count, 2 * first)}
+    me = jnp.stack([src_me, ch_me])
+    hat = transform_responses(room_spectra, me)
+    x_own, hat = lax.optimization_barrier((x_own, hat))
+    rest = [d for d in range(chips - 1, 0, -1) if d != first]
+    lanes.update({d: swap(x_own, "ch", ch_count, 2 * d) for d in rest})
 
     row = jnp.arange(ch_count * channels, dtype=jnp.int32)
     takes = ((row // channels) ^ ch_me) * channels + row % channels
     order = (takes[:, None] == row[None, :]).astype(BF16)
     own_order = dot(order, decoder).astype(BF16)
 
-    me = jnp.stack([src_me, ch_me])
-    hat, done = transform_responses(room_spectra, me)
-
     def add(s_list, flips, total, last):
         return add_sources(
             s_list, flips, own, me, render_slot, hat, total, last, src_count, channels, parts
         )
 
-    def transform(x_list, after=None):
-        mine = transform_signals(x_list, own, block_len, parts, after)
+    def transform(x_list):
+        mine = transform_signals(x_list, own, block_len, parts)
         return mine, swap(mine, "ch", ch_count, 1)
 
-    near, far = range(0, 2), range(2, chips)
-    near_mine, near_given = transform([x_own, lanes[0]], done)
-    total = add([near_mine], [[2 * d for d in near]], None, False)
-    *late, total = lax.optimization_barrier((*lanes[1:], total))
+    near_mine, near_given = transform([x_own, lanes[first]])
+    total = add([near_mine], [[0, 2 * first]], None, False)
+    *late, total = lax.optimization_barrier((*[lanes[d] for d in rest], total))
     far_mine, far_given = transform(late)
-    flips = [[2 * d + 1 for d in near], [2 * d for d in far]]
-    total = add([near_given, far_mine], flips, total, False)
-    total = add([far_given], [[2 * d + 1 for d in far]], total, True)
+    total = add([near_given, far_mine], [[1, 2 * first + 1], [2 * d for d in rest]], total, False)
+    total = add([far_given], [[2 * d + 1 for d in rest]], total, True)
 
     parts_in = [total[0]] + [swap(total[d], "src", src_count, d) for d in range(1, src_count)]
     each = blocks // src_count

time: 51.1 us -> 51.1 us (level)
  local copies, waits for them, and re-layouts: 1.12 us -> 0.05 us
  waiting for transfers between devices: 14.9 us -> 15.9 us
    reshape x1 -> x0, local copies, waits for them, and re-layouts: 1.08 us -> none  [per_device(): x_own = dry_signal.reshape(own * frames, block_len)]
    ppermute x12, waiting for transfers between devices: 14.9 us -> 15.9 us  [swap(): return lax.ppermute(value, axis, [(i, i ^ flip) for i in range(count)])]
  transfers between devices with their start and end apart: 12 -> 12, of which waited for: 6 -> 7; matrix products, arithmetic and copies ran while one was open for 0% -> 0% of each run, Pallas kernels for 28% -> 28%
where the time goes in v8:
time: 51.1 us; the launch traced here: 51 us
  Pallas kernels  18.5 us (36%)
  waiting for transfers between devices  15.9 us (31%)
  starting transfers between devices  14 us (27%)
  matrix products  2.21 us (4%)
    ppermute x12, waiting for transfers between devices, swap(): return lax.ppermute(value, axis, [(i, i ^ flip) for i in range(count)])  15.9 us
    ppermute x12, starting transfers between devices, swap(): return lax.ppermute(value, axis, [(i, i ^ flip) for i in range(count)])  14 us
    pallas_call x3, Pallas kernels, add_sources(): pl.pallas_call(body, in_specs=[smem, smem] + [vmem] * (len(operands) - 2)...  8.34 us
    pallas_call x1, Pallas kernels, transform_responses(): pl.pallas_call(functools.partial(response_kernel, rows, bins), in_specs=[...  6.4 us
    pallas_call x2, Pallas kernels, transform_signals(): pl.pallas_call(functools.partial(spectra_kernel, len(x_list), rows), in_s...  3.34 us
    dot_general x1, matrix products, per_device(): lax.dot_general(gathered, matrix, (((0,), (0,)), ((), ())), preferred_ele...  2.21 us
  transfers between devices with their start and end apart: 12, of which 7 were waited for; matrix products, arithmetic and copies ran while one was open for 0% of the time, Pallas kernels for 28%

profile of v8, /device:TPU:0, one launch (start us, length us, event | category | flops | bytes accessed | tf_op | source)
XLA Modules:
  0.0 51.0 jit_solution(11977262075284656094)
XLA Ops:
  0.0 0.0 copy-start
  0.0 4.0 %collective-permute-start.2 = (bf16[40,2,1024]{2,1,0:T(2,128)(2,1)}, bf16[40,2,1024]{2,1,0:T(2,128)(2,1)S(1)}, u32[]{:S(2)}, u32[]{:S(2)}) collective-permute-start(bf16[40,2,1024]{2,1,0:T(2,128)(2,1)} %bitcast.7), channel_id=1, source_target_pairs={{0,4},{1,5},{2,6},{3,7},{4,0},{5,1},{6,2},{7,3},{8,12},{9,13},{10,... | collective-permute-start | bytes 491528 | tf_op jit(solution)/shard_map/ppermute | solution.py:392
  4.0 0.1 pad_add_fusion.me_ref
  4.1 0.0 copy-start.4
  4.1 0.0 copy-start.1
  4.1 0.0 copy-start.3
  4.1 6.4 %shard_map.91.refs_1_.refs_2_ = bf16[16,8,384,128]{3,2,1,0:T(8,128)(2,1)S(1)} custom-call(s32[2]{0:T(128)S(1)} %pad_add_fusion.me_ref, bf16[16,8,8,2,1024]{4,3,2,1,0:T(2,128)(2,1)} %room_hbm.1, bf16[384,256]{1,0:T(8,128)(2,1)} %constant.50.clone.table_hbm), custom_call_target="tpu_custom_call" | custom-call | flops 1048576 | bytes 65536 | tf_op jit(solution)/shard_map/pallas_call | solution.py:153
  10.5 0.0 copy-done.4
  10.5 0.0 copy-start.6
  10.6 1.4 %collective-permute-start = (bf16[40,2,1024]{2,1,0:T(2,128)(2,1)S(1)}, bf16[40,2,1024]{2,1,0:T(2,128)(2,1)S(1)}, u32[]{:S(2)}, u32[]{:S(2)}) collective-permute-start(bf16[40,2,1024]{2,1,0:T(2,128)(2,1)S(1)} %bitcast.8), channel_id=1, source_target_pairs={{0,6},{1,7},{2,4},{3,5},{4,2},{5,3},{6,0},{7,1},{8,14},{9,15},{10,... | collective-permute-start | bytes 491528 | tf_op jit(solution)/shard_map/ppermute | solution.py:392
  12.0 0.3 collective-permute-start.1
  12.3 0.0 collective-permute-done.2.refs_1_
  12.3 0.0 copy-done.1
  12.3 0.0 copy-done.3
  12.3 1.7 %shard_map.92.refs_0_ = bf16[8,4,96,128]{3,2,1,0:T(8,128)(2,1)S(1)} custom-call(bf16[40,2,1024]{2,1,0:T(2,128)(2,1)S(1)} %bitcast.10, bf16[40,2,1024]{2,1,0:T(2,128)(2,1)S(1)} %collective-permute-done.2.refs_1_, bf16[2,8,1024,128]{3,2,1,0:T(8,128)(2,1)S(1)} %copy-done.1, bf16[2,192,160]{2,1,0:T(8,128)(2,1)S(1)} %copy-done.3), custom_call_target="tpu_custom_call" | custom-call | flops 1048576 | bytes 65536 | tf_op jit(solution)/shard_map/pallas_call | solution.py:208
  14.0 0.1 collective-permute-start.4
  14.0 0.0 copy-done.6
  14.1 1.5 %shard_map.93.refs_3_ = f32[8,4,192,128]{3,2,1,0:T(8,128)S(1)} custom-call(s32[2]{0:T(128)S(1)} %pad_add_fusion.me_ref, s32[16]{0:T(128)S(1)} %copy-done.6, bf16[8,4,96,128]{3,2,1,0:T(8,128)(2,1)S(1)} %shard_map.92.refs_0_, bf16[16,8,384,128]{3,2,1,0:T(8,128)(2,1)S(1)} %shard_map.91.refs_1_.refs_2_), custom_call_target="tpu_custom_call" | custom-call | flops 1048576 | bytes 65536 | tf_op jit(solution)/shard_map/pallas_call | solution.py:343
  15.6 3.9 %collective-permute-done.refs_0_ = bf16[40,2,1024]{2,1,0:T(2,128)(2,1)S(1)} collective-permute-done((bf16[40,2,1024]{2,1,0:T(2,128)(2,1)S(1)}, bf16[40,2,1024]{2,1,0:T(2,128)(2,1)S(1)}, u32[]{:S(2)}, u32[]{:S(2)}) %collective-permute-start) | collective-permute-done | bytes 163872 | tf_op jit(solution)/shard_map/ppermute | solution.py:392
  19.5 1.3 %collective-permute-done.1.refs_1_ = bf16[40,2,1024]{2,1,0:T(2,128)(2,1)S(1)} collective-permute-done((bf16[40,2,1024]{2,1,0:T(2,128)(2,1)S(1)}, bf16[40,2,1024]{2,1,0:T(2,128)(2,1)S(1)}, u32[]{:S(2)}, u32[]{:S(2)}) %collective-permute-start.1) | collective-permute-done | bytes 163872 | tf_op jit(solution)/shard_map/ppermute | solution.py:392
  20.9 1.7 %shard_map.94.refs_1_ = bf16[8,4,96,128]{3,2,1,0:T(8,128)(2,1)S(1)} custom-call(bf16[40,2,1024]{2,1,0:T(2,128)(2,1)S(1)} %collective-permute-done.refs_0_, bf16[40,2,1024]{2,1,0:T(2,128)(2,1)S(1)} %collective-permute-done.1.refs_1_, bf16[2,8,1024,128]{3,2,1,0:T(8,128)(2,1)S(1)} %copy-done.1, bf16[2,192,160]{2,1,0:T(8,128)(2,1)S(1)} %copy-done.3), custom_call_target="tpu_custom_call" | custom-call | flops 1048576 | bytes 65536 | tf_op jit(solution)/shard_map/pallas_call | solution.py:208
  22.5 0.0 copy-start.2
  22.5 0.0 copy-start.5
  22.6 0.1 collective-permute-start.3
  22.6 0.0 collective-permute-done.4.refs_0_
  22.7 3.1 %shard_map.95.refs_2_ = f32[8,4,192,128]{3,2,1,0:T(8,128)S(1)} custom-call(s32[2]{0:T(128)S(1)} %pad_add_fusion.me_ref, s32[16]{0:T(128)S(1)} %copy-done.6, bf16[8,4,96,128]{3,2,1,0:T(8,128)(2,1)S(1)} %collective-permute-done.4.refs_0_, bf16[8,4,96,128]{3,2,1,0:T(8,128)(2,1)S(1)} %shard_map.94.refs_1_, ...), custom_call_target="tpu_custom_call", output_to_operand_aliasing={{}: (5, {})} | custom-call | flops 1048576 | bytes 65536 | tf_op jit(solution)/shard_map/pallas_call | solution.py:343
  25.8 0.0 collective-permute-done.3.refs_0_
  25.8 0.0 copy-done.2
  25.8 0.0 copy-done.5
  25.8 3.7 %shard_map.96 = (bf16[8,8,1024]{2,1,0:T(8,128)(2,1)S(1)}, bf16[8,8,1024]{2,1,0:T(8,128)(2,1)S(1)}, bf16[8,8,1024]{2,1,0:T(8,128)(2,1)S(1)}, bf16[8,8,1024]{2,1,0:T(8,128)(2,1)S(1)}) custom-call(s32[2]{0:T(128)S(1)} %pad_add_fusion.me_ref, s32[16]{0:T(128)S(1)} %copy-done.6, bf16[8,4,96,128]{3,2,1,0:T(8,128)(2,1)S(1)} %collective-permute-done.3.refs_0_, ...), custom_call_target="tpu_custom_call" | custom-call | flops 1048576 | bytes 65536 | tf_op jit(solution)/shard_map/pallas_call | solution.py:343
  29.5 1.6 %collective-permute-start.5 = (bf16[8,8,1024]{2,1,0:T(8,128)(2,1)S(1)}, bf16[8,8,1024]{2,1,0:T(8,128)(2,1)S(1)}, u32[]{:S(2)}, u32[]{:S(2)}) collective-permute-start(bf16[8,8,1024]{2,1,0:T(8,128)(2,1)S(1)} %get-tuple-element.28), channel_id=1, source_target_pairs={{0,8},{8,0},{16,24},{24,16},{1,9},{9,1},{17,25},{25,17},{2,10},{10... | collective-permute-start | bytes 393224 | tf_op jit(solution)/shard_map/ppermute | solution.py:392
  31.0 1.5 %collective-permute-start.6 = (bf16[8,8,1024]{2,1,0:T(8,128)(2,1)S(1)}, bf16[8,8,1024]{2,1,0:T(8,128)(2,1)S(1)}, u32[]{:S(2)}, u32[]{:S(2)}) collective-permute-start(bf16[8,8,1024]{2,1,0:T(8,128)(2,1)S(1)} %get-tuple-element.29), channel_id=1, source_target_pairs={{0,16},{8,24},{16,0},{24,8},{1,17},{9,25},{17,1},{25,9},{2,18},{10... | collective-permute-start | bytes 393224 | tf_op jit(solution)/shard_map/ppermute | solution.py:392
  32.6 0.5 collective-permute-start.7
  33.1 2.8 %collective-permute-done.5.refs_1_ = bf16[8,8,1024]{2,1,0:T(8,128)(2,1)S(1)} collective-permute-done((bf16[8,8,1024]{2,1,0:T(8,128)(2,1)S(1)}, bf16[8,8,1024]{2,1,0:T(8,128)(2,1)S(1)}, u32[]{:S(2)}, u32[]{:S(2)}) %collective-permute-start.5) | collective-permute-done | bytes 131104 | tf_op jit(solution)/shard_map/ppermute | solution.py:392
  35.9 3.6 %collective-permute-done.6.refs_2_ = bf16[8,8,1024]{2,1,0:T(8,128)(2,1)S(1)} collective-permute-done((bf16[8,8,1024]{2,1,0:T(8,128)(2,1)S(1)}, bf16[8,8,1024]{2,1,0:T(8,128)(2,1)S(1)}, u32[]{:S(2)}, u32[]{:S(2)}) %collective-permute-start.6) | collective-permute-done | bytes 131104 | tf_op jit(solution)/shard_map/ppermute | solution.py:392
  39.5 0.0 collective-permute-done.7.refs_3_
  39.5 0.5 shard_map.97
  39.9 0.1 collective-permute-start.8
  40.0 1.2 %collective-permute-done.8 = bf16[32,1024]{1,0:T(8,128)(2,1)S(1)} collective-permute-done((bf16[32,1024]{1,0:T(8,128)(2,1)S(1)}, bf16[32,1024]{1,0:T(8,128)(2,1)S(1)}, u32[]{:S(2)}, u32[]{:S(2)}) %collective-permute-start.8) | collective-permute-done | bytes 65568 | tf_op jit(solution)/shard_map/ppermute | solution.py:392
  41.3 2.2 %collective-permute-start.11 = (bf16[16,1024]{1,0:T(8,128)(2,1)S(1)}, bf16[16,1024]{1,0:T(8,128)(2,1)S(1)}, u32[]{:S(2)}, u32[]{:S(2)}) collective-permute-start(bf16[16,1024]{1,0:T(8,128)(2,1)S(1)} %pad_maximum_fusion.3), channel_id=1, source_target_pairs={{0,6},{1,7},{2,4},{3,5},{4,2},{5,3},{6,0},{7,1},{8,14},{9,15},{10,... | collective-permute-start | bytes 98312 | tf_op jit(solution)/shard_map/ppermute | solution.py:392
  43.5 0.0 collective-permute-start.9
  43.5 2.2 %collective-permute-start.10 = (bf16[16,1024]{1,0:T(8,128)(2,1)S(1)}, bf16[16,1024]{1,0:T(8,128)(2,1)S(1)}, u32[]{:S(2)}, u32[]{:S(2)}) collective-permute-start(bf16[16,1024]{1,0:T(8,128)(2,1)S(1)} %pad_maximum_fusion.2), channel_id=1, source_target_pairs={{0,4},{1,5},{2,6},{3,7},{4,0},{5,1},{6,2},{7,3},{8,12},{9,13},{10,... | collective-permute-start | bytes 98312 | tf_op jit(solution)/shard_map/ppermute | solution.py:392
  45.7 2.0 %collective-permute-done.9 = bf16[16,1024]{1,0:T(8,128)(2,1)S(1)} collective-permute-done((bf16[16,1024]{1,0:T(8,128)(2,1)S(1)}, bf16[16,1024]{1,0:T(8,128)(2,1)S(1)}, u32[]{:S(2)}, u32[]{:S(2)}) %collective-permute-start.9) | collective-permute-done | bytes 32800 | tf_op jit(solution)/shard_map/ppermute | solution.py:392
  47.8 1.0 %collective-permute-done.10 = bf16[16,1024]{1,0:T(8,128)(2,1)S(1)} collective-permute-done((bf16[16,1024]{1,0:T(8,128)(2,1)S(1)}, bf16[16,1024]{1,0:T(8,128)(2,1)S(1)}, u32[]{:S(2)}, u32[]{:S(2)}) %collective-permute-start.10) | collective-permute-done | bytes 32800 | tf_op jit(solution)/shard_map/ppermute | solution.py:392
  48.8 0.0 collective-permute-done.11
  48.8 0.0 copy-done
  48.8 2.2 %convolution_convert_fusion = bf16[1024,1024]{1,0:T(8,128)(2,1)} fusion(bf16[64,1024]{1,0:T(8,128)(2,1)S(1)} %constant_dynamic-update-slice_fusion, bf16[64,1024]{1,0:T(8,128)(2,1)S(1)} %copy-done, s32[64]{0:T(128)S(1)} %fusion.2), kind=kOutput, calls=%fused_computation | convolution fusion | flops 143724544 | bytes 2359552 | tf_op jit(solution)/shard_map/dot_general | solution.py:443
  (10 shorter events, 0.0 us)
Async XLA Ops:
  0.0 48.8 %copy-start = (bf16[64,1024]{1,0:T(8,128)(2,1)S(1)}, bf16[64,1024]{1,0:T(8,128)(2,1)}, u32[]{:S(2)}) copy-start(bf16[64,1024]{1,0:T(8,128)(2,1)} %param.12) | copy-start | bytes 393220
  0.0 12.3 %collective-permute-start.2 = (bf16[40,2,1024]{2,1,0:T(2,128)(2,1)}, bf16[40,2,1024]{2,1,0:T(2,128)(2,1)S(1)}, u32[]{:S(2)}, u32[]{:S(2)}) collective-permute-start(bf16[40,2,1024]{2,1,0:T(2,128)(2,1)} %bitcast.7), channel_id=1, source_target_pairs={{0,4},{1,5},{2,6},{3,7},{4,0},{5,1},{6,2},{7,3},{8,12},{9,13},{10,... | collective-permute-start | bytes 491528 | tf_op jit(solution)/shard_map/ppermute | solution.py:392
  4.1 6.4 %copy-start.4 = (bf16[2,40960]{1,0:T(2,128)(2,1)S(1)}, bf16[2,40960]{1,0:T(2,128)(2,1)}, u32[]{:S(2)}) copy-start(bf16[2,40960]{1,0:T(2,128)(2,1)} %param.9) | copy-start | bytes 491524
  4.1 8.2 %copy-start.1 = (bf16[2,8,1024,128]{3,2,1,0:T(8,128)(2,1)S(1)}, bf16[2,8,1024,128]{3,2,1,0:T(8,128)(2,1)}, u32[]{:S(2)}) copy-start(bf16[2,8,1024,128]{3,2,1,0:T(8,128)(2,1)} %constant.51.clone.refs_2_) | copy-start | bytes 12582916
  4.1 8.2 %copy-start.3 = (bf16[2,192,160]{2,1,0:T(8,128)(2,1)S(1)}, bf16[2,192,160]{2,1,0:T(8,128)(2,1)}, u32[]{:S(2)}) copy-start(bf16[2,192,160]{2,1,0:T(8,128)(2,1)} %constant.52.clone.refs_3_) | copy-start | bytes 368644
  10.5 3.5 %copy-start.6 = (s32[16]{0:T(128)S(1)}, s32[16]{0:T(128)}, u32[]{:S(2)}) copy-start(s32[16]{0:T(128)} %slot_ref.5) | copy-start | bytes 196
  10.6 9.0 %collective-permute-start = (bf16[40,2,1024]{2,1,0:T(2,128)(2,1)S(1)}, bf16[40,2,1024]{2,1,0:T(2,128)(2,1)S(1)}, u32[]{:S(2)}, u32[]{:S(2)}) collective-permute-start(bf16[40,2,1024]{2,1,0:T(2,128)(2,1)S(1)} %bitcast.8), channel_id=1, source_target_pairs={{0,6},{1,7},{2,4},{3,5},{4,2},{5,3},{6,0},{7,1},{8,14},{9,15},{10,... | collective-permute-start | bytes 491528 | tf_op jit(solution)/shard_map/ppermute | solution.py:392
  12.0 8.9 %collective-permute-start.1 = (bf16[40,2,1024]{2,1,0:T(2,128)(2,1)S(1)}, bf16[40,2,1024]{2,1,0:T(2,128)(2,1)S(1)}, u32[]{:S(2)}, u32[]{:S(2)}) collective-permute-start(bf16[40,2,1024]{2,1,0:T(2,128)(2,1)S(1)} %bitcast.9), channel_id=1, source_target_pairs={{0,2},{1,3},{2,0},{3,1},{4,6},{5,7},{6,4},{7,5},{8,10},{9,11},{10,... | collective-permute-start | bytes 491528 | tf_op jit(solution)/shard_map/ppermute | solution.py:392
  14.0 8.7 %collective-permute-start.4 = (bf16[8,4,96,128]{3,2,1,0:T(8,128)(2,1)S(1)}, bf16[8,4,96,128]{3,2,1,0:T(8,128)(2,1)S(1)}, u32[]{:S(2)}, u32[]{:S(2)}) collective-permute-start(bf16[8,4,96,128]{3,2,1,0:T(8,128)(2,1)S(1)} %shard_map.92.refs_0_), channel_id=1, source_target_pairs={{0,1},{1,0},{2,3},{3,2},{4,5},{5,4},{6,7},{7,6},{8,9},{9,8},{10,11... | collective-permute-start | bytes 2359304 | tf_op jit(solution)/shard_map/ppermute | solution.py:392
  22.5 3.2 %copy-start.2 = (bf16[2,8,1024,128]{3,2,1,0:T(8,128)(2,1)S(1)}, bf16[2,8,1024,128]{3,2,1,0:T(8,128)(2,1)}, u32[]{:S(2)}) copy-start(bf16[2,8,1024,128]{3,2,1,0:T(8,128)(2,1)} %constant.54.clone.refs_4_) | copy-start | bytes 12582916
  22.5 3.2 %copy-start.5 = (bf16[2,128,192]{2,1,0:T(8,128)(2,1)S(1)}, bf16[2,128,192]{2,1,0:T(8,128)(2,1)}, u32[]{:S(2)}) copy-start(bf16[2,128,192]{2,1,0:T(8,128)(2,1)} %constant.53.clone.refs_3_) | copy-start | bytes 294916
  22.6 3.2 %collective-permute-start.3 = (bf16[8,4,96,128]{3,2,1,0:T(8,128)(2,1)S(1)}, bf16[8,4,96,128]{3,2,1,0:T(8,128)(2,1)S(1)}, u32[]{:S(2)}, u32[]{:S(2)}) collective-permute-start(bf16[8,4,96,128]{3,2,1,0:T(8,128)(2,1)S(1)} %shard_map.94.refs_1_), channel_id=1, source_target_pairs={{0,1},{1,0},{2,3},{3,2},{4,5},{5,4},{6,7},{7,6},{8,9},{9,8},{10,11... | collective-permute-start | bytes 2359304 | tf_op jit(solution)/shard_map/ppermute | solution.py:392
  29.5 6.4 %collective-permute-start.5 = (bf16[8,8,1024]{2,1,0:T(8,128)(2,1)S(1)}, bf16[8,8,1024]{2,1,0:T(8,128)(2,1)S(1)}, u32[]{:S(2)}, u32[]{:S(2)}) collective-permute-start(bf16[8,8,1024]{2,1,0:T(8,128)(2,1)S(1)} %get-tuple-element.28), channel_id=1, source_target_pairs={{0,8},{8,0},{16,24},{24,16},{1,9},{9,1},{17,25},{25,17},{2,10},{10... | collective-permute-start | bytes 393224 | tf_op jit(solution)/shard_map/ppermute | solution.py:392
  31.0 8.4 %collective-permute-start.6 = (bf16[8,8,1024]{2,1,0:T(8,128)(2,1)S(1)}, bf16[8,8,1024]{2,1,0:T(8,128)(2,1)S(1)}, u32[]{:S(2)}, u32[]{:S(2)}) collective-permute-start(bf16[8,8,1024]{2,1,0:T(8,128)(2,1)S(1)} %get-tuple-element.29), channel_id=1, source_target_pairs={{0,16},{8,24},{16,0},{24,8},{1,17},{9,25},{17,1},{25,9},{2,18},{10... | collective-permute-start | bytes 393224 | tf_op jit(solution)/shard_map/ppermute | solution.py:392
  32.6 6.9 %collective-permute-start.7 = (bf16[8,8,1024]{2,1,0:T(8,128)(2,1)S(1)}, bf16[8,8,1024]{2,1,0:T(8,128)(2,1)S(1)}, u32[]{:S(2)}, u32[]{:S(2)}) collective-permute-start(bf16[8,8,1024]{2,1,0:T(8,128)(2,1)S(1)} %get-tuple-element.30), channel_id=1, source_target_pairs={{0,24},{8,16},{16,8},{24,0},{1,25},{9,17},{17,9},{25,1},{2,26},{10... | collective-permute-start | bytes 393224 | tf_op jit(solution)/shard_map/ppermute | solution.py:392
  39.9 1.3 %collective-permute-start.8 = (bf16[32,1024]{1,0:T(8,128)(2,1)S(1)}, bf16[32,1024]{1,0:T(8,128)(2,1)S(1)}, u32[]{:S(2)}, u32[]{:S(2)}) collective-permute-start(bf16[32,1024]{1,0:T(8,128)(2,1)S(1)} %pad_maximum_fusion), channel_id=1, source_target_pairs={{0,1},{1,0},{2,3},{3,2},{4,5},{5,4},{6,7},{7,6},{8,9},{9,8},{10,11... | collective-permute-start | bytes 196616 | tf_op jit(solution)/shard_map/ppermute | solution.py:392
  41.3 7.5 %collective-permute-start.11 = (bf16[16,1024]{1,0:T(8,128)(2,1)S(1)}, bf16[16,1024]{1,0:T(8,128)(2,1)S(1)}, u32[]{:S(2)}, u32[]{:S(2)}) collective-permute-start(bf16[16,1024]{1,0:T(8,128)(2,1)S(1)} %pad_maximum_fusion.3), channel_id=1, source_target_pairs={{0,6},{1,7},{2,4},{3,5},{4,2},{5,3},{6,0},{7,1},{8,14},{9,15},{10,... | collective-permute-start | bytes 98312 | tf_op jit(solution)/shard_map/ppermute | solution.py:392
  43.5 4.2 %collective-permute-start.9 = (bf16[16,1024]{1,0:T(8,128)(2,1)S(1)}, bf16[16,1024]{1,0:T(8,128)(2,1)S(1)}, u32[]{:S(2)}, u32[]{:S(2)}) collective-permute-start(bf16[16,1024]{1,0:T(8,128)(2,1)S(1)} %pad_maximum_fusion.1), channel_id=1, source_target_pairs={{0,2},{1,3},{2,0},{3,1},{4,6},{5,7},{6,4},{7,5},{8,10},{9,11},{10,... | collective-permute-start | bytes 98312 | tf_op jit(solution)/shard_map/ppermute | solution.py:392
  43.5 5.2 %collective-permute-start.10 = (bf16[16,1024]{1,0:T(8,128)(2,1)S(1)}, bf16[16,1024]{1,0:T(8,128)(2,1)S(1)}, u32[]{:S(2)}, u32[]{:S(2)}) collective-permute-start(bf16[16,1024]{1,0:T(8,128)(2,1)S(1)} %pad_maximum_fusion.2), channel_id=1, source_target_pairs={{0,4},{1,5},{2,6},{3,7},{4,0},{5,1},{6,2},{7,3},{8,12},{9,13},{10,... | collective-permute-start | bytes 98312 | tf_op jit(solution)/shard_map/ppermute | solution.py:392

commit v9 on v8

--- a/solution.py
+++ b/solution.py
@@ -215,14 +215,22 @@
     )(*operands)
 
 
-def mix_kernel(flips, own, channels, blocks, shares, has_total, last, me_ref, slot_ref, *refs):
+def first_axis(ch):
+    return 1 + ch % 2
+
+
+def second_axis(ch):
+    return 2 - ch % 2
+
+
+def mix_kernel(flips, own, channels, blocks, shares, staged, has_total, last, me_ref, slot_ref, *refs):
     refs = list(refs)
     s_refs = [refs.pop(0) for _ in flips]
     hat_ref = refs.pop(0)
     total_ref = refs.pop(0) if has_total else None
     if last:
         back_ref, inv_ref = refs.pop(0), refs.pop(0)
-        out_refs = [refs.pop(0) for _ in range(shares)]
+        out_refs = [refs.pop(0) for _ in range(3 if staged else shares)]
         y_ref, left_re, left_im, time_ref = refs
     else:
         (out_ref,) = refs
@@ -303,11 +311,18 @@
                 for c in range(channels):
                     row = c * blocks + t * each
                     time_ref[t, c, :, here] = part[row : row + each]
-        for d in range(shares):
-            out_refs[d][...] = time_ref[me_ref[0] ^ d].astype(BF16)
-
-
-def add_sources(s_list, flips, own, me, slots, hat, total, last, shares, channels, parts):
+        if staged:
+            near, other = first_axis(me_ref[1]), second_axis(me_ref[1])
+            out_refs[0][0] = time_ref[me_ref[0] ^ near].astype(BF16)
+            out_refs[0][1] = time_ref[me_ref[0] ^ 3].astype(BF16)
+            out_refs[1][...] = time_ref[me_ref[0] ^ other].astype(BF16)
+            out_refs[2][...] = time_ref[me_ref[0]].astype(BF16)
+        else:
+            for d in range(shares):
+                out_refs[d][...] = time_ref[me_ref[0] ^ d].astype(BF16)
+
+
+def add_sources(s_list, flips, own, me, slots, hat, total, last, shares, staged, channels, parts):
     slabs = hat.shape[1]
     bins = slabs * SLAB
     frames = parts + SEGS * KEEP
@@ -328,7 +343,9 @@
     if last:
         operands += [jnp.asarray(back), jnp.asarray(inverse)]
         each = blocks // shares
-        out_shape = [jax.ShapeDtypeStruct((channels, each, bins), BF16)] * shares
+        share = (channels, each, bins)
+        shapes = [(2, *share), share, share] if staged else [share] * shares
+        out_shape = [jax.ShapeDtypeStruct(shape, BF16) for shape in shapes]
         scratch = [
             pltpu.VMEM((slabs, channels // 2, 2 * wide, SLAB), BF16),
             pltpu.VMEM((channels * blocks, bins), BF16),
@@ -338,12 +355,12 @@
     else:
         out_shape = jax.ShapeDtypeStruct((slabs, channels // 2, 2 * wide, SLAB), F32)
     body = functools.partial(
-        mix_kernel, tuple(flips), own, channels, blocks, shares, total is not None, last
+        mix_kernel, tuple(flips), own, channels, blocks, shares, staged, total is not None, last
     )
     return pl.pallas_call(
         body,
         in_specs=[smem, smem] + [vmem] * (len(operands) - 2),
-        out_specs=[vmem] * shares if last else vmem,
+        out_specs=[vmem] * len(out_shape) if last else vmem,
         out_shape=out_shape,
         scratch_shapes=scratch,
         input_output_aliases=aliases,
@@ -352,27 +369,31 @@
     )(*operands)
 
 
-def sum_kernel(count, each, me_ref, *refs):
-    parts, outs, sum_ref = refs[:count], refs[count:-1], refs[-1]
-    total = parts[0][...].astype(F32)
-    for part in parts[1:]:
-        total = total + part[...].astype(F32)
+def sum_kernel(chips, me_ref, own_ref, first_ref, second_ref, mate_ref, *refs):
+    outs, sum_ref = refs[:-1], refs[-1]
+    total = own_ref[...].astype(F32) + first_ref[0].astype(F32) + second_ref[...].astype(F32)
     sum_ref[...] = total
-    for d in range(each):
-        outs[d][...] = sum_ref[:, pl.ds(me_ref[0] ^ d, 1), :].reshape(outs[d].shape).astype(BF16)
-
-
-def sum_groups(parts, me):
-    channels, each, bins = parts[0].shape
+
+    def piece(d):
+        return sum_ref[:, pl.ds(me_ref[0] ^ d, 1), :].reshape(outs[0].shape)
+
+    mate_ref[...] = jnp.concatenate([piece(2 * d + 1) for d in range(chips)], axis=0).astype(BF16)
+    for d in range(chips):
+        outs[d][...] = piece(2 * d).astype(BF16)
+
+
+def sum_groups(own, first, second, me, chips):
+    channels, _, bins = own.shape
     vmem = pl.BlockSpec(memory_space=pltpu.VMEM)
     return pl.pallas_call(
-        functools.partial(sum_kernel, len(parts), each),
-        in_specs=[pl.BlockSpec(memory_space=pltpu.SMEM)] + [vmem] * len(parts),
-        out_specs=[vmem] * each,
-        out_shape=[jax.ShapeDtypeStruct((channels, bins), BF16)] * each,
-        scratch_shapes=[pltpu.VMEM(parts[0].shape, F32)],
+        functools.partial(sum_kernel, chips),
+        in_specs=[pl.BlockSpec(memory_space=pltpu.SMEM)] + [vmem] * 3,
+        out_specs=[vmem] * (chips + 1),
+        out_shape=[jax.ShapeDtypeStruct((chips * channels, bins), BF16)]
+        + [jax.ShapeDtypeStruct((channels, bins), BF16)] * chips,
+        scratch_shapes=[pltpu.VMEM(own.shape, F32)],
         compiler_params=pltpu.CompilerParams(vmem_limit_bytes=8 * 2**20),
-    )(me[None], *parts)
+    )(me[None], own, first, second)
 
 
 def per_device(src_count, ch_count, dry_signal, room_spectra, render_slot, decoder):
@@ -383,6 +404,8 @@
     src_me = lax.axis_index("src").astype(jnp.int32)
     ch_me = lax.axis_index("ch").astype(jnp.int32)
 
+    staged = src_count == 4 and blocks == src_count * ch_count
+
     if own == 1:
         x_own = dry_signal.reshape(frames, block_len)
     else:
@@ -393,12 +416,12 @@
 
     chips = ch_count // 2
     first = chips // 2
-    lanes = {first: swap(x_own, "ch", ch_count, 2 * first)}
+    lanes = {d: swap(x_own, "ch", ch_count, 2 * d) for d in (first, *range(1, first))}
     me = jnp.stack([src_me, ch_me])
     hat = transform_responses(room_spectra, me)
-    x_own, hat = lax.optimization_barrier((x_own, hat))
-    rest = [d for d in range(chips - 1, 0, -1) if d != first]
-    lanes.update({d: swap(x_own, "ch", ch_count, 2 * d) for d in rest})
+    lanes[first], hat = lax.optimization_barrier((lanes[first], hat))
+    lanes.update({first ^ d: swap(lanes[first], "ch", ch_count, 2 * d) for d in range(1, first)})
+    rest = [d for d in range(1, chips) if d not in (1, first)]
 
     row = jnp.arange(ch_count * channels, dtype=jnp.int32)
     takes = ((row // channels) ^ ch_me) * channels + row % channels
@@ -407,36 +430,49 @@
 
     def add(s_list, flips, total, last):
         return add_sources(
-            s_list, flips, own, me, render_slot, hat, total, last, src_count, channels, parts
+            s_list, flips, own, me, render_slot, hat, total, last, src_count, staged, channels, parts
         )
 
     def transform(x_list):
         mine = transform_signals(x_list, own, block_len, parts)
         return mine, swap(mine, "ch", ch_count, 1)
 
-    near_mine, near_given = transform([x_own, lanes[first]])
-    total = add([near_mine], [[0, 2 * first]], None, False)
+    near = [0, first, 1]
+    near_mine, near_given = transform([x_own, lanes[first], lanes[1]])
+    total = add([near_mine], [[2 * d for d in near]], None, False)
     *late, total = lax.optimization_barrier((*[lanes[d] for d in rest], total))
     far_mine, far_given = transform(late)
-    total = add([near_given, far_mine], [[1, 2 * first + 1], [2 * d for d in rest]], total, False)
+    flips = [[2 * d + 1 for d in near], [2 * d for d in rest]]
+    total = add([near_given, far_mine], flips, total, False)
     total = add([far_given], [[2 * d + 1 for d in rest]], total, True)
 
-    parts_in = [total[0]] + [swap(total[d], "src", src_count, d) for d in range(1, src_count)]
-    each = blocks // src_count
-    if each == ch_count:
-        pieces = sum_groups(parts_in, ch_me)
-        given = swap(jnp.concatenate(pieces[1::2], axis=0), "ch", ch_count, 1)
+    if staged:
+
+        def along(value, axis_of):
+            pairs = [
+                (src * ch_count + ch, (src ^ axis_of(ch)) * ch_count + ch)
+                for src in range(src_count)
+                for ch in range(ch_count)
+            ]
+            return lax.ppermute(value, ("src", "ch"), pairs)
+
+        goes_first, goes_second, stays = total
+        came_first = along(goes_first, first_axis)
+        goes_second = goes_second.astype(F32) + came_first[1].astype(F32)
+        came_second = along(goes_second.astype(BF16), second_axis)
+        to_mate, *pieces = sum_groups(stays, came_first, came_second, ch_me, chips)
+        given = swap(to_mate, "ch", ch_count, 1)
         both = [
-            jnp.concatenate([pieces[2 * d], given[d * channels : (d + 1) * channels]], axis=0)
+            jnp.concatenate([pieces[d], given[d * channels : (d + 1) * channels]], axis=0)
             for d in range(chips)
         ]
         both[1:] = [swap(both[d], "ch", ch_count, 2 * d) for d in range(1, chips)]
         gathered = jnp.concatenate(both, axis=0)
         matrix = own_order
     else:
-        signal = parts_in[0].astype(F32)
-        for part in parts_in[1:]:
-            signal = signal + part.astype(F32)
+        signal = total[0].astype(F32)
+        for d in range(1, src_count):
+            signal = signal + swap(total[d], "src", src_count, d).astype(F32)
         signal = signal.astype(BF16).reshape(channels, -1)
         gathered = lax.all_to_all(signal, "ch", split_axis=1, concat_axis=0, tiled=True)
         matrix = decoder

time: 51.1 us -> 52.9 us (1.035)
  starting transfers between devices: 14 us -> 15.1 us
  waiting for transfers between devices: 15.9 us -> 16.5 us
    ppermute x0 -> x2, waiting for transfers between devices: none -> 8.21 us  [along(): return lax.ppermute(value, ('src', 'ch'), pairs)]
    ppermute x12 -> x9, waiting for transfers between devices: 15.9 us -> 8.32 us  [swap(): return lax.ppermute(value, axis, [(i, i ^ flip) for i in range(count)])]
    ppermute x0 -> x2, starting transfers between devices: none -> 3.26 us  [along(): return lax.ppermute(value, ('src', 'ch'), pairs)]
    ppermute x12 -> x9, starting transfers between devices: 14 us -> 11.8 us  [swap(): return lax.ppermute(value, axis, [(i, i ^ flip) for i in range(count)])]
  transfers between devices with their start and end apart: 12 -> 11, of which waited for: 7 -> 7; matrix products, arithmetic and copies ran while one was open for 0% -> 0% of each run, Pallas kernels for 28% -> 25%
where the time goes in v9:
time: 52.9 us; the launch traced here: 52.7 us
  Pallas kernels  18.5 us (35%)
  waiting for transfers between devices  16.5 us (31%)
  starting transfers between devices  15.1 us (29%)
  matrix products  2.21 us (4%)
    ppermute x9, starting transfers between devices, swap(): return lax.ppermute(value, axis, [(i, i ^ flip) for i in range(count)])  11.8 us
    ppermute x9, waiting for transfers between devices, swap(): return lax.ppermute(value, axis, [(i, i ^ flip) for i in range(count)])  8.32 us
    pallas_call x3, Pallas kernels, add_sources(): pl.pallas_call(body, in_specs=[smem, smem] + [vmem] * (len(operands) - 2)...  8.3 us
    ppermute x2, waiting for transfers between devices, along(): return lax.ppermute(value, ('src', 'ch'), pairs)  8.21 us
    pallas_call x1, Pallas kernels, transform_responses(): pl.pallas_call(functools.partial(response_kernel, rows, bins), in_specs=[...  6.37 us
    pallas_call x2, Pallas kernels, transform_signals(): pl.pallas_call(functools.partial(spectra_kernel, len(x_list), rows), in_s...  3.59 us
    ppermute x2, starting transfers between devices, along(): return lax.ppermute(value, ('src', 'ch'), pairs)  3.26 us
    dot_general x1, matrix products, per_device(): lax.dot_general(gathered, matrix, (((0,), (0,)), ((), ())), preferred_ele...  2.21 us
  transfers between devices with their start and end apart: 11, of which 7 were waited for; matrix products, arithmetic and copies ran while one was open for 0% of the time, Pallas kernels for 25%

profile of v9, /device:TPU:0, one launch (start us, length us, event | category | flops | bytes accessed | tf_op | source)
XLA Modules:
  0.0 52.7 jit_solution(6744480013593129551)
XLA Ops:
  0.0 0.0 copy-start
  0.0 4.0 %collective-permute-start = (bf16[40,2,1024]{2,1,0:T(2,128)(2,1)}, bf16[40,2,1024]{2,1,0:T(2,128)(2,1)S(1)}, u32[]{:S(2)}, u32[]{:S(2)}) collective-permute-start(bf16[40,2,1024]{2,1,0:T(2,128)(2,1)} %bitcast.12), channel_id=1, source_target_pairs={{0,4},{1,5},{2,6},{3,7},{4,0},{5,1},{6,2},{7,3},{8,12},{9,13},{10,... | collective-permute-start | bytes 491528 | tf_op jit(solution)/shard_map/ppermute | solution.py:415
  4.0 1.6 %collective-permute-start.2 = (bf16[40,2,1024]{2,1,0:T(2,128)(2,1)}, bf16[40,2,1024]{2,1,0:T(2,128)(2,1)S(1)}, u32[]{:S(2)}, u32[]{:S(2)}) collective-permute-start(bf16[40,2,1024]{2,1,0:T(2,128)(2,1)} %bitcast.13), channel_id=1, source_target_pairs={{0,2},{1,3},{2,0},{3,1},{4,6},{5,7},{6,4},{7,5},{8,10},{9,11},{10,... | collective-permute-start | bytes 491528 | tf_op jit(solution)/shard_map/ppermute | solution.py:415
  5.6 0.1 pad_add_fusion.me_ref
  5.7 0.0 copy-start.1
  5.7 0.0 copy-start.3
  5.7 0.0 copy-start.4
  5.7 6.4 %shard_map.91.refs_1_.refs_2_ = bf16[16,8,384,128]{3,2,1,0:T(8,128)(2,1)S(1)} custom-call(s32[2]{0:T(128)S(1)} %pad_add_fusion.me_ref, bf16[16,8,8,2,1024]{4,3,2,1,0:T(2,128)(2,1)} %room_hbm.1, bf16[384,256]{1,0:T(8,128)(2,1)} %constant.50.clone.table_hbm), custom_call_target="tpu_custom_call" | custom-call | flops 1048576 | bytes 65536 | tf_op jit(solution)/shard_map/pallas_call | solution.py:153
  12.1 0.0 copy-start.6
  12.1 0.0 collective-permute-done.refs_1_
  12.1 0.1 collective-permute-done.2.refs_2_
  12.3 0.0 copy-done.1
  12.3 0.0 copy-done.3
  12.3 0.0 copy-done.4
  12.3 2.1 %shard_map.92.refs_0_ = bf16[8,6,96,128]{3,2,1,0:T(8,128)(2,1)S(1)} custom-call(bf16[40,2,1024]{2,1,0:T(2,128)(2,1)S(1)} %bitcast.14, bf16[40,2,1024]{2,1,0:T(2,128)(2,1)S(1)} %collective-permute-done.refs_1_, bf16[40,2,1024]{2,1,0:T(2,128)(2,1)S(1)} %collective-permute-done.2.refs_2_, bf16[2,8,1024,128]{3,2,1,0:T(8,128)(2,1)S(1)} %copy-done.1, ...), custom_call_target="tpu_custom_call" | custom-call | flops 1048576 | bytes 65536 | tf_op jit(solution)/shard_map/pallas_call | solution.py:208
  14.4 0.1 collective-permute-start.4
  14.4 1.6 %collective-permute-start.1 = (bf16[40,2,1024]{2,1,0:T(2,128)(2,1)S(1)}, bf16[40,2,1024]{2,1,0:T(2,128)(2,1)S(1)}, u32[]{:S(2)}, u32[]{:S(2)}) collective-permute-start(bf16[40,2,1024]{2,1,0:T(2,128)(2,1)S(1)} %collective-permute-done.refs_1_), channel_id=1, source_target_pairs={{0,2},{1,3},{2,0},{3,1},{4,6},{5,7},{6,4},{7,5},{8,10},{9,11},{10,... | collective-permute-start | bytes 491528 | tf_op jit(solution)/shard_map/ppermute | solution.py:415
  16.0 0.0 copy-done.6
  16.0 2.2 %shard_map.93.refs_3_ = f32[8,4,192,128]{3,2,1,0:T(8,128)S(1)} custom-call(s32[2]{0:T(128)S(1)} %pad_add_fusion.me_ref, s32[16]{0:T(128)S(1)} %copy-done.6, bf16[8,6,96,128]{3,2,1,0:T(8,128)(2,1)S(1)} %shard_map.92.refs_0_, bf16[16,8,384,128]{3,2,1,0:T(8,128)(2,1)S(1)} %shard_map.91.refs_1_.refs_2_), custom_call_target="tpu_custom_call" | custom-call | flops 1048576 | bytes 65536 | tf_op jit(solution)/shard_map/pallas_call | solution.py:360
  18.2 2.8 %collective-permute-done.1.refs_0_ = bf16[40,2,1024]{2,1,0:T(2,128)(2,1)S(1)} collective-permute-done((bf16[40,2,1024]{2,1,0:T(2,128)(2,1)S(1)}, bf16[40,2,1024]{2,1,0:T(2,128)(2,1)S(1)}, u32[]{:S(2)}, u32[]{:S(2)}) %collective-permute-start.1) | collective-permute-done | bytes 163872 | tf_op jit(solution)/shard_map/ppermute | solution.py:415
  21.1 1.5 %shard_map.94.refs_1_ = bf16[8,2,96,128]{3,2,1,0:T(8,128)(2,1)S(1)} custom-call(bf16[40,2,1024]{2,1,0:T(2,128)(2,1)S(1)} %collective-permute-done.1.refs_0_, bf16[2,8,1024,128]{3,2,1,0:T(8,128)(2,1)S(1)} %copy-done.1, bf16[2,192,160]{2,1,0:T(8,128)(2,1)S(1)} %copy-done.3), custom_call_target="tpu_custom_call" | custom-call | flops 1048576 | bytes 65536 | tf_op jit(solution)/shard_map/pallas_call | solution.py:208
  22.6 0.0 copy-start.2
  22.6 0.0 copy-start.5
  22.6 0.1 collective-permute-start.3
  22.7 0.0 collective-permute-done.4.refs_0_
  22.7 3.1 %shard_map.95.refs_2_ = f32[8,4,192,128]{3,2,1,0:T(8,128)S(1)} custom-call(s32[2]{0:T(128)S(1)} %pad_add_fusion.me_ref, s32[16]{0:T(128)S(1)} %copy-done.6, bf16[8,6,96,128]{3,2,1,0:T(8,128)(2,1)S(1)} %collective-permute-done.4.refs_0_, bf16[8,2,96,128]{3,2,1,0:T(8,128)(2,1)S(1)} %shard_map.94.refs_1_, ...), custom_call_target="tpu_custom_call", output_to_operand_aliasing={{}: (5, {})} | custom-call | flops 1048576 | bytes 65536 | tf_op jit(solution)/shard_map/pallas_call | solution.py:360
  25.8 0.0 collective-permute-done.3.refs_0_
  25.8 0.0 copy-done.2
  25.8 0.0 copy-done.5
  25.8 3.0 %shard_map.96 = (bf16[2,8,8,1024]{3,2,1,0:T(8,128)(2,1)S(1)}, bf16[8,8,1024]{2,1,0:T(8,128)(2,1)S(1)}, bf16[8,8,1024]{2,1,0:T(8,128)(2,1)S(1)}) custom-call(s32[2]{0:T(128)S(1)} %pad_add_fusion.me_ref, s32[16]{0:T(128)S(1)} %copy-done.6, bf16[8,2,96,128]{3,2,1,0:T(8,128)(2,1)S(1)} %collective-permute-done.3.refs_0_, ...), custom_call_target="tpu_custom_call" | custom-call | flops 1048576 | bytes 65536 | tf_op jit(solution)/shard_map/pallas_call | solution.py:360
  28.8 1.6 %collective-permute-start.5 = (bf16[2,8,8,1024]{3,2,1,0:T(8,128)(2,1)S(1)}, bf16[2,8,8,1024]{3,2,1,0:T(8,128)(2,1)S(1)}, u32[]{:S(2)}, u32[]{:S(2)}) collective-permute-start(bf16[2,8,8,1024]{3,2,1,0:T(8,128)(2,1)S(1)} %get-tuple-element.22), channel_id=1, source_target_pairs={{0,8},{1,17},{2,10},{3,19},{4,12},{5,21},{6,14},{7,23},{8,0},{9,25... | collective-permute-start | bytes 786440 | tf_op jit(solution)/shard_map/ppermute | solution.py:457
  30.4 4.8 %collective-permute-done.5.first_ref = bf16[2,8,8,1024]{3,2,1,0:T(8,128)(2,1)S(1)} collective-permute-done((bf16[2,8,8,1024]{3,2,1,0:T(8,128)(2,1)S(1)}, bf16[2,8,8,1024]{3,2,1,0:T(8,128)(2,1)S(1)}, u32[]{:S(2)}, u32[]{:S(2)}) %collective-permute-start.5) | collective-permute-done | bytes 262176 | tf_op jit(solution)/shard_map/ppermute | solution.py:457
  35.3 1.6 %collective-permute-start.6 = (bf16[8,8,1024]{2,1,0:T(8,128)(2,1)S(1)}, bf16[8,8,1024]{2,1,0:T(8,128)(2,1)S(1)}, u32[]{:S(2)}, u32[]{:S(2)}) collective-permute-start(bf16[8,8,1024]{2,1,0:T(8,128)(2,1)S(1)} %fusion), channel_id=1, source_target_pairs={{0,16},{1,9},{2,18},{3,11},{4,20},{5,13},{6,22},{7,15},{8,24},{9,1... | collective-permute-start | bytes 393224 | tf_op jit(solution)/shard_map/ppermute | solution.py:457
  36.9 3.4 %collective-permute-done.6.second_ref = bf16[8,8,1024]{2,1,0:T(8,128)(2,1)S(1)} collective-permute-done((bf16[8,8,1024]{2,1,0:T(8,128)(2,1)S(1)}, bf16[8,8,1024]{2,1,0:T(8,128)(2,1)S(1)}, u32[]{:S(2)}, u32[]{:S(2)}) %collective-permute-start.6) | collective-permute-done | bytes 131104 | tf_op jit(solution)/shard_map/ppermute | solution.py:457
  40.3 0.3 shard_map.97
  40.6 0.1 collective-permute-start.7
  40.7 1.2 %collective-permute-done.7 = bf16[32,1024]{1,0:T(8,128)(2,1)S(1)} collective-permute-done((bf16[32,1024]{1,0:T(8,128)(2,1)S(1)}, bf16[32,1024]{1,0:T(8,128)(2,1)S(1)}, u32[]{:S(2)}, u32[]{:S(2)}) %collective-permute-start.7) | collective-permute-done | bytes 65568 | tf_op jit(solution)/shard_map/ppermute | solution.py:415
  41.9 3.3 %collective-permute-start.10 = (bf16[16,1024]{1,0:T(8,128)(2,1)S(1)}, bf16[16,1024]{1,0:T(8,128)(2,1)S(1)}, u32[]{:S(2)}, u32[]{:S(2)}) collective-permute-start(bf16[16,1024]{1,0:T(8,128)(2,1)S(1)} %pad_maximum_fusion.2), channel_id=1, source_target_pairs={{0,6},{1,7},{2,4},{3,5},{4,2},{5,3},{6,0},{7,1},{8,14},{9,15},{10,... | collective-permute-start | bytes 98312 | tf_op jit(solution)/shard_map/ppermute | solution.py:415
  45.3 0.0 collective-permute-start.8
  45.3 1.1 %collective-permute-start.9 = (bf16[16,1024]{1,0:T(8,128)(2,1)S(1)}, bf16[16,1024]{1,0:T(8,128)(2,1)S(1)}, u32[]{:S(2)}, u32[]{:S(2)}) collective-permute-start(bf16[16,1024]{1,0:T(8,128)(2,1)S(1)} %pad_maximum_fusion.1), channel_id=1, source_target_pairs={{0,4},{1,5},{2,6},{3,7},{4,0},{5,1},{6,2},{7,3},{8,12},{9,13},{10,... | collective-permute-start | bytes 98312 | tf_op jit(solution)/shard_map/ppermute | solution.py:415
  46.4 3.0 %collective-permute-done.8 = bf16[16,1024]{1,0:T(8,128)(2,1)S(1)} collective-permute-done((bf16[16,1024]{1,0:T(8,128)(2,1)S(1)}, bf16[16,1024]{1,0:T(8,128)(2,1)S(1)}, u32[]{:S(2)}, u32[]{:S(2)}) %collective-permute-start.8) | collective-permute-done | bytes 32800 | tf_op jit(solution)/shard_map/ppermute | solution.py:415
  49.4 1.1 %collective-permute-done.9 = bf16[16,1024]{1,0:T(8,128)(2,1)S(1)} collective-permute-done((bf16[16,1024]{1,0:T(8,128)(2,1)S(1)}, bf16[16,1024]{1,0:T(8,128)(2,1)S(1)}, u32[]{:S(2)}, u32[]{:S(2)}) %collective-permute-start.9) | collective-permute-done | bytes 32800 | tf_op jit(solution)/shard_map/ppermute | solution.py:415
  50.5 0.0 collective-permute-done.10
  50.5 0.0 copy-done
  50.5 2.2 %convolution_convert_fusion = bf16[1024,1024]{1,0:T(8,128)(2,1)} fusion(bf16[64,1024]{1,0:T(8,128)(2,1)S(1)} %constant_dynamic-update-slice_fusion, bf16[64,1024]{1,0:T(8,128)(2,1)S(1)} %copy-done, s32[64]{0:T(128)S(1)} %fusion.3), kind=kOutput, calls=%fused_computation | convolution fusion | flops 143724544 | bytes 2359552 | tf_op jit(solution)/shard_map/dot_general | solution.py:479
  (10 shorter events, 0.1 us)
Async XLA Ops:
  0.0 50.5 %copy-start = (bf16[64,1024]{1,0:T(8,128)(2,1)S(1)}, bf16[64,1024]{1,0:T(8,128)(2,1)}, u32[]{:S(2)}) copy-start(bf16[64,1024]{1,0:T(8,128)(2,1)} %param.12) | copy-start | bytes 393220
  0.0 12.1 %collective-permute-start = (bf16[40,2,1024]{2,1,0:T(2,128)(2,1)}, bf16[40,2,1024]{2,1,0:T(2,128)(2,1)S(1)}, u32[]{:S(2)}, u32[]{:S(2)}) collective-permute-start(bf16[40,2,1024]{2,1,0:T(2,128)(2,1)} %bitcast.12), channel_id=1, source_target_pairs={{0,4},{1,5},{2,6},{3,7},{4,0},{5,1},{6,2},{7,3},{8,12},{9,13},{10,... | collective-permute-start | bytes 491528 | tf_op jit(solution)/shard_map/ppermute | solution.py:415
  4.0 8.2 %collective-permute-start.2 = (bf16[40,2,1024]{2,1,0:T(2,128)(2,1)}, bf16[40,2,1024]{2,1,0:T(2,128)(2,1)S(1)}, u32[]{:S(2)}, u32[]{:S(2)}) collective-permute-start(bf16[40,2,1024]{2,1,0:T(2,128)(2,1)} %bitcast.13), channel_id=1, source_target_pairs={{0,2},{1,3},{2,0},{3,1},{4,6},{5,7},{6,4},{7,5},{8,10},{9,11},{10,... | collective-permute-start | bytes 491528 | tf_op jit(solution)/shard_map/ppermute | solution.py:415
  5.7 6.6 %copy-start.1 = (bf16[2,8,1024,128]{3,2,1,0:T(8,128)(2,1)S(1)}, bf16[2,8,1024,128]{3,2,1,0:T(8,128)(2,1)}, u32[]{:S(2)}) copy-start(bf16[2,8,1024,128]{3,2,1,0:T(8,128)(2,1)} %constant.51.clone.refs_3_.refs_1_) | copy-start | bytes 12582916
  5.7 6.6 %copy-start.3 = (bf16[2,192,160]{2,1,0:T(8,128)(2,1)S(1)}, bf16[2,192,160]{2,1,0:T(8,128)(2,1)}, u32[]{:S(2)}) copy-start(bf16[2,192,160]{2,1,0:T(8,128)(2,1)} %constant.52.clone.refs_4_.refs_2_) | copy-start | bytes 368644
  5.7 6.6 %copy-start.4 = (bf16[2,40960]{1,0:T(2,128)(2,1)S(1)}, bf16[2,40960]{1,0:T(2,128)(2,1)}, u32[]{:S(2)}) copy-start(bf16[2,40960]{1,0:T(2,128)(2,1)} %param.9) | copy-start | bytes 491524
  12.1 3.9 %copy-start.6 = (s32[16]{0:T(128)S(1)}, s32[16]{0:T(128)}, u32[]{:S(2)}) copy-start(s32[16]{0:T(128)} %slot_ref.5) | copy-start | bytes 196
  14.4 8.3 %collective-permute-start.4 = (bf16[8,6,96,128]{3,2,1,0:T(8,128)(2,1)S(1)}, bf16[8,6,96,128]{3,2,1,0:T(8,128)(2,1)S(1)}, u32[]{:S(2)}, u32[]{:S(2)}) collective-permute-start(bf16[8,6,96,128]{3,2,1,0:T(8,128)(2,1)S(1)} %shard_map.92.refs_0_), channel_id=1, source_target_pairs={{0,1},{1,0},{2,3},{3,2},{4,5},{5,4},{6,7},{7,6},{8,9},{9,8},{10,11... | collective-permute-start | bytes 3538952 | tf_op jit(solution)/shard_map/ppermute | solution.py:415
  14.4 6.6 %collective-permute-start.1 = (bf16[40,2,1024]{2,1,0:T(2,128)(2,1)S(1)}, bf16[40,2,1024]{2,1,0:T(2,128)(2,1)S(1)}, u32[]{:S(2)}, u32[]{:S(2)}) collective-permute-start(bf16[40,2,1024]{2,1,0:T(2,128)(2,1)S(1)} %collective-permute-done.refs_1_), channel_id=1, source_target_pairs={{0,2},{1,3},{2,0},{3,1},{4,6},{5,7},{6,4},{7,5},{8,10},{9,11},{10,... | collective-permute-start | bytes 491528 | tf_op jit(solution)/shard_map/ppermute | solution.py:415
  22.6 3.2 %copy-start.2 = (bf16[2,8,1024,128]{3,2,1,0:T(8,128)(2,1)S(1)}, bf16[2,8,1024,128]{3,2,1,0:T(8,128)(2,1)}, u32[]{:S(2)}) copy-start(bf16[2,8,1024,128]{3,2,1,0:T(8,128)(2,1)} %constant.54.clone.refs_4_) | copy-start | bytes 12582916
  22.6 3.2 %copy-start.5 = (bf16[2,128,192]{2,1,0:T(8,128)(2,1)S(1)}, bf16[2,128,192]{2,1,0:T(8,128)(2,1)}, u32[]{:S(2)}) copy-start(bf16[2,128,192]{2,1,0:T(8,128)(2,1)} %constant.53.clone.refs_3_) | copy-start | bytes 294916
  22.6 3.2 %collective-permute-start.3 = (bf16[8,2,96,128]{3,2,1,0:T(8,128)(2,1)S(1)}, bf16[8,2,96,128]{3,2,1,0:T(8,128)(2,1)S(1)}, u32[]{:S(2)}, u32[]{:S(2)}) collective-permute-start(bf16[8,2,96,128]{3,2,1,0:T(8,128)(2,1)S(1)} %shard_map.94.refs_1_), channel_id=1, source_target_pairs={{0,1},{1,0},{2,3},{3,2},{4,5},{5,4},{6,7},{7,6},{8,9},{9,8},{10,11... | collective-permute-start | bytes 1179656 | tf_op jit(solution)/shard_map/ppermute | solution.py:415
  28.8 6.4 %collective-permute-start.5 = (bf16[2,8,8,1024]{3,2,1,0:T(8,128)(2,1)S(1)}, bf16[2,8,8,1024]{3,2,1,0:T(8,128)(2,1)S(1)}, u32[]{:S(2)}, u32[]{:S(2)}) collective-permute-start(bf16[2,8,8,1024]{3,2,1,0:T(8,128)(2,1)S(1)} %get-tuple-element.22), channel_id=1, source_target_pairs={{0,8},{1,17},{2,10},{3,19},{4,12},{5,21},{6,14},{7,23},{8,0},{9,25... | collective-permute-start | bytes 786440 | tf_op jit(solution)/shard_map/ppermute | solution.py:457
  35.3 5.0 %collective-permute-start.6 = (bf16[8,8,1024]{2,1,0:T(8,128)(2,1)S(1)}, bf16[8,8,1024]{2,1,0:T(8,128)(2,1)S(1)}, u32[]{:S(2)}, u32[]{:S(2)}) collective-permute-start(bf16[8,8,1024]{2,1,0:T(8,128)(2,1)S(1)} %fusion), channel_id=1, source_target_pairs={{0,16},{1,9},{2,18},{3,11},{4,20},{5,13},{6,22},{7,15},{8,24},{9,1... | collective-permute-start | bytes 393224 | tf_op jit(solution)/shard_map/ppermute | solution.py:457
  40.6 1.3 %collective-permute-start.7 = (bf16[32,1024]{1,0:T(8,128)(2,1)S(1)}, bf16[32,1024]{1,0:T(8,128)(2,1)S(1)}, u32[]{:S(2)}, u32[]{:S(2)}) collective-permute-start(bf16[32,1024]{1,0:T(8,128)(2,1)S(1)} %get-tuple-element.25), channel_id=1, source_target_pairs={{0,1},{1,0},{2,3},{3,2},{4,5},{5,4},{6,7},{7,6},{8,9},{9,8},{10,11... | collective-permute-start | bytes 196616 | tf_op jit(solution)/shard_map/ppermute | solution.py:415
  41.9 8.6 %collective-permute-start.10 = (bf16[16,1024]{1,0:T(8,128)(2,1)S(1)}, bf16[16,1024]{1,0:T(8,128)(2,1)S(1)}, u32[]{:S(2)}, u32[]{:S(2)}) collective-permute-start(bf16[16,1024]{1,0:T(8,128)(2,1)S(1)} %pad_maximum_fusion.2), channel_id=1, source_target_pairs={{0,6},{1,7},{2,4},{3,5},{4,2},{5,3},{6,0},{7,1},{8,14},{9,15},{10,... | collective-permute-start | bytes 98312 | tf_op jit(solution)/shard_map/ppermute | solution.py:415
  45.3 4.1 %collective-permute-start.8 = (bf16[16,1024]{1,0:T(8,128)(2,1)S(1)}, bf16[16,1024]{1,0:T(8,128)(2,1)S(1)}, u32[]{:S(2)}, u32[]{:S(2)}) collective-permute-start(bf16[16,1024]{1,0:T(8,128)(2,1)S(1)} %pad_maximum_fusion), channel_id=1, source_target_pairs={{0,2},{1,3},{2,0},{3,1},{4,6},{5,7},{6,4},{7,5},{8,10},{9,11},{10,... | collective-permute-start | bytes 98312 | tf_op jit(solution)/shard_map/ppermute | solution.py:415
  45.3 5.2 %collective-permute-start.9 = (bf16[16,1024]{1,0:T(8,128)(2,1)S(1)}, bf16[16,1024]{1,0:T(8,128)(2,1)S(1)}, u32[]{:S(2)}, u32[]{:S(2)}) collective-permute-start(bf16[16,1024]{1,0:T(8,128)(2,1)S(1)} %pad_maximum_fusion.1), channel_id=1, source_target_pairs={{0,4},{1,5},{2,6},{3,7},{4,0},{5,1},{6,2},{7,3},{8,12},{9,13},{10,... | collective-permute-start | bytes 98312 | tf_op jit(solution)/shard_map/ppermute | solution.py:415

commit v10 on v8

--- a/solution.py
+++ b/solution.py
@@ -343,7 +343,7 @@
     return pl.pallas_call(
         body,
         in_specs=[smem, smem] + [vmem] * (len(operands) - 2),
-        out_specs=[vmem] * shares if last else vmem,
+        out_specs=[vmem] * len(out_shape) if last else vmem,
         out_shape=out_shape,
         scratch_shapes=scratch,
         input_output_aliases=aliases,
@@ -352,27 +352,57 @@
     )(*operands)
 
 
-def sum_kernel(count, each, me_ref, *refs):
-    parts, outs, sum_ref = refs[:count], refs[count:-1], refs[-1]
+def sum_kernel(count, chips, me_ref, *refs):
+    parts, mate_ref, outs, sum_ref = refs[:count], refs[count], refs[count + 1 : -1], refs[-1]
     total = parts[0][...].astype(F32)
     for part in parts[1:]:
         total = total + part[...].astype(F32)
     sum_ref[...] = total
-    for d in range(each):
-        outs[d][...] = sum_ref[:, pl.ds(me_ref[0] ^ d, 1), :].reshape(outs[d].shape).astype(BF16)
-
-
-def sum_groups(parts, me):
-    channels, each, bins = parts[0].shape
+
+    def piece(d):
+        return sum_ref[:, pl.ds(me_ref[1] ^ d, 1), :].reshape(outs[0].shape)
+
+    mate_ref[...] = jnp.concatenate([piece(2 * d + 1) for d in range(chips)], axis=0).astype(BF16)
+    for d in range(chips):
+        outs[d][...] = piece(2 * d).astype(BF16)
+
+
+def sum_groups(parts, me, chips):
+    channels, _, bins = parts[0].shape
     vmem = pl.BlockSpec(memory_space=pltpu.VMEM)
     return pl.pallas_call(
-        functools.partial(sum_kernel, len(parts), each),
+        functools.partial(sum_kernel, len(parts), chips),
         in_specs=[pl.BlockSpec(memory_space=pltpu.SMEM)] + [vmem] * len(parts),
-        out_specs=[vmem] * each,
-        out_shape=[jax.ShapeDtypeStruct((channels, bins), BF16)] * each,
+        out_specs=[vmem] * (chips + 1),
+        out_shape=[jax.ShapeDtypeStruct((chips * channels, bins), BF16)]
+        + [jax.ShapeDtypeStruct((channels, bins), BF16)] * chips,
         scratch_shapes=[pltpu.VMEM(parts[0].shape, F32)],
         compiler_params=pltpu.CompilerParams(vmem_limit_bytes=8 * 2**20),
-    )(me[None], *parts)
+    )(me, *parts)
+
+
+def decode_kernel(count, *refs):
+    signal_refs, matrix_ref, out_ref = refs[:count], refs[count], refs[-1]
+    rows = out_ref.shape[0]
+    here = pl.ds(pl.multiple_of(pl.program_id(0) * rows, rows), rows)
+    signal = jnp.concatenate([ref[:, here] for ref in signal_refs], axis=0)
+    out_ref[...] = lax.dot_general(
+        signal, matrix_ref[...], (((0,), (0,)), ((), ())), preferred_element_type=F32
+    ).astype(BF16)
+
+
+def decode(signals, matrix):
+    samples, speakers = signals[0].shape[1], matrix.shape[1]
+    rows = min(256, samples)
+    vmem = pl.BlockSpec(memory_space=pltpu.VMEM)
+    return pl.pallas_call(
+        functools.partial(decode_kernel, len(signals)),
+        grid=(samples // rows,),
+        in_specs=[vmem] * (len(signals) + 1),
+        out_specs=pl.BlockSpec((rows, speakers), lambda i: (i, 0)),
+        out_shape=jax.ShapeDtypeStruct((samples, speakers), BF16),
+        compiler_params=pltpu.CompilerParams(vmem_limit_bytes=8 * 2**20),
+    )(*signals, matrix)
 
 
 def per_device(src_count, ch_count, dry_signal, room_spectra, render_slot, decoder):
@@ -392,13 +422,9 @@
         return lax.ppermute(value, axis, [(i, i ^ flip) for i in range(count)])
 
     chips = ch_count // 2
-    first = chips // 2
-    lanes = {first: swap(x_own, "ch", ch_count, 2 * first)}
+    lanes = [x_own] + [swap(x_own, "ch", ch_count, 2 * d) for d in range(1, chips)]
     me = jnp.stack([src_me, ch_me])
     hat = transform_responses(room_spectra, me)
-    x_own, hat = lax.optimization_barrier((x_own, hat))
-    rest = [d for d in range(chips - 1, 0, -1) if d != first]
-    lanes.update({d: swap(x_own, "ch", ch_count, 2 * d) for d in rest})
 
     row = jnp.arange(ch_count * channels, dtype=jnp.int32)
     takes = ((row // channels) ^ ch_me) * channels + row % channels
@@ -414,36 +440,31 @@
         mine = transform_signals(x_list, own, block_len, parts)
         return mine, swap(mine, "ch", ch_count, 1)
 
-    near_mine, near_given = transform([x_own, lanes[first]])
-    total = add([near_mine], [[0, 2 * first]], None, False)
-    *late, total = lax.optimization_barrier((*[lanes[d] for d in rest], total))
+    near, far = range(0, 2), range(2, chips)
+    x_near, hat = lax.optimization_barrier((x_own, hat))
+    near_mine, near_given = transform([x_near, lanes[1]])
+    total = add([near_mine], [[2 * d for d in near]], None, False)
+    *late, total = lax.optimization_barrier((*lanes[2:], total))
     far_mine, far_given = transform(late)
-    total = add([near_given, far_mine], [[1, 2 * first + 1], [2 * d for d in rest]], total, False)
-    total = add([far_given], [[2 * d + 1 for d in rest]], total, True)
-
-    parts_in = [total[0]] + [swap(total[d], "src", src_count, d) for d in range(1, src_count)]
-    each = blocks // src_count
-    if each == ch_count:
-        pieces = sum_groups(parts_in, ch_me)
-        given = swap(jnp.concatenate(pieces[1::2], axis=0), "ch", ch_count, 1)
+    flips = [[2 * d + 1 for d in near], [2 * d for d in far]]
+    total = add([near_given, far_mine], flips, total, False)
+    total = add([far_given], [[2 * d + 1 for d in far]], total, True)
+
+    sums = [total[0]] + [swap(total[d], "src", src_count, d) for d in range(1, src_count)]
+    if blocks == src_count * ch_count:
+        to_mate, *pieces = sum_groups(sums, me, chips)
+        given = swap(to_mate, "ch", ch_count, 1)
         both = [
-            jnp.concatenate([pieces[2 * d], given[d * channels : (d + 1) * channels]], axis=0)
+            jnp.concatenate([pieces[d], given[d * channels : (d + 1) * channels]], axis=0)
             for d in range(chips)
         ]
         both[1:] = [swap(both[d], "ch", ch_count, 2 * d) for d in range(1, chips)]
-        gathered = jnp.concatenate(both, axis=0)
-        matrix = own_order
-    else:
-        signal = parts_in[0].astype(F32)
-        for part in parts_in[1:]:
-            signal = signal + part.astype(F32)
-        signal = signal.astype(BF16).reshape(channels, -1)
-        gathered = lax.all_to_all(signal, "ch", split_axis=1, concat_axis=0, tiled=True)
-        matrix = decoder
-    decoded = lax.dot_general(
-        gathered, matrix, (((0,), (0,)), ((), ())), preferred_element_type=F32
-    )
-    return decoded.astype(BF16)
+        return decode(both, own_order)
+    signal = sums[0].astype(F32)
+    for part in sums[1:]:
+        signal = signal + part.astype(F32)
+    signal = signal.astype(BF16).reshape(channels, -1)
+    return decode([lax.all_to_all(signal, "ch", split_axis=1, concat_axis=0, tiled=True)], decoder)
 
 
 def solution(mesh):

time: 51.1 us -> 49.9 us (0.977)
  Pallas kernels: 18.5 us -> 21.5 us
  waiting for transfers between devices: 15.9 us -> 13.9 us
  matrix products: 2.21 us -> 0.22 us
    pallas_call x1 -> x2, Pallas kernels: 0.45 us -> 3.41 us  [the longest x1 2.56 us: decode(): pl.pallas_call(functools.partial(decode_kernel, len(signals)), grid=(samp...]
    ppermute x12, waiting for transfers between devices: 15.9 us -> 13.9 us  [swap(): return lax.ppermute(value, axis, [(i, i ^ flip) for i in range(count)])]
    dot_general x1, matrix products: 2.21 us -> 0.22 us  [dot(): return jnp.dot(left, right, preferred_element_type=F32)]
  transfers between devices with their start and end apart: 12 -> 12, of which waited for: 7 -> 7; matrix products, arithmetic and copies ran while one was open for 0% -> 1% of each run, Pallas kernels for 28% -> 29%
where the time goes in v10:
time: 49.9 us; the launch traced here: 49.8 us
  Pallas kernels  21.5 us (43%)
  waiting for transfers between devices  13.9 us (28%)
  starting transfers between devices  13.8 us (28%)
    ppermute x12, waiting for transfers between devices, swap(): return lax.ppermute(value, axis, [(i, i ^ flip) for i in range(count)])  13.9 us
    ppermute x12, starting transfers between devices, swap(): return lax.ppermute(value, axis, [(i, i ^ flip) for i in range(count)])  13.8 us
    pallas_call x3, Pallas kernels, add_sources(): pl.pallas_call(body, in_specs=[smem, smem] + [vmem] * (len(operands) - 2)...  8.34 us
    pallas_call x1, Pallas kernels, transform_responses(): pl.pallas_call(functools.partial(response_kernel, rows, bins), in_specs=[...  6.37 us
    pallas_call x2, Pallas kernels, transform_signals(): pl.pallas_call(functools.partial(spectra_kernel, len(x_list), rows), in_s...  3.34 us
    pallas_call x1, Pallas kernels, decode(): pl.pallas_call(functools.partial(decode_kernel, len(signals)), grid=(samp...  2.56 us
  transfers between devices with their start and end apart: 12, of which 7 were waited for; matrix products, arithmetic and copies ran while one was open for 1% of the time, Pallas kernels for 29%

profile of v10, /device:TPU:0, one launch (start us, length us, event | category | flops | bytes accessed | tf_op | source)
XLA Modules:
  0.0 49.8 jit_solution(7872506588011485084)
XLA Ops:
  0.0 0.0 copy-start
  0.0 3.0 %collective-permute-start.2 = (bf16[40,2,1024]{2,1,0:T(2,128)(2,1)}, bf16[40,2,1024]{2,1,0:T(2,128)(2,1)S(1)}, u32[]{:S(2)}, u32[]{:S(2)}) collective-permute-start(bf16[40,2,1024]{2,1,0:T(2,128)(2,1)} %bitcast.6), channel_id=1, source_target_pairs={{0,2},{1,3},{2,0},{3,1},{4,6},{5,7},{6,4},{7,5},{8,10},{9,11},{10,... | collective-permute-start | bytes 491528 | tf_op jit(solution)/shard_map/ppermute | solution.py:422
  3.0 2.6 %collective-permute-start = (bf16[40,2,1024]{2,1,0:T(2,128)(2,1)}, bf16[40,2,1024]{2,1,0:T(2,128)(2,1)S(1)}, u32[]{:S(2)}, u32[]{:S(2)}) collective-permute-start(bf16[40,2,1024]{2,1,0:T(2,128)(2,1)} %bitcast.7), channel_id=1, source_target_pairs={{0,4},{1,5},{2,6},{3,7},{4,0},{5,1},{6,2},{7,3},{8,12},{9,13},{10,... | collective-permute-start | bytes 491528 | tf_op jit(solution)/shard_map/ppermute | solution.py:422
  5.6 0.0 collective-permute-start.1
  5.6 0.1 pad_add_fusion.me_ref
  5.7 0.0 copy-start.1
  5.7 0.0 copy-start.3
  5.7 0.0 copy-start.4
  5.7 6.4 %shard_map.91.refs_1_.refs_2_ = bf16[16,8,384,128]{3,2,1,0:T(8,128)(2,1)S(1)} custom-call(s32[2]{0:T(128)S(1)} %pad_add_fusion.me_ref, bf16[16,8,8,2,1024]{4,3,2,1,0:T(2,128)(2,1)} %room_hbm.1, bf16[384,256]{1,0:T(8,128)(2,1)} %constant.50.clone.table_hbm), custom_call_target="tpu_custom_call" | custom-call | flops 1048576 | bytes 65536 | tf_op jit(solution)/shard_map/pallas_call | solution.py:153
  12.1 0.0 copy-start.6
  12.1 0.0 collective-permute-done.2.refs_1_
  12.1 0.0 copy-done.1
  12.1 0.0 copy-done.3
  12.1 0.0 copy-done.4
  12.1 1.7 %shard_map.92.refs_0_ = bf16[8,4,96,128]{3,2,1,0:T(8,128)(2,1)S(1)} custom-call(bf16[40,2,1024]{2,1,0:T(2,128)(2,1)S(1)} %bitcast.9, bf16[40,2,1024]{2,1,0:T(2,128)(2,1)S(1)} %collective-permute-done.2.refs_1_, bf16[2,8,1024,128]{3,2,1,0:T(8,128)(2,1)S(1)} %copy-done.1, bf16[2,192,160]{2,1,0:T(8,128)(2,1)S(1)} %copy-done.3), custom_call_target="tpu_custom_call" | custom-call | flops 1048576 | bytes 65536 | tf_op jit(solution)/shard_map/pallas_call | solution.py:208
  13.8 0.1 collective-permute-start.4
  13.9 0.0 copy-done.6
  13.9 1.5 %shard_map.93.refs_3_ = f32[8,4,192,128]{3,2,1,0:T(8,128)S(1)} custom-call(s32[2]{0:T(128)S(1)} %pad_add_fusion.me_ref, s32[16]{0:T(128)S(1)} %copy-done.6, bf16[8,4,96,128]{3,2,1,0:T(8,128)(2,1)S(1)} %shard_map.92.refs_0_, bf16[16,8,384,128]{3,2,1,0:T(8,128)(2,1)S(1)} %shard_map.91.refs_1_.refs_2_), custom_call_target="tpu_custom_call" | custom-call | flops 1048576 | bytes 65536 | tf_op jit(solution)/shard_map/pallas_call | solution.py:343
  15.4 2.8 %collective-permute-done.refs_0_ = bf16[40,2,1024]{2,1,0:T(2,128)(2,1)S(1)} collective-permute-done((bf16[40,2,1024]{2,1,0:T(2,128)(2,1)}, bf16[40,2,1024]{2,1,0:T(2,128)(2,1)S(1)}, u32[]{:S(2)}, u32[]{:S(2)}) %collective-permute-start) | collective-permute-done | bytes 163872 | tf_op jit(solution)/shard_map/ppermute | solution.py:422
  18.3 0.0 collective-permute-done.1.refs_1_
  18.3 1.7 %shard_map.94.refs_1_ = bf16[8,4,96,128]{3,2,1,0:T(8,128)(2,1)S(1)} custom-call(bf16[40,2,1024]{2,1,0:T(2,128)(2,1)S(1)} %collective-permute-done.refs_0_, bf16[40,2,1024]{2,1,0:T(2,128)(2,1)S(1)} %collective-permute-done.1.refs_1_, bf16[2,8,1024,128]{3,2,1,0:T(8,128)(2,1)S(1)} %copy-done.1, bf16[2,192,160]{2,1,0:T(8,128)(2,1)S(1)} %copy-done.3), custom_call_target="tpu_custom_call" | custom-call | flops 1048576 | bytes 65536 | tf_op jit(solution)/shard_map/pallas_call | solution.py:208
  20.0 0.0 copy-start.2
  20.0 0.0 copy-start.5
  20.0 0.1 collective-permute-start.3
  20.1 0.0 collective-permute-done.4.refs_0_
  20.1 3.1 %shard_map.95.refs_2_ = f32[8,4,192,128]{3,2,1,0:T(8,128)S(1)} custom-call(s32[2]{0:T(128)S(1)} %pad_add_fusion.me_ref, s32[16]{0:T(128)S(1)} %copy-done.6, bf16[8,4,96,128]{3,2,1,0:T(8,128)(2,1)S(1)} %collective-permute-done.4.refs_0_, bf16[8,4,96,128]{3,2,1,0:T(8,128)(2,1)S(1)} %shard_map.94.refs_1_, ...), custom_call_target="tpu_custom_call", output_to_operand_aliasing={{}: (5, {})} | custom-call | flops 1048576 | bytes 65536 | tf_op jit(solution)/shard_map/pallas_call | solution.py:343
  23.2 0.0 collective-permute-done.3.refs_0_
  23.2 0.0 copy-done.2
  23.2 0.0 copy-done.5
  23.2 3.7 %shard_map.96 = (bf16[8,8,1024]{2,1,0:T(8,128)(2,1)S(1)}, bf16[8,8,1024]{2,1,0:T(8,128)(2,1)S(1)}, bf16[8,8,1024]{2,1,0:T(8,128)(2,1)S(1)}, bf16[8,8,1024]{2,1,0:T(8,128)(2,1)S(1)}) custom-call(s32[2]{0:T(128)S(1)} %pad_add_fusion.me_ref, s32[16]{0:T(128)S(1)} %copy-done.6, bf16[8,4,96,128]{3,2,1,0:T(8,128)(2,1)S(1)} %collective-permute-done.3.refs_0_, ...), custom_call_target="tpu_custom_call" | custom-call | flops 1048576 | bytes 65536 | tf_op jit(solution)/shard_map/pallas_call | solution.py:343
  26.9 1.6 %collective-permute-start.5 = (bf16[8,8,1024]{2,1,0:T(8,128)(2,1)S(1)}, bf16[8,8,1024]{2,1,0:T(8,128)(2,1)S(1)}, u32[]{:S(2)}, u32[]{:S(2)}) collective-permute-start(bf16[8,8,1024]{2,1,0:T(8,128)(2,1)S(1)} %get-tuple-element.25), channel_id=1, source_target_pairs={{0,8},{8,0},{16,24},{24,16},{1,9},{9,1},{17,25},{25,17},{2,10},{10... | collective-permute-start | bytes 393224 | tf_op jit(solution)/shard_map/ppermute | solution.py:422
  28.5 1.5 %collective-permute-start.6 = (bf16[8,8,1024]{2,1,0:T(8,128)(2,1)S(1)}, bf16[8,8,1024]{2,1,0:T(8,128)(2,1)S(1)}, u32[]{:S(2)}, u32[]{:S(2)}) collective-permute-start(bf16[8,8,1024]{2,1,0:T(8,128)(2,1)S(1)} %get-tuple-element.26), channel_id=1, source_target_pairs={{0,16},{8,24},{16,0},{24,8},{1,17},{9,25},{17,1},{25,9},{2,18},{10... | collective-permute-start | bytes 393224 | tf_op jit(solution)/shard_map/ppermute | solution.py:422
  30.0 0.5 collective-permute-start.7
  30.5 2.7 %collective-permute-done.5.refs_1_ = bf16[8,8,1024]{2,1,0:T(8,128)(2,1)S(1)} collective-permute-done((bf16[8,8,1024]{2,1,0:T(8,128)(2,1)S(1)}, bf16[8,8,1024]{2,1,0:T(8,128)(2,1)S(1)}, u32[]{:S(2)}, u32[]{:S(2)}) %collective-permute-start.5) | collective-permute-done | bytes 131104 | tf_op jit(solution)/shard_map/ppermute | solution.py:422
  33.2 3.7 %collective-permute-done.6.refs_2_ = bf16[8,8,1024]{2,1,0:T(8,128)(2,1)S(1)} collective-permute-done((bf16[8,8,1024]{2,1,0:T(8,128)(2,1)S(1)}, bf16[8,8,1024]{2,1,0:T(8,128)(2,1)S(1)}, u32[]{:S(2)}, u32[]{:S(2)}) %collective-permute-start.6) | collective-permute-done | bytes 131104 | tf_op jit(solution)/shard_map/ppermute | solution.py:422
  36.9 0.0 collective-permute-done.7.refs_3_
  36.9 0.9 %shard_map.97 = (bf16[32,1024]{1,0:T(8,128)(2,1)S(1)}, bf16[8,1024]{1,0:T(8,128)(2,1)S(1)}, bf16[8,1024]{1,0:T(8,128)(2,1)S(1)}, bf16[8,1024]{1,0:T(8,128)(2,1)S(1)}, bf16[8,1024]{1,0:T(8,128)(2,1)S(1)}) custom-call(s32[2]{0:T(128)S(1)} %pad_add_fusion.me_ref, bf16[8,8,1024]{2,1,0:T(8,128)(2,1)S(1)} %get-tuple-element.24.refs_0_, ...), custom_call_target="tpu_custom_call" | custom-call | tf_op jit(solution)/shard_map/pallas_call | solution.py:373
  37.8 0.1 collective-permute-start.8
  37.8 0.0 copy-done
  37.9 0.2 convolution_convert_fusion.refs_4_
  38.1 1.0 %collective-permute-done.8 = bf16[32,1024]{1,0:T(8,128)(2,1)S(1)} collective-permute-done((bf16[32,1024]{1,0:T(8,128)(2,1)S(1)}, bf16[32,1024]{1,0:T(8,128)(2,1)S(1)}, u32[]{:S(2)}, u32[]{:S(2)}) %collective-permute-start.8) | collective-permute-done | bytes 65568 | tf_op jit(solution)/shard_map/ppermute | solution.py:422
  39.1 2.4 %collective-permute-start.11 = (bf16[16,1024]{1,0:T(8,128)(2,1)S(1)}, bf16[16,1024]{1,0:T(8,128)(2,1)S(1)}, u32[]{:S(2)}, u32[]{:S(2)}) collective-permute-start(bf16[16,1024]{1,0:T(8,128)(2,1)S(1)} %pad_maximum_fusion.3), channel_id=1, source_target_pairs={{0,6},{1,7},{2,4},{3,5},{4,2},{5,3},{6,0},{7,1},{8,14},{9,15},{10,... | collective-permute-start | bytes 98312 | tf_op jit(solution)/shard_map/ppermute | solution.py:422
  41.5 1.8 %collective-permute-start.10 = (bf16[16,1024]{1,0:T(8,128)(2,1)S(1)}, bf16[16,1024]{1,0:T(8,128)(2,1)S(1)}, u32[]{:S(2)}, u32[]{:S(2)}) collective-permute-start(bf16[16,1024]{1,0:T(8,128)(2,1)S(1)} %pad_maximum_fusion.2), channel_id=1, source_target_pairs={{0,4},{1,5},{2,6},{3,7},{4,0},{5,1},{6,2},{7,3},{8,12},{9,13},{10,... | collective-permute-start | bytes 98312 | tf_op jit(solution)/shard_map/ppermute | solution.py:422
  43.3 0.3 collective-permute-start.9
  43.6 1.3 %collective-permute-done.11.refs_3_ = bf16[16,1024]{1,0:T(8,128)(2,1)S(1)} collective-permute-done((bf16[16,1024]{1,0:T(8,128)(2,1)S(1)}, bf16[16,1024]{1,0:T(8,128)(2,1)S(1)}, u32[]{:S(2)}, u32[]{:S(2)}) %collective-permute-start.11) | collective-permute-done | bytes 32800 | tf_op jit(solution)/shard_map/ppermute | solution.py:422
  44.9 1.4 %collective-permute-done.10.refs_2_ = bf16[16,1024]{1,0:T(8,128)(2,1)S(1)} collective-permute-done((bf16[16,1024]{1,0:T(8,128)(2,1)S(1)}, bf16[16,1024]{1,0:T(8,128)(2,1)S(1)}, u32[]{:S(2)}, u32[]{:S(2)}) %collective-permute-start.10) | collective-permute-done | bytes 32800 | tf_op jit(solution)/shard_map/ppermute | solution.py:422
  46.3 0.9 %collective-permute-done.9.refs_1_ = bf16[16,1024]{1,0:T(8,128)(2,1)S(1)} collective-permute-done((bf16[16,1024]{1,0:T(8,128)(2,1)S(1)}, bf16[16,1024]{1,0:T(8,128)(2,1)S(1)}, u32[]{:S(2)}, u32[]{:S(2)}) %collective-permute-start.9) | collective-permute-done | bytes 32800 | tf_op jit(solution)/shard_map/ppermute | solution.py:422
  47.2 2.6 %shard_map.98 = bf16[1024,1024]{1,0:T(8,128)(2,1)} custom-call(bf16[16,1024]{1,0:T(8,128)(2,1)S(1)} %pad_maximum_fusion.refs_0_, bf16[16,1024]{1,0:T(8,128)(2,1)S(1)} %collective-permute-done.9.refs_1_, bf16[16,1024]{1,0:T(8,128)(2,1)S(1)} %collective-permute-done.10.refs_2_, bf16[16,1024]{1,0:T(8,128)(2,1)S(1)} %collective-permute-done.11.refs_3_, ...), custom_call_target="tpu_custom_call" | custom-call | tf_op jit(solution)/shard_map/pallas_call | solution.py:398
  (6 shorter events, 0.0 us)
Async XLA Ops:
  0.0 37.8 %copy-start = (bf16[64,1024]{1,0:T(8,128)(2,1)S(1)}, bf16[64,1024]{1,0:T(8,128)(2,1)}, u32[]{:S(2)}) copy-start(bf16[64,1024]{1,0:T(8,128)(2,1)} %param.12) | copy-start | bytes 393220
  0.0 12.1 %collective-permute-start.2 = (bf16[40,2,1024]{2,1,0:T(2,128)(2,1)}, bf16[40,2,1024]{2,1,0:T(2,128)(2,1)S(1)}, u32[]{:S(2)}, u32[]{:S(2)}) collective-permute-start(bf16[40,2,1024]{2,1,0:T(2,128)(2,1)} %bitcast.6), channel_id=1, source_target_pairs={{0,2},{1,3},{2,0},{3,1},{4,6},{5,7},{6,4},{7,5},{8,10},{9,11},{10,... | collective-permute-start | bytes 491528 | tf_op jit(solution)/shard_map/ppermute | solution.py:422
  3.0 15.3 %collective-permute-start = (bf16[40,2,1024]{2,1,0:T(2,128)(2,1)}, bf16[40,2,1024]{2,1,0:T(2,128)(2,1)S(1)}, u32[]{:S(2)}, u32[]{:S(2)}) collective-permute-start(bf16[40,2,1024]{2,1,0:T(2,128)(2,1)} %bitcast.7), channel_id=1, source_target_pairs={{0,4},{1,5},{2,6},{3,7},{4,0},{5,1},{6,2},{7,3},{8,12},{9,13},{10,... | collective-permute-start | bytes 491528 | tf_op jit(solution)/shard_map/ppermute | solution.py:422
  5.6 12.7 %collective-permute-start.1 = (bf16[40,2,1024]{2,1,0:T(2,128)(2,1)}, bf16[40,2,1024]{2,1,0:T(2,128)(2,1)S(1)}, u32[]{:S(2)}, u32[]{:S(2)}) collective-permute-start(bf16[40,2,1024]{2,1,0:T(2,128)(2,1)} %bitcast.8), channel_id=1, source_target_pairs={{0,6},{1,7},{2,4},{3,5},{4,2},{5,3},{6,0},{7,1},{8,14},{9,15},{10,... | collective-permute-start | bytes 491528 | tf_op jit(solution)/shard_map/ppermute | solution.py:422
  5.7 6.4 %copy-start.1 = (bf16[2,8,1024,128]{3,2,1,0:T(8,128)(2,1)S(1)}, bf16[2,8,1024,128]{3,2,1,0:T(8,128)(2,1)}, u32[]{:S(2)}) copy-start(bf16[2,8,1024,128]{3,2,1,0:T(8,128)(2,1)} %constant.51.clone.refs_2_) | copy-start | bytes 12582916
  5.7 6.4 %copy-start.3 = (bf16[2,192,160]{2,1,0:T(8,128)(2,1)S(1)}, bf16[2,192,160]{2,1,0:T(8,128)(2,1)}, u32[]{:S(2)}) copy-start(bf16[2,192,160]{2,1,0:T(8,128)(2,1)} %constant.52.clone.refs_3_) | copy-start | bytes 368644
  5.7 6.4 %copy-start.4 = (bf16[2,40960]{1,0:T(2,128)(2,1)S(1)}, bf16[2,40960]{1,0:T(2,128)(2,1)}, u32[]{:S(2)}) copy-start(bf16[2,40960]{1,0:T(2,128)(2,1)} %param.9) | copy-start | bytes 491524
  12.1 1.8 %copy-start.6 = (s32[16]{0:T(128)S(1)}, s32[16]{0:T(128)}, u32[]{:S(2)}) copy-start(s32[16]{0:T(128)} %slot_ref.5) | copy-start | bytes 196
  13.8 6.3 %collective-permute-start.4 = (bf16[8,4,96,128]{3,2,1,0:T(8,128)(2,1)S(1)}, bf16[8,4,96,128]{3,2,1,0:T(8,128)(2,1)S(1)}, u32[]{:S(2)}, u32[]{:S(2)}) collective-permute-start(bf16[8,4,96,128]{3,2,1,0:T(8,128)(2,1)S(1)} %shard_map.92.refs_0_), channel_id=1, source_target_pairs={{0,1},{1,0},{2,3},{3,2},{4,5},{5,4},{6,7},{7,6},{8,9},{9,8},{10,11... | collective-permute-start | bytes 2359304 | tf_op jit(solution)/shard_map/ppermute | solution.py:422
  20.0 3.2 %copy-start.2 = (bf16[2,8,1024,128]{3,2,1,0:T(8,128)(2,1)S(1)}, bf16[2,8,1024,128]{3,2,1,0:T(8,128)(2,1)}, u32[]{:S(2)}) copy-start(bf16[2,8,1024,128]{3,2,1,0:T(8,128)(2,1)} %constant.54.clone.refs_4_) | copy-start | bytes 12582916
  20.0 3.2 %copy-start.5 = (bf16[2,128,192]{2,1,0:T(8,128)(2,1)S(1)}, bf16[2,128,192]{2,1,0:T(8,128)(2,1)}, u32[]{:S(2)}) copy-start(bf16[2,128,192]{2,1,0:T(8,128)(2,1)} %constant.53.clone.refs_3_) | copy-start | bytes 294916
  20.0 3.2 %collective-permute-start.3 = (bf16[8,4,96,128]{3,2,1,0:T(8,128)(2,1)S(1)}, bf16[8,4,96,128]{3,2,1,0:T(8,128)(2,1)S(1)}, u32[]{:S(2)}, u32[]{:S(2)}) collective-permute-start(bf16[8,4,96,128]{3,2,1,0:T(8,128)(2,1)S(1)} %shard_map.94.refs_1_), channel_id=1, source_target_pairs={{0,1},{1,0},{2,3},{3,2},{4,5},{5,4},{6,7},{7,6},{8,9},{9,8},{10,11... | collective-permute-start | bytes 2359304 | tf_op jit(solution)/shard_map/ppermute | solution.py:422
  26.9 6.3 %collective-permute-start.5 = (bf16[8,8,1024]{2,1,0:T(8,128)(2,1)S(1)}, bf16[8,8,1024]{2,1,0:T(8,128)(2,1)S(1)}, u32[]{:S(2)}, u32[]{:S(2)}) collective-permute-start(bf16[8,8,1024]{2,1,0:T(8,128)(2,1)S(1)} %get-tuple-element.25), channel_id=1, source_target_pairs={{0,8},{8,0},{16,24},{24,16},{1,9},{9,1},{17,25},{25,17},{2,10},{10... | collective-permute-start | bytes 393224 | tf_op jit(solution)/shard_map/ppermute | solution.py:422
  28.5 8.4 %collective-permute-start.6 = (bf16[8,8,1024]{2,1,0:T(8,128)(2,1)S(1)}, bf16[8,8,1024]{2,1,0:T(8,128)(2,1)S(1)}, u32[]{:S(2)}, u32[]{:S(2)}) collective-permute-start(bf16[8,8,1024]{2,1,0:T(8,128)(2,1)S(1)} %get-tuple-element.26), channel_id=1, source_target_pairs={{0,16},{8,24},{16,0},{24,8},{1,17},{9,25},{17,1},{25,9},{2,18},{10... | collective-permute-start | bytes 393224 | tf_op jit(solution)/shard_map/ppermute | solution.py:422
  30.0 6.9 %collective-permute-start.7 = (bf16[8,8,1024]{2,1,0:T(8,128)(2,1)S(1)}, bf16[8,8,1024]{2,1,0:T(8,128)(2,1)S(1)}, u32[]{:S(2)}, u32[]{:S(2)}) collective-permute-start(bf16[8,8,1024]{2,1,0:T(8,128)(2,1)S(1)} %get-tuple-element.27), channel_id=1, source_target_pairs={{0,24},{8,16},{16,8},{24,0},{1,25},{9,17},{17,9},{25,1},{2,26},{10... | collective-permute-start | bytes 393224 | tf_op jit(solution)/shard_map/ppermute | solution.py:422
  37.8 1.3 %collective-permute-start.8 = (bf16[32,1024]{1,0:T(8,128)(2,1)S(1)}, bf16[32,1024]{1,0:T(8,128)(2,1)S(1)}, u32[]{:S(2)}, u32[]{:S(2)}) collective-permute-start(bf16[32,1024]{1,0:T(8,128)(2,1)S(1)} %get-tuple-element.29), channel_id=1, source_target_pairs={{0,1},{1,0},{2,3},{3,2},{4,5},{5,4},{6,7},{7,6},{8,9},{9,8},{10,11... | collective-permute-start | bytes 196616 | tf_op jit(solution)/shard_map/ppermute | solution.py:422
  39.1 5.8 %collective-permute-start.11 = (bf16[16,1024]{1,0:T(8,128)(2,1)S(1)}, bf16[16,1024]{1,0:T(8,128)(2,1)S(1)}, u32[]{:S(2)}, u32[]{:S(2)}) collective-permute-start(bf16[16,1024]{1,0:T(8,128)(2,1)S(1)} %pad_maximum_fusion.3), channel_id=1, source_target_pairs={{0,6},{1,7},{2,4},{3,5},{4,2},{5,3},{6,0},{7,1},{8,14},{9,15},{10,... | collective-permute-start | bytes 98312 | tf_op jit(solution)/shard_map/ppermute | solution.py:422
  41.5 4.8 %collective-permute-start.10 = (bf16[16,1024]{1,0:T(8,128)(2,1)S(1)}, bf16[16,1024]{1,0:T(8,128)(2,1)S(1)}, u32[]{:S(2)}, u32[]{:S(2)}) collective-permute-start(bf16[16,1024]{1,0:T(8,128)(2,1)S(1)} %pad_maximum_fusion.2), channel_id=1, source_target_pairs={{0,4},{1,5},{2,6},{3,7},{4,0},{5,1},{6,2},{7,3},{8,12},{9,13},{10,... | collective-permute-start | bytes 98312 | tf_op jit(solution)/shard_map/ppermute | solution.py:422
  43.3 3.9 %collective-permute-start.9 = (bf16[16,1024]{1,0:T(8,128)(2,1)S(1)}, bf16[16,1024]{1,0:T(8,128)(2,1)S(1)}, u32[]{:S(2)}, u32[]{:S(2)}) collective-permute-start(bf16[16,1024]{1,0:T(8,128)(2,1)S(1)} %pad_maximum_fusion.1), channel_id=1, source_target_pairs={{0,2},{1,3},{2,0},{3,1},{4,6},{5,7},{6,4},{7,5},{8,10},{9,11},{10,... | collective-permute-start | bytes 98312 | tf_op jit(solution)/shard_map/ppermute | solution.py:422

commit v11 on v8

--- a/solution.py
+++ b/solution.py
@@ -343,7 +343,7 @@
     return pl.pallas_call(
         body,
         in_specs=[smem, smem] + [vmem] * (len(operands) - 2),
-        out_specs=[vmem] * shares if last else vmem,
+        out_specs=[vmem] * len(out_shape) if last else vmem,
         out_shape=out_shape,
         scratch_shapes=scratch,
         input_output_aliases=aliases,
@@ -352,27 +352,34 @@
     )(*operands)
 
 
-def sum_kernel(count, each, me_ref, *refs):
+def sum_kernel(count, me_ref, *refs):
     parts, outs, sum_ref = refs[:count], refs[count:-1], refs[-1]
     total = parts[0][...].astype(F32)
     for part in parts[1:]:
         total = total + part[...].astype(F32)
     sum_ref[...] = total
-    for d in range(each):
-        outs[d][...] = sum_ref[:, pl.ds(me_ref[0] ^ d, 1), :].reshape(outs[d].shape).astype(BF16)
+    for d in range(len(outs)):
+        outs[d][...] = sum_ref[:, pl.ds(me_ref[1] ^ d, 1), :].reshape(outs[d].shape).astype(BF16)
 
 
 def sum_groups(parts, me):
     channels, each, bins = parts[0].shape
     vmem = pl.BlockSpec(memory_space=pltpu.VMEM)
     return pl.pallas_call(
-        functools.partial(sum_kernel, len(parts), each),
+        functools.partial(sum_kernel, len(parts)),
         in_specs=[pl.BlockSpec(memory_space=pltpu.SMEM)] + [vmem] * len(parts),
         out_specs=[vmem] * each,
         out_shape=[jax.ShapeDtypeStruct((channels, bins), BF16)] * each,
         scratch_shapes=[pltpu.VMEM(parts[0].shape, F32)],
         compiler_params=pltpu.CompilerParams(vmem_limit_bytes=8 * 2**20),
-    )(me[None], *parts)
+    )(me, *parts)
+
+
+def decode(signal, matrix):
+    decoded = lax.dot_general(
+        signal, matrix, (((0,), (0,)), ((), ())), preferred_element_type=F32
+    )
+    return decoded.astype(BF16)
 
 
 def per_device(src_count, ch_count, dry_signal, room_spectra, render_slot, decoder):
@@ -393,17 +400,15 @@
 
     chips = ch_count // 2
     first = chips // 2
-    lanes = {first: swap(x_own, "ch", ch_count, 2 * first)}
+    far = [d for d in range(chips - 1, 0, -1) if d != first]
+    lanes = {d: swap(x_own, "ch", ch_count, 2 * d) for d in (first, *far)}
     me = jnp.stack([src_me, ch_me])
     hat = transform_responses(room_spectra, me)
-    x_own, hat = lax.optimization_barrier((x_own, hat))
-    rest = [d for d in range(chips - 1, 0, -1) if d != first]
-    lanes.update({d: swap(x_own, "ch", ch_count, 2 * d) for d in rest})
 
     row = jnp.arange(ch_count * channels, dtype=jnp.int32)
     takes = ((row // channels) ^ ch_me) * channels + row % channels
     order = (takes[:, None] == row[None, :]).astype(BF16)
-    own_order = dot(order, decoder).astype(BF16)
+    own_order = lax.optimization_barrier(dot(order, decoder).astype(BF16))
 
     def add(s_list, flips, total, last):
         return add_sources(
@@ -414,36 +419,31 @@
         mine = transform_signals(x_list, own, block_len, parts)
         return mine, swap(mine, "ch", ch_count, 1)
 
-    near_mine, near_given = transform([x_own, lanes[first]])
-    total = add([near_mine], [[0, 2 * first]], None, False)
-    *late, total = lax.optimization_barrier((*[lanes[d] for d in rest], total))
+    near = [0, first]
+    x_near, hat = lax.optimization_barrier((x_own, hat))
+    near_mine, near_given = transform([x_near, lanes[first]])
+    total = add([near_mine], [[2 * d for d in near]], None, False)
+    *late, total = lax.optimization_barrier((*[lanes[d] for d in far], total))
     far_mine, far_given = transform(late)
-    total = add([near_given, far_mine], [[1, 2 * first + 1], [2 * d for d in rest]], total, False)
-    total = add([far_given], [[2 * d + 1 for d in rest]], total, True)
-
-    parts_in = [total[0]] + [swap(total[d], "src", src_count, d) for d in range(1, src_count)]
-    each = blocks // src_count
-    if each == ch_count:
-        pieces = sum_groups(parts_in, ch_me)
+    flips = [[2 * d + 1 for d in near], [2 * d for d in far]]
+    total = add([near_given, far_mine], flips, total, False)
+    total = add([far_given], [[2 * d + 1 for d in far]], total, True)
+
+    sums = [total[0]] + [swap(total[d], "src", src_count, d) for d in range(1, src_count)]
+    if blocks == src_count * ch_count:
+        pieces = sum_groups(sums, me)
         given = swap(jnp.concatenate(pieces[1::2], axis=0), "ch", ch_count, 1)
         both = [
             jnp.concatenate([pieces[2 * d], given[d * channels : (d + 1) * channels]], axis=0)
             for d in range(chips)
         ]
         both[1:] = [swap(both[d], "ch", ch_count, 2 * d) for d in range(1, chips)]
-        gathered = jnp.concatenate(both, axis=0)
-        matrix = own_order
-    else:
-        signal = parts_in[0].astype(F32)
-        for part in parts_in[1:]:
-            signal = signal + part.astype(F32)
-        signal = signal.astype(BF16).reshape(channels, -1)
-        gathered = lax.all_to_all(signal, "ch", split_axis=1, concat_axis=0, tiled=True)
-        matrix = decoder
-    decoded = lax.dot_general(
-        gathered, matrix, (((0,), (0,)), ((), ())), preferred_element_type=F32
-    )
-    return decoded.astype(BF16)
+        return decode(jnp.concatenate(both, axis=0), own_order)
+    signal = sums[0].astype(F32)
+    for part in sums[1:]:
+        signal = signal + part.astype(F32)
+    signal = signal.astype(BF16).reshape(channels, -1)
+    return decode(lax.all_to_all(signal, "ch", split_axis=1, concat_axis=0, tiled=True), decoder)
 
 
 def solution(mesh):

time: 51.1 us -> 51 us (level)
  waiting for transfers between devices: 15.9 us -> 14.9 us
    ppermute x12, waiting for transfers between devices: 15.9 us -> 14.9 us  [swap(): return lax.ppermute(value, axis, [(i, i ^ flip) for i in range(count)])]
    pallas_call x1, Pallas kernels: 0.45 us -> 0.99 us  [sum_groups(): pl.pallas_call(functools.partial(sum_kernel, len(parts)), in_specs=[pl.Bl...]
    dot_general x1 -> x2, matrix products: 2.21 us -> 2.27 us  [the longest x1 2.05 us: decode(): lax.dot_general(signal, matrix, (((0,), (0,)), ((), ())), preferred_eleme...]
  transfers between devices with their start and end apart: 12 -> 12, of which waited for: 7 -> 6; matrix products, arithmetic and copies ran while one was open for 0% -> 1% of each run, Pallas kernels for 28% -> 28%
where the time goes in v11:
time: 51 us; the launch traced here: 50.9 us
  Pallas kernels  19 us (37%)
  waiting for transfers between devices  14.9 us (29%)
  starting transfers between devices  14.3 us (28%)
  matrix products  2.27 us (4%)
    ppermute x12, waiting for transfers between devices, swap(): return lax.ppermute(value, axis, [(i, i ^ flip) for i in range(count)])  14.9 us
    ppermute x12, starting transfers between devices, swap(): return lax.ppermute(value, axis, [(i, i ^ flip) for i in range(count)])  14.3 us
    pallas_call x3, Pallas kernels, add_sources(): pl.pallas_call(body, in_specs=[smem, smem] + [vmem] * (len(operands) - 2)...  8.34 us
    pallas_call x1, Pallas kernels, transform_responses(): pl.pallas_call(functools.partial(response_kernel, rows, bins), in_specs=[...  6.37 us
    pallas_call x2, Pallas kernels, transform_signals(): pl.pallas_call(functools.partial(spectra_kernel, len(x_list), rows), in_s...  3.34 us
    dot_general x1, matrix products, decode(): lax.dot_general(signal, matrix, (((0,), (0,)), ((), ())), preferred_eleme...  2.05 us
  transfers between devices with their start and end apart: 12, of which 6 were waited for; matrix products, arithmetic and copies ran while one was open for 1% of the time, Pallas kernels for 28%

profile of v11, /device:TPU:0, one launch (start us, length us, event | category | flops | bytes accessed | tf_op | source)
XLA Modules:
  0.0 50.9 jit_solution(12038186007497993014)
XLA Ops:
  0.0 0.0 copy-start
  0.0 4.0 %collective-permute-start.2 = (bf16[40,2,1024]{2,1,0:T(2,128)(2,1)}, bf16[40,2,1024]{2,1,0:T(2,128)(2,1)S(1)}, u32[]{:S(2)}, u32[]{:S(2)}) collective-permute-start(bf16[40,2,1024]{2,1,0:T(2,128)(2,1)} %bitcast.8), channel_id=1, source_target_pairs={{0,4},{1,5},{2,6},{3,7},{4,0},{5,1},{6,2},{7,3},{8,12},{9,13},{10,... | collective-permute-start | bytes 491528 | tf_op jit(solution)/shard_map/ppermute | solution.py:399
  4.0 1.3 %collective-permute-start = (bf16[40,2,1024]{2,1,0:T(2,128)(2,1)}, bf16[40,2,1024]{2,1,0:T(2,128)(2,1)S(1)}, u32[]{:S(2)}, u32[]{:S(2)}) collective-permute-start(bf16[40,2,1024]{2,1,0:T(2,128)(2,1)} %bitcast.9), channel_id=1, source_target_pairs={{0,6},{1,7},{2,4},{3,5},{4,2},{5,3},{6,0},{7,1},{8,14},{9,15},{10,... | collective-permute-start | bytes 491528 | tf_op jit(solution)/shard_map/ppermute | solution.py:399
  5.4 0.2 collective-permute-start.1
  5.6 0.1 pad_add_fusion.me_ref
  5.7 0.0 copy-start.1
  5.7 0.0 copy-start.3
  5.7 0.0 copy-start.4
  5.7 6.4 %shard_map.91.refs_1_.refs_2_ = bf16[16,8,384,128]{3,2,1,0:T(8,128)(2,1)S(1)} custom-call(s32[2]{0:T(128)S(1)} %pad_add_fusion.me_ref, bf16[16,8,8,2,1024]{4,3,2,1,0:T(2,128)(2,1)} %room_hbm.1, bf16[384,256]{1,0:T(8,128)(2,1)} %constant.50.clone.table_hbm), custom_call_target="tpu_custom_call" | custom-call | flops 1048576 | bytes 65536 | tf_op jit(solution)/shard_map/pallas_call | solution.py:153
  12.1 0.0 copy-start.6
  12.1 4.3 %collective-permute-done.2.refs_1_ = bf16[40,2,1024]{2,1,0:T(2,128)(2,1)S(1)} collective-permute-done((bf16[40,2,1024]{2,1,0:T(2,128)(2,1)}, bf16[40,2,1024]{2,1,0:T(2,128)(2,1)S(1)}, u32[]{:S(2)}, u32[]{:S(2)}) %collective-permute-start.2) | collective-permute-done | bytes 163872 | tf_op jit(solution)/shard_map/ppermute | solution.py:399
  16.3 0.0 copy-done.1
  16.3 0.0 copy-done.3
  16.3 0.0 copy-done.4
  16.4 1.7 %shard_map.92.refs_0_ = bf16[8,4,96,128]{3,2,1,0:T(8,128)(2,1)S(1)} custom-call(bf16[40,2,1024]{2,1,0:T(2,128)(2,1)S(1)} %bitcast.11, bf16[40,2,1024]{2,1,0:T(2,128)(2,1)S(1)} %collective-permute-done.2.refs_1_, bf16[2,8,1024,128]{3,2,1,0:T(8,128)(2,1)S(1)} %copy-done.1, bf16[2,192,160]{2,1,0:T(8,128)(2,1)S(1)} %copy-done.3), custom_call_target="tpu_custom_call" | custom-call | flops 1048576 | bytes 65536 | tf_op jit(solution)/shard_map/pallas_call | solution.py:208
  18.0 0.1 collective-permute-start.4
  18.1 0.0 copy-done.6
  18.1 1.5 %shard_map.93.refs_3_ = f32[8,4,192,128]{3,2,1,0:T(8,128)S(1)} custom-call(s32[2]{0:T(128)S(1)} %pad_add_fusion.me_ref, s32[16]{0:T(128)S(1)} %copy-done.6, bf16[8,4,96,128]{3,2,1,0:T(8,128)(2,1)S(1)} %shard_map.92.refs_0_, bf16[16,8,384,128]{3,2,1,0:T(8,128)(2,1)S(1)} %shard_map.91.refs_1_.refs_2_), custom_call_target="tpu_custom_call" | custom-call | flops 1048576 | bytes 65536 | tf_op jit(solution)/shard_map/pallas_call | solution.py:343
  19.7 0.0 collective-permute-done.refs_0_
  19.7 0.0 collective-permute-done.1.refs_1_
  19.7 1.7 %shard_map.94.refs_1_ = bf16[8,4,96,128]{3,2,1,0:T(8,128)(2,1)S(1)} custom-call(bf16[40,2,1024]{2,1,0:T(2,128)(2,1)S(1)} %collective-permute-done.refs_0_, bf16[40,2,1024]{2,1,0:T(2,128)(2,1)S(1)} %collective-permute-done.1.refs_1_, bf16[2,8,1024,128]{3,2,1,0:T(8,128)(2,1)S(1)} %copy-done.1, bf16[2,192,160]{2,1,0:T(8,128)(2,1)S(1)} %copy-done.3), custom_call_target="tpu_custom_call" | custom-call | flops 1048576 | bytes 65536 | tf_op jit(solution)/shard_map/pallas_call | solution.py:208
  21.4 0.6 %collective-permute-start.3 = (bf16[8,4,96,128]{3,2,1,0:T(8,128)(2,1)S(1)}, bf16[8,4,96,128]{3,2,1,0:T(8,128)(2,1)S(1)}, u32[]{:S(2)}, u32[]{:S(2)}) collective-permute-start(bf16[8,4,96,128]{3,2,1,0:T(8,128)(2,1)S(1)} %shard_map.94.refs_1_), channel_id=1, source_target_pairs={{0,1},{1,0},{2,3},{3,2},{4,5},{5,4},{6,7},{7,6},{8,9},{9,8},{10,11... | collective-permute-start | bytes 2359304 | tf_op jit(solution)/shard_map/ppermute | solution.py:399
  21.9 0.0 copy-start.2
  21.9 0.0 copy-start.5
  21.9 0.0 collective-permute-done.4.refs_0_
  21.9 3.1 %shard_map.95.refs_2_ = f32[8,4,192,128]{3,2,1,0:T(8,128)S(1)} custom-call(s32[2]{0:T(128)S(1)} %pad_add_fusion.me_ref, s32[16]{0:T(128)S(1)} %copy-done.6, bf16[8,4,96,128]{3,2,1,0:T(8,128)(2,1)S(1)} %collective-permute-done.4.refs_0_, bf16[8,4,96,128]{3,2,1,0:T(8,128)(2,1)S(1)} %shard_map.94.refs_1_, ...), custom_call_target="tpu_custom_call", output_to_operand_aliasing={{}: (5, {})} | custom-call | flops 1048576 | bytes 65536 | tf_op jit(solution)/shard_map/pallas_call | solution.py:343
  25.0 0.0 collective-permute-done.3.refs_0_
  25.1 0.0 copy-done.2
  25.1 0.0 copy-done.5
  25.1 3.7 %shard_map.96 = (bf16[8,8,1024]{2,1,0:T(8,128)(2,1)S(1)}, bf16[8,8,1024]{2,1,0:T(8,128)(2,1)S(1)}, bf16[8,8,1024]{2,1,0:T(8,128)(2,1)S(1)}, bf16[8,8,1024]{2,1,0:T(8,128)(2,1)S(1)}) custom-call(s32[2]{0:T(128)S(1)} %pad_add_fusion.me_ref, s32[16]{0:T(128)S(1)} %copy-done.6, bf16[8,4,96,128]{3,2,1,0:T(8,128)(2,1)S(1)} %collective-permute-done.3.refs_0_, ...), custom_call_target="tpu_custom_call" | custom-call | flops 1048576 | bytes 65536 | tf_op jit(solution)/shard_map/pallas_call | solution.py:343
  28.8 1.9 %collective-permute-start.5 = (bf16[8,8,1024]{2,1,0:T(8,128)(2,1)S(1)}, bf16[8,8,1024]{2,1,0:T(8,128)(2,1)S(1)}, u32[]{:S(2)}, u32[]{:S(2)}) collective-permute-start(bf16[8,8,1024]{2,1,0:T(8,128)(2,1)S(1)} %get-tuple-element.28), channel_id=1, source_target_pairs={{0,8},{8,0},{16,24},{24,16},{1,9},{9,1},{17,25},{25,17},{2,10},{10... | collective-permute-start | bytes 393224 | tf_op jit(solution)/shard_map/ppermute | solution.py:399
  30.7 1.5 %collective-permute-start.6 = (bf16[8,8,1024]{2,1,0:T(8,128)(2,1)S(1)}, bf16[8,8,1024]{2,1,0:T(8,128)(2,1)S(1)}, u32[]{:S(2)}, u32[]{:S(2)}) collective-permute-start(bf16[8,8,1024]{2,1,0:T(8,128)(2,1)S(1)} %get-tuple-element.29), channel_id=1, source_target_pairs={{0,16},{8,24},{16,0},{24,8},{1,17},{9,25},{17,1},{25,9},{2,18},{10... | collective-permute-start | bytes 393224 | tf_op jit(solution)/shard_map/ppermute | solution.py:399
  32.2 0.1 collective-permute-start.7
  32.3 0.0 copy-done
  32.3 0.2 convolution_convert_fusion.1
  32.6 2.0 %collective-permute-done.5.refs_1_ = bf16[8,8,1024]{2,1,0:T(8,128)(2,1)S(1)} collective-permute-done((bf16[8,8,1024]{2,1,0:T(8,128)(2,1)S(1)}, bf16[8,8,1024]{2,1,0:T(8,128)(2,1)S(1)}, u32[]{:S(2)}, u32[]{:S(2)}) %collective-permute-start.5) | collective-permute-done | bytes 131104 | tf_op jit(solution)/shard_map/ppermute | solution.py:399
  34.6 4.1 %collective-permute-done.6.refs_2_ = bf16[8,8,1024]{2,1,0:T(8,128)(2,1)S(1)} collective-permute-done((bf16[8,8,1024]{2,1,0:T(8,128)(2,1)S(1)}, bf16[8,8,1024]{2,1,0:T(8,128)(2,1)S(1)}, u32[]{:S(2)}, u32[]{:S(2)}) %collective-permute-start.6) | collective-permute-done | bytes 131104 | tf_op jit(solution)/shard_map/ppermute | solution.py:399
  38.7 0.0 collective-permute-done.7.refs_3_
  38.7 1.0 %shard_map.97 = (bf16[8,1024]{1,0:T(8,128)(2,1)S(1)}, bf16[8,1024]{1,0:T(8,128)(2,1)S(1)}, bf16[8,1024]{1,0:T(8,128)(2,1)S(1)}, bf16[8,1024]{1,0:T(8,128)(2,1)S(...) custom-call(s32[2]{0:T(128)S(1)} %pad_add_fusion.me_ref, ...), custom_call_target="tpu_custom_call" | custom-call | tf_op jit(solution)/shard_map/pallas_call | solution.py:368
  39.7 0.1 collective-permute-start.8
  39.8 1.2 %collective-permute-done.8 = bf16[32,1024]{1,0:T(8,128)(2,1)S(1)} collective-permute-done((bf16[32,1024]{1,0:T(8,128)(2,1)S(1)}, bf16[32,1024]{1,0:T(8,128)(2,1)S(1)}, u32[]{:S(2)}, u32[]{:S(2)}) %collective-permute-start.8) | collective-permute-done | bytes 65568 | tf_op jit(solution)/shard_map/ppermute | solution.py:399
  41.0 2.5 %collective-permute-start.11 = (bf16[16,1024]{1,0:T(8,128)(2,1)S(1)}, bf16[16,1024]{1,0:T(8,128)(2,1)S(1)}, u32[]{:S(2)}, u32[]{:S(2)}) collective-permute-start(bf16[16,1024]{1,0:T(8,128)(2,1)S(1)} %pad_maximum_fusion.3), channel_id=1, source_target_pairs={{0,6},{1,7},{2,4},{3,5},{4,2},{5,3},{6,0},{7,1},{8,14},{9,15},{10,... | collective-permute-start | bytes 98312 | tf_op jit(solution)/shard_map/ppermute | solution.py:399
  43.5 0.0 collective-permute-start.9
  43.6 1.9 %collective-permute-start.10 = (bf16[16,1024]{1,0:T(8,128)(2,1)S(1)}, bf16[16,1024]{1,0:T(8,128)(2,1)S(1)}, u32[]{:S(2)}, u32[]{:S(2)}) collective-permute-start(bf16[16,1024]{1,0:T(8,128)(2,1)S(1)} %pad_maximum_fusion.2), channel_id=1, source_target_pairs={{0,4},{1,5},{2,6},{3,7},{4,0},{5,1},{6,2},{7,3},{8,12},{9,13},{10,... | collective-permute-start | bytes 98312 | tf_op jit(solution)/shard_map/ppermute | solution.py:399
  45.5 2.2 %collective-permute-done.9 = bf16[16,1024]{1,0:T(8,128)(2,1)S(1)} collective-permute-done((bf16[16,1024]{1,0:T(8,128)(2,1)S(1)}, bf16[16,1024]{1,0:T(8,128)(2,1)S(1)}, u32[]{:S(2)}, u32[]{:S(2)}) %collective-permute-start.9) | collective-permute-done | bytes 32800 | tf_op jit(solution)/shard_map/ppermute | solution.py:399
  47.7 1.1 %collective-permute-done.10 = bf16[16,1024]{1,0:T(8,128)(2,1)S(1)} collective-permute-done((bf16[16,1024]{1,0:T(8,128)(2,1)S(1)}, bf16[16,1024]{1,0:T(8,128)(2,1)S(1)}, u32[]{:S(2)}, u32[]{:S(2)}) %collective-permute-start.10) | collective-permute-done | bytes 32800 | tf_op jit(solution)/shard_map/ppermute | solution.py:399
  48.8 0.0 collective-permute-done.11
  48.8 2.1 %convolution_convert_fusion = bf16[1024,1024]{1,0:T(8,128)(2,1)} fusion(bf16[64,1024]{1,0:T(8,128)(2,1)S(1)} %constant_dynamic-update-slice_fusion, bf16[64,1024]{1,0:T(8,128)(2,1)S(1)} %convolution_convert_fusion.1), kind=kOutput, calls=%fused_computation | convolution fusion | flops 135266304 | bytes 2359296 | tf_op jit(solution)/shard_map/dot_general | solution.py:379
  (10 shorter events, 0.0 us)
Async XLA Ops:
  0.0 32.3 %copy-start = (bf16[64,1024]{1,0:T(8,128)(2,1)S(1)}, bf16[64,1024]{1,0:T(8,128)(2,1)}, u32[]{:S(2)}) copy-start(bf16[64,1024]{1,0:T(8,128)(2,1)} %param.12) | copy-start | bytes 393220
  0.0 16.3 %collective-permute-start.2 = (bf16[40,2,1024]{2,1,0:T(2,128)(2,1)}, bf16[40,2,1024]{2,1,0:T(2,128)(2,1)S(1)}, u32[]{:S(2)}, u32[]{:S(2)}) collective-permute-start(bf16[40,2,1024]{2,1,0:T(2,128)(2,1)} %bitcast.8), channel_id=1, source_target_pairs={{0,4},{1,5},{2,6},{3,7},{4,0},{5,1},{6,2},{7,3},{8,12},{9,13},{10,... | collective-permute-start | bytes 491528 | tf_op jit(solution)/shard_map/ppermute | solution.py:399
  4.0 15.6 %collective-permute-start = (bf16[40,2,1024]{2,1,0:T(2,128)(2,1)}, bf16[40,2,1024]{2,1,0:T(2,128)(2,1)S(1)}, u32[]{:S(2)}, u32[]{:S(2)}) collective-permute-start(bf16[40,2,1024]{2,1,0:T(2,128)(2,1)} %bitcast.9), channel_id=1, source_target_pairs={{0,6},{1,7},{2,4},{3,5},{4,2},{5,3},{6,0},{7,1},{8,14},{9,15},{10,... | collective-permute-start | bytes 491528 | tf_op jit(solution)/shard_map/ppermute | solution.py:399
  5.4 14.3 %collective-permute-start.1 = (bf16[40,2,1024]{2,1,0:T(2,128)(2,1)}, bf16[40,2,1024]{2,1,0:T(2,128)(2,1)S(1)}, u32[]{:S(2)}, u32[]{:S(2)}) collective-permute-start(bf16[40,2,1024]{2,1,0:T(2,128)(2,1)} %bitcast.10), channel_id=1, source_target_pairs={{0,2},{1,3},{2,0},{3,1},{4,6},{5,7},{6,4},{7,5},{8,10},{9,11},{10,... | collective-permute-start | bytes 491528 | tf_op jit(solution)/shard_map/ppermute | solution.py:399
  5.7 10.6 %copy-start.1 = (bf16[2,8,1024,128]{3,2,1,0:T(8,128)(2,1)S(1)}, bf16[2,8,1024,128]{3,2,1,0:T(8,128)(2,1)}, u32[]{:S(2)}) copy-start(bf16[2,8,1024,128]{3,2,1,0:T(8,128)(2,1)} %constant.51.clone.refs_2_) | copy-start | bytes 12582916
  5.7 10.7 %copy-start.3 = (bf16[2,192,160]{2,1,0:T(8,128)(2,1)S(1)}, bf16[2,192,160]{2,1,0:T(8,128)(2,1)}, u32[]{:S(2)}) copy-start(bf16[2,192,160]{2,1,0:T(8,128)(2,1)} %constant.52.clone.refs_3_) | copy-start | bytes 368644
  5.7 10.7 %copy-start.4 = (bf16[2,40960]{1,0:T(2,128)(2,1)S(1)}, bf16[2,40960]{1,0:T(2,128)(2,1)}, u32[]{:S(2)}) copy-start(bf16[2,40960]{1,0:T(2,128)(2,1)} %param.9) | copy-start | bytes 491524
  12.1 6.0 %copy-start.6 = (s32[16]{0:T(128)S(1)}, s32[16]{0:T(128)}, u32[]{:S(2)}) copy-start(s32[16]{0:T(128)} %slot_ref.5) | copy-start | bytes 196
  18.0 3.9 %collective-permute-start.4 = (bf16[8,4,96,128]{3,2,1,0:T(8,128)(2,1)S(1)}, bf16[8,4,96,128]{3,2,1,0:T(8,128)(2,1)S(1)}, u32[]{:S(2)}, u32[]{:S(2)}) collective-permute-start(bf16[8,4,96,128]{3,2,1,0:T(8,128)(2,1)S(1)} %shard_map.92.refs_0_), channel_id=1, source_target_pairs={{0,1},{1,0},{2,3},{3,2},{4,5},{5,4},{6,7},{7,6},{8,9},{9,8},{10,11... | collective-permute-start | bytes 2359304 | tf_op jit(solution)/shard_map/ppermute | solution.py:399
  21.4 3.7 %collective-permute-start.3 = (bf16[8,4,96,128]{3,2,1,0:T(8,128)(2,1)S(1)}, bf16[8,4,96,128]{3,2,1,0:T(8,128)(2,1)S(1)}, u32[]{:S(2)}, u32[]{:S(2)}) collective-permute-start(bf16[8,4,96,128]{3,2,1,0:T(8,128)(2,1)S(1)} %shard_map.94.refs_1_), channel_id=1, source_target_pairs={{0,1},{1,0},{2,3},{3,2},{4,5},{5,4},{6,7},{7,6},{8,9},{9,8},{10,11... | collective-permute-start | bytes 2359304 | tf_op jit(solution)/shard_map/ppermute | solution.py:399
  21.9 3.1 %copy-start.2 = (bf16[2,8,1024,128]{3,2,1,0:T(8,128)(2,1)S(1)}, bf16[2,8,1024,128]{3,2,1,0:T(8,128)(2,1)}, u32[]{:S(2)}) copy-start(bf16[2,8,1024,128]{3,2,1,0:T(8,128)(2,1)} %constant.54.clone.refs_4_) | copy-start | bytes 12582916
  21.9 3.1 %copy-start.5 = (bf16[2,128,192]{2,1,0:T(8,128)(2,1)S(1)}, bf16[2,128,192]{2,1,0:T(8,128)(2,1)}, u32[]{:S(2)}) copy-start(bf16[2,128,192]{2,1,0:T(8,128)(2,1)} %constant.53.clone.refs_3_) | copy-start | bytes 294916
  28.8 5.8 %collective-permute-start.5 = (bf16[8,8,1024]{2,1,0:T(8,128)(2,1)S(1)}, bf16[8,8,1024]{2,1,0:T(8,128)(2,1)S(1)}, u32[]{:S(2)}, u32[]{:S(2)}) collective-permute-start(bf16[8,8,1024]{2,1,0:T(8,128)(2,1)S(1)} %get-tuple-element.28), channel_id=1, source_target_pairs={{0,8},{8,0},{16,24},{24,16},{1,9},{9,1},{17,25},{25,17},{2,10},{10... | collective-permute-start | bytes 393224 | tf_op jit(solution)/shard_map/ppermute | solution.py:399
  30.7 8.0 %collective-permute-start.6 = (bf16[8,8,1024]{2,1,0:T(8,128)(2,1)S(1)}, bf16[8,8,1024]{2,1,0:T(8,128)(2,1)S(1)}, u32[]{:S(2)}, u32[]{:S(2)}) collective-permute-start(bf16[8,8,1024]{2,1,0:T(8,128)(2,1)S(1)} %get-tuple-element.29), channel_id=1, source_target_pairs={{0,16},{8,24},{16,0},{24,8},{1,17},{9,25},{17,1},{25,9},{2,18},{10... | collective-permute-start | bytes 393224 | tf_op jit(solution)/shard_map/ppermute | solution.py:399
  32.2 6.5 %collective-permute-start.7 = (bf16[8,8,1024]{2,1,0:T(8,128)(2,1)S(1)}, bf16[8,8,1024]{2,1,0:T(8,128)(2,1)S(1)}, u32[]{:S(2)}, u32[]{:S(2)}) collective-permute-start(bf16[8,8,1024]{2,1,0:T(8,128)(2,1)S(1)} %get-tuple-element.30), channel_id=1, source_target_pairs={{0,24},{8,16},{16,8},{24,0},{1,25},{9,17},{17,9},{25,1},{2,26},{10... | collective-permute-start | bytes 393224 | tf_op jit(solution)/shard_map/ppermute | solution.py:399
  39.7 1.3 %collective-permute-start.8 = (bf16[32,1024]{1,0:T(8,128)(2,1)S(1)}, bf16[32,1024]{1,0:T(8,128)(2,1)S(1)}, u32[]{:S(2)}, u32[]{:S(2)}) collective-permute-start(bf16[32,1024]{1,0:T(8,128)(2,1)S(1)} %pad_maximum_fusion), channel_id=1, source_target_pairs={{0,1},{1,0},{2,3},{3,2},{4,5},{5,4},{6,7},{7,6},{8,9},{9,8},{10,11... | collective-permute-start | bytes 196616 | tf_op jit(solution)/shard_map/ppermute | solution.py:399
  41.0 7.8 %collective-permute-start.11 = (bf16[16,1024]{1,0:T(8,128)(2,1)S(1)}, bf16[16,1024]{1,0:T(8,128)(2,1)S(1)}, u32[]{:S(2)}, u32[]{:S(2)}) collective-permute-start(bf16[16,1024]{1,0:T(8,128)(2,1)S(1)} %pad_maximum_fusion.3), channel_id=1, source_target_pairs={{0,6},{1,7},{2,4},{3,5},{4,2},{5,3},{6,0},{7,1},{8,14},{9,15},{10,... | collective-permute-start | bytes 98312 | tf_op jit(solution)/shard_map/ppermute | solution.py:399
  43.5 4.1 %collective-permute-start.9 = (bf16[16,1024]{1,0:T(8,128)(2,1)S(1)}, bf16[16,1024]{1,0:T(8,128)(2,1)S(1)}, u32[]{:S(2)}, u32[]{:S(2)}) collective-permute-start(bf16[16,1024]{1,0:T(8,128)(2,1)S(1)} %pad_maximum_fusion.1), channel_id=1, source_target_pairs={{0,2},{1,3},{2,0},{3,1},{4,6},{5,7},{6,4},{7,5},{8,10},{9,11},{10,... | collective-permute-start | bytes 98312 | tf_op jit(solution)/shard_map/ppermute | solution.py:399
  43.6 5.2 %collective-permute-start.10 = (bf16[16,1024]{1,0:T(8,128)(2,1)S(1)}, bf16[16,1024]{1,0:T(8,128)(2,1)S(1)}, u32[]{:S(2)}, u32[]{:S(2)}) collective-permute-start(bf16[16,1024]{1,0:T(8,128)(2,1)S(1)} %pad_maximum_fusion.2), channel_id=1, source_target_pairs={{0,4},{1,5},{2,6},{3,7},{4,0},{5,1},{6,2},{7,3},{8,12},{9,13},{10,... | collective-permute-start | bytes 98312 | tf_op jit(solution)/shard_map/ppermute | solution.py:399

commit v12 on v11

--- a/solution.py
+++ b/solution.py
@@ -110,14 +110,15 @@
     return jnp.concatenate([ref[(*index, first + i)] for i in range(LANES // SLAB)], axis=-1)
 
 
-def response_kernel(rows, bins, me_ref, room_hbm, table_hbm, hat_ref, room_ref, table_ref, sems):
+def response_kernel(rows, bins, src_ref, ch_ref, slot_ref, room_hbm, table_hbm, hat_ref, room_ref, table_ref, sems):
     depth = room_ref.shape[1] * room_ref.shape[2] * 2
     flat = room_ref.reshape(rows, depth, bins)
     plain, packed, _ = lane_masks(0, LANES)
     plain, packed = plain.astype(BF16), packed.astype(BF16)
 
     def copy(r):
-        return pltpu.make_async_copy(room_hbm.at[r], room_ref.at[r], sems.at[r])
+        row = lax.rem(slot_ref[r], rows)
+        return pltpu.make_async_copy(room_hbm.at[row], room_ref.at[r], sems.at[r])
 
     table_copy = pltpu.make_async_copy(table_hbm, table_ref, sems.at[rows])
     table_copy.start()
@@ -145,14 +146,14 @@
     lax.fori_loop(0, rows // ROWS, some, 0)
 
 
-def transform_responses(room, me):
+def transform_responses(room, me, slots):
     rows, parts, channels, _, bins = room.shape
     slabs = bins // SLAB
     _, resp, _ = step_tables(parts, parts + SEGS * KEEP, channels)
     hbm = pl.BlockSpec(memory_space=pltpu.HBM)
     return pl.pallas_call(
         functools.partial(response_kernel, rows, bins),
-        in_specs=[pl.BlockSpec(memory_space=pltpu.SMEM), hbm, hbm],
+        in_specs=[pl.BlockSpec(memory_space=pltpu.SMEM)] * 3 + [hbm, hbm],
         out_specs=pl.BlockSpec(memory_space=pltpu.VMEM),
         out_shape=pltpu.VMEM((rows, slabs, channels * 2 * STEPS, SLAB), BF16),
         scratch_shapes=[
@@ -163,7 +164,8 @@
         compiler_params=pltpu.CompilerParams(vmem_limit_bytes=8 * 2**20),
         cost_estimate=COST,
     )(
-        me,
+        *me,
+        slots,
         pltpu.with_memory_space_constraint(room, pltpu.HBM),
         pltpu.with_memory_space_constraint(jnp.asarray(resp), pltpu.HBM),
     )
@@ -215,7 +217,7 @@
     )(*operands)
 
 
-def mix_kernel(flips, own, channels, blocks, shares, has_total, last, me_ref, slot_ref, *refs):
+def mix_kernel(flips, own, channels, blocks, shares, has_total, last, src_ref, ch_ref, *refs):
     refs = list(refs)
     s_refs = [refs.pop(0) for _ in flips]
     hat_ref = refs.pop(0)
@@ -235,8 +237,7 @@
     for ref, some in zip(s_refs, flips):
         for k, flip in enumerate(some):
             for i in range(own):
-                slot = lax.rem(slot_ref[(me_ref[1] ^ flip) * own + i], hat_ref.shape[0])
-                sources.append((ref, k * own + i, slot))
+                sources.append((ref, k * own + i, (ch_ref[0] ^ flip) * own + i))
     groups = -(-len(sources) // GROUP)
     size = -(-len(sources) // groups)
 
@@ -304,10 +305,10 @@
                     row = c * blocks + t * each
                     time_ref[t, c, :, here] = part[row : row + each]
         for d in range(shares):
-            out_refs[d][...] = time_ref[me_ref[0] ^ d].astype(BF16)
-
-
-def add_sources(s_list, flips, own, me, slots, hat, total, last, shares, channels, parts):
+            out_refs[d][...] = time_ref[src_ref[0] ^ d].astype(BF16)
+
+
+def add_sources(s_list, flips, own, me, hat, total, last, shares, channels, parts):
     slabs = hat.shape[1]
     bins = slabs * SLAB
     frames = parts + SEGS * KEEP
@@ -318,7 +319,7 @@
     vmem = pl.BlockSpec(memory_space=pltpu.VMEM)
     smem = pl.BlockSpec(memory_space=pltpu.SMEM)
 
-    operands = [me, slots] + list(s_list) + [pltpu.with_memory_space_constraint(hat, pltpu.VMEM)]
+    operands = [*me] + list(s_list) + [pltpu.with_memory_space_constraint(hat, pltpu.VMEM)]
     aliases = {}
     if total is not None:
         if not last:
@@ -342,7 +343,7 @@
     )
     return pl.pallas_call(
         body,
-        in_specs=[smem, smem] + [vmem] * (len(operands) - 2),
+        in_specs=[smem] * 2 + [vmem] * (len(operands) - 2),
         out_specs=[vmem] * len(out_shape) if last else vmem,
         out_shape=out_shape,
         scratch_shapes=scratch,
@@ -352,14 +353,14 @@
     )(*operands)
 
 
-def sum_kernel(count, me_ref, *refs):
+def sum_kernel(count, ch_ref, *refs):
     parts, outs, sum_ref = refs[:count], refs[count:-1], refs[-1]
     total = parts[0][...].astype(F32)
     for part in parts[1:]:
         total = total + part[...].astype(F32)
     sum_ref[...] = total
     for d in range(len(outs)):
-        outs[d][...] = sum_ref[:, pl.ds(me_ref[1] ^ d, 1), :].reshape(outs[d].shape).astype(BF16)
+        outs[d][...] = sum_ref[:, pl.ds(ch_ref[0] ^ d, 1), :].reshape(outs[d].shape).astype(BF16)
 
 
 def sum_groups(parts, me):
@@ -400,10 +401,11 @@
 
     chips = ch_count // 2
     first = chips // 2
-    far = [d for d in range(chips - 1, 0, -1) if d != first]
-    lanes = {d: swap(x_own, "ch", ch_count, 2 * d) for d in (first, *far)}
-    me = jnp.stack([src_me, ch_me])
-    hat = transform_responses(room_spectra, me)
+    far = [first] + [d for d in range(chips - 1, 0, -1) if d != first]
+    mate = swap(x_own, "ch", ch_count, 1)
+    lanes = {d: swap(x_own, "ch", ch_count, 2 * d) for d in far}
+    me = (src_me[None], ch_me[None])
+    hat = transform_responses(room_spectra, me, render_slot)
 
     row = jnp.arange(ch_count * channels, dtype=jnp.int32)
     takes = ((row // channels) ^ ch_me) * channels + row % channels
@@ -412,26 +414,21 @@
 
     def add(s_list, flips, total, last):
         return add_sources(
-            s_list, flips, own, me, render_slot, hat, total, last, src_count, channels, parts
+            s_list, flips, own, me, hat, total, last, src_count, channels, parts
         )
 
-    def transform(x_list):
-        mine = transform_signals(x_list, own, block_len, parts)
-        return mine, swap(mine, "ch", ch_count, 1)
-
-    near = [0, first]
     x_near, hat = lax.optimization_barrier((x_own, hat))
-    near_mine, near_given = transform([x_near, lanes[first]])
-    total = add([near_mine], [[2 * d for d in near]], None, False)
+    near = transform_signals([x_near, mate], own, block_len, parts)
+    total = add([near], [[0, 1]], None, False)
     *late, total = lax.optimization_barrier((*[lanes[d] for d in far], total))
-    far_mine, far_given = transform(late)
-    flips = [[2 * d + 1 for d in near], [2 * d for d in far]]
-    total = add([near_given, far_mine], flips, total, False)
-    total = add([far_given], [[2 * d + 1 for d in far]], total, True)
+    mine = transform_signals(late, own, block_len, parts)
+    given = swap(mine, "ch", ch_count, 1)
+    total = add([mine], [[2 * d for d in far]], total, False)
+    total = add([given], [[2 * d + 1 for d in far]], total, True)
 
     sums = [total[0]] + [swap(total[d], "src", src_count, d) for d in range(1, src_count)]
     if blocks == src_count * ch_count:
-        pieces = sum_groups(sums, me)
+        pieces = sum_groups(sums, ch_me[None])
         given = swap(jnp.concatenate(pieces[1::2], axis=0), "ch", ch_count, 1)
         both = [
             jnp.concatenate([pieces[2 * d], given[d * channels : (d + 1) * channels]], axis=0)

time: 51 us -> 50.5 us (level)
  Pallas kernels: 19 us -> 17.5 us
  local copies, waits for them, and re-layouts: 0.05 us -> 0.7 us
    pallas_call x3, Pallas kernels: 8.34 us -> 6.94 us  [add_sources(): pl.pallas_call(body, in_specs=[smem] * 2 + [vmem] * (len(operands) - 2),...]
    unnamed x17, local copies, waits for them, and re-layouts: 0.04 us -> 0.69 us
    pallas_call x1, Pallas kernels: 0.99 us -> 0.45 us  [sum_groups(): pl.pallas_call(functools.partial(sum_kernel, len(parts)), in_specs=[pl.Bl...]
  transfers between devices with their start and end apart: 12 -> 12, of which waited for: 6 -> 8; matrix products, arithmetic and copies ran while one was open for 1% -> 0% of each run, Pallas kernels for 28% -> 22%
where the time goes in v12:
time: 50.5 us; the launch traced here: 50.3 us
  Pallas kernels  17.5 us (35%)
  waiting for transfers between devices  14.9 us (30%)
  starting transfers between devices  14.8 us (29%)
  matrix products  2.28 us (5%)
  local copies, waits for them, and re-layouts  0.7 us (1%)
    ppermute x12, waiting for transfers between devices, swap(): return lax.ppermute(value, axis, [(i, i ^ flip) for i in range(count)])  14.9 us
    ppermute x12, starting transfers between devices, swap(): return lax.ppermute(value, axis, [(i, i ^ flip) for i in range(count)])  14.8 us
    pallas_call x3, Pallas kernels, add_sources(): pl.pallas_call(body, in_specs=[smem] * 2 + [vmem] * (len(operands) - 2),...  6.94 us
    pallas_call x1, Pallas kernels, transform_responses(): pl.pallas_call(functools.partial(response_kernel, rows, bins), in_specs=[...  6.38 us
    pallas_call x2, Pallas kernels, transform_signals(): pl.pallas_call(functools.partial(spectra_kernel, len(x_list), rows), in_s...  3.73 us
    dot_general x1, matrix products, decode(): lax.dot_general(signal, matrix, (((0,), (0,)), ((), ())), preferred_eleme...  2.05 us
  transfers between devices with their start and end apart: 12, of which 8 were waited for; matrix products, arithmetic and copies ran while one was open for 0% of the time, Pallas kernels for 22%

profile of v12, /device:TPU:0, one launch (start us, length us, event | category | flops | bytes accessed | tf_op | source)
XLA Modules:
  0.0 50.3 jit_solution(15187346838597916469)
XLA Ops:
  0.0 0.0 copy-start
  0.0 0.5 collective-permute-start.3
  0.5 3.7 %collective-permute-start = (bf16[40,2,1024]{2,1,0:T(2,128)(2,1)}, bf16[40,2,1024]{2,1,0:T(2,128)(2,1)S(1)}, u32[]{:S(2)}, u32[]{:S(2)}) collective-permute-start(bf16[40,2,1024]{2,1,0:T(2,128)(2,1)} %bitcast.9), channel_id=1, source_target_pairs={{0,4},{1,5},{2,6},{3,7},{4,0},{5,1},{6,2},{7,3},{8,12},{9,13},{10,... | collective-permute-start | bytes 491528 | tf_op jit(solution)/shard_map/ppermute | solution.py:400
  4.1 1.3 %collective-permute-start.1 = (bf16[40,2,1024]{2,1,0:T(2,128)(2,1)}, bf16[40,2,1024]{2,1,0:T(2,128)(2,1)S(1)}, u32[]{:S(2)}, u32[]{:S(2)}) collective-permute-start(bf16[40,2,1024]{2,1,0:T(2,128)(2,1)} %bitcast.10), channel_id=1, source_target_pairs={{0,6},{1,7},{2,4},{3,5},{4,2},{5,3},{6,0},{7,1},{8,14},{9,15},{10,... | collective-permute-start | bytes 491528 | tf_op jit(solution)/shard_map/ppermute | solution.py:400
  5.5 0.2 collective-permute-start.2
  5.7 0.0 copy-start.6
  5.7 0.7 %copy-done.6 = s32[16]{0:T(128)S(1)} copy-done((s32[16]{0:T(128)S(1)}, s32[16]{0:T(128)}, u32[]{:S(2)}) %copy-start.6) | copy-done | bytes 88
  6.3 0.0 copy-start.1
  6.3 0.0 copy-start.3
  6.4 0.0 copy-start.4
  6.4 6.4 %shard_map.91.refs_1_ = bf16[16,8,384,128]{3,2,1,0:T(8,128)(2,1)S(1)} custom-call(s32[1]{0:T(128)} %bitcast.1.src_ref, s32[1]{0:T(128)} %bitcast.ch_ref, s32[16]{0:T(128)S(1)} %copy-done.6, bf16[16,8,8,2,1024]{4,3,2,1,0:T(2,128)(2,1)} %room_hbm.1, bf16[384,256]{1,0:T(8,128)(2,1)} %constant.50.clone.table_hbm), custom_call_target="tpu_custom_call" | custom-call | flops 1048576 | bytes 65536 | tf_op jit(solution)/shard_map/pallas_call | solution.py:154
  12.7 0.0 collective-permute-done.3.refs_1_
  12.7 0.0 copy-done.1
  12.8 0.0 copy-done.3
  12.8 0.0 copy-done.4
  12.8 1.7 %shard_map.92.refs_0_ = bf16[8,4,96,128]{3,2,1,0:T(8,128)(2,1)S(1)} custom-call(bf16[40,2,1024]{2,1,0:T(2,128)(2,1)S(1)} %bitcast.12, bf16[40,2,1024]{2,1,0:T(2,128)(2,1)S(1)} %collective-permute-done.3.refs_1_, bf16[2,8,1024,128]{3,2,1,0:T(8,128)(2,1)S(1)} %copy-done.1, bf16[2,192,160]{2,1,0:T(8,128)(2,1)S(1)} %copy-done.3), custom_call_target="tpu_custom_call" | custom-call | flops 1048576 | bytes 65536 | tf_op jit(solution)/shard_map/pallas_call | solution.py:210
  14.4 1.0 %shard_map.93.refs_2_ = f32[8,4,192,128]{3,2,1,0:T(8,128)S(1)} custom-call(s32[1]{0:T(128)} %bitcast.1.src_ref, s32[1]{0:T(128)} %bitcast.ch_ref, bf16[8,4,96,128]{3,2,1,0:T(8,128)(2,1)S(1)} %shard_map.92.refs_0_, bf16[16,8,384,128]{3,2,1,0:T(8,128)(2,1)S(1)} %shard_map.91.refs_1_), custom_call_target="tpu_custom_call" | custom-call | flops 1048576 | bytes 65536 | tf_op jit(solution)/shard_map/pallas_call | solution.py:344
  15.5 1.0 %collective-permute-done.refs_0_ = bf16[40,2,1024]{2,1,0:T(2,128)(2,1)S(1)} collective-permute-done((bf16[40,2,1024]{2,1,0:T(2,128)(2,1)}, bf16[40,2,1024]{2,1,0:T(2,128)(2,1)S(1)}, u32[]{:S(2)}, u32[]{:S(2)}) %collective-permute-start) | collective-permute-done | bytes 163872 | tf_op jit(solution)/shard_map/ppermute | solution.py:400
  16.4 0.0 collective-permute-done.1.refs_1_
  16.4 1.1 %collective-permute-done.2.refs_2_ = bf16[40,2,1024]{2,1,0:T(2,128)(2,1)S(1)} collective-permute-done((bf16[40,2,1024]{2,1,0:T(2,128)(2,1)}, bf16[40,2,1024]{2,1,0:T(2,128)(2,1)S(1)}, u32[]{:S(2)}, u32[]{:S(2)}) %collective-permute-start.2) | collective-permute-done | bytes 163872 | tf_op jit(solution)/shard_map/ppermute | solution.py:400
  17.5 2.1 %shard_map.94.refs_0_ = bf16[8,6,96,128]{3,2,1,0:T(8,128)(2,1)S(1)} custom-call(bf16[40,2,1024]{2,1,0:T(2,128)(2,1)S(1)} %collective-permute-done.refs_0_, bf16[40,2,1024]{2,1,0:T(2,128)(2,1)S(1)} %collective-permute-done.1.refs_1_, bf16[40,2,1024]{2,1,0:T(2,128)(2,1)S(1)} %collective-permute-done.2.refs_2_, bf16[2,8,1024,128]{3,2,1,0:T(8,128)(2,1)S(1)} %copy-done.1, ...), custom_call_target="tpu_custom_call" | custom-call | flops 1048576 | bytes 65536 | tf_op jit(solution)/shard_map/pallas_call | solution.py:210
  19.6 0.1 collective-permute-start.4
  19.7 0.0 copy-start.2
  19.7 0.0 copy-start.5
  19.7 1.9 %shard_map.95.refs_2_ = f32[8,4,192,128]{3,2,1,0:T(8,128)S(1)} custom-call(s32[1]{0:T(128)} %bitcast.1.src_ref, s32[1]{0:T(128)} %bitcast.ch_ref, bf16[8,6,96,128]{3,2,1,0:T(8,128)(2,1)S(1)} %shard_map.94.refs_0_, bf16[16,8,384,128]{3,2,1,0:T(8,128)(2,1)S(1)} %shard_map.91.refs_1_, ...), custom_call_target="tpu_custom_call", output_to_operand_aliasing={{}: (4, {})} | custom-call | flops 1048576 | bytes 65536 | tf_op jit(solution)/shard_map/pallas_call | solution.py:344
  21.6 0.9 %collective-permute-done.4.refs_0_ = bf16[8,6,96,128]{3,2,1,0:T(8,128)(2,1)S(1)} collective-permute-done((bf16[8,6,96,128]{3,2,1,0:T(8,128)(2,1)S(1)}, bf16[8,6,96,128]{3,2,1,0:T(8,128)(2,1)S(1)}, u32[]{:S(2)}, u32[]{:S(2)}) %collective-permute-start.4) | collective-permute-done | bytes 1179680 | tf_op jit(solution)/shard_map/ppermute | solution.py:400
  22.5 0.0 copy-done.2
  22.5 0.0 copy-done.5
  22.5 4.0 %shard_map.96 = (bf16[8,8,1024]{2,1,0:T(8,128)(2,1)S(1)}, bf16[8,8,1024]{2,1,0:T(8,128)(2,1)S(1)}, bf16[8,8,1024]{2,1,0:T(8,128)(2,1)S(1)}, bf16[8,8,1024]{2,1,0:T(8,128)(2,1)S(1)}) custom-call(s32[1]{0:T(128)} %bitcast.1.src_ref, s32[1]{0:T(128)} %bitcast.ch_ref, bf16[8,6,96,128]{3,2,1,0:T(8,128)(2,1)S(1)} %collective-permute-done.4.refs_0_, ...), custom_call_target="tpu_custom_call" | custom-call | flops 1048576 | bytes 65536 | tf_op jit(solution)/shard_map/pallas_call | solution.py:344
  26.5 1.6 %collective-permute-start.5 = (bf16[8,8,1024]{2,1,0:T(8,128)(2,1)S(1)}, bf16[8,8,1024]{2,1,0:T(8,128)(2,1)S(1)}, u32[]{:S(2)}, u32[]{:S(2)}) collective-permute-start(bf16[8,8,1024]{2,1,0:T(8,128)(2,1)S(1)} %get-tuple-element.30), channel_id=1, source_target_pairs={{0,8},{8,0},{16,24},{24,16},{1,9},{9,1},{17,25},{25,17},{2,10},{10... | collective-permute-start | bytes 393224 | tf_op jit(solution)/shard_map/ppermute | solution.py:400
  28.1 1.5 %collective-permute-start.6 = (bf16[8,8,1024]{2,1,0:T(8,128)(2,1)S(1)}, bf16[8,8,1024]{2,1,0:T(8,128)(2,1)S(1)}, u32[]{:S(2)}, u32[]{:S(2)}) collective-permute-start(bf16[8,8,1024]{2,1,0:T(8,128)(2,1)S(1)} %get-tuple-element.31), channel_id=1, source_target_pairs={{0,16},{8,24},{16,0},{24,8},{1,17},{9,25},{17,1},{25,9},{2,18},{10... | collective-permute-start | bytes 393224 | tf_op jit(solution)/shard_map/ppermute | solution.py:400
  29.6 0.4 collective-permute-start.7
  30.1 0.0 copy-done
  30.1 0.2 convolution_convert_fusion.1
  30.3 2.1 %collective-permute-done.5.refs_1_ = bf16[8,8,1024]{2,1,0:T(8,128)(2,1)S(1)} collective-permute-done((bf16[8,8,1024]{2,1,0:T(8,128)(2,1)S(1)}, bf16[8,8,1024]{2,1,0:T(8,128)(2,1)S(1)}, u32[]{:S(2)}, u32[]{:S(2)}) %collective-permute-start.5) | collective-permute-done | bytes 131104 | tf_op jit(solution)/shard_map/ppermute | solution.py:400
  32.4 3.8 %collective-permute-done.6.refs_2_ = bf16[8,8,1024]{2,1,0:T(8,128)(2,1)S(1)} collective-permute-done((bf16[8,8,1024]{2,1,0:T(8,128)(2,1)S(1)}, bf16[8,8,1024]{2,1,0:T(8,128)(2,1)S(1)}, u32[]{:S(2)}, u32[]{:S(2)}) %collective-permute-start.6) | collective-permute-done | bytes 131104 | tf_op jit(solution)/shard_map/ppermute | solution.py:400
  36.2 0.0 collective-permute-done.7.refs_3_
  36.2 0.5 shard_map.97
  36.7 0.1 collective-permute-start.8
  36.8 1.2 %collective-permute-done.8 = bf16[32,1024]{1,0:T(8,128)(2,1)S(1)} collective-permute-done((bf16[32,1024]{1,0:T(8,128)(2,1)S(1)}, bf16[32,1024]{1,0:T(8,128)(2,1)S(1)}, u32[]{:S(2)}, u32[]{:S(2)}) %collective-permute-start.8) | collective-permute-done | bytes 65568 | tf_op jit(solution)/shard_map/ppermute | solution.py:400
  38.0 3.6 %collective-permute-start.11 = (bf16[16,1024]{1,0:T(8,128)(2,1)S(1)}, bf16[16,1024]{1,0:T(8,128)(2,1)S(1)}, u32[]{:S(2)}, u32[]{:S(2)}) collective-permute-start(bf16[16,1024]{1,0:T(8,128)(2,1)S(1)} %pad_maximum_fusion.3), channel_id=1, source_target_pairs={{0,6},{1,7},{2,4},{3,5},{4,2},{5,3},{6,0},{7,1},{8,14},{9,15},{10,... | collective-permute-start | bytes 98312 | tf_op jit(solution)/shard_map/ppermute | solution.py:400
  41.6 1.9 %collective-permute-start.9 = (bf16[16,1024]{1,0:T(8,128)(2,1)S(1)}, bf16[16,1024]{1,0:T(8,128)(2,1)S(1)}, u32[]{:S(2)}, u32[]{:S(2)}) collective-permute-start(bf16[16,1024]{1,0:T(8,128)(2,1)S(1)} %pad_maximum_fusion.1), channel_id=1, source_target_pairs={{0,2},{1,3},{2,0},{3,1},{4,6},{5,7},{6,4},{7,5},{8,10},{9,11},{10,... | collective-permute-start | bytes 98312 | tf_op jit(solution)/shard_map/ppermute | solution.py:400
  43.4 0.0 collective-permute-start.10
  43.4 2.0 %collective-permute-done.9 = bf16[16,1024]{1,0:T(8,128)(2,1)S(1)} collective-permute-done((bf16[16,1024]{1,0:T(8,128)(2,1)S(1)}, bf16[16,1024]{1,0:T(8,128)(2,1)S(1)}, u32[]{:S(2)}, u32[]{:S(2)}) %collective-permute-start.9) | collective-permute-done | bytes 32800 | tf_op jit(solution)/shard_map/ppermute | solution.py:400
  45.5 2.8 %collective-permute-done.10 = bf16[16,1024]{1,0:T(8,128)(2,1)S(1)} collective-permute-done((bf16[16,1024]{1,0:T(8,128)(2,1)S(1)}, bf16[16,1024]{1,0:T(8,128)(2,1)S(1)}, u32[]{:S(2)}, u32[]{:S(2)}) %collective-permute-start.10) | collective-permute-done | bytes 32800 | tf_op jit(solution)/shard_map/ppermute | solution.py:400
  48.2 0.0 collective-permute-done.11
  48.3 2.1 %convolution_convert_fusion = bf16[1024,1024]{1,0:T(8,128)(2,1)} fusion(bf16[64,1024]{1,0:T(8,128)(2,1)S(1)} %constant_dynamic-update-slice_fusion, bf16[64,1024]{1,0:T(8,128)(2,1)S(1)} %convolution_convert_fusion.1), kind=kOutput, calls=%fused_computation | convolution fusion | flops 135266304 | bytes 2359296 | tf_op jit(solution)/shard_map/dot_general | solution.py:380
  (10 shorter events, 0.0 us)
Async XLA Ops:
  0.0 30.1 %copy-start = (bf16[64,1024]{1,0:T(8,128)(2,1)S(1)}, bf16[64,1024]{1,0:T(8,128)(2,1)}, u32[]{:S(2)}) copy-start(bf16[64,1024]{1,0:T(8,128)(2,1)} %param.12) | copy-start | bytes 393220
  0.0 12.7 %collective-permute-start.3 = (bf16[40,2,1024]{2,1,0:T(2,128)(2,1)}, bf16[40,2,1024]{2,1,0:T(2,128)(2,1)S(1)}, u32[]{:S(2)}, u32[]{:S(2)}) collective-permute-start(bf16[40,2,1024]{2,1,0:T(2,128)(2,1)} %bitcast.8), channel_id=1, source_target_pairs={{0,1},{1,0},{2,3},{3,2},{4,5},{5,4},{6,7},{7,6},{8,9},{9,8},{10,11... | collective-permute-start | bytes 491528 | tf_op jit(solution)/shard_map/ppermute | solution.py:400
  0.5 16.0 %collective-permute-start = (bf16[40,2,1024]{2,1,0:T(2,128)(2,1)}, bf16[40,2,1024]{2,1,0:T(2,128)(2,1)S(1)}, u32[]{:S(2)}, u32[]{:S(2)}) collective-permute-start(bf16[40,2,1024]{2,1,0:T(2,128)(2,1)} %bitcast.9), channel_id=1, source_target_pairs={{0,4},{1,5},{2,6},{3,7},{4,0},{5,1},{6,2},{7,3},{8,12},{9,13},{10,... | collective-permute-start | bytes 491528 | tf_op jit(solution)/shard_map/ppermute | solution.py:400
  4.1 12.3 %collective-permute-start.1 = (bf16[40,2,1024]{2,1,0:T(2,128)(2,1)}, bf16[40,2,1024]{2,1,0:T(2,128)(2,1)S(1)}, u32[]{:S(2)}, u32[]{:S(2)}) collective-permute-start(bf16[40,2,1024]{2,1,0:T(2,128)(2,1)} %bitcast.10), channel_id=1, source_target_pairs={{0,6},{1,7},{2,4},{3,5},{4,2},{5,3},{6,0},{7,1},{8,14},{9,15},{10,... | collective-permute-start | bytes 491528 | tf_op jit(solution)/shard_map/ppermute | solution.py:400
  5.5 12.0 %collective-permute-start.2 = (bf16[40,2,1024]{2,1,0:T(2,128)(2,1)}, bf16[40,2,1024]{2,1,0:T(2,128)(2,1)S(1)}, u32[]{:S(2)}, u32[]{:S(2)}) collective-permute-start(bf16[40,2,1024]{2,1,0:T(2,128)(2,1)} %bitcast.11), channel_id=1, source_target_pairs={{0,2},{1,3},{2,0},{3,1},{4,6},{5,7},{6,4},{7,5},{8,10},{9,11},{10,... | collective-permute-start | bytes 491528 | tf_op jit(solution)/shard_map/ppermute | solution.py:400
  5.7 0.7 %copy-start.6 = (s32[16]{0:T(128)S(1)}, s32[16]{0:T(128)}, u32[]{:S(2)}) copy-start(s32[16]{0:T(128)} %slot_ref.1) | copy-start | bytes 196
  6.3 6.4 %copy-start.1 = (bf16[2,8,1024,128]{3,2,1,0:T(8,128)(2,1)S(1)}, bf16[2,8,1024,128]{3,2,1,0:T(8,128)(2,1)}, u32[]{:S(2)}) copy-start(bf16[2,8,1024,128]{3,2,1,0:T(8,128)(2,1)} %constant.51.clone.refs_2_.refs_3_) | copy-start | bytes 12582916
  6.3 6.4 %copy-start.3 = (bf16[2,192,160]{2,1,0:T(8,128)(2,1)S(1)}, bf16[2,192,160]{2,1,0:T(8,128)(2,1)}, u32[]{:S(2)}) copy-start(bf16[2,192,160]{2,1,0:T(8,128)(2,1)} %constant.52.clone.refs_3_.refs_4_) | copy-start | bytes 368644
  6.4 6.4 %copy-start.4 = (bf16[2,40960]{1,0:T(2,128)(2,1)S(1)}, bf16[2,40960]{1,0:T(2,128)(2,1)}, u32[]{:S(2)}) copy-start(bf16[2,40960]{1,0:T(2,128)(2,1)} %param.9) | copy-start | bytes 491524
  19.6 2.9 %collective-permute-start.4 = (bf16[8,6,96,128]{3,2,1,0:T(8,128)(2,1)S(1)}, bf16[8,6,96,128]{3,2,1,0:T(8,128)(2,1)S(1)}, u32[]{:S(2)}, u32[]{:S(2)}) collective-permute-start(bf16[8,6,96,128]{3,2,1,0:T(8,128)(2,1)S(1)} %shard_map.94.refs_0_), channel_id=1, source_target_pairs={{0,1},{1,0},{2,3},{3,2},{4,5},{5,4},{6,7},{7,6},{8,9},{9,8},{10,11... | collective-permute-start | bytes 3538952 | tf_op jit(solution)/shard_map/ppermute | solution.py:400
  19.7 2.8 %copy-start.2 = (bf16[2,8,1024,128]{3,2,1,0:T(8,128)(2,1)S(1)}, bf16[2,8,1024,128]{3,2,1,0:T(8,128)(2,1)}, u32[]{:S(2)}) copy-start(bf16[2,8,1024,128]{3,2,1,0:T(8,128)(2,1)} %constant.54.clone.refs_4_) | copy-start | bytes 12582916
  19.7 2.8 %copy-start.5 = (bf16[2,128,192]{2,1,0:T(8,128)(2,1)S(1)}, bf16[2,128,192]{2,1,0:T(8,128)(2,1)}, u32[]{:S(2)}) copy-start(bf16[2,128,192]{2,1,0:T(8,128)(2,1)} %constant.53.clone.refs_3_) | copy-start | bytes 294916
  26.5 5.9 %collective-permute-start.5 = (bf16[8,8,1024]{2,1,0:T(8,128)(2,1)S(1)}, bf16[8,8,1024]{2,1,0:T(8,128)(2,1)S(1)}, u32[]{:S(2)}, u32[]{:S(2)}) collective-permute-start(bf16[8,8,1024]{2,1,0:T(8,128)(2,1)S(1)} %get-tuple-element.30), channel_id=1, source_target_pairs={{0,8},{8,0},{16,24},{24,16},{1,9},{9,1},{17,25},{25,17},{2,10},{10... | collective-permute-start | bytes 393224 | tf_op jit(solution)/shard_map/ppermute | solution.py:400
  28.1 8.1 %collective-permute-start.6 = (bf16[8,8,1024]{2,1,0:T(8,128)(2,1)S(1)}, bf16[8,8,1024]{2,1,0:T(8,128)(2,1)S(1)}, u32[]{:S(2)}, u32[]{:S(2)}) collective-permute-start(bf16[8,8,1024]{2,1,0:T(8,128)(2,1)S(1)} %get-tuple-element.31), channel_id=1, source_target_pairs={{0,16},{8,24},{16,0},{24,8},{1,17},{9,25},{17,1},{25,9},{2,18},{10... | collective-permute-start | bytes 393224 | tf_op jit(solution)/shard_map/ppermute | solution.py:400
  29.6 6.5 %collective-permute-start.7 = (bf16[8,8,1024]{2,1,0:T(8,128)(2,1)S(1)}, bf16[8,8,1024]{2,1,0:T(8,128)(2,1)S(1)}, u32[]{:S(2)}, u32[]{:S(2)}) collective-permute-start(bf16[8,8,1024]{2,1,0:T(8,128)(2,1)S(1)} %get-tuple-element.32), channel_id=1, source_target_pairs={{0,24},{8,16},{16,8},{24,0},{1,25},{9,17},{17,9},{25,1},{2,26},{10... | collective-permute-start | bytes 393224 | tf_op jit(solution)/shard_map/ppermute | solution.py:400
  36.7 1.3 %collective-permute-start.8 = (bf16[32,1024]{1,0:T(8,128)(2,1)S(1)}, bf16[32,1024]{1,0:T(8,128)(2,1)S(1)}, u32[]{:S(2)}, u32[]{:S(2)}) collective-permute-start(bf16[32,1024]{1,0:T(8,128)(2,1)S(1)} %pad_maximum_fusion), channel_id=1, source_target_pairs={{0,1},{1,0},{2,3},{3,2},{4,5},{5,4},{6,7},{7,6},{8,9},{9,8},{10,11... | collective-permute-start | bytes 196616 | tf_op jit(solution)/shard_map/ppermute | solution.py:400
  38.0 10.2 %collective-permute-start.11 = (bf16[16,1024]{1,0:T(8,128)(2,1)S(1)}, bf16[16,1024]{1,0:T(8,128)(2,1)S(1)}, u32[]{:S(2)}, u32[]{:S(2)}) collective-permute-start(bf16[16,1024]{1,0:T(8,128)(2,1)S(1)} %pad_maximum_fusion.3), channel_id=1, source_target_pairs={{0,6},{1,7},{2,4},{3,5},{4,2},{5,3},{6,0},{7,1},{8,14},{9,15},{10,... | collective-permute-start | bytes 98312 | tf_op jit(solution)/shard_map/ppermute | solution.py:400
  41.6 3.9 %collective-permute-start.9 = (bf16[16,1024]{1,0:T(8,128)(2,1)S(1)}, bf16[16,1024]{1,0:T(8,128)(2,1)S(1)}, u32[]{:S(2)}, u32[]{:S(2)}) collective-permute-start(bf16[16,1024]{1,0:T(8,128)(2,1)S(1)} %pad_maximum_fusion.1), channel_id=1, source_target_pairs={{0,2},{1,3},{2,0},{3,1},{4,6},{5,7},{6,4},{7,5},{8,10},{9,11},{10,... | collective-permute-start | bytes 98312 | tf_op jit(solution)/shard_map/ppermute | solution.py:400
  43.4 4.8 %collective-permute-start.10 = (bf16[16,1024]{1,0:T(8,128)(2,1)S(1)}, bf16[16,1024]{1,0:T(8,128)(2,1)S(1)}, u32[]{:S(2)}, u32[]{:S(2)}) collective-permute-start(bf16[16,1024]{1,0:T(8,128)(2,1)S(1)} %pad_maximum_fusion.2), channel_id=1, source_target_pairs={{0,4},{1,5},{2,6},{3,7},{4,0},{5,1},{6,2},{7,3},{8,12},{9,13},{10,... | collective-permute-start | bytes 98312 | tf_op jit(solution)/shard_map/ppermute | solution.py:400

commit v13 on v12

--- a/solution.py
+++ b/solution.py
@@ -408,7 +408,9 @@
     hat = transform_responses(room_spectra, me, render_slot)
 
     row = jnp.arange(ch_count * channels, dtype=jnp.int32)
-    takes = ((row // channels) ^ ch_me) * channels + row % channels
+    chip_order = [0] + list(range(chips - 2, 0, -1)) + [chips - 1]
+    flips = np.array([2 * d + core for d in chip_order for core in range(2)], dtype=np.int32)
+    takes = (jnp.asarray(np.repeat(flips, channels)) ^ ch_me) * channels + row % channels
     order = (takes[:, None] == row[None, :]).astype(BF16)
     own_order = lax.optimization_barrier(dot(order, decoder).astype(BF16))
 
@@ -430,12 +432,12 @@
     if blocks == src_count * ch_count:
         pieces = sum_groups(sums, ch_me[None])
         given = swap(jnp.concatenate(pieces[1::2], axis=0), "ch", ch_count, 1)
-        both = [
-            jnp.concatenate([pieces[2 * d], given[d * channels : (d + 1) * channels]], axis=0)
-            for d in range(chips)
-        ]
-        both[1:] = [swap(both[d], "ch", ch_count, 2 * d) for d in range(1, chips)]
-        return decode(jnp.concatenate(both, axis=0), own_order)
+        both = {
+            d: jnp.concatenate([pieces[2 * d], given[d * channels : (d + 1) * channels]], axis=0)
+            for d in chip_order
+        }
+        arrived = [both[0]] + [swap(both[d], "ch", ch_count, 2 * d) for d in chip_order[1:]]
+        return decode(jnp.concatenate(arrived, axis=0), own_order)
     signal = sums[0].astype(F32)
     for part in sums[1:]:
         signal = signal + part.astype(F32)

time: 50.5 us -> 49.1 us (0.972)
  waiting for transfers between devices: 14.9 us -> 13.4 us
    ppermute x12, waiting for transfers between devices: 14.9 us -> 13.4 us  [swap(): return lax.ppermute(value, axis, [(i, i ^ flip) for i in range(count)])]
where the time goes in v13:
time: 49.1 us; the launch traced here: 49 us
  Pallas kernels  17.5 us (36%)
  starting transfers between devices  14.9 us (30%)
  waiting for transfers between devices  13.4 us (27%)
  matrix products  2.28 us (5%)
  local copies, waits for them, and re-layouts  0.71 us (1%)
    ppermute x12, starting transfers between devices, swap(): return lax.ppermute(value, axis, [(i, i ^ flip) for i in range(count)])  14.9 us
    ppermute x12, waiting for transfers between devices, swap(): return lax.ppermute(value, axis, [(i, i ^ flip) for i in range(count)])  13.4 us
    pallas_call x3, Pallas kernels, add_sources(): pl.pallas_call(body, in_specs=[smem] * 2 + [vmem] * (len(operands) - 2),...  6.94 us
    pallas_call x1, Pallas kernels, transform_responses(): pl.pallas_call(functools.partial(response_kernel, rows, bins), in_specs=[...  6.38 us
    pallas_call x2, Pallas kernels, transform_signals(): pl.pallas_call(functools.partial(spectra_kernel, len(x_list), rows), in_s...  3.73 us
    dot_general x1, matrix products, decode(): lax.dot_general(signal, matrix, (((0,), (0,)), ((), ())), preferred_eleme...  2.05 us
  transfers between devices with their start and end apart: 12, of which 8 were waited for; matrix products, arithmetic and copies ran while one was open for 0% of the time, Pallas kernels for 22%

profile of v13, /device:TPU:0, one launch (start us, length us, event | category | flops | bytes accessed | tf_op | source)
XLA Modules:
  0.0 49.0 jit_solution(819884712397913341)
XLA Ops:
  0.0 0.0 copy-start
  0.0 0.5 collective-permute-start.3
  0.5 3.7 %collective-permute-start = (bf16[40,2,1024]{2,1,0:T(2,128)(2,1)}, bf16[40,2,1024]{2,1,0:T(2,128)(2,1)S(1)}, u32[]{:S(2)}, u32[]{:S(2)}) collective-permute-start(bf16[40,2,1024]{2,1,0:T(2,128)(2,1)} %bitcast.9), channel_id=1, source_target_pairs={{0,4},{1,5},{2,6},{3,7},{4,0},{5,1},{6,2},{7,3},{8,12},{9,13},{10,... | collective-permute-start | bytes 491528 | tf_op jit(solution)/shard_map/ppermute | solution.py:400
  4.1 1.3 %collective-permute-start.1 = (bf16[40,2,1024]{2,1,0:T(2,128)(2,1)}, bf16[40,2,1024]{2,1,0:T(2,128)(2,1)S(1)}, u32[]{:S(2)}, u32[]{:S(2)}) collective-permute-start(bf16[40,2,1024]{2,1,0:T(2,128)(2,1)} %bitcast.10), channel_id=1, source_target_pairs={{0,6},{1,7},{2,4},{3,5},{4,2},{5,3},{6,0},{7,1},{8,14},{9,15},{10,... | collective-permute-start | bytes 491528 | tf_op jit(solution)/shard_map/ppermute | solution.py:400
  5.5 0.2 collective-permute-start.2
  5.7 0.0 copy-start.6
  5.7 0.7 %copy-done.6 = s32[16]{0:T(128)S(1)} copy-done((s32[16]{0:T(128)S(1)}, s32[16]{0:T(128)}, u32[]{:S(2)}) %copy-start.6) | copy-done | bytes 88
  6.3 0.0 copy-start.1
  6.4 0.0 copy-start.4
  6.4 6.4 %shard_map.100.refs_1_ = bf16[16,8,384,128]{3,2,1,0:T(8,128)(2,1)S(1)} custom-call(s32[1]{0:T(128)} %bitcast.1.src_ref, s32[1]{0:T(128)} %bitcast.ch_ref, s32[16]{0:T(128)S(1)} %copy-done.6, bf16[16,8,8,2,1024]{4,3,2,1,0:T(2,128)(2,1)} %room_hbm.1, bf16[384,256]{1,0:T(8,128)(2,1)} %constant.37.clone.table_hbm), custom_call_target="tpu_custom_call" | custom-call | flops 1048576 | bytes 65536 | tf_op jit(solution)/shard_map/pallas_call | solution.py:154
  12.7 0.0 collective-permute-done.3.refs_1_
  12.7 0.0 copy-done.1
  12.8 0.0 copy-done.3
  12.8 0.0 copy-done.4
  12.8 1.7 %shard_map.101.refs_0_ = bf16[8,4,96,128]{3,2,1,0:T(8,128)(2,1)S(1)} custom-call(bf16[40,2,1024]{2,1,0:T(2,128)(2,1)S(1)} %bitcast.12, bf16[40,2,1024]{2,1,0:T(2,128)(2,1)S(1)} %collective-permute-done.3.refs_1_, bf16[2,8,1024,128]{3,2,1,0:T(8,128)(2,1)S(1)} %copy-done.1, bf16[2,192,160]{2,1,0:T(8,128)(2,1)S(1)} %copy-done.3), custom_call_target="tpu_custom_call" | custom-call | flops 1048576 | bytes 65536 | tf_op jit(solution)/shard_map/pallas_call | solution.py:210
  14.4 1.0 %shard_map.102.refs_2_ = f32[8,4,192,128]{3,2,1,0:T(8,128)S(1)} custom-call(s32[1]{0:T(128)} %bitcast.1.src_ref, s32[1]{0:T(128)} %bitcast.ch_ref, bf16[8,4,96,128]{3,2,1,0:T(8,128)(2,1)S(1)} %shard_map.101.refs_0_, bf16[16,8,384,128]{3,2,1,0:T(8,128)(2,1)S(1)} %shard_map.100.refs_1_), custom_call_target="tpu_custom_call" | custom-call | flops 1048576 | bytes 65536 | tf_op jit(solution)/shard_map/pallas_call | solution.py:344
  15.5 0.0 copy-start.7
  15.5 1.0 %collective-permute-done.refs_0_ = bf16[40,2,1024]{2,1,0:T(2,128)(2,1)S(1)} collective-permute-done((bf16[40,2,1024]{2,1,0:T(2,128)(2,1)}, bf16[40,2,1024]{2,1,0:T(2,128)(2,1)S(1)}, u32[]{:S(2)}, u32[]{:S(2)}) %collective-permute-start) | collective-permute-done | bytes 163872 | tf_op jit(solution)/shard_map/ppermute | solution.py:400
  16.4 0.0 collective-permute-done.1.refs_1_
  16.4 1.1 %collective-permute-done.2.refs_2_ = bf16[40,2,1024]{2,1,0:T(2,128)(2,1)S(1)} collective-permute-done((bf16[40,2,1024]{2,1,0:T(2,128)(2,1)}, bf16[40,2,1024]{2,1,0:T(2,128)(2,1)S(1)}, u32[]{:S(2)}, u32[]{:S(2)}) %collective-permute-start.2) | collective-permute-done | bytes 163872 | tf_op jit(solution)/shard_map/ppermute | solution.py:400
  17.5 2.1 %shard_map.103.refs_0_ = bf16[8,6,96,128]{3,2,1,0:T(8,128)(2,1)S(1)} custom-call(bf16[40,2,1024]{2,1,0:T(2,128)(2,1)S(1)} %collective-permute-done.refs_0_, bf16[40,2,1024]{2,1,0:T(2,128)(2,1)S(1)} %collective-permute-done.1.refs_1_, bf16[40,2,1024]{2,1,0:T(2,128)(2,1)S(1)} %collective-permute-done.2.refs_2_, bf16[2,8,1024,128]{3,2,1,0:T(8,128)(2,1)S(1)} %copy-done.1, ...), custom_call_target="tpu_custom_call" | custom-call | flops 1048576 | bytes 65536 | tf_op jit(solution)/shard_map/pallas_call | solution.py:210
  19.6 0.1 collective-permute-start.4
  19.7 0.0 copy-done.7
  19.7 0.0 copy-start.2
  19.7 0.0 copy-start.5
  19.7 1.9 %shard_map.104.refs_2_ = f32[8,4,192,128]{3,2,1,0:T(8,128)S(1)} custom-call(s32[1]{0:T(128)} %bitcast.1.src_ref, s32[1]{0:T(128)} %bitcast.ch_ref, bf16[8,6,96,128]{3,2,1,0:T(8,128)(2,1)S(1)} %shard_map.103.refs_0_, bf16[16,8,384,128]{3,2,1,0:T(8,128)(2,1)S(1)} %shard_map.100.refs_1_, ...), custom_call_target="tpu_custom_call", output_to_operand_aliasing={{}: (4, {})} | custom-call | flops 1048576 | bytes 65536 | tf_op jit(solution)/shard_map/pallas_call | solution.py:344
  21.6 0.9 %collective-permute-done.4.refs_0_ = bf16[8,6,96,128]{3,2,1,0:T(8,128)(2,1)S(1)} collective-permute-done((bf16[8,6,96,128]{3,2,1,0:T(8,128)(2,1)S(1)}, bf16[8,6,96,128]{3,2,1,0:T(8,128)(2,1)S(1)}, u32[]{:S(2)}, u32[]{:S(2)}) %collective-permute-start.4) | collective-permute-done | bytes 1179680 | tf_op jit(solution)/shard_map/ppermute | solution.py:400
  22.5 0.0 copy-done.2
  22.5 0.0 copy-done.5
  22.5 4.0 %shard_map.105 = (bf16[8,8,1024]{2,1,0:T(8,128)(2,1)S(1)}, bf16[8,8,1024]{2,1,0:T(8,128)(2,1)S(1)}, bf16[8,8,1024]{2,1,0:T(8,128)(2,1)S(1)}, bf16[8,8,1024]{2,1,0:T(8,128)(2,1)S(1)}) custom-call(s32[1]{0:T(128)} %bitcast.1.src_ref, s32[1]{0:T(128)} %bitcast.ch_ref, bf16[8,6,96,128]{3,2,1,0:T(8,128)(2,1)S(1)} %collective-permute-done.4.refs_0_, ...), custom_call_target="tpu_custom_call" | custom-call | flops 1048576 | bytes 65536 | tf_op jit(solution)/shard_map/pallas_call | solution.py:344
  26.5 1.6 %collective-permute-start.5 = (bf16[8,8,1024]{2,1,0:T(8,128)(2,1)S(1)}, bf16[8,8,1024]{2,1,0:T(8,128)(2,1)S(1)}, u32[]{:S(2)}, u32[]{:S(2)}) collective-permute-start(bf16[8,8,1024]{2,1,0:T(8,128)(2,1)S(1)} %get-tuple-element.30), channel_id=1, source_target_pairs={{0,8},{8,0},{16,24},{24,16},{1,9},{9,1},{17,25},{25,17},{2,10},{10... | collective-permute-start | bytes 393224 | tf_op jit(solution)/shard_map/ppermute | solution.py:400
  28.1 1.5 %collective-permute-start.6 = (bf16[8,8,1024]{2,1,0:T(8,128)(2,1)S(1)}, bf16[8,8,1024]{2,1,0:T(8,128)(2,1)S(1)}, u32[]{:S(2)}, u32[]{:S(2)}) collective-permute-start(bf16[8,8,1024]{2,1,0:T(8,128)(2,1)S(1)} %get-tuple-element.31), channel_id=1, source_target_pairs={{0,16},{8,24},{16,0},{24,8},{1,17},{9,25},{17,1},{25,9},{2,18},{10... | collective-permute-start | bytes 393224 | tf_op jit(solution)/shard_map/ppermute | solution.py:400
  29.6 0.4 collective-permute-start.7
  30.1 0.0 copy-done
  30.1 0.2 convolution_convert_fusion.1
  30.3 2.1 %collective-permute-done.5.refs_1_ = bf16[8,8,1024]{2,1,0:T(8,128)(2,1)S(1)} collective-permute-done((bf16[8,8,1024]{2,1,0:T(8,128)(2,1)S(1)}, bf16[8,8,1024]{2,1,0:T(8,128)(2,1)S(1)}, u32[]{:S(2)}, u32[]{:S(2)}) %collective-permute-start.5) | collective-permute-done | bytes 131104 | tf_op jit(solution)/shard_map/ppermute | solution.py:400
  32.4 3.8 %collective-permute-done.6.refs_2_ = bf16[8,8,1024]{2,1,0:T(8,128)(2,1)S(1)} collective-permute-done((bf16[8,8,1024]{2,1,0:T(8,128)(2,1)S(1)}, bf16[8,8,1024]{2,1,0:T(8,128)(2,1)S(1)}, u32[]{:S(2)}, u32[]{:S(2)}) %collective-permute-start.6) | collective-permute-done | bytes 131104 | tf_op jit(solution)/shard_map/ppermute | solution.py:400
  36.2 0.0 collective-permute-done.7.refs_3_
  36.2 0.5 shard_map.106
  36.7 0.1 collective-permute-start.8
  36.8 1.2 %collective-permute-done.8 = bf16[32,1024]{1,0:T(8,128)(2,1)S(1)} collective-permute-done((bf16[32,1024]{1,0:T(8,128)(2,1)S(1)}, bf16[32,1024]{1,0:T(8,128)(2,1)S(1)}, u32[]{:S(2)}, u32[]{:S(2)}) %collective-permute-start.8) | collective-permute-done | bytes 65568 | tf_op jit(solution)/shard_map/ppermute | solution.py:400
  38.0 3.6 %collective-permute-start.11 = (bf16[16,1024]{1,0:T(8,128)(2,1)S(1)}, bf16[16,1024]{1,0:T(8,128)(2,1)S(1)}, u32[]{:S(2)}, u32[]{:S(2)}) collective-permute-start(bf16[16,1024]{1,0:T(8,128)(2,1)S(1)} %pad_maximum_fusion.3), channel_id=1, source_target_pairs={{0,6},{1,7},{2,4},{3,5},{4,2},{5,3},{6,0},{7,1},{8,14},{9,15},{10,... | collective-permute-start | bytes 98312 | tf_op jit(solution)/shard_map/ppermute | solution.py:400
  41.6 1.4 %collective-permute-start.9 = (bf16[16,1024]{1,0:T(8,128)(2,1)S(1)}, bf16[16,1024]{1,0:T(8,128)(2,1)S(1)}, u32[]{:S(2)}, u32[]{:S(2)}) collective-permute-start(bf16[16,1024]{1,0:T(8,128)(2,1)S(1)} %pad_maximum_fusion.1), channel_id=1, source_target_pairs={{0,4},{1,5},{2,6},{3,7},{4,0},{5,1},{6,2},{7,3},{8,12},{9,13},{10,... | collective-permute-start | bytes 98312 | tf_op jit(solution)/shard_map/ppermute | solution.py:400
  43.0 0.5 %collective-permute-start.10 = (bf16[16,1024]{1,0:T(8,128)(2,1)S(1)}, bf16[16,1024]{1,0:T(8,128)(2,1)S(1)}, u32[]{:S(2)}, u32[]{:S(2)}) collective-permute-start(bf16[16,1024]{1,0:T(8,128)(2,1)S(1)} %pad_maximum_fusion.2), channel_id=1, source_target_pairs={{0,2},{1,3},{2,0},{3,1},{4,6},{5,7},{6,4},{7,5},{8,10},{9,11},{10,... | collective-permute-start | bytes 98312 | tf_op jit(solution)/shard_map/ppermute | solution.py:400
  43.5 3.3 %collective-permute-done.9 = bf16[16,1024]{1,0:T(8,128)(2,1)S(1)} collective-permute-done((bf16[16,1024]{1,0:T(8,128)(2,1)S(1)}, bf16[16,1024]{1,0:T(8,128)(2,1)S(1)}, u32[]{:S(2)}, u32[]{:S(2)}) %collective-permute-start.9) | collective-permute-done | bytes 32800 | tf_op jit(solution)/shard_map/ppermute | solution.py:400
  46.8 0.1 collective-permute-done.10
  46.9 0.0 collective-permute-done.11
  46.9 2.1 %convolution_convert_fusion = bf16[1024,1024]{1,0:T(8,128)(2,1)} fusion(bf16[64,1024]{1,0:T(8,128)(2,1)S(1)} %constant_dynamic-update-slice_fusion, bf16[64,1024]{1,0:T(8,128)(2,1)S(1)} %convolution_convert_fusion.1), kind=kOutput, calls=%fused_computation | convolution fusion | flops 135266304 | bytes 2359296 | tf_op jit(solution)/shard_map/dot_general | solution.py:380
  (11 shorter events, 0.0 us)
Async XLA Ops:
  0.0 30.1 %copy-start = (bf16[64,1024]{1,0:T(8,128)(2,1)S(1)}, bf16[64,1024]{1,0:T(8,128)(2,1)}, u32[]{:S(2)}) copy-start(bf16[64,1024]{1,0:T(8,128)(2,1)} %param.13) | copy-start | bytes 393220
  0.0 12.7 %collective-permute-start.3 = (bf16[40,2,1024]{2,1,0:T(2,128)(2,1)}, bf16[40,2,1024]{2,1,0:T(2,128)(2,1)S(1)}, u32[]{:S(2)}, u32[]{:S(2)}) collective-permute-start(bf16[40,2,1024]{2,1,0:T(2,128)(2,1)} %bitcast.8), channel_id=1, source_target_pairs={{0,1},{1,0},{2,3},{3,2},{4,5},{5,4},{6,7},{7,6},{8,9},{9,8},{10,11... | collective-permute-start | bytes 491528 | tf_op jit(solution)/shard_map/ppermute | solution.py:400
  0.5 16.0 %collective-permute-start = (bf16[40,2,1024]{2,1,0:T(2,128)(2,1)}, bf16[40,2,1024]{2,1,0:T(2,128)(2,1)S(1)}, u32[]{:S(2)}, u32[]{:S(2)}) collective-permute-start(bf16[40,2,1024]{2,1,0:T(2,128)(2,1)} %bitcast.9), channel_id=1, source_target_pairs={{0,4},{1,5},{2,6},{3,7},{4,0},{5,1},{6,2},{7,3},{8,12},{9,13},{10,... | collective-permute-start | bytes 491528 | tf_op jit(solution)/shard_map/ppermute | solution.py:400
  4.1 12.3 %collective-permute-start.1 = (bf16[40,2,1024]{2,1,0:T(2,128)(2,1)}, bf16[40,2,1024]{2,1,0:T(2,128)(2,1)S(1)}, u32[]{:S(2)}, u32[]{:S(2)}) collective-permute-start(bf16[40,2,1024]{2,1,0:T(2,128)(2,1)} %bitcast.10), channel_id=1, source_target_pairs={{0,6},{1,7},{2,4},{3,5},{4,2},{5,3},{6,0},{7,1},{8,14},{9,15},{10,... | collective-permute-start | bytes 491528 | tf_op jit(solution)/shard_map/ppermute | solution.py:400
  5.5 12.0 %collective-permute-start.2 = (bf16[40,2,1024]{2,1,0:T(2,128)(2,1)}, bf16[40,2,1024]{2,1,0:T(2,128)(2,1)S(1)}, u32[]{:S(2)}, u32[]{:S(2)}) collective-permute-start(bf16[40,2,1024]{2,1,0:T(2,128)(2,1)} %bitcast.11), channel_id=1, source_target_pairs={{0,2},{1,3},{2,0},{3,1},{4,6},{5,7},{6,4},{7,5},{8,10},{9,11},{10,... | collective-permute-start | bytes 491528 | tf_op jit(solution)/shard_map/ppermute | solution.py:400
  5.7 0.7 %copy-start.6 = (s32[16]{0:T(128)S(1)}, s32[16]{0:T(128)}, u32[]{:S(2)}) copy-start(s32[16]{0:T(128)} %slot_ref.1) | copy-start | bytes 196
  6.3 6.4 %copy-start.1 = (bf16[2,8,1024,128]{3,2,1,0:T(8,128)(2,1)S(1)}, bf16[2,8,1024,128]{3,2,1,0:T(8,128)(2,1)}, u32[]{:S(2)}) copy-start(bf16[2,8,1024,128]{3,2,1,0:T(8,128)(2,1)} %constant.39.clone.refs_2_.refs_3_) | copy-start | bytes 12582916
  6.3 6.4 %copy-start.3 = (bf16[2,192,160]{2,1,0:T(8,128)(2,1)S(1)}, bf16[2,192,160]{2,1,0:T(8,128)(2,1)}, u32[]{:S(2)}) copy-start(bf16[2,192,160]{2,1,0:T(8,128)(2,1)} %constant.40.clone.refs_3_.refs_4_) | copy-start | bytes 368644
  6.4 6.4 %copy-start.4 = (bf16[2,40960]{1,0:T(2,128)(2,1)S(1)}, bf16[2,40960]{1,0:T(2,128)(2,1)}, u32[]{:S(2)}) copy-start(bf16[2,40960]{1,0:T(2,128)(2,1)} %param.10) | copy-start | bytes 491524
  15.5 4.2 %copy-start.7 = (s32[64]{0:T(128)S(1)}, s32[64]{0:T(128)}, u32[]{:S(2)}) copy-start(s32[64]{0:T(128)} %constant.38.clone) | copy-start | bytes 772
  19.6 2.9 %collective-permute-start.4 = (bf16[8,6,96,128]{3,2,1,0:T(8,128)(2,1)S(1)}, bf16[8,6,96,128]{3,2,1,0:T(8,128)(2,1)S(1)}, u32[]{:S(2)}, u32[]{:S(2)}) collective-permute-start(bf16[8,6,96,128]{3,2,1,0:T(8,128)(2,1)S(1)} %shard_map.103.refs_0_), channel_id=1, source_target_pairs={{0,1},{1,0},{2,3},{3,2},{4,5},{5,4},{6,7},{7,6},{8,9},{9,8},{10,11... | collective-permute-start | bytes 3538952 | tf_op jit(solution)/shard_map/ppermute | solution.py:400
  19.7 2.8 %copy-start.2 = (bf16[2,8,1024,128]{3,2,1,0:T(8,128)(2,1)S(1)}, bf16[2,8,1024,128]{3,2,1,0:T(8,128)(2,1)}, u32[]{:S(2)}) copy-start(bf16[2,8,1024,128]{3,2,1,0:T(8,128)(2,1)} %constant.42.clone.refs_4_) | copy-start | bytes 12582916
  19.7 2.8 %copy-start.5 = (bf16[2,128,192]{2,1,0:T(8,128)(2,1)S(1)}, bf16[2,128,192]{2,1,0:T(8,128)(2,1)}, u32[]{:S(2)}) copy-start(bf16[2,128,192]{2,1,0:T(8,128)(2,1)} %constant.41.clone.refs_3_) | copy-start | bytes 294916
  26.5 5.9 %collective-permute-start.5 = (bf16[8,8,1024]{2,1,0:T(8,128)(2,1)S(1)}, bf16[8,8,1024]{2,1,0:T(8,128)(2,1)S(1)}, u32[]{:S(2)}, u32[]{:S(2)}) collective-permute-start(bf16[8,8,1024]{2,1,0:T(8,128)(2,1)S(1)} %get-tuple-element.30), channel_id=1, source_target_pairs={{0,8},{8,0},{16,24},{24,16},{1,9},{9,1},{17,25},{25,17},{2,10},{10... | collective-permute-start | bytes 393224 | tf_op jit(solution)/shard_map/ppermute | solution.py:400
  28.1 8.1 %collective-permute-start.6 = (bf16[8,8,1024]{2,1,0:T(8,128)(2,1)S(1)}, bf16[8,8,1024]{2,1,0:T(8,128)(2,1)S(1)}, u32[]{:S(2)}, u32[]{:S(2)}) collective-permute-start(bf16[8,8,1024]{2,1,0:T(8,128)(2,1)S(1)} %get-tuple-element.31), channel_id=1, source_target_pairs={{0,16},{8,24},{16,0},{24,8},{1,17},{9,25},{17,1},{25,9},{2,18},{10... | collective-permute-start | bytes 393224 | tf_op jit(solution)/shard_map/ppermute | solution.py:400
  29.6 6.5 %collective-permute-start.7 = (bf16[8,8,1024]{2,1,0:T(8,128)(2,1)S(1)}, bf16[8,8,1024]{2,1,0:T(8,128)(2,1)S(1)}, u32[]{:S(2)}, u32[]{:S(2)}) collective-permute-start(bf16[8,8,1024]{2,1,0:T(8,128)(2,1)S(1)} %get-tuple-element.32), channel_id=1, source_target_pairs={{0,24},{8,16},{16,8},{24,0},{1,25},{9,17},{17,9},{25,1},{2,26},{10... | collective-permute-start | bytes 393224 | tf_op jit(solution)/shard_map/ppermute | solution.py:400
  36.7 1.3 %collective-permute-start.8 = (bf16[32,1024]{1,0:T(8,128)(2,1)S(1)}, bf16[32,1024]{1,0:T(8,128)(2,1)S(1)}, u32[]{:S(2)}, u32[]{:S(2)}) collective-permute-start(bf16[32,1024]{1,0:T(8,128)(2,1)S(1)} %pad_maximum_fusion), channel_id=1, source_target_pairs={{0,1},{1,0},{2,3},{3,2},{4,5},{5,4},{6,7},{7,6},{8,9},{9,8},{10,11... | collective-permute-start | bytes 196616 | tf_op jit(solution)/shard_map/ppermute | solution.py:400
  38.0 8.9 %collective-permute-start.11 = (bf16[16,1024]{1,0:T(8,128)(2,1)S(1)}, bf16[16,1024]{1,0:T(8,128)(2,1)S(1)}, u32[]{:S(2)}, u32[]{:S(2)}) collective-permute-start(bf16[16,1024]{1,0:T(8,128)(2,1)S(1)} %pad_maximum_fusion.3), channel_id=1, source_target_pairs={{0,6},{1,7},{2,4},{3,5},{4,2},{5,3},{6,0},{7,1},{8,14},{9,15},{10,... | collective-permute-start | bytes 98312 | tf_op jit(solution)/shard_map/ppermute | solution.py:400
  41.6 5.3 %collective-permute-start.9 = (bf16[16,1024]{1,0:T(8,128)(2,1)S(1)}, bf16[16,1024]{1,0:T(8,128)(2,1)S(1)}, u32[]{:S(2)}, u32[]{:S(2)}) collective-permute-start(bf16[16,1024]{1,0:T(8,128)(2,1)S(1)} %pad_maximum_fusion.1), channel_id=1, source_target_pairs={{0,4},{1,5},{2,6},{3,7},{4,0},{5,1},{6,2},{7,3},{8,12},{9,13},{10,... | collective-permute-start | bytes 98312 | tf_op jit(solution)/shard_map/ppermute | solution.py:400
  43.0 4.0 %collective-permute-start.10 = (bf16[16,1024]{1,0:T(8,128)(2,1)S(1)}, bf16[16,1024]{1,0:T(8,128)(2,1)S(1)}, u32[]{:S(2)}, u32[]{:S(2)}) collective-permute-start(bf16[16,1024]{1,0:T(8,128)(2,1)S(1)} %pad_maximum_fusion.2), channel_id=1, source_target_pairs={{0,2},{1,3},{2,0},{3,1},{4,6},{5,7},{6,4},{7,5},{8,10},{9,11},{10,... | collective-permute-start | bytes 98312 | tf_op jit(solution)/shard_map/ppermute | solution.py:400

commit v14 on v13

--- a/solution.py
+++ b/solution.py
@@ -436,7 +436,13 @@
             d: jnp.concatenate([pieces[2 * d], given[d * channels : (d + 1) * channels]], axis=0)
             for d in chip_order
         }
-        arrived = [both[0]] + [swap(both[d], "ch", ch_count, 2 * d) for d in chip_order[1:]]
+        if chips == 4:
+            size = 2 * channels
+            two = swap(jnp.concatenate([both[2], both[3]], axis=0), "ch", ch_count, 4)
+            one = swap(jnp.concatenate([both[1], two[size:]], axis=0), "ch", ch_count, 2)
+            arrived = [both[0], two[:size], one]
+        else:
+            arrived = [both[0]] + [swap(both[d], "ch", ch_count, 2 * d) for d in chip_order[1:]]
         return decode(jnp.concatenate(arrived, axis=0), own_order)
     signal = sums[0].astype(F32)
     for part in sums[1:]:

time: 49.1 us -> 53.3 us (1.086)
  waiting for transfers between devices: 13.4 us -> 18.1 us
  starting transfers between devices: 14.9 us -> 14.3 us
    ppermute x12 -> x11, waiting for transfers between devices: 13.4 us -> 18.1 us  [swap(): return lax.ppermute(value, axis, [(i, i ^ flip) for i in range(count)])]
    ppermute x12 -> x11, starting transfers between devices: 14.9 us -> 14.3 us  [swap(): return lax.ppermute(value, axis, [(i, i ^ flip) for i in range(count)])]
  transfers between devices with their start and end apart: 12 -> 11, of which waited for: 8 -> 8; matrix products, arithmetic and copies ran while one was open for 0% -> 0% of each run, Pallas kernels for 22% -> 21%
where the time goes in v14:
time: 53.3 us; the launch traced here: 53.1 us
  waiting for transfers between devices  18.1 us (34%)
  Pallas kernels  17.5 us (33%)
  starting transfers between devices  14.3 us (27%)
  matrix products  2.28 us (4%)
  local copies, waits for them, and re-layouts  0.7 us (1%)
    ppermute x11, waiting for transfers between devices, swap(): return lax.ppermute(value, axis, [(i, i ^ flip) for i in range(count)])  18.1 us
    ppermute x11, starting transfers between devices, swap(): return lax.ppermute(value, axis, [(i, i ^ flip) for i in range(count)])  14.3 us
    pallas_call x3, Pallas kernels, add_sources(): pl.pallas_call(body, in_specs=[smem] * 2 + [vmem] * (len(operands) - 2),...  6.94 us
    pallas_call x1, Pallas kernels, transform_responses(): pl.pallas_call(functools.partial(response_kernel, rows, bins), in_specs=[...  6.38 us
    pallas_call x2, Pallas kernels, transform_signals(): pl.pallas_call(functools.partial(spectra_kernel, len(x_list), rows), in_s...  3.73 us
    dot_general x1, matrix products, decode(): lax.dot_general(signal, matrix, (((0,), (0,)), ((), ())), preferred_eleme...  2.05 us
  transfers between devices with their start and end apart: 11, of which 8 were waited for; matrix products, arithmetic and copies ran while one was open for 0% of the time, Pallas kernels for 21%

profile of v14, /device:TPU:0, one launch (start us, length us, event | category | flops | bytes accessed | tf_op | source)
XLA Modules:
  0.0 53.1 jit_solution(13005472408995019513)
XLA Ops:
  0.0 0.0 copy-start
  0.0 0.5 collective-permute-start.3
  0.5 3.7 %collective-permute-start = (bf16[40,2,1024]{2,1,0:T(2,128)(2,1)}, bf16[40,2,1024]{2,1,0:T(2,128)(2,1)S(1)}, u32[]{:S(2)}, u32[]{:S(2)}) collective-permute-start(bf16[40,2,1024]{2,1,0:T(2,128)(2,1)} %bitcast.8), channel_id=1, source_target_pairs={{0,4},{1,5},{2,6},{3,7},{4,0},{5,1},{6,2},{7,3},{8,12},{9,13},{10,... | collective-permute-start | bytes 491528 | tf_op jit(solution)/shard_map/ppermute | solution.py:400
  4.1 1.3 %collective-permute-start.1 = (bf16[40,2,1024]{2,1,0:T(2,128)(2,1)}, bf16[40,2,1024]{2,1,0:T(2,128)(2,1)S(1)}, u32[]{:S(2)}, u32[]{:S(2)}) collective-permute-start(bf16[40,2,1024]{2,1,0:T(2,128)(2,1)} %bitcast.9), channel_id=1, source_target_pairs={{0,6},{1,7},{2,4},{3,5},{4,2},{5,3},{6,0},{7,1},{8,14},{9,15},{10,... | collective-permute-start | bytes 491528 | tf_op jit(solution)/shard_map/ppermute | solution.py:400
  5.5 0.2 collective-permute-start.2
  5.7 0.0 copy-start.6
  5.7 0.7 %copy-done.6 = s32[16]{0:T(128)S(1)} copy-done((s32[16]{0:T(128)S(1)}, s32[16]{0:T(128)}, u32[]{:S(2)}) %copy-start.6) | copy-done | bytes 88
  6.3 0.0 copy-start.1
  6.3 0.0 copy-start.3
  6.4 0.0 copy-start.4
  6.4 6.4 %shard_map.100.refs_1_ = bf16[16,8,384,128]{3,2,1,0:T(8,128)(2,1)S(1)} custom-call(s32[1]{0:T(128)} %bitcast.1.src_ref, s32[1]{0:T(128)} %bitcast.ch_ref, s32[16]{0:T(128)S(1)} %copy-done.6, bf16[16,8,8,2,1024]{4,3,2,1,0:T(2,128)(2,1)} %room_hbm.1, bf16[384,256]{1,0:T(8,128)(2,1)} %constant.37.clone.table_hbm), custom_call_target="tpu_custom_call" | custom-call | flops 1048576 | bytes 65536 | tf_op jit(solution)/shard_map/pallas_call | solution.py:154
  12.7 0.0 collective-permute-done.3.refs_1_
  12.7 0.0 copy-done.1
  12.8 0.0 copy-done.3
  12.8 0.0 copy-done.4
  12.8 1.7 %shard_map.101.refs_0_ = bf16[8,4,96,128]{3,2,1,0:T(8,128)(2,1)S(1)} custom-call(bf16[40,2,1024]{2,1,0:T(2,128)(2,1)S(1)} %bitcast.11, bf16[40,2,1024]{2,1,0:T(2,128)(2,1)S(1)} %collective-permute-done.3.refs_1_, bf16[2,8,1024,128]{3,2,1,0:T(8,128)(2,1)S(1)} %copy-done.1, bf16[2,192,160]{2,1,0:T(8,128)(2,1)S(1)} %copy-done.3), custom_call_target="tpu_custom_call" | custom-call | flops 1048576 | bytes 65536 | tf_op jit(solution)/shard_map/pallas_call | solution.py:210
  14.4 1.0 %shard_map.102.refs_2_ = f32[8,4,192,128]{3,2,1,0:T(8,128)S(1)} custom-call(s32[1]{0:T(128)} %bitcast.1.src_ref, s32[1]{0:T(128)} %bitcast.ch_ref, bf16[8,4,96,128]{3,2,1,0:T(8,128)(2,1)S(1)} %shard_map.101.refs_0_, bf16[16,8,384,128]{3,2,1,0:T(8,128)(2,1)S(1)} %shard_map.100.refs_1_), custom_call_target="tpu_custom_call" | custom-call | flops 1048576 | bytes 65536 | tf_op jit(solution)/shard_map/pallas_call | solution.py:344
  15.5 1.0 %collective-permute-done.refs_0_ = bf16[40,2,1024]{2,1,0:T(2,128)(2,1)S(1)} collective-permute-done((bf16[40,2,1024]{2,1,0:T(2,128)(2,1)}, bf16[40,2,1024]{2,1,0:T(2,128)(2,1)S(1)}, u32[]{:S(2)}, u32[]{:S(2)}) %collective-permute-start) | collective-permute-done | bytes 163872 | tf_op jit(solution)/shard_map/ppermute | solution.py:400
  16.4 0.0 collective-permute-done.1.refs_1_
  16.4 1.1 %collective-permute-done.2.refs_2_ = bf16[40,2,1024]{2,1,0:T(2,128)(2,1)S(1)} collective-permute-done((bf16[40,2,1024]{2,1,0:T(2,128)(2,1)}, bf16[40,2,1024]{2,1,0:T(2,128)(2,1)S(1)}, u32[]{:S(2)}, u32[]{:S(2)}) %collective-permute-start.2) | collective-permute-done | bytes 163872 | tf_op jit(solution)/shard_map/ppermute | solution.py:400
  17.5 2.1 %shard_map.103.refs_0_ = bf16[8,6,96,128]{3,2,1,0:T(8,128)(2,1)S(1)} custom-call(bf16[40,2,1024]{2,1,0:T(2,128)(2,1)S(1)} %collective-permute-done.refs_0_, bf16[40,2,1024]{2,1,0:T(2,128)(2,1)S(1)} %collective-permute-done.1.refs_1_, bf16[40,2,1024]{2,1,0:T(2,128)(2,1)S(1)} %collective-permute-done.2.refs_2_, bf16[2,8,1024,128]{3,2,1,0:T(8,128)(2,1)S(1)} %copy-done.1, ...), custom_call_target="tpu_custom_call" | custom-call | flops 1048576 | bytes 65536 | tf_op jit(solution)/shard_map/pallas_call | solution.py:210
  19.6 0.0 copy-start.2
  19.6 0.0 copy-start.5
  19.6 0.1 collective-permute-start.4
  19.7 1.9 %shard_map.104.refs_2_ = f32[8,4,192,128]{3,2,1,0:T(8,128)S(1)} custom-call(s32[1]{0:T(128)} %bitcast.1.src_ref, s32[1]{0:T(128)} %bitcast.ch_ref, bf16[8,6,96,128]{3,2,1,0:T(8,128)(2,1)S(1)} %shard_map.103.refs_0_, bf16[16,8,384,128]{3,2,1,0:T(8,128)(2,1)S(1)} %shard_map.100.refs_1_, ...), custom_call_target="tpu_custom_call", output_to_operand_aliasing={{}: (4, {})} | custom-call | flops 1048576 | bytes 65536 | tf_op jit(solution)/shard_map/pallas_call | solution.py:344
  21.6 0.0 copy-start.7
  21.6 0.9 %collective-permute-done.4.refs_0_ = bf16[8,6,96,128]{3,2,1,0:T(8,128)(2,1)S(1)} collective-permute-done((bf16[8,6,96,128]{3,2,1,0:T(8,128)(2,1)S(1)}, bf16[8,6,96,128]{3,2,1,0:T(8,128)(2,1)S(1)}, u32[]{:S(2)}, u32[]{:S(2)}) %collective-permute-start.4) | collective-permute-done | bytes 1179680 | tf_op jit(solution)/shard_map/ppermute | solution.py:400
  22.5 0.0 copy-done.2
  22.5 0.0 copy-done.5
  22.5 4.0 %shard_map.105 = (bf16[8,8,1024]{2,1,0:T(8,128)(2,1)S(1)}, bf16[8,8,1024]{2,1,0:T(8,128)(2,1)S(1)}, bf16[8,8,1024]{2,1,0:T(8,128)(2,1)S(1)}, bf16[8,8,1024]{2,1,0:T(8,128)(2,1)S(1)}) custom-call(s32[1]{0:T(128)} %bitcast.1.src_ref, s32[1]{0:T(128)} %bitcast.ch_ref, bf16[8,6,96,128]{3,2,1,0:T(8,128)(2,1)S(1)} %collective-permute-done.4.refs_0_, ...), custom_call_target="tpu_custom_call" | custom-call | flops 1048576 | bytes 65536 | tf_op jit(solution)/shard_map/pallas_call | solution.py:344
  26.5 1.6 %collective-permute-start.5 = (bf16[8,8,1024]{2,1,0:T(8,128)(2,1)S(1)}, bf16[8,8,1024]{2,1,0:T(8,128)(2,1)S(1)}, u32[]{:S(2)}, u32[]{:S(2)}) collective-permute-start(bf16[8,8,1024]{2,1,0:T(8,128)(2,1)S(1)} %get-tuple-element.30), channel_id=1, source_target_pairs={{0,8},{8,0},{16,24},{24,16},{1,9},{9,1},{17,25},{25,17},{2,10},{10... | collective-permute-start | bytes 393224 | tf_op jit(solution)/shard_map/ppermute | solution.py:400
  28.1 1.5 %collective-permute-start.6 = (bf16[8,8,1024]{2,1,0:T(8,128)(2,1)S(1)}, bf16[8,8,1024]{2,1,0:T(8,128)(2,1)S(1)}, u32[]{:S(2)}, u32[]{:S(2)}) collective-permute-start(bf16[8,8,1024]{2,1,0:T(8,128)(2,1)S(1)} %get-tuple-element.31), channel_id=1, source_target_pairs={{0,16},{8,24},{16,0},{24,8},{1,17},{9,25},{17,1},{25,9},{2,18},{10... | collective-permute-start | bytes 393224 | tf_op jit(solution)/shard_map/ppermute | solution.py:400
  29.7 0.4 collective-permute-start.7
  30.1 2.3 %collective-permute-done.5.refs_1_ = bf16[8,8,1024]{2,1,0:T(8,128)(2,1)S(1)} collective-permute-done((bf16[8,8,1024]{2,1,0:T(8,128)(2,1)S(1)}, bf16[8,8,1024]{2,1,0:T(8,128)(2,1)S(1)}, u32[]{:S(2)}, u32[]{:S(2)}) %collective-permute-start.5) | collective-permute-done | bytes 131104 | tf_op jit(solution)/shard_map/ppermute | solution.py:400
  32.4 3.8 %collective-permute-done.6.refs_2_ = bf16[8,8,1024]{2,1,0:T(8,128)(2,1)S(1)} collective-permute-done((bf16[8,8,1024]{2,1,0:T(8,128)(2,1)S(1)}, bf16[8,8,1024]{2,1,0:T(8,128)(2,1)S(1)}, u32[]{:S(2)}, u32[]{:S(2)}) %collective-permute-start.6) | collective-permute-done | bytes 131104 | tf_op jit(solution)/shard_map/ppermute | solution.py:400
  36.2 0.0 collective-permute-done.7.refs_3_
  36.2 0.5 shard_map.106
  36.7 0.1 collective-permute-start.8
  36.8 1.2 %collective-permute-done.8 = bf16[32,1024]{1,0:T(8,128)(2,1)S(1)} collective-permute-done((bf16[32,1024]{1,0:T(8,128)(2,1)S(1)}, bf16[32,1024]{1,0:T(8,128)(2,1)S(1)}, u32[]{:S(2)}, u32[]{:S(2)}) %collective-permute-start.8) | collective-permute-done | bytes 65568 | tf_op jit(solution)/shard_map/ppermute | solution.py:400
  38.0 4.9 %collective-permute-start.9 = (bf16[32,1024]{1,0:T(8,128)(2,1)S(1)}, bf16[32,1024]{1,0:T(8,128)(2,1)S(1)}, u32[]{:S(2)}, u32[]{:S(2)}) collective-permute-start(bf16[32,1024]{1,0:T(8,128)(2,1)S(1)} %pad_maximum_fusion.1), channel_id=1, source_target_pairs={{0,4},{1,5},{2,6},{3,7},{4,0},{5,1},{6,2},{7,3},{8,12},{9,13},{10,... | collective-permute-start | bytes 196616 | tf_op jit(solution)/shard_map/ppermute | solution.py:400
  42.9 0.0 copy-done.7
  42.9 3.8 %collective-permute-done.9 = bf16[32,1024]{1,0:T(8,128)(2,1)S(1)} collective-permute-done((bf16[32,1024]{1,0:T(8,128)(2,1)S(1)}, bf16[32,1024]{1,0:T(8,128)(2,1)S(1)}, u32[]{:S(2)}, u32[]{:S(2)}) %collective-permute-start.9) | collective-permute-done | bytes 65568 | tf_op jit(solution)/shard_map/ppermute | solution.py:400
  46.7 0.1 collective-permute-start.10
  46.8 0.0 copy-done
  46.8 0.2 convolution_convert_fusion.1
  47.0 4.0 %collective-permute-done.10 = bf16[32,1024]{1,0:T(8,128)(2,1)S(1)} collective-permute-done((bf16[32,1024]{1,0:T(8,128)(2,1)S(1)}, bf16[32,1024]{1,0:T(8,128)(2,1)S(1)}, u32[]{:S(2)}, u32[]{:S(2)}) %collective-permute-start.10) | collective-permute-done | bytes 65568 | tf_op jit(solution)/shard_map/ppermute | solution.py:400
  51.0 2.1 %convolution_convert_fusion = bf16[1024,1024]{1,0:T(8,128)(2,1)} fusion(bf16[64,1024]{1,0:T(8,128)(2,1)S(1)} %convolution_convert_fusion.1, bf16[32,1024]{1,0:T(8,128)(2,1)S(1)} %collective-permute-done.10, bf16[16,1024]{1,0:T(8,128)(2,1)S(1)} %get-tuple-element.45, bf16[8,1024]{1,0:T(8,128)(2,1)S(1)} %get-tuple-element.41, ...), kind=kOutput, calls=%fused_computation | convolution fusion | flops 135790592 | bytes 2359296 | tf_op jit(solution)/shard_map/dot_general | solution.py:380
  (6 shorter events, 0.0 us)
Async XLA Ops:
  0.0 46.8 %copy-start = (bf16[64,1024]{1,0:T(8,128)(2,1)S(1)}, bf16[64,1024]{1,0:T(8,128)(2,1)}, u32[]{:S(2)}) copy-start(bf16[64,1024]{1,0:T(8,128)(2,1)} %param.13) | copy-start | bytes 393220
  0.0 12.7 %collective-permute-start.3 = (bf16[40,2,1024]{2,1,0:T(2,128)(2,1)}, bf16[40,2,1024]{2,1,0:T(2,128)(2,1)S(1)}, u32[]{:S(2)}, u32[]{:S(2)}) collective-permute-start(bf16[40,2,1024]{2,1,0:T(2,128)(2,1)} %bitcast.7), channel_id=1, source_target_pairs={{0,1},{1,0},{2,3},{3,2},{4,5},{5,4},{6,7},{7,6},{8,9},{9,8},{10,11... | collective-permute-start | bytes 491528 | tf_op jit(solution)/shard_map/ppermute | solution.py:400
  0.5 16.0 %collective-permute-start = (bf16[40,2,1024]{2,1,0:T(2,128)(2,1)}, bf16[40,2,1024]{2,1,0:T(2,128)(2,1)S(1)}, u32[]{:S(2)}, u32[]{:S(2)}) collective-permute-start(bf16[40,2,1024]{2,1,0:T(2,128)(2,1)} %bitcast.8), channel_id=1, source_target_pairs={{0,4},{1,5},{2,6},{3,7},{4,0},{5,1},{6,2},{7,3},{8,12},{9,13},{10,... | collective-permute-start | bytes 491528 | tf_op jit(solution)/shard_map/ppermute | solution.py:400
  4.1 12.3 %collective-permute-start.1 = (bf16[40,2,1024]{2,1,0:T(2,128)(2,1)}, bf16[40,2,1024]{2,1,0:T(2,128)(2,1)S(1)}, u32[]{:S(2)}, u32[]{:S(2)}) collective-permute-start(bf16[40,2,1024]{2,1,0:T(2,128)(2,1)} %bitcast.9), channel_id=1, source_target_pairs={{0,6},{1,7},{2,4},{3,5},{4,2},{5,3},{6,0},{7,1},{8,14},{9,15},{10,... | collective-permute-start | bytes 491528 | tf_op jit(solution)/shard_map/ppermute | solution.py:400
  5.5 12.0 %collective-permute-start.2 = (bf16[40,2,1024]{2,1,0:T(2,128)(2,1)}, bf16[40,2,1024]{2,1,0:T(2,128)(2,1)S(1)}, u32[]{:S(2)}, u32[]{:S(2)}) collective-permute-start(bf16[40,2,1024]{2,1,0:T(2,128)(2,1)} %bitcast.10), channel_id=1, source_target_pairs={{0,2},{1,3},{2,0},{3,1},{4,6},{5,7},{6,4},{7,5},{8,10},{9,11},{10,... | collective-permute-start | bytes 491528 | tf_op jit(solution)/shard_map/ppermute | solution.py:400
  5.7 0.7 %copy-start.6 = (s32[16]{0:T(128)S(1)}, s32[16]{0:T(128)}, u32[]{:S(2)}) copy-start(s32[16]{0:T(128)} %slot_ref.1) | copy-start | bytes 196
  6.3 6.4 %copy-start.1 = (bf16[2,8,1024,128]{3,2,1,0:T(8,128)(2,1)S(1)}, bf16[2,8,1024,128]{3,2,1,0:T(8,128)(2,1)}, u32[]{:S(2)}) copy-start(bf16[2,8,1024,128]{3,2,1,0:T(8,128)(2,1)} %constant.39.clone.refs_2_.refs_3_) | copy-start | bytes 12582916
  6.3 6.4 %copy-start.3 = (bf16[2,192,160]{2,1,0:T(8,128)(2,1)S(1)}, bf16[2,192,160]{2,1,0:T(8,128)(2,1)}, u32[]{:S(2)}) copy-start(bf16[2,192,160]{2,1,0:T(8,128)(2,1)} %constant.40.clone.refs_3_.refs_4_) | copy-start | bytes 368644
  6.4 6.4 %copy-start.4 = (bf16[2,40960]{1,0:T(2,128)(2,1)S(1)}, bf16[2,40960]{1,0:T(2,128)(2,1)}, u32[]{:S(2)}) copy-start(bf16[2,40960]{1,0:T(2,128)(2,1)} %param.10) | copy-start | bytes 491524
  19.6 2.9 %copy-start.2 = (bf16[2,8,1024,128]{3,2,1,0:T(8,128)(2,1)S(1)}, bf16[2,8,1024,128]{3,2,1,0:T(8,128)(2,1)}, u32[]{:S(2)}) copy-start(bf16[2,8,1024,128]{3,2,1,0:T(8,128)(2,1)} %constant.42.clone.refs_4_) | copy-start | bytes 12582916
  19.6 2.9 %copy-start.5 = (bf16[2,128,192]{2,1,0:T(8,128)(2,1)S(1)}, bf16[2,128,192]{2,1,0:T(8,128)(2,1)}, u32[]{:S(2)}) copy-start(bf16[2,128,192]{2,1,0:T(8,128)(2,1)} %constant.41.clone.refs_3_) | copy-start | bytes 294916
  19.6 2.9 %collective-permute-start.4 = (bf16[8,6,96,128]{3,2,1,0:T(8,128)(2,1)S(1)}, bf16[8,6,96,128]{3,2,1,0:T(8,128)(2,1)S(1)}, u32[]{:S(2)}, u32[]{:S(2)}) collective-permute-start(bf16[8,6,96,128]{3,2,1,0:T(8,128)(2,1)S(1)} %shard_map.103.refs_0_), channel_id=1, source_target_pairs={{0,1},{1,0},{2,3},{3,2},{4,5},{5,4},{6,7},{7,6},{8,9},{9,8},{10,11... | collective-permute-start | bytes 3538952 | tf_op jit(solution)/shard_map/ppermute | solution.py:400
  21.6 21.3 %copy-start.7 = (s32[64]{0:T(128)S(1)}, s32[64]{0:T(128)}, u32[]{:S(2)}) copy-start(s32[64]{0:T(128)} %constant.38.clone) | copy-start | bytes 772
  26.5 5.9 %collective-permute-start.5 = (bf16[8,8,1024]{2,1,0:T(8,128)(2,1)S(1)}, bf16[8,8,1024]{2,1,0:T(8,128)(2,1)S(1)}, u32[]{:S(2)}, u32[]{:S(2)}) collective-permute-start(bf16[8,8,1024]{2,1,0:T(8,128)(2,1)S(1)} %get-tuple-element.30), channel_id=1, source_target_pairs={{0,8},{8,0},{16,24},{24,16},{1,9},{9,1},{17,25},{25,17},{2,10},{10... | collective-permute-start | bytes 393224 | tf_op jit(solution)/shard_map/ppermute | solution.py:400
  28.1 8.1 %collective-permute-start.6 = (bf16[8,8,1024]{2,1,0:T(8,128)(2,1)S(1)}, bf16[8,8,1024]{2,1,0:T(8,128)(2,1)S(1)}, u32[]{:S(2)}, u32[]{:S(2)}) collective-permute-start(bf16[8,8,1024]{2,1,0:T(8,128)(2,1)S(1)} %get-tuple-element.31), channel_id=1, source_target_pairs={{0,16},{8,24},{16,0},{24,8},{1,17},{9,25},{17,1},{25,9},{2,18},{10... | collective-permute-start | bytes 393224 | tf_op jit(solution)/shard_map/ppermute | solution.py:400
  29.7 6.5 %collective-permute-start.7 = (bf16[8,8,1024]{2,1,0:T(8,128)(2,1)S(1)}, bf16[8,8,1024]{2,1,0:T(8,128)(2,1)S(1)}, u32[]{:S(2)}, u32[]{:S(2)}) collective-permute-start(bf16[8,8,1024]{2,1,0:T(8,128)(2,1)S(1)} %get-tuple-element.32), channel_id=1, source_target_pairs={{0,24},{8,16},{16,8},{24,0},{1,25},{9,17},{17,9},{25,1},{2,26},{10... | collective-permute-start | bytes 393224 | tf_op jit(solution)/shard_map/ppermute | solution.py:400
  36.7 1.3 %collective-permute-start.8 = (bf16[32,1024]{1,0:T(8,128)(2,1)S(1)}, bf16[32,1024]{1,0:T(8,128)(2,1)S(1)}, u32[]{:S(2)}, u32[]{:S(2)}) collective-permute-start(bf16[32,1024]{1,0:T(8,128)(2,1)S(1)} %pad_maximum_fusion), channel_id=1, source_target_pairs={{0,1},{1,0},{2,3},{3,2},{4,5},{5,4},{6,7},{7,6},{8,9},{9,8},{10,11... | collective-permute-start | bytes 196616 | tf_op jit(solution)/shard_map/ppermute | solution.py:400
  38.0 8.7 %collective-permute-start.9 = (bf16[32,1024]{1,0:T(8,128)(2,1)S(1)}, bf16[32,1024]{1,0:T(8,128)(2,1)S(1)}, u32[]{:S(2)}, u32[]{:S(2)}) collective-permute-start(bf16[32,1024]{1,0:T(8,128)(2,1)S(1)} %pad_maximum_fusion.1), channel_id=1, source_target_pairs={{0,4},{1,5},{2,6},{3,7},{4,0},{5,1},{6,2},{7,3},{8,12},{9,13},{10,... | collective-permute-start | bytes 196616 | tf_op jit(solution)/shard_map/ppermute | solution.py:400
  46.7 4.3 %collective-permute-start.10 = (bf16[32,1024]{1,0:T(8,128)(2,1)S(1)}, bf16[32,1024]{1,0:T(8,128)(2,1)S(1)}, u32[]{:S(2)}, u32[]{:S(2)}) collective-permute-start(bf16[32,1024]{1,0:T(8,128)(2,1)S(1)} %pad_maximum_fusion.2), channel_id=1, source_target_pairs={{0,2},{1,3},{2,0},{3,1},{4,6},{5,7},{6,4},{7,5},{8,10},{9,11},{10,... | collective-permute-start | bytes 196616 | tf_op jit(solution)/shard_map/ppermute | solution.py:400

commit v15 on v13

--- a/solution.py
+++ b/solution.py
@@ -401,7 +401,7 @@
 
     chips = ch_count // 2
     first = chips // 2
-    far = [first] + [d for d in range(chips - 1, 0, -1) if d != first]
+    far = list(range(1, chips))
     mate = swap(x_own, "ch", ch_count, 1)
     lanes = {d: swap(x_own, "ch", ch_count, 2 * d) for d in far}
     me = (src_me[None], ch_me[None])

time: 49.1 us -> 49.7 us (1.012)
  waiting for transfers between devices: 13.4 us -> 14.5 us
  starting transfers between devices: 14.9 us -> 14.4 us
    ppermute x12, waiting for transfers between devices: 13.4 us -> 14.5 us  [swap(): return lax.ppermute(value, axis, [(i, i ^ flip) for i in range(count)])]
  transfers between devices with their start and end apart: 12 -> 12, of which waited for: 8 -> 7; matrix products, arithmetic and copies ran while one was open for 0% -> 0% of each run, Pallas kernels for 22% -> 22%
where the time goes in v15:
time: 49.7 us; the launch traced here: 49.6 us
  Pallas kernels  17.5 us (35%)
  waiting for transfers between devices  14.5 us (29%)
  starting transfers between devices  14.4 us (29%)
  matrix products  2.28 us (5%)
  local copies, waits for them, and re-layouts  0.71 us (1%)
    ppermute x12, waiting for transfers between devices, swap(): return lax.ppermute(value, axis, [(i, i ^ flip) for i in range(count)])  14.5 us
    ppermute x12, starting transfers between devices, swap(): return lax.ppermute(value, axis, [(i, i ^ flip) for i in range(count)])  14.4 us
    pallas_call x3, Pallas kernels, add_sources(): pl.pallas_call(body, in_specs=[smem] * 2 + [vmem] * (len(operands) - 2),...  6.94 us
    pallas_call x1, Pallas kernels, transform_responses(): pl.pallas_call(functools.partial(response_kernel, rows, bins), in_specs=[...  6.37 us
    pallas_call x2, Pallas kernels, transform_signals(): pl.pallas_call(functools.partial(spectra_kernel, len(x_list), rows), in_s...  3.73 us
    dot_general x1, matrix products, decode(): lax.dot_general(signal, matrix, (((0,), (0,)), ((), ())), preferred_eleme...  2.05 us
  transfers between devices with their start and end apart: 12, of which 7 were waited for; matrix products, arithmetic and copies ran while one was open for 0% of the time, Pallas kernels for 22%

profile of v15, /device:TPU:0, one launch (start us, length us, event | category | flops | bytes accessed | tf_op | source)
XLA Modules:
  0.0 49.6 jit_solution(76548496837124871)
XLA Ops:
  0.0 0.0 copy-start
  0.0 0.5 collective-permute-start.3
  0.5 2.6 %collective-permute-start = (bf16[40,2,1024]{2,1,0:T(2,128)(2,1)}, bf16[40,2,1024]{2,1,0:T(2,128)(2,1)S(1)}, u32[]{:S(2)}, u32[]{:S(2)}) collective-permute-start(bf16[40,2,1024]{2,1,0:T(2,128)(2,1)} %bitcast.9), channel_id=1, source_target_pairs={{0,2},{1,3},{2,0},{3,1},{4,6},{5,7},{6,4},{7,5},{8,10},{9,11},{10,... | collective-permute-start | bytes 491528 | tf_op jit(solution)/shard_map/ppermute | solution.py:400
  3.1 2.6 %collective-permute-start.1 = (bf16[40,2,1024]{2,1,0:T(2,128)(2,1)}, bf16[40,2,1024]{2,1,0:T(2,128)(2,1)S(1)}, u32[]{:S(2)}, u32[]{:S(2)}) collective-permute-start(bf16[40,2,1024]{2,1,0:T(2,128)(2,1)} %bitcast.10), channel_id=1, source_target_pairs={{0,4},{1,5},{2,6},{3,7},{4,0},{5,1},{6,2},{7,3},{8,12},{9,13},{10,... | collective-permute-start | bytes 491528 | tf_op jit(solution)/shard_map/ppermute | solution.py:400
  5.7 0.0 collective-permute-start.2
  5.7 0.0 copy-start.6
  5.7 0.7 %copy-done.6 = s32[16]{0:T(128)S(1)} copy-done((s32[16]{0:T(128)S(1)}, s32[16]{0:T(128)}, u32[]{:S(2)}) %copy-start.6) | copy-done | bytes 88
  6.3 0.0 copy-start.1
  6.3 0.0 copy-start.3
  6.4 6.4 %shard_map.100.refs_1_ = bf16[16,8,384,128]{3,2,1,0:T(8,128)(2,1)S(1)} custom-call(s32[1]{0:T(128)} %bitcast.1.src_ref, s32[1]{0:T(128)} %bitcast.ch_ref, s32[16]{0:T(128)S(1)} %copy-done.6, bf16[16,8,8,2,1024]{4,3,2,1,0:T(2,128)(2,1)} %room_hbm.1, bf16[384,256]{1,0:T(8,128)(2,1)} %constant.37.clone.table_hbm), custom_call_target="tpu_custom_call" | custom-call | flops 1048576 | bytes 65536 | tf_op jit(solution)/shard_map/pallas_call | solution.py:154
  12.7 0.0 collective-permute-done.3.refs_1_
  12.7 0.0 copy-done.1
  12.8 0.0 copy-done.3
  12.8 0.0 copy-done.4
  12.8 1.7 %shard_map.101.refs_0_ = bf16[8,4,96,128]{3,2,1,0:T(8,128)(2,1)S(1)} custom-call(bf16[40,2,1024]{2,1,0:T(2,128)(2,1)S(1)} %bitcast.12, bf16[40,2,1024]{2,1,0:T(2,128)(2,1)S(1)} %collective-permute-done.3.refs_1_, bf16[2,8,1024,128]{3,2,1,0:T(8,128)(2,1)S(1)} %copy-done.1, bf16[2,192,160]{2,1,0:T(8,128)(2,1)S(1)} %copy-done.3), custom_call_target="tpu_custom_call" | custom-call | flops 1048576 | bytes 65536 | tf_op jit(solution)/shard_map/pallas_call | solution.py:210
  14.4 1.0 %shard_map.102.refs_2_ = f32[8,4,192,128]{3,2,1,0:T(8,128)S(1)} custom-call(s32[1]{0:T(128)} %bitcast.1.src_ref, s32[1]{0:T(128)} %bitcast.ch_ref, bf16[8,4,96,128]{3,2,1,0:T(8,128)(2,1)S(1)} %shard_map.101.refs_0_, bf16[16,8,384,128]{3,2,1,0:T(8,128)(2,1)S(1)} %shard_map.100.refs_1_), custom_call_target="tpu_custom_call" | custom-call | flops 1048576 | bytes 65536 | tf_op jit(solution)/shard_map/pallas_call | solution.py:344
  15.5 0.0 copy-start.7
  15.5 0.0 collective-permute-done.refs_0_
  15.5 2.8 %collective-permute-done.1.refs_1_ = bf16[40,2,1024]{2,1,0:T(2,128)(2,1)S(1)} collective-permute-done((bf16[40,2,1024]{2,1,0:T(2,128)(2,1)}, bf16[40,2,1024]{2,1,0:T(2,128)(2,1)S(1)}, u32[]{:S(2)}, u32[]{:S(2)}) %collective-permute-start.1) | collective-permute-done | bytes 163872 | tf_op jit(solution)/shard_map/ppermute | solution.py:400
  18.3 0.0 collective-permute-done.2.refs_2_
  18.3 2.1 %shard_map.103.refs_0_ = bf16[8,6,96,128]{3,2,1,0:T(8,128)(2,1)S(1)} custom-call(bf16[40,2,1024]{2,1,0:T(2,128)(2,1)S(1)} %collective-permute-done.refs_0_, bf16[40,2,1024]{2,1,0:T(2,128)(2,1)S(1)} %collective-permute-done.1.refs_1_, bf16[40,2,1024]{2,1,0:T(2,128)(2,1)S(1)} %collective-permute-done.2.refs_2_, bf16[2,8,1024,128]{3,2,1,0:T(8,128)(2,1)S(1)} %copy-done.1, ...), custom_call_target="tpu_custom_call" | custom-call | flops 1048576 | bytes 65536 | tf_op jit(solution)/shard_map/pallas_call | solution.py:210
  20.4 0.1 collective-permute-start.4
  20.5 0.0 copy-done.7
  20.5 0.0 copy-start.2
  20.5 0.0 copy-start.5
  20.5 1.9 %shard_map.104.refs_2_ = f32[8,4,192,128]{3,2,1,0:T(8,128)S(1)} custom-call(s32[1]{0:T(128)} %bitcast.1.src_ref, s32[1]{0:T(128)} %bitcast.ch_ref, bf16[8,6,96,128]{3,2,1,0:T(8,128)(2,1)S(1)} %shard_map.103.refs_0_, bf16[16,8,384,128]{3,2,1,0:T(8,128)(2,1)S(1)} %shard_map.100.refs_1_, ...), custom_call_target="tpu_custom_call", output_to_operand_aliasing={{}: (4, {})} | custom-call | flops 1048576 | bytes 65536 | tf_op jit(solution)/shard_map/pallas_call | solution.py:344
  22.4 0.9 %collective-permute-done.4.refs_0_ = bf16[8,6,96,128]{3,2,1,0:T(8,128)(2,1)S(1)} collective-permute-done((bf16[8,6,96,128]{3,2,1,0:T(8,128)(2,1)S(1)}, bf16[8,6,96,128]{3,2,1,0:T(8,128)(2,1)S(1)}, u32[]{:S(2)}, u32[]{:S(2)}) %collective-permute-start.4) | collective-permute-done | bytes 1179680 | tf_op jit(solution)/shard_map/ppermute | solution.py:400
  23.3 0.0 copy-done.2
  23.3 0.0 copy-done.5
  23.3 4.0 %shard_map.105 = (bf16[8,8,1024]{2,1,0:T(8,128)(2,1)S(1)}, bf16[8,8,1024]{2,1,0:T(8,128)(2,1)S(1)}, bf16[8,8,1024]{2,1,0:T(8,128)(2,1)S(1)}, bf16[8,8,1024]{2,1,0:T(8,128)(2,1)S(1)}) custom-call(s32[1]{0:T(128)} %bitcast.1.src_ref, s32[1]{0:T(128)} %bitcast.ch_ref, bf16[8,6,96,128]{3,2,1,0:T(8,128)(2,1)S(1)} %collective-permute-done.4.refs_0_, ...), custom_call_target="tpu_custom_call" | custom-call | flops 1048576 | bytes 65536 | tf_op jit(solution)/shard_map/pallas_call | solution.py:344
  27.3 1.6 %collective-permute-start.5 = (bf16[8,8,1024]{2,1,0:T(8,128)(2,1)S(1)}, bf16[8,8,1024]{2,1,0:T(8,128)(2,1)S(1)}, u32[]{:S(2)}, u32[]{:S(2)}) collective-permute-start(bf16[8,8,1024]{2,1,0:T(8,128)(2,1)S(1)} %get-tuple-element.30), channel_id=1, source_target_pairs={{0,8},{8,0},{16,24},{24,16},{1,9},{9,1},{17,25},{25,17},{2,10},{10... | collective-permute-start | bytes 393224 | tf_op jit(solution)/shard_map/ppermute | solution.py:400
  28.9 1.5 %collective-permute-start.6 = (bf16[8,8,1024]{2,1,0:T(8,128)(2,1)S(1)}, bf16[8,8,1024]{2,1,0:T(8,128)(2,1)S(1)}, u32[]{:S(2)}, u32[]{:S(2)}) collective-permute-start(bf16[8,8,1024]{2,1,0:T(8,128)(2,1)S(1)} %get-tuple-element.31), channel_id=1, source_target_pairs={{0,16},{8,24},{16,0},{24,8},{1,17},{9,25},{17,1},{25,9},{2,18},{10... | collective-permute-start | bytes 393224 | tf_op jit(solution)/shard_map/ppermute | solution.py:400
  30.4 0.5 collective-permute-start.7
  30.9 0.0 copy-done
  30.9 0.2 convolution_convert_fusion.1
  31.1 2.1 %collective-permute-done.5.refs_1_ = bf16[8,8,1024]{2,1,0:T(8,128)(2,1)S(1)} collective-permute-done((bf16[8,8,1024]{2,1,0:T(8,128)(2,1)S(1)}, bf16[8,8,1024]{2,1,0:T(8,128)(2,1)S(1)}, u32[]{:S(2)}, u32[]{:S(2)}) %collective-permute-start.5) | collective-permute-done | bytes 131104 | tf_op jit(solution)/shard_map/ppermute | solution.py:400
  33.2 3.7 %collective-permute-done.6.refs_2_ = bf16[8,8,1024]{2,1,0:T(8,128)(2,1)S(1)} collective-permute-done((bf16[8,8,1024]{2,1,0:T(8,128)(2,1)S(1)}, bf16[8,8,1024]{2,1,0:T(8,128)(2,1)S(1)}, u32[]{:S(2)}, u32[]{:S(2)}) %collective-permute-start.6) | collective-permute-done | bytes 131104 | tf_op jit(solution)/shard_map/ppermute | solution.py:400
  37.0 0.0 collective-permute-done.7.refs_3_
  37.0 0.5 shard_map.106
  37.4 0.1 collective-permute-start.8
  37.5 1.2 %collective-permute-done.8 = bf16[32,1024]{1,0:T(8,128)(2,1)S(1)} collective-permute-done((bf16[32,1024]{1,0:T(8,128)(2,1)S(1)}, bf16[32,1024]{1,0:T(8,128)(2,1)S(1)}, u32[]{:S(2)}, u32[]{:S(2)}) %collective-permute-start.8) | collective-permute-done | bytes 65568 | tf_op jit(solution)/shard_map/ppermute | solution.py:400
  38.8 2.5 %collective-permute-start.11 = (bf16[16,1024]{1,0:T(8,128)(2,1)S(1)}, bf16[16,1024]{1,0:T(8,128)(2,1)S(1)}, u32[]{:S(2)}, u32[]{:S(2)}) collective-permute-start(bf16[16,1024]{1,0:T(8,128)(2,1)S(1)} %pad_maximum_fusion.3), channel_id=1, source_target_pairs={{0,6},{1,7},{2,4},{3,5},{4,2},{5,3},{6,0},{7,1},{8,14},{9,15},{10,... | collective-permute-start | bytes 98312 | tf_op jit(solution)/shard_map/ppermute | solution.py:400
  41.3 2.3 %collective-permute-start.9 = (bf16[16,1024]{1,0:T(8,128)(2,1)S(1)}, bf16[16,1024]{1,0:T(8,128)(2,1)S(1)}, u32[]{:S(2)}, u32[]{:S(2)}) collective-permute-start(bf16[16,1024]{1,0:T(8,128)(2,1)S(1)} %pad_maximum_fusion.1), channel_id=1, source_target_pairs={{0,4},{1,5},{2,6},{3,7},{4,0},{5,1},{6,2},{7,3},{8,12},{9,13},{10,... | collective-permute-start | bytes 98312 | tf_op jit(solution)/shard_map/ppermute | solution.py:400
  43.6 0.2 collective-permute-start.10
  43.8 2.4 %collective-permute-done.9 = bf16[16,1024]{1,0:T(8,128)(2,1)S(1)} collective-permute-done((bf16[16,1024]{1,0:T(8,128)(2,1)S(1)}, bf16[16,1024]{1,0:T(8,128)(2,1)S(1)}, u32[]{:S(2)}, u32[]{:S(2)}) %collective-permute-start.9) | collective-permute-done | bytes 32800 | tf_op jit(solution)/shard_map/ppermute | solution.py:400
  46.2 1.4 %collective-permute-done.10 = bf16[16,1024]{1,0:T(8,128)(2,1)S(1)} collective-permute-done((bf16[16,1024]{1,0:T(8,128)(2,1)S(1)}, bf16[16,1024]{1,0:T(8,128)(2,1)S(1)}, u32[]{:S(2)}, u32[]{:S(2)}) %collective-permute-start.10) | collective-permute-done | bytes 32800 | tf_op jit(solution)/shard_map/ppermute | solution.py:400
  47.5 0.0 collective-permute-done.11
  47.5 2.1 %convolution_convert_fusion = bf16[1024,1024]{1,0:T(8,128)(2,1)} fusion(bf16[64,1024]{1,0:T(8,128)(2,1)S(1)} %constant_dynamic-update-slice_fusion, bf16[64,1024]{1,0:T(8,128)(2,1)S(1)} %convolution_convert_fusion.1), kind=kOutput, calls=%fused_computation | convolution fusion | flops 135266304 | bytes 2359296 | tf_op jit(solution)/shard_map/dot_general | solution.py:380
  (11 shorter events, 0.0 us)
Async XLA Ops:
  0.0 30.9 %copy-start = (bf16[64,1024]{1,0:T(8,128)(2,1)S(1)}, bf16[64,1024]{1,0:T(8,128)(2,1)}, u32[]{:S(2)}) copy-start(bf16[64,1024]{1,0:T(8,128)(2,1)} %param.13) | copy-start | bytes 393220
  0.0 12.7 %collective-permute-start.3 = (bf16[40,2,1024]{2,1,0:T(2,128)(2,1)}, bf16[40,2,1024]{2,1,0:T(2,128)(2,1)S(1)}, u32[]{:S(2)}, u32[]{:S(2)}) collective-permute-start(bf16[40,2,1024]{2,1,0:T(2,128)(2,1)} %bitcast.8), channel_id=1, source_target_pairs={{0,1},{1,0},{2,3},{3,2},{4,5},{5,4},{6,7},{7,6},{8,9},{9,8},{10,11... | collective-permute-start | bytes 491528 | tf_op jit(solution)/shard_map/ppermute | solution.py:400
  0.5 15.0 %collective-permute-start = (bf16[40,2,1024]{2,1,0:T(2,128)(2,1)}, bf16[40,2,1024]{2,1,0:T(2,128)(2,1)S(1)}, u32[]{:S(2)}, u32[]{:S(2)}) collective-permute-start(bf16[40,2,1024]{2,1,0:T(2,128)(2,1)} %bitcast.9), channel_id=1, source_target_pairs={{0,2},{1,3},{2,0},{3,1},{4,6},{5,7},{6,4},{7,5},{8,10},{9,11},{10,... | collective-permute-start | bytes 491528 | tf_op jit(solution)/shard_map/ppermute | solution.py:400
  3.1 15.2 %collective-permute-start.1 = (bf16[40,2,1024]{2,1,0:T(2,128)(2,1)}, bf16[40,2,1024]{2,1,0:T(2,128)(2,1)S(1)}, u32[]{:S(2)}, u32[]{:S(2)}) collective-permute-start(bf16[40,2,1024]{2,1,0:T(2,128)(2,1)} %bitcast.10), channel_id=1, source_target_pairs={{0,4},{1,5},{2,6},{3,7},{4,0},{5,1},{6,2},{7,3},{8,12},{9,13},{10,... | collective-permute-start | bytes 491528 | tf_op jit(solution)/shard_map/ppermute | solution.py:400
  5.7 12.6 %collective-permute-start.2 = (bf16[40,2,1024]{2,1,0:T(2,128)(2,1)}, bf16[40,2,1024]{2,1,0:T(2,128)(2,1)S(1)}, u32[]{:S(2)}, u32[]{:S(2)}) collective-permute-start(bf16[40,2,1024]{2,1,0:T(2,128)(2,1)} %bitcast.11), channel_id=1, source_target_pairs={{0,6},{1,7},{2,4},{3,5},{4,2},{5,3},{6,0},{7,1},{8,14},{9,15},{10,... | collective-permute-start | bytes 491528 | tf_op jit(solution)/shard_map/ppermute | solution.py:400
  5.7 0.7 %copy-start.6 = (s32[16]{0:T(128)S(1)}, s32[16]{0:T(128)}, u32[]{:S(2)}) copy-start(s32[16]{0:T(128)} %slot_ref.1) | copy-start | bytes 196
  6.3 6.4 %copy-start.1 = (bf16[2,8,1024,128]{3,2,1,0:T(8,128)(2,1)S(1)}, bf16[2,8,1024,128]{3,2,1,0:T(8,128)(2,1)}, u32[]{:S(2)}) copy-start(bf16[2,8,1024,128]{3,2,1,0:T(8,128)(2,1)} %constant.39.clone.refs_2_.refs_3_) | copy-start | bytes 12582916
  6.3 6.4 %copy-start.3 = (bf16[2,192,160]{2,1,0:T(8,128)(2,1)S(1)}, bf16[2,192,160]{2,1,0:T(8,128)(2,1)}, u32[]{:S(2)}) copy-start(bf16[2,192,160]{2,1,0:T(8,128)(2,1)} %constant.40.clone.refs_3_.refs_4_) | copy-start | bytes 368644
  6.4 6.4 %copy-start.4 = (bf16[2,40960]{1,0:T(2,128)(2,1)S(1)}, bf16[2,40960]{1,0:T(2,128)(2,1)}, u32[]{:S(2)}) copy-start(bf16[2,40960]{1,0:T(2,128)(2,1)} %param.10) | copy-start | bytes 491524
  15.5 5.0 %copy-start.7 = (s32[64]{0:T(128)S(1)}, s32[64]{0:T(128)}, u32[]{:S(2)}) copy-start(s32[64]{0:T(128)} %constant.38.clone) | copy-start | bytes 772
  20.4 2.9 %collective-permute-start.4 = (bf16[8,6,96,128]{3,2,1,0:T(8,128)(2,1)S(1)}, bf16[8,6,96,128]{3,2,1,0:T(8,128)(2,1)S(1)}, u32[]{:S(2)}, u32[]{:S(2)}) collective-permute-start(bf16[8,6,96,128]{3,2,1,0:T(8,128)(2,1)S(1)} %shard_map.103.refs_0_), channel_id=1, source_target_pairs={{0,1},{1,0},{2,3},{3,2},{4,5},{5,4},{6,7},{7,6},{8,9},{9,8},{10,11... | collective-permute-start | bytes 3538952 | tf_op jit(solution)/shard_map/ppermute | solution.py:400
  20.5 2.8 %copy-start.2 = (bf16[2,8,1024,128]{3,2,1,0:T(8,128)(2,1)S(1)}, bf16[2,8,1024,128]{3,2,1,0:T(8,128)(2,1)}, u32[]{:S(2)}) copy-start(bf16[2,8,1024,128]{3,2,1,0:T(8,128)(2,1)} %constant.42.clone.refs_4_) | copy-start | bytes 12582916
  20.5 2.8 %copy-start.5 = (bf16[2,128,192]{2,1,0:T(8,128)(2,1)S(1)}, bf16[2,128,192]{2,1,0:T(8,128)(2,1)}, u32[]{:S(2)}) copy-start(bf16[2,128,192]{2,1,0:T(8,128)(2,1)} %constant.41.clone.refs_3_) | copy-start | bytes 294916
  27.3 5.9 %collective-permute-start.5 = (bf16[8,8,1024]{2,1,0:T(8,128)(2,1)S(1)}, bf16[8,8,1024]{2,1,0:T(8,128)(2,1)S(1)}, u32[]{:S(2)}, u32[]{:S(2)}) collective-permute-start(bf16[8,8,1024]{2,1,0:T(8,128)(2,1)S(1)} %get-tuple-element.30), channel_id=1, source_target_pairs={{0,8},{8,0},{16,24},{24,16},{1,9},{9,1},{17,25},{25,17},{2,10},{10... | collective-permute-start | bytes 393224 | tf_op jit(solution)/shard_map/ppermute | solution.py:400
  28.9 8.1 %collective-permute-start.6 = (bf16[8,8,1024]{2,1,0:T(8,128)(2,1)S(1)}, bf16[8,8,1024]{2,1,0:T(8,128)(2,1)S(1)}, u32[]{:S(2)}, u32[]{:S(2)}) collective-permute-start(bf16[8,8,1024]{2,1,0:T(8,128)(2,1)S(1)} %get-tuple-element.31), channel_id=1, source_target_pairs={{0,16},{8,24},{16,0},{24,8},{1,17},{9,25},{17,1},{25,9},{2,18},{10... | collective-permute-start | bytes 393224 | tf_op jit(solution)/shard_map/ppermute | solution.py:400
  30.4 6.6 %collective-permute-start.7 = (bf16[8,8,1024]{2,1,0:T(8,128)(2,1)S(1)}, bf16[8,8,1024]{2,1,0:T(8,128)(2,1)S(1)}, u32[]{:S(2)}, u32[]{:S(2)}) collective-permute-start(bf16[8,8,1024]{2,1,0:T(8,128)(2,1)S(1)} %get-tuple-element.32), channel_id=1, source_target_pairs={{0,24},{8,16},{16,8},{24,0},{1,25},{9,17},{17,9},{25,1},{2,26},{10... | collective-permute-start | bytes 393224 | tf_op jit(solution)/shard_map/ppermute | solution.py:400
  37.4 1.3 %collective-permute-start.8 = (bf16[32,1024]{1,0:T(8,128)(2,1)S(1)}, bf16[32,1024]{1,0:T(8,128)(2,1)S(1)}, u32[]{:S(2)}, u32[]{:S(2)}) collective-permute-start(bf16[32,1024]{1,0:T(8,128)(2,1)S(1)} %pad_maximum_fusion), channel_id=1, source_target_pairs={{0,1},{1,0},{2,3},{3,2},{4,5},{5,4},{6,7},{7,6},{8,9},{9,8},{10,11... | collective-permute-start | bytes 196616 | tf_op jit(solution)/shard_map/ppermute | solution.py:400
  38.8 8.8 %collective-permute-start.11 = (bf16[16,1024]{1,0:T(8,128)(2,1)S(1)}, bf16[16,1024]{1,0:T(8,128)(2,1)S(1)}, u32[]{:S(2)}, u32[]{:S(2)}) collective-permute-start(bf16[16,1024]{1,0:T(8,128)(2,1)S(1)} %pad_maximum_fusion.3), channel_id=1, source_target_pairs={{0,6},{1,7},{2,4},{3,5},{4,2},{5,3},{6,0},{7,1},{8,14},{9,15},{10,... | collective-permute-start | bytes 98312 | tf_op jit(solution)/shard_map/ppermute | solution.py:400
  41.3 4.8 %collective-permute-start.9 = (bf16[16,1024]{1,0:T(8,128)(2,1)S(1)}, bf16[16,1024]{1,0:T(8,128)(2,1)S(1)}, u32[]{:S(2)}, u32[]{:S(2)}) collective-permute-start(bf16[16,1024]{1,0:T(8,128)(2,1)S(1)} %pad_maximum_fusion.1), channel_id=1, source_target_pairs={{0,4},{1,5},{2,6},{3,7},{4,0},{5,1},{6,2},{7,3},{8,12},{9,13},{10,... | collective-permute-start | bytes 98312 | tf_op jit(solution)/shard_map/ppermute | solution.py:400
  43.6 3.9 %collective-permute-start.10 = (bf16[16,1024]{1,0:T(8,128)(2,1)S(1)}, bf16[16,1024]{1,0:T(8,128)(2,1)S(1)}, u32[]{:S(2)}, u32[]{:S(2)}) collective-permute-start(bf16[16,1024]{1,0:T(8,128)(2,1)S(1)} %pad_maximum_fusion.2), channel_id=1, source_target_pairs={{0,2},{1,3},{2,0},{3,1},{4,6},{5,7},{6,4},{7,5},{8,10},{9,11},{10,... | collective-permute-start | bytes 98312 | tf_op jit(solution)/shard_map/ppermute | solution.py:400

commit v16 on v13

--- a/solution.py
+++ b/solution.py
@@ -428,7 +428,7 @@
     total = add([mine], [[2 * d for d in far]], total, False)
     total = add([given], [[2 * d + 1 for d in far]], total, True)
 
-    sums = [total[0]] + [swap(total[d], "src", src_count, d) for d in range(1, src_count)]
+    sums = [total[0]] + [swap(total[d], "src", src_count, d) for d in range(src_count - 1, 0, -1)]
     if blocks == src_count * ch_count:
         pieces = sum_groups(sums, ch_me[None])
         given = swap(jnp.concatenate(pieces[1::2], axis=0), "ch", ch_count, 1)

time: 49.1 us -> 48.9 us (level)
  transfers between devices with their start and end apart: 12 -> 12, of which waited for: 8 -> 9; matrix products, arithmetic and copies ran while one was open for 0% -> 1% of each run, Pallas kernels for 22% -> 23%
where the time goes in v16:
time: 48.9 us; the launch traced here: 48.7 us
  Pallas kernels  17.5 us (36%)
  starting transfers between devices  14.9 us (30%)
  waiting for transfers between devices  13.2 us (27%)
  matrix products  2.28 us (5%)
  local copies, waits for them, and re-layouts  0.71 us (1%)
    ppermute x12, starting transfers between devices, swap(): return lax.ppermute(value, axis, [(i, i ^ flip) for i in range(count)])  14.9 us
    ppermute x12, waiting for transfers between devices, swap(): return lax.ppermute(value, axis, [(i, i ^ flip) for i in range(count)])  13.2 us
    pallas_call x3, Pallas kernels, add_sources(): pl.pallas_call(body, in_specs=[smem] * 2 + [vmem] * (len(operands) - 2),...  6.94 us
    pallas_call x1, Pallas kernels, transform_responses(): pl.pallas_call(functools.partial(response_kernel, rows, bins), in_specs=[...  6.38 us
    pallas_call x2, Pallas kernels, transform_signals(): pl.pallas_call(functools.partial(spectra_kernel, len(x_list), rows), in_s...  3.73 us
    dot_general x1, matrix products, decode(): lax.dot_general(signal, matrix, (((0,), (0,)), ((), ())), preferred_eleme...  2.05 us
  transfers between devices with their start and end apart: 12, of which 9 were waited for; matrix products, arithmetic and copies ran while one was open for 1% of the time, Pallas kernels for 23%

profile of v16, /device:TPU:0, one launch (start us, length us, event | category | flops | bytes accessed | tf_op | source)
XLA Modules:
  0.0 48.7 jit_solution(2508122460442686483)
XLA Ops:
  0.0 0.0 copy-start
  0.0 0.5 collective-permute-start.3
  0.5 3.7 %collective-permute-start = (bf16[40,2,1024]{2,1,0:T(2,128)(2,1)}, bf16[40,2,1024]{2,1,0:T(2,128)(2,1)S(1)}, u32[]{:S(2)}, u32[]{:S(2)}) collective-permute-start(bf16[40,2,1024]{2,1,0:T(2,128)(2,1)} %bitcast.9), channel_id=1, source_target_pairs={{0,4},{1,5},{2,6},{3,7},{4,0},{5,1},{6,2},{7,3},{8,12},{9,13},{10,... | collective-permute-start | bytes 491528 | tf_op jit(solution)/shard_map/ppermute | solution.py:400
  4.1 1.3 %collective-permute-start.1 = (bf16[40,2,1024]{2,1,0:T(2,128)(2,1)}, bf16[40,2,1024]{2,1,0:T(2,128)(2,1)S(1)}, u32[]{:S(2)}, u32[]{:S(2)}) collective-permute-start(bf16[40,2,1024]{2,1,0:T(2,128)(2,1)} %bitcast.10), channel_id=1, source_target_pairs={{0,6},{1,7},{2,4},{3,5},{4,2},{5,3},{6,0},{7,1},{8,14},{9,15},{10,... | collective-permute-start | bytes 491528 | tf_op jit(solution)/shard_map/ppermute | solution.py:400
  5.5 0.2 collective-permute-start.2
  5.7 0.0 copy-start.6
  5.7 0.7 %copy-done.6 = s32[16]{0:T(128)S(1)} copy-done((s32[16]{0:T(128)S(1)}, s32[16]{0:T(128)}, u32[]{:S(2)}) %copy-start.6) | copy-done | bytes 88
  6.3 0.0 copy-start.1
  6.3 0.0 copy-start.3
  6.4 6.4 %shard_map.100.refs_1_ = bf16[16,8,384,128]{3,2,1,0:T(8,128)(2,1)S(1)} custom-call(s32[1]{0:T(128)} %bitcast.1.src_ref, s32[1]{0:T(128)} %bitcast.ch_ref, s32[16]{0:T(128)S(1)} %copy-done.6, bf16[16,8,8,2,1024]{4,3,2,1,0:T(2,128)(2,1)} %room_hbm.1, bf16[384,256]{1,0:T(8,128)(2,1)} %constant.37.clone.table_hbm), custom_call_target="tpu_custom_call" | custom-call | flops 1048576 | bytes 65536 | tf_op jit(solution)/shard_map/pallas_call | solution.py:154
  12.7 0.0 collective-permute-done.3.refs_1_
  12.7 0.0 copy-done.1
  12.8 0.0 copy-done.3
  12.8 0.0 copy-done.4
  12.8 1.7 %shard_map.101.refs_0_ = bf16[8,4,96,128]{3,2,1,0:T(8,128)(2,1)S(1)} custom-call(bf16[40,2,1024]{2,1,0:T(2,128)(2,1)S(1)} %bitcast.12, bf16[40,2,1024]{2,1,0:T(2,128)(2,1)S(1)} %collective-permute-done.3.refs_1_, bf16[2,8,1024,128]{3,2,1,0:T(8,128)(2,1)S(1)} %copy-done.1, bf16[2,192,160]{2,1,0:T(8,128)(2,1)S(1)} %copy-done.3), custom_call_target="tpu_custom_call" | custom-call | flops 1048576 | bytes 65536 | tf_op jit(solution)/shard_map/pallas_call | solution.py:210
  14.4 1.0 %shard_map.102.refs_2_ = f32[8,4,192,128]{3,2,1,0:T(8,128)S(1)} custom-call(s32[1]{0:T(128)} %bitcast.1.src_ref, s32[1]{0:T(128)} %bitcast.ch_ref, bf16[8,4,96,128]{3,2,1,0:T(8,128)(2,1)S(1)} %shard_map.101.refs_0_, bf16[16,8,384,128]{3,2,1,0:T(8,128)(2,1)S(1)} %shard_map.100.refs_1_), custom_call_target="tpu_custom_call" | custom-call | flops 1048576 | bytes 65536 | tf_op jit(solution)/shard_map/pallas_call | solution.py:344
  15.5 0.0 copy-start.7
  15.5 1.0 %collective-permute-done.refs_0_ = bf16[40,2,1024]{2,1,0:T(2,128)(2,1)S(1)} collective-permute-done((bf16[40,2,1024]{2,1,0:T(2,128)(2,1)}, bf16[40,2,1024]{2,1,0:T(2,128)(2,1)S(1)}, u32[]{:S(2)}, u32[]{:S(2)}) %collective-permute-start) | collective-permute-done | bytes 163872 | tf_op jit(solution)/shard_map/ppermute | solution.py:400
  16.4 0.0 collective-permute-done.1.refs_1_
  16.4 1.1 %collective-permute-done.2.refs_2_ = bf16[40,2,1024]{2,1,0:T(2,128)(2,1)S(1)} collective-permute-done((bf16[40,2,1024]{2,1,0:T(2,128)(2,1)}, bf16[40,2,1024]{2,1,0:T(2,128)(2,1)S(1)}, u32[]{:S(2)}, u32[]{:S(2)}) %collective-permute-start.2) | collective-permute-done | bytes 163872 | tf_op jit(solution)/shard_map/ppermute | solution.py:400
  17.5 2.1 %shard_map.103.refs_0_ = bf16[8,6,96,128]{3,2,1,0:T(8,128)(2,1)S(1)} custom-call(bf16[40,2,1024]{2,1,0:T(2,128)(2,1)S(1)} %collective-permute-done.refs_0_, bf16[40,2,1024]{2,1,0:T(2,128)(2,1)S(1)} %collective-permute-done.1.refs_1_, bf16[40,2,1024]{2,1,0:T(2,128)(2,1)S(1)} %collective-permute-done.2.refs_2_, bf16[2,8,1024,128]{3,2,1,0:T(8,128)(2,1)S(1)} %copy-done.1, ...), custom_call_target="tpu_custom_call" | custom-call | flops 1048576 | bytes 65536 | tf_op jit(solution)/shard_map/pallas_call | solution.py:210
  19.6 0.1 collective-permute-start.4
  19.7 0.0 copy-done.7
  19.7 0.0 copy-start.2
  19.7 0.0 copy-start.5
  19.7 1.9 %shard_map.104.refs_2_ = f32[8,4,192,128]{3,2,1,0:T(8,128)S(1)} custom-call(s32[1]{0:T(128)} %bitcast.1.src_ref, s32[1]{0:T(128)} %bitcast.ch_ref, bf16[8,6,96,128]{3,2,1,0:T(8,128)(2,1)S(1)} %shard_map.103.refs_0_, bf16[16,8,384,128]{3,2,1,0:T(8,128)(2,1)S(1)} %shard_map.100.refs_1_, ...), custom_call_target="tpu_custom_call", output_to_operand_aliasing={{}: (4, {})} | custom-call | flops 1048576 | bytes 65536 | tf_op jit(solution)/shard_map/pallas_call | solution.py:344
  21.6 0.9 %collective-permute-done.4.refs_0_ = bf16[8,6,96,128]{3,2,1,0:T(8,128)(2,1)S(1)} collective-permute-done((bf16[8,6,96,128]{3,2,1,0:T(8,128)(2,1)S(1)}, bf16[8,6,96,128]{3,2,1,0:T(8,128)(2,1)S(1)}, u32[]{:S(2)}, u32[]{:S(2)}) %collective-permute-start.4) | collective-permute-done | bytes 1179680 | tf_op jit(solution)/shard_map/ppermute | solution.py:400
  22.5 0.0 copy-done.2
  22.5 0.0 copy-done.5
  22.5 4.0 %shard_map.105 = (bf16[8,8,1024]{2,1,0:T(8,128)(2,1)S(1)}, bf16[8,8,1024]{2,1,0:T(8,128)(2,1)S(1)}, bf16[8,8,1024]{2,1,0:T(8,128)(2,1)S(1)}, bf16[8,8,1024]{2,1,0:T(8,128)(2,1)S(1)}) custom-call(s32[1]{0:T(128)} %bitcast.1.src_ref, s32[1]{0:T(128)} %bitcast.ch_ref, bf16[8,6,96,128]{3,2,1,0:T(8,128)(2,1)S(1)} %collective-permute-done.4.refs_0_, ...), custom_call_target="tpu_custom_call" | custom-call | flops 1048576 | bytes 65536 | tf_op jit(solution)/shard_map/pallas_call | solution.py:344
  26.5 2.6 %collective-permute-start.5 = (bf16[8,8,1024]{2,1,0:T(8,128)(2,1)S(1)}, bf16[8,8,1024]{2,1,0:T(8,128)(2,1)S(1)}, u32[]{:S(2)}, u32[]{:S(2)}) collective-permute-start(bf16[8,8,1024]{2,1,0:T(8,128)(2,1)S(1)} %get-tuple-element.30), channel_id=1, source_target_pairs={{0,24},{8,16},{16,8},{24,0},{1,25},{9,17},{17,9},{25,1},{2,26},{10... | collective-permute-start | bytes 393224 | tf_op jit(solution)/shard_map/ppermute | solution.py:400
  29.1 0.5 %collective-permute-start.6 = (bf16[8,8,1024]{2,1,0:T(8,128)(2,1)S(1)}, bf16[8,8,1024]{2,1,0:T(8,128)(2,1)S(1)}, u32[]{:S(2)}, u32[]{:S(2)}) collective-permute-start(bf16[8,8,1024]{2,1,0:T(8,128)(2,1)S(1)} %get-tuple-element.31), channel_id=1, source_target_pairs={{0,16},{8,24},{16,0},{24,8},{1,17},{9,25},{17,1},{25,9},{2,18},{10... | collective-permute-start | bytes 393224 | tf_op jit(solution)/shard_map/ppermute | solution.py:400
  29.6 0.5 collective-permute-start.7
  30.1 0.0 copy-done
  30.1 0.2 convolution_convert_fusion.1
  30.3 2.9 %collective-permute-done.5.refs_1_ = bf16[8,8,1024]{2,1,0:T(8,128)(2,1)S(1)} collective-permute-done((bf16[8,8,1024]{2,1,0:T(8,128)(2,1)S(1)}, bf16[8,8,1024]{2,1,0:T(8,128)(2,1)S(1)}, u32[]{:S(2)}, u32[]{:S(2)}) %collective-permute-start.5) | collective-permute-done | bytes 131104 | tf_op jit(solution)/shard_map/ppermute | solution.py:400
  33.2 2.6 %collective-permute-done.6.refs_2_ = bf16[8,8,1024]{2,1,0:T(8,128)(2,1)S(1)} collective-permute-done((bf16[8,8,1024]{2,1,0:T(8,128)(2,1)S(1)}, bf16[8,8,1024]{2,1,0:T(8,128)(2,1)S(1)}, u32[]{:S(2)}, u32[]{:S(2)}) %collective-permute-start.6) | collective-permute-done | bytes 131104 | tf_op jit(solution)/shard_map/ppermute | solution.py:400
  35.8 0.1 collective-permute-done.7.refs_3_
  36.0 0.5 shard_map.106
  36.4 0.1 collective-permute-start.8
  36.5 1.2 %collective-permute-done.8 = bf16[32,1024]{1,0:T(8,128)(2,1)S(1)} collective-permute-done((bf16[32,1024]{1,0:T(8,128)(2,1)S(1)}, bf16[32,1024]{1,0:T(8,128)(2,1)S(1)}, u32[]{:S(2)}, u32[]{:S(2)}) %collective-permute-start.8) | collective-permute-done | bytes 65568 | tf_op jit(solution)/shard_map/ppermute | solution.py:400
  37.8 3.6 %collective-permute-start.11 = (bf16[16,1024]{1,0:T(8,128)(2,1)S(1)}, bf16[16,1024]{1,0:T(8,128)(2,1)S(1)}, u32[]{:S(2)}, u32[]{:S(2)}) collective-permute-start(bf16[16,1024]{1,0:T(8,128)(2,1)S(1)} %pad_maximum_fusion.3), channel_id=1, source_target_pairs={{0,6},{1,7},{2,4},{3,5},{4,2},{5,3},{6,0},{7,1},{8,14},{9,15},{10,... | collective-permute-start | bytes 98312 | tf_op jit(solution)/shard_map/ppermute | solution.py:400
  41.3 1.4 %collective-permute-start.9 = (bf16[16,1024]{1,0:T(8,128)(2,1)S(1)}, bf16[16,1024]{1,0:T(8,128)(2,1)S(1)}, u32[]{:S(2)}, u32[]{:S(2)}) collective-permute-start(bf16[16,1024]{1,0:T(8,128)(2,1)S(1)} %pad_maximum_fusion.1), channel_id=1, source_target_pairs={{0,4},{1,5},{2,6},{3,7},{4,0},{5,1},{6,2},{7,3},{8,12},{9,13},{10,... | collective-permute-start | bytes 98312 | tf_op jit(solution)/shard_map/ppermute | solution.py:400
  42.7 0.5 %collective-permute-start.10 = (bf16[16,1024]{1,0:T(8,128)(2,1)S(1)}, bf16[16,1024]{1,0:T(8,128)(2,1)S(1)}, u32[]{:S(2)}, u32[]{:S(2)}) collective-permute-start(bf16[16,1024]{1,0:T(8,128)(2,1)S(1)} %pad_maximum_fusion.2), channel_id=1, source_target_pairs={{0,2},{1,3},{2,0},{3,1},{4,6},{5,7},{6,4},{7,5},{8,10},{9,11},{10,... | collective-permute-start | bytes 98312 | tf_op jit(solution)/shard_map/ppermute | solution.py:400
  43.3 3.3 %collective-permute-done.9 = bf16[16,1024]{1,0:T(8,128)(2,1)S(1)} collective-permute-done((bf16[16,1024]{1,0:T(8,128)(2,1)S(1)}, bf16[16,1024]{1,0:T(8,128)(2,1)S(1)}, u32[]{:S(2)}, u32[]{:S(2)}) %collective-permute-start.9) | collective-permute-done | bytes 32800 | tf_op jit(solution)/shard_map/ppermute | solution.py:400
  46.6 0.1 collective-permute-done.10
  46.7 0.0 collective-permute-done.11
  46.7 2.1 %convolution_convert_fusion = bf16[1024,1024]{1,0:T(8,128)(2,1)} fusion(bf16[64,1024]{1,0:T(8,128)(2,1)S(1)} %constant_dynamic-update-slice_fusion, bf16[64,1024]{1,0:T(8,128)(2,1)S(1)} %convolution_convert_fusion.1), kind=kOutput, calls=%fused_computation | convolution fusion | flops 135266304 | bytes 2359296 | tf_op jit(solution)/shard_map/dot_general | solution.py:380
  (11 shorter events, 0.0 us)
Async XLA Ops:
  0.0 30.1 %copy-start = (bf16[64,1024]{1,0:T(8,128)(2,1)S(1)}, bf16[64,1024]{1,0:T(8,128)(2,1)}, u32[]{:S(2)}) copy-start(bf16[64,1024]{1,0:T(8,128)(2,1)} %param.13) | copy-start | bytes 393220
  0.0 12.7 %collective-permute-start.3 = (bf16[40,2,1024]{2,1,0:T(2,128)(2,1)}, bf16[40,2,1024]{2,1,0:T(2,128)(2,1)S(1)}, u32[]{:S(2)}, u32[]{:S(2)}) collective-permute-start(bf16[40,2,1024]{2,1,0:T(2,128)(2,1)} %bitcast.8), channel_id=1, source_target_pairs={{0,1},{1,0},{2,3},{3,2},{4,5},{5,4},{6,7},{7,6},{8,9},{9,8},{10,11... | collective-permute-start | bytes 491528 | tf_op jit(solution)/shard_map/ppermute | solution.py:400
  0.5 16.0 %collective-permute-start = (bf16[40,2,1024]{2,1,0:T(2,128)(2,1)}, bf16[40,2,1024]{2,1,0:T(2,128)(2,1)S(1)}, u32[]{:S(2)}, u32[]{:S(2)}) collective-permute-start(bf16[40,2,1024]{2,1,0:T(2,128)(2,1)} %bitcast.9), channel_id=1, source_target_pairs={{0,4},{1,5},{2,6},{3,7},{4,0},{5,1},{6,2},{7,3},{8,12},{9,13},{10,... | collective-permute-start | bytes 491528 | tf_op jit(solution)/shard_map/ppermute | solution.py:400
  4.1 12.3 %collective-permute-start.1 = (bf16[40,2,1024]{2,1,0:T(2,128)(2,1)}, bf16[40,2,1024]{2,1,0:T(2,128)(2,1)S(1)}, u32[]{:S(2)}, u32[]{:S(2)}) collective-permute-start(bf16[40,2,1024]{2,1,0:T(2,128)(2,1)} %bitcast.10), channel_id=1, source_target_pairs={{0,6},{1,7},{2,4},{3,5},{4,2},{5,3},{6,0},{7,1},{8,14},{9,15},{10,... | collective-permute-start | bytes 491528 | tf_op jit(solution)/shard_map/ppermute | solution.py:400
  5.5 12.0 %collective-permute-start.2 = (bf16[40,2,1024]{2,1,0:T(2,128)(2,1)}, bf16[40,2,1024]{2,1,0:T(2,128)(2,1)S(1)}, u32[]{:S(2)}, u32[]{:S(2)}) collective-permute-start(bf16[40,2,1024]{2,1,0:T(2,128)(2,1)} %bitcast.11), channel_id=1, source_target_pairs={{0,2},{1,3},{2,0},{3,1},{4,6},{5,7},{6,4},{7,5},{8,10},{9,11},{10,... | collective-permute-start | bytes 491528 | tf_op jit(solution)/shard_map/ppermute | solution.py:400
  5.7 0.7 %copy-start.6 = (s32[16]{0:T(128)S(1)}, s32[16]{0:T(128)}, u32[]{:S(2)}) copy-start(s32[16]{0:T(128)} %slot_ref.1) | copy-start | bytes 196
  6.3 6.4 %copy-start.1 = (bf16[2,8,1024,128]{3,2,1,0:T(8,128)(2,1)S(1)}, bf16[2,8,1024,128]{3,2,1,0:T(8,128)(2,1)}, u32[]{:S(2)}) copy-start(bf16[2,8,1024,128]{3,2,1,0:T(8,128)(2,1)} %constant.39.clone.refs_2_.refs_3_) | copy-start | bytes 12582916
  6.3 6.4 %copy-start.3 = (bf16[2,192,160]{2,1,0:T(8,128)(2,1)S(1)}, bf16[2,192,160]{2,1,0:T(8,128)(2,1)}, u32[]{:S(2)}) copy-start(bf16[2,192,160]{2,1,0:T(8,128)(2,1)} %constant.40.clone.refs_3_.refs_4_) | copy-start | bytes 368644
  6.4 6.4 %copy-start.4 = (bf16[2,40960]{1,0:T(2,128)(2,1)S(1)}, bf16[2,40960]{1,0:T(2,128)(2,1)}, u32[]{:S(2)}) copy-start(bf16[2,40960]{1,0:T(2,128)(2,1)} %param.10) | copy-start | bytes 491524
  15.5 4.2 %copy-start.7 = (s32[64]{0:T(128)S(1)}, s32[64]{0:T(128)}, u32[]{:S(2)}) copy-start(s32[64]{0:T(128)} %constant.38.clone) | copy-start | bytes 772
  19.6 2.9 %collective-permute-start.4 = (bf16[8,6,96,128]{3,2,1,0:T(8,128)(2,1)S(1)}, bf16[8,6,96,128]{3,2,1,0:T(8,128)(2,1)S(1)}, u32[]{:S(2)}, u32[]{:S(2)}) collective-permute-start(bf16[8,6,96,128]{3,2,1,0:T(8,128)(2,1)S(1)} %shard_map.103.refs_0_), channel_id=1, source_target_pairs={{0,1},{1,0},{2,3},{3,2},{4,5},{5,4},{6,7},{7,6},{8,9},{9,8},{10,11... | collective-permute-start | bytes 3538952 | tf_op jit(solution)/shard_map/ppermute | solution.py:400
  19.7 2.8 %copy-start.2 = (bf16[2,8,1024,128]{3,2,1,0:T(8,128)(2,1)S(1)}, bf16[2,8,1024,128]{3,2,1,0:T(8,128)(2,1)}, u32[]{:S(2)}) copy-start(bf16[2,8,1024,128]{3,2,1,0:T(8,128)(2,1)} %constant.42.clone.refs_4_) | copy-start | bytes 12582916
  19.7 2.8 %copy-start.5 = (bf16[2,128,192]{2,1,0:T(8,128)(2,1)S(1)}, bf16[2,128,192]{2,1,0:T(8,128)(2,1)}, u32[]{:S(2)}) copy-start(bf16[2,128,192]{2,1,0:T(8,128)(2,1)} %constant.41.clone.refs_3_) | copy-start | bytes 294916
  26.5 6.7 %collective-permute-start.5 = (bf16[8,8,1024]{2,1,0:T(8,128)(2,1)S(1)}, bf16[8,8,1024]{2,1,0:T(8,128)(2,1)S(1)}, u32[]{:S(2)}, u32[]{:S(2)}) collective-permute-start(bf16[8,8,1024]{2,1,0:T(8,128)(2,1)S(1)} %get-tuple-element.30), channel_id=1, source_target_pairs={{0,24},{8,16},{16,8},{24,0},{1,25},{9,17},{17,9},{25,1},{2,26},{10... | collective-permute-start | bytes 393224 | tf_op jit(solution)/shard_map/ppermute | solution.py:400
  29.1 6.7 %collective-permute-start.6 = (bf16[8,8,1024]{2,1,0:T(8,128)(2,1)S(1)}, bf16[8,8,1024]{2,1,0:T(8,128)(2,1)S(1)}, u32[]{:S(2)}, u32[]{:S(2)}) collective-permute-start(bf16[8,8,1024]{2,1,0:T(8,128)(2,1)S(1)} %get-tuple-element.31), channel_id=1, source_target_pairs={{0,16},{8,24},{16,0},{24,8},{1,17},{9,25},{17,1},{25,9},{2,18},{10... | collective-permute-start | bytes 393224 | tf_op jit(solution)/shard_map/ppermute | solution.py:400
  29.6 6.4 %collective-permute-start.7 = (bf16[8,8,1024]{2,1,0:T(8,128)(2,1)S(1)}, bf16[8,8,1024]{2,1,0:T(8,128)(2,1)S(1)}, u32[]{:S(2)}, u32[]{:S(2)}) collective-permute-start(bf16[8,8,1024]{2,1,0:T(8,128)(2,1)S(1)} %get-tuple-element.32), channel_id=1, source_target_pairs={{0,8},{8,0},{16,24},{24,16},{1,9},{9,1},{17,25},{25,17},{2,10},{10... | collective-permute-start | bytes 393224 | tf_op jit(solution)/shard_map/ppermute | solution.py:400
  36.4 1.3 %collective-permute-start.8 = (bf16[32,1024]{1,0:T(8,128)(2,1)S(1)}, bf16[32,1024]{1,0:T(8,128)(2,1)S(1)}, u32[]{:S(2)}, u32[]{:S(2)}) collective-permute-start(bf16[32,1024]{1,0:T(8,128)(2,1)S(1)} %pad_maximum_fusion), channel_id=1, source_target_pairs={{0,1},{1,0},{2,3},{3,2},{4,5},{5,4},{6,7},{7,6},{8,9},{9,8},{10,11... | collective-permute-start | bytes 196616 | tf_op jit(solution)/shard_map/ppermute | solution.py:400
  37.8 8.9 %collective-permute-start.11 = (bf16[16,1024]{1,0:T(8,128)(2,1)S(1)}, bf16[16,1024]{1,0:T(8,128)(2,1)S(1)}, u32[]{:S(2)}, u32[]{:S(2)}) collective-permute-start(bf16[16,1024]{1,0:T(8,128)(2,1)S(1)} %pad_maximum_fusion.3), channel_id=1, source_target_pairs={{0,6},{1,7},{2,4},{3,5},{4,2},{5,3},{6,0},{7,1},{8,14},{9,15},{10,... | collective-permute-start | bytes 98312 | tf_op jit(solution)/shard_map/ppermute | solution.py:400
  41.3 5.3 %collective-permute-start.9 = (bf16[16,1024]{1,0:T(8,128)(2,1)S(1)}, bf16[16,1024]{1,0:T(8,128)(2,1)S(1)}, u32[]{:S(2)}, u32[]{:S(2)}) collective-permute-start(bf16[16,1024]{1,0:T(8,128)(2,1)S(1)} %pad_maximum_fusion.1), channel_id=1, source_target_pairs={{0,4},{1,5},{2,6},{3,7},{4,0},{5,1},{6,2},{7,3},{8,12},{9,13},{10,... | collective-permute-start | bytes 98312 | tf_op jit(solution)/shard_map/ppermute | solution.py:400
  42.7 4.0 %collective-permute-start.10 = (bf16[16,1024]{1,0:T(8,128)(2,1)S(1)}, bf16[16,1024]{1,0:T(8,128)(2,1)S(1)}, u32[]{:S(2)}, u32[]{:S(2)}) collective-permute-start(bf16[16,1024]{1,0:T(8,128)(2,1)S(1)} %pad_maximum_fusion.2), channel_id=1, source_target_pairs={{0,2},{1,3},{2,0},{3,1},{4,6},{5,7},{6,4},{7,5},{8,10},{9,11},{10,... | collective-permute-start | bytes 98312 | tf_op jit(solution)/shard_map/ppermute | solution.py:400
